TPU v7x, 32 devices: a whole 2x2x4 slice. The times are simulated.
32 devices in a mesh: tile: 4 (over y, core), freq: 8 (over z, x).
Axes of the slice: x: 2, y: 2, z: 4, core: 2. Of those that a mesh axis runs over, the one named last changes fastest.
Arguments:
- sensitivity: float32 [4, 32, 2, 1024, 512], P('tile', 'freq'), may hold values from -0.25 to 0.25
- models: float32 [1024, 256], P(('tile', 'freq')), may hold values from -6 to 6
- observed: float32 [4, 40, 1024], P('tile', None, 'freq'), may hold values from -6 to 6
- waveform: float32 [128], replicated, may hold values from -0.5 to 0.5
- cell_index: int32 [4, 512], P('tile'), may hold values from 0 to 1023, as said below
- gate_index: int32 [40], replicated, may hold values from 10 to 127, as said below
Outputs:
- updated: float32 [1024, 256], P(('tile', 'freq'))
- misfit: float32 [256], replicated
Inputs may be any that keep to these rules, and one draw needn't show every extreme that they name: `cell_index`: each tile's indices are distinct. Tile t holds, in some order, the 256 global cells from t * 256 on and the 256 cells of one other tile's block (from u * 256 on, u != t). Every global cell belongs to one or more tiles. `gate_index`: strictly increasing; the last gate is sample 128 - 1.
All inputs are finite; a program needn't handle non-finite values.
Results may differ from a plain program's by a relative error of at most 0.00017.
Values sent between devices are 32-bit elements; how exact they have to be, the bound alone decides.
No kernel may reach another device: no remote copies, remote signals or barrier semaphores. Data moves between devices by JAX's collectives and lax.ppermute only.
A program may use at most 64 MiB of HBM per device.

v0:
```python
import functools
import math

import jax
import jax.numpy as jnp
from jax import lax
from jax.experimental import pallas as pl
from jax.experimental.pallas import tpu as pltpu
from jax.sharding import PartitionSpec as P

HIGH = lax.Precision.HIGHEST
PHASE_RATE = 0.37
STEP_LENGTH = 0.5
EPSILON = 1e-06
GROUP = 8
LANES = 128
CHUNKS = 4

NN = (((1,), (0,)), ((), ()))
NT = (((1,), (1,)), ((), ()))


def gate_table(freqs, waveform, gate_index):
    samples = waveform.shape[0]
    freq_col = jnp.arange(freqs, dtype=jnp.float32)[:, None] + 0.5
    time_row = jnp.arange(samples, dtype=jnp.float32)[None, :] + 0.5
    phases = PHASE_RATE * freq_col * time_row
    kernel = jnp.stack([jnp.cos(phases), jnp.sin(phases)], axis=1) / math.sqrt(freqs)
    steps = jnp.arange(samples)
    lag = gate_index[:, None] - steps[None, :]
    picked = jnp.sum(
        jnp.where(lag[:, :, None] == steps[None, None, :], waveform[None, None, :], 0.0), axis=-1
    )
    return jnp.einsum("gk,fpk->gfp", picked, kernel, precision=HIGH).reshape(gate_index.shape[0], freqs * 2)


def split(x):
    high = x.astype(jnp.bfloat16)
    return high, (x - high.astype(jnp.float32)).astype(jnp.bfloat16)


def split_outside(x):
    high = lax.reduce_precision(x, 8, 7)
    return high.astype(jnp.bfloat16), (x - high).astype(jnp.bfloat16)


def three_pass(a, b, dims):
    dot = functools.partial(lax.dot_general, dimension_numbers=dims, preferred_element_type=jnp.float32)
    return dot(a[0], b[0]) + (dot(a[0], b[1]) + dot(a[1], b[0]))


def chunk_kernel(sens_ref, model_h, model_l, gate_h, gate_l, obs_ref, terms_in, square_in, terms_ref, square_ref):
    @pl.when(pl.program_id(0) == 0)
    def _():
        terms_ref[...] = terms_in[...]
        square_ref[...] = square_in[...]

    rows = sens_ref.shape[0] * sens_ref.shape[1]
    sens = split(sens_ref[...].reshape(rows, sens_ref.shape[2]))
    gates = (gate_h[...], gate_l[...])
    predicted = three_pass((model_h[...], model_l[...]), sens, NT)
    misfit_rows = three_pass(split(predicted), gates, NN) - obs_ref[0]
    square_ref[...] += jnp.sum(misfit_rows * misfit_rows, axis=1, keepdims=True)
    back = three_pass(split(misfit_rows), gates, NT)
    terms_ref[...] += three_pass(split(back), sens, NN)


def chunk_step(sens, models_t, gates, obs, terms, square):
    spectra, soundings, cells = sens.shape
    groups = soundings // GROUP
    members = terms.shape[0]
    whole = lambda a: pl.BlockSpec(a.shape, lambda i: (0,) * a.ndim)
    return pl.pallas_call(
        chunk_kernel,
        grid=(groups,),
        in_specs=[pl.BlockSpec((spectra, GROUP, cells), lambda i: (0, i, 0))]
        + [whole(a) for a in (*models_t, *gates)]
        + [pl.BlockSpec((1, 1, obs.shape[2]), lambda i: (i, 0, 0)), whole(terms), whole(square)],
        out_specs=[whole(terms), whole(square)],
        out_shape=[
            jax.ShapeDtypeStruct(terms.shape, jnp.float32),
            jax.ShapeDtypeStruct(square.shape, jnp.float32),
        ],
        input_output_aliases={6: 0, 7: 1},
        compiler_params=pltpu.CompilerParams(
            dimension_semantics=("arbitrary",), vmem_limit_bytes=40 * 1024 * 1024
        ),
        cost_estimate=pl.CostEstimate(
            flops=12 * spectra * soundings * cells * members * 2,
            bytes_accessed=4 * spectra * soundings * cells,
            transcendentals=0,
        ),
        name="chunk_step",
    )(sens, *models_t, *gates, obs, terms, square)


def body(sensitivity, models, observed, waveform, cell_index, gate_index):
    both = ("tile", "freq")
    tiles, owners, devices = lax.axis_size("tile"), lax.axis_size("freq"), lax.axis_size(both)
    _, own_freqs, parts, soundings, cells = sensitivity.shape
    freqs = own_freqs * owners
    owned, members = models.shape
    ncells = owned * devices
    gates = gate_index.shape[0]
    total = tiles * soundings * gates
    own_soundings = soundings // owners
    per_chunk = own_soundings // CHUNKS
    block_cells = owned * owners
    me = lax.axis_index("tile")

    block = sensitivity[0].reshape(own_freqs * parts, owners, CHUNKS, per_chunk, cells)
    received = []
    for k in range(CHUNKS):
        piece = jnp.swapaxes(block[:, :, k], 0, 1)
        received.append(lax.all_to_all(piece, "freq", split_axis=0, concat_axis=0, tiled=True))

    tile_cells = cell_index[0]
    home = tile_cells // block_cells
    borrowed_from = jnp.max(jnp.where(home == me, -1, home))
    all_models = lax.all_gather(models, both, axis=0, tiled=True)
    models_t = split_outside(jnp.take(all_models, tile_cells, axis=0).T)
    all_borrowed = lax.all_gather(borrowed_from.reshape(1), "tile", axis=0, tiled=True)

    table = gate_table(freqs, waveform, gate_index).T
    wide = table[:, None, :, None] * jnp.eye(GROUP, dtype=jnp.float32)[None, :, None, :]
    wide = split_outside(wide.reshape(freqs * parts * GROUP, gates * GROUP))
    obs = observed[0].reshape(gates, own_soundings // GROUP, GROUP)
    obs = jnp.swapaxes(obs, 0, 1).reshape(own_soundings // GROUP, 1, gates * GROUP)

    terms = jnp.zeros((members, cells), jnp.float32)
    square = jnp.zeros((members, LANES), jnp.float32)
    groups = per_chunk // GROUP
    for k in range(CHUNKS):
        sens = received[k].reshape(freqs * parts, per_chunk, cells)
        terms, square = chunk_step(sens, models_t, wide, obs[k * groups : (k + 1) * groups], terms, square)

    place = tile_cells % block_cells + jnp.where(home == me, 0, block_cells)
    order = (place[:, None] == jnp.arange(cells)[None, :]).astype(jnp.float32)
    terms = jnp.dot(terms, order, precision=HIGH)
    sent = jnp.concatenate([terms, square], axis=1).reshape(devices, members // devices, cells + LANES)
    got = lax.all_to_all(sent, both, split_axis=0, concat_axis=0, tiled=True)
    got = jnp.sum(got.reshape(tiles, owners, members // devices, cells + LANES), axis=1)
    lent = (all_borrowed[None, :] == jnp.arange(tiles)[:, None]).astype(jnp.float32)
    gradient = got[:, :, :block_cells] + jnp.sum(
        lent[:, :, None, None] * got[None, :, :, block_cells:cells], axis=1
    )
    misfit = jnp.sum(got[:, :, cells], axis=0) / (2.0 * total)
    scale = jnp.sqrt(jnp.sum(gradient * gradient, axis=(0, 2)) / ncells + EPSILON)
    step = STEP_LENGTH * (misfit / scale)[None, :, None] * gradient
    step = step.reshape(tiles, members // devices, owners, owned).transpose(0, 2, 1, 3)
    step = step.reshape(devices, members // devices, owned)
    spread = jnp.broadcast_to(misfit[None, :, None], (devices, members // devices, LANES - owned))
    back = lax.all_to_all(jnp.concatenate([step, spread], axis=2), both, split_axis=0, concat_axis=0, tiled=True)
    back = back.reshape(members, LANES)
    return (models - back[:, :owned].T, back[:, owned])


def solution(mesh):
    in_specs = (
        P("tile", "freq", None, None, None),
        P(("tile", "freq"), None),
        P("tile", None, "freq"),
        P(),
        P("tile", None),
        P(),
    )
    out_specs = (P(("tile", "freq"), None), P())
    return jax.shard_map(body, mesh=mesh, in_specs=in_specs, out_specs=out_specs, check_vma=False)
```

profile of v0, /device:TPU:0, one launch (start us, length us, event | category | flops | bytes accessed | tf_op | source)
XLA Modules:
  0.0 520.4 jit_solution(577772713732971157)
XLA Ops:
  7.2 11.4 %fusion.10 = (f32[8,8,1,32,512]{4,3,2,1,0:T(8,128)S(1)}, f32[8,8,1,32,512]{4,3,2,1,0:T(8,128)}, f32[8,8,1,32,512]{4,3,2,1,0:T(8,128)}, f32[8,8,1,32,512]{4,3,2,1,0:T(8,128)}) fusion(f32[8,8,4,32,512]{4,3,2,1,0:T(8,128)} %bitcast.56), kind=kLoop, calls=%fused_computation.56 | loop fusion | bytes 33554432 | tf_op jit(solution)/shard_map/slice | solution.py:114
  18.6 2.6 copy.126
  21.1 7.3 %all-to-all-start.3 = ((f32[8,8,32,512]{3,2,1,0:T(8,128)}), f32[8,8,32,512]{3,2,1,0:T(8,128)}, u32[]{:S(2)}, u32[]{:S(2)}) async-start(f32[8,8,32,512]{3,2,1,0:T(8,128)} %bitcast.60), calls=%async_computation.3 | async-start | bytes 8388608 | tf_op jit(solution)/shard_map/all_to_all | solution.py:115
  28.4 5.0 copy.127
  33.4 88.2 %all-to-all-done.3 = f32[8,8,32,512]{3,2,1,0:T(8,128)} async-done(((f32[8,8,32,512]{3,2,1,0:T(8,128)}), f32[8,8,32,512]{3,2,1,0:T(8,128)}, u32[]{:S(2)}, u32[]{:S(2)}) %all-to-all-start.3) | async-done | bytes 4194336 | tf_op jit(solution)/shard_map/all_to_all | solution.py:115
  121.7 4.6 all-to-all-start.2
  126.3 5.0 copy.128
  131.3 87.5 %all-to-all-done.2 = f32[8,8,32,512]{3,2,1,0:T(8,128)} async-done(((f32[8,8,32,512]{3,2,1,0:T(8,128)}), f32[8,8,32,512]{3,2,1,0:T(8,128)}, u32[]{:S(2)}, u32[]{:S(2)}) %all-to-all-start.2) | async-done | bytes 4194336 | tf_op jit(solution)/shard_map/all_to_all | solution.py:115
  218.8 4.6 all-to-all-start.1
  223.4 5.0 copy.129
  228.4 87.5 %all-to-all-done.1 = f32[8,8,32,512]{3,2,1,0:T(8,128)} async-done(((f32[8,8,32,512]{3,2,1,0:T(8,128)}), f32[8,8,32,512]{3,2,1,0:T(8,128)}, u32[]{:S(2)}, u32[]{:S(2)}) %all-to-all-start.1) | async-done | bytes 4194336 | tf_op jit(solution)/shard_map/all_to_all | solution.py:115
  315.9 4.7 all-to-all-start
  321.6 1.9 select_reduce_fusion
  323.7 5.4 %broadcast_multiply_fusion = f32[64,8,40,8]{1,0,3,2:T(8,128)} fusion(f32[8,8]{0,1:T(8,128)S(1)} %fusion.5, f32[64,40]{0,1:T(8,128)S(1)} %fusion.12), kind=kLoop, calls=%fused_computation.1 | loop fusion | flops 163840 | bytes 665856 | tf_op jit(solution)/shard_map/mul | solution.py:125
  329.1 8.4 %mul.100 = f32[512,320]{0,1:T(8,128)S(1)} reshape(f32[64,8,40,8]{1,0,3,2:T(8,128)} %broadcast_multiply_fusion) | data formatting | bytes 1310720 | tf_op jit(solution)/shard_map/mul | solution.py:125
  339.5 94.2 %all-gather.2.cloned.1.call-done = f32[1024,256]{1,0:T(8,128)} async-done(((f32[32,256]{1,0:T(8,128)}), f32[1024,256]{1,0:T(8,128)}) %all-gather.2.cloned.1.call-update) | async-done | bytes 1048592 | tf_op jit(solution)/shard_map/all_gather | solution.py:120
  433.7 2.8 gather_fusion
  436.9 9.8 %chunk_step.4 = (f32[256,512]{1,0:T(8,128)S(1)}, f32[256,128]{1,0:T(8,128)S(1)}) custom-call(f32[64,32,512]{2,1,0:T(8,128)} %bitcast.20.sens_ref, bf16[256,512]{1,0:T(8,128)(2,1)S(1)} %get-tuple-element.35.model_h, bf16[256,512]{1,0:T(8,128)(2,1)S(1)} %get-tuple-element.34.model_l, ...), custom_call_target="tpu_custom_call", output_to_operand_aliasing={{0}: (6, {}), {1}: (7, {})} | custom-call | flops 6442450944 | bytes 4194304 | tf_op jit(solution)/shard_map/chunk_step/pallas_call | solution.py:73
  446.6 9.8 %chunk_step.5 = (f32[256,512]{1,0:T(8,128)S(1)}, f32[256,128]{1,0:T(8,128)S(1)}) custom-call(f32[64,32,512]{2,1,0:T(8,128)} %bitcast.17.sens_ref, bf16[256,512]{1,0:T(8,128)(2,1)S(1)} %get-tuple-element.35.model_h, bf16[256,512]{1,0:T(8,128)(2,1)S(1)} %get-tuple-element.34.model_l, ...), custom_call_target="tpu_custom_call", output_to_operand_aliasing={{0}: (6, {}), {1}: (7, {})} | custom-call | flops 6442450944 | bytes 4194304 | tf_op jit(solution)/shard_map/chunk_step/pallas_call | solution.py:73
  456.4 9.8 %chunk_step.6 = (f32[256,512]{1,0:T(8,128)S(1)}, f32[256,128]{1,0:T(8,128)S(1)}) custom-call(f32[64,32,512]{2,1,0:T(8,128)} %bitcast.13.sens_ref, bf16[256,512]{1,0:T(8,128)(2,1)S(1)} %get-tuple-element.35.model_h, bf16[256,512]{1,0:T(8,128)(2,1)S(1)} %get-tuple-element.34.model_l, ...), custom_call_target="tpu_custom_call", output_to_operand_aliasing={{0}: (6, {}), {1}: (7, {})} | custom-call | flops 6442450944 | bytes 4194304 | tf_op jit(solution)/shard_map/chunk_step/pallas_call | solution.py:73
  466.2 9.7 %chunk_step.7 = (f32[256,512]{1,0:T(8,128)S(1)}, f32[256,128]{1,0:T(8,128)S(1)}) custom-call(f32[64,32,512]{2,1,0:T(8,128)} %bitcast.3.sens_ref, bf16[256,512]{1,0:T(8,128)(2,1)S(1)} %get-tuple-element.35.model_h, bf16[256,512]{1,0:T(8,128)(2,1)S(1)} %get-tuple-element.34.model_l, ...), custom_call_target="tpu_custom_call", output_to_operand_aliasing={{0}: (6, {}), {1}: (7, {})} | custom-call | flops 6442450944 | bytes 4194304 | tf_op jit(solution)/shard_map/chunk_step/pallas_call | solution.py:73
  476.0 0.8 fusion
  476.8 0.9 maximum_bitcast_fusion
  477.6 3.6 all-to-all-start.4
  481.8 1.4 dynamic-update-slice
  483.2 5.5 %all-reduce = s32[4]{0:T(128)S(1)} all-reduce(s32[4]{0:T(128)S(1)} %dynamic-update-slice), channel_id=1, replica_groups=mesh['tile'=4,'freq'=8] {'tile'}, use_global_device_ids=true, to_apply=%add | all-reduce | flops 4 | bytes 32
  488.8 11.6 %all-to-all-done.4 = f32[32,8,640]{2,1,0:T(8,128)S(1)} async-done(((f32[32,8,640]{2,1,0:T(8,128)}), f32[32,8,640]{2,1,0:T(8,128)S(1)}, u32[]{:S(2)}, u32[]{:S(2)}) %all-to-all-start.4) | async-done | bytes 655392 | tf_op jit(solution)/shard_map/all_to_all | solution.py:141
  501.1 0.8 pad_maximum_fusion
  501.8 2.6 all-to-all-start.5
  504.5 7.6 %all-to-all-done.5 = f32[32,8,128]{2,1,0:T(8,128)S(1)} async-done(((f32[32,8,128]{2,1,0:T(8,128)}), f32[32,8,128]{2,1,0:T(8,128)S(1)}, u32[]{:S(2)}, u32[]{:S(2)}) %all-to-all-start.5) | async-done | bytes 131104 | tf_op jit(solution)/shard_map/all_to_all | solution.py:153
  512.1 0.7 slice_reduce_fusion
  512.9 0.7 copy.117
  (58 shorter events, 4.8 us)
Async XLA Ops:
  21.1 100.5 %all-to-all-start.3 = ((f32[8,8,32,512]{3,2,1,0:T(8,128)}), f32[8,8,32,512]{3,2,1,0:T(8,128)}, u32[]{:S(2)}, u32[]{:S(2)}) async-start(f32[8,8,32,512]{3,2,1,0:T(8,128)} %bitcast.60), calls=%async_computation.3 | async-start | bytes 8388608 | tf_op jit(solution)/shard_map/all_to_all | solution.py:115
  121.7 97.1 %all-to-all-start.2 = ((f32[8,8,32,512]{3,2,1,0:T(8,128)}), f32[8,8,32,512]{3,2,1,0:T(8,128)}, u32[]{:S(2)}, u32[]{:S(2)}) async-start(f32[8,8,32,512]{3,2,1,0:T(8,128)} %bitcast.59), calls=%async_computation.2 | async-start | bytes 8388608 | tf_op jit(solution)/shard_map/all_to_all | solution.py:115
  218.8 97.1 %all-to-all-start.1 = ((f32[8,8,32,512]{3,2,1,0:T(8,128)}), f32[8,8,32,512]{3,2,1,0:T(8,128)}, u32[]{:S(2)}, u32[]{:S(2)}) async-start(f32[8,8,32,512]{3,2,1,0:T(8,128)} %bitcast.58), calls=%async_computation.1 | async-start | bytes 8388608 | tf_op jit(solution)/shard_map/all_to_all | solution.py:115
  315.9 5.6 %copy-start.3 = (s32[40]{0:T(128)S(1)}, s32[40]{0:T(128)}, u32[]{:S(2)}) copy-start(s32[40]{0:T(128)} %param.11) | copy-start | bytes 484
  315.9 5.7 %copy-start.4 = (f32[128]{0:T(128)S(1)}, f32[128]{0:T(128)}, u32[]{:S(2)}) copy-start(f32[128]{0:T(128)} %param.9) | copy-start | bytes 1540
  315.9 150.3 %all-to-all-start = ((f32[8,8,32,512]{3,2,1,0:T(8,128)}), f32[8,8,32,512]{3,2,1,0:T(8,128)}, u32[]{:S(2)}, u32[]{:S(2)}) async-start(f32[8,8,32,512]{3,2,1,0:T(8,128)} %bitcast.57), calls=%async_computation | async-start | bytes 8388608 | tf_op jit(solution)/shard_map/all_to_all | solution.py:115
  320.6 113.1 %all-gather.2.cloned.1.call-start = ((), (), s32[]{:S(2)}) async-start(), calls=%async_computation.6 | async-start | bytes 1081344 | tf_op jit(solution)/shard_map/all_gather | solution.py:120
  329.1 8.7 %copy-start.1 = (f32[1,40,128]{2,1,0:T(8,128)S(1)}, f32[1,40,128]{2,1,0:T(8,128)}, u32[]{:S(2)}) copy-start(f32[1,40,128]{2,1,0:T(8,128)} %param.8) | copy-start | bytes 61444
  329.1 9.6 %copy-start.2 = (s32[1,512]{1,0:T(1,128)S(1)}, s32[1,512]{1,0:T(1,128)}, u32[]{:S(2)}) copy-start(s32[1,512]{1,0:T(1,128)} %param.10) | copy-start | bytes 6148
  466.2 15.0 %copy-start.5 = (u32[32]{0:T(128)S(1)}, u32[32]{0:T(128)}, u32[]{:S(2)}) copy-start(u32[32]{0:T(128)} %constant.78) | copy-start | bytes 388
  476.0 28.4 %copy-start = (f32[32,256]{1,0:T(8,128)S(1)}, f32[32,256]{1,0:T(8,128)}, u32[]{:S(2)}) copy-start(f32[32,256]{1,0:T(8,128)} %param.7) | copy-start | bytes 98308
  477.6 22.7 %all-to-all-start.4 = ((f32[32,8,640]{2,1,0:T(8,128)}), f32[32,8,640]{2,1,0:T(8,128)S(1)}, u32[]{:S(2)}, u32[]{:S(2)}) async-start(f32[32,8,640]{2,1,0:T(8,128)} %maximum_bitcast_fusion), calls=%async_computation.4 | async-start | bytes 1310720 | tf_op jit(solution)/shard_map/all_to_all | solution.py:141
  501.8 10.3 %all-to-all-start.5 = ((f32[32,8,128]{2,1,0:T(8,128)}), f32[32,8,128]{2,1,0:T(8,128)S(1)}, u32[]{:S(2)}, u32[]{:S(2)}) async-start(f32[32,8,128]{2,1,0:T(8,128)} %pad_maximum_fusion), calls=%async_computation.5 | async-start | bytes 262144 | tf_op jit(solution)/shard_map/all_to_all | solution.py:153
Sparse Core Ops, SparseCore 0:
  324.5 109.1 all-gather.1
where the time goes:
time: 521 us; the launch traced here: 520 us
  waiting for transfers between devices  377 us (72%)
  local copies, waits for them, and re-layouts  45.5 us (9%)
  Pallas kernels  39 us (7%)
  starting transfers between devices  27.4 us (5%)
  between operations  14.4 us (3%)
  other arithmetic  10.4 us (2%)
  blocking collectives  5.53 us (1%)
    all_to_all x4, waiting for transfers between devices, body(): lax.all_to_all(piece, 'freq', split_axis=0, concat_axis=0, tiled=True)  263 us
    all_gather x1, waiting for transfers between devices, body(): all_models = lax.all_gather(models, both, axis=0, tiled=True)  94.2 us
    pallas_call x4, Pallas kernels, chunk_step(): pl.pallas_call(chunk_kernel, grid=(groups,), in_specs=[pl.BlockSpec((spec...  39 us
    all_to_all x4, starting transfers between devices, body(): lax.all_to_all(piece, 'freq', split_axis=0, concat_axis=0, tiled=True)  21.1 us
    unnamed x22, local copies, waits for them, and re-layouts  20.6 us
    all_to_all x1, waiting for transfers between devices, body(): got = lax.all_to_all(sent, both, split_axis=0, concat_axis=0, tiled=True)  11.6 us
    slice x1, local copies, waits for them, and re-layouts, body(): piece = jnp.swapaxes(block[:, :, k], 0, 1)  11.4 us
  transfers between devices with their start and end apart: 7, of which 6 were waited for; matrix products, arithmetic and copies ran while one was open for 7% of the time, Pallas kernels for 6%

commit v1 on v0

v1 whole, which is shorter than its diff:
```python
import functools
import math

import jax
import jax.numpy as jnp
from jax import lax
from jax.experimental import pallas as pl
from jax.experimental.pallas import tpu as pltpu
from jax.sharding import PartitionSpec as P

HIGH = lax.Precision.HIGHEST
PHASE_RATE = 0.37
STEP_LENGTH = 0.5
EPSILON = 1e-06
GROUP = 8
LANES = 128
CHUNKS = 5
WINDOW = 2

NN = (((1,), (0,)), ((), ()))
NT = (((1,), (1,)), ((), ()))


def bits_of(size):
    assert size & (size - 1) == 0
    return [1 << b for b in reversed(range(size.bit_length() - 1))]


def swap(x, axis, k):
    size = lax.axis_size(axis)
    return lax.ppermute(x, axis, [(i, i ^ k) for i in range(size)])


def gather_doubling(x, axis):
    for k in bits_of(lax.axis_size(axis)):
        x = jnp.concatenate([x, swap(x, axis, k)], axis=0)
    return x


def place_of(offset, size):
    place = 0
    for b, k in enumerate(bits_of(size)):
        place = place + jnp.where(offset & k != 0, 1 << b, 0)
    return place


def gate_table(owner_order, own_freqs, freqs, waveform, gate_index):
    samples = waveform.shape[0]
    freq_ids = (owner_order[:, None] * own_freqs + jnp.arange(own_freqs)[None, :]).reshape(freqs)
    freq_col = freq_ids.astype(jnp.float32)[:, None] + 0.5
    time_row = jnp.arange(samples, dtype=jnp.float32)[None, :] + 0.5
    phases = PHASE_RATE * freq_col * time_row
    kernel = jnp.stack([jnp.cos(phases), jnp.sin(phases)], axis=1) / math.sqrt(freqs)
    steps = jnp.arange(samples)
    lag = gate_index[:, None] - steps[None, :]
    picked = jnp.sum(
        jnp.where(lag[:, :, None] == steps[None, None, :], waveform[None, None, :], 0.0), axis=-1
    )
    return jnp.einsum("gk,fpk->gfp", picked, kernel, precision=HIGH).reshape(gate_index.shape[0], freqs * 2)


def split(x):
    high = x.astype(jnp.bfloat16)
    return high, (x - high.astype(jnp.float32)).astype(jnp.bfloat16)


def split_outside(x):
    high = lax.reduce_precision(x, 8, 7)
    return high.astype(jnp.bfloat16), (x - high).astype(jnp.bfloat16)


def three_pass(a, b, dims):
    dot = functools.partial(lax.dot_general, dimension_numbers=dims, preferred_element_type=jnp.float32)
    return dot(a[0], b[0]) + (dot(a[0], b[1]) + dot(a[1], b[0]))


def chunk_kernel(pieces, *refs):
    sens_refs = refs[:pieces]
    model_h, model_l, gate_h, gate_l, obs_ref, terms_in, square_in, terms_ref, square_ref = refs[pieces:]

    @pl.when(pl.program_id(0) == 0)
    def _():
        terms_ref[...] = terms_in[...]
        square_ref[...] = square_in[...]

    sens = [split(r[...].reshape(r.shape[0] * r.shape[1], r.shape[2])) for r in sens_refs]
    sens = tuple(jnp.concatenate([s[i] for s in sens], axis=0) for i in range(2))
    gates = (gate_h[...], gate_l[...])
    predicted = three_pass((model_h[...], model_l[...]), sens, NT)
    misfit_rows = three_pass(split(predicted), gates, NN) - obs_ref[0]
    square_ref[...] += jnp.sum(misfit_rows * misfit_rows, axis=1, keepdims=True)
    back = three_pass(split(misfit_rows), gates, NT)
    terms_ref[...] += three_pass(split(back), sens, NN)


def chunk_step(sens, models_t, gates, obs, terms, square):
    spectra, soundings, cells = sens[0].shape
    pieces = len(sens)
    groups = soundings // GROUP
    members = terms.shape[0]
    whole = lambda a: pl.BlockSpec(a.shape, lambda i: (0,) * a.ndim)
    return pl.pallas_call(
        functools.partial(chunk_kernel, pieces),
        grid=(groups,),
        in_specs=[pl.BlockSpec((spectra, GROUP, cells), lambda i: (0, i, 0))] * pieces
        + [whole(a) for a in (*models_t, *gates)]
        + [pl.BlockSpec((1, 1, obs.shape[2]), lambda i: (i, 0, 0)), whole(terms), whole(square)],
        out_specs=[whole(terms), whole(square)],
        out_shape=[
            jax.ShapeDtypeStruct(terms.shape, jnp.float32),
            jax.ShapeDtypeStruct(square.shape, jnp.float32),
        ],
        input_output_aliases={pieces + 5: 0, pieces + 6: 1},
        compiler_params=pltpu.CompilerParams(
            dimension_semantics=("arbitrary",), vmem_limit_bytes=40 * 1024 * 1024
        ),
        cost_estimate=pl.CostEstimate(
            flops=12 * pieces * spectra * soundings * cells * members * 2,
            bytes_accessed=4 * pieces * spectra * soundings * cells,
            transcendentals=0,
        ),
        name="chunk_step",
    )(*sens, *models_t, *gates, obs, terms, square)


def chunk_groups(groups):
    count = min(CHUNKS, groups)
    if count == 1:
        return [groups]
    rest = groups - 1
    base, extra = divmod(rest, count - 1)
    return [base + (i < extra) for i in range(count - 1)] + [1]


def body(sensitivity, models, observed, waveform, cell_index, gate_index):
    both = ("tile", "freq")
    tiles, owners, devices = lax.axis_size("tile"), lax.axis_size("freq"), lax.axis_size(both)
    _, own_freqs, parts, soundings, cells = sensitivity.shape
    freqs = own_freqs * owners
    owned, members = models.shape
    ncells = owned * devices
    gates = gate_index.shape[0]
    total = tiles * soundings * gates
    own_soundings = soundings // owners
    block_cells = owned * owners
    me, my_freq = lax.axis_index("tile"), lax.axis_index("freq")

    block = sensitivity[0].reshape(own_freqs * parts, soundings, cells)
    sizes = chunk_groups(own_soundings // GROUP)
    starts = [sum(sizes[:i]) for i in range(len(sizes))]
    distances = sorted(range(1, owners), reverse=True)
    received = []
    source = block
    for i, (start, size) in enumerate(zip(starts, sizes)):
        if i >= WINDOW:
            source, received[i - WINDOW] = lax.optimization_barrier((block, received[i - WINDOW]))
        piece = lambda k: lax.dynamic_slice_in_dim(
            source, (my_freq ^ k) * own_soundings + start * GROUP, size * GROUP, 1
        )
        received.append([piece(0)] + [swap(piece(k), "freq", k) for k in distances])

    tile_cells = cell_index[0]
    home = tile_cells // block_cells
    borrowed_from = jnp.max(jnp.where(home == me, -1, home))
    all_models = gather_doubling(gather_doubling(models, "freq"), "tile")
    row = tile_cells % owned
    device = (tile_cells // owned) % owners
    spot = place_of(home ^ me, tiles) * block_cells + place_of(device ^ my_freq, owners) * owned + row
    models_t = split_outside(jnp.take(all_models, spot, axis=0).T)
    all_borrowed = gather_doubling(borrowed_from.reshape(1), "tile")
    all_borrowed = jnp.take(all_borrowed, place_of(jnp.arange(tiles) ^ me, tiles))

    order = my_freq ^ jnp.array([0] + distances, jnp.int32)
    table = gate_table(order, own_freqs, freqs, waveform, gate_index).T
    wide = table[:, None, :, None] * jnp.eye(GROUP, dtype=jnp.float32)[None, :, None, :]
    wide = split_outside(wide.reshape(freqs * parts * GROUP, gates * GROUP))
    obs = observed[0].reshape(gates, own_soundings // GROUP, GROUP)
    obs = jnp.swapaxes(obs, 0, 1).reshape(own_soundings // GROUP, 1, gates * GROUP)

    terms = jnp.zeros((members, cells), jnp.float32)
    square = jnp.zeros((members, LANES), jnp.float32)
    for i, (start, size) in enumerate(zip(starts, sizes)):
        terms, square = chunk_step(received[i], models_t, wide, obs[start : start + size], terms, square)

    place = tile_cells % block_cells + jnp.where(home == me, 0, block_cells)
    order = (place[:, None] == jnp.arange(cells)[None, :]).astype(jnp.float32)
    terms = jnp.dot(terms, order, precision=HIGH)
    sent = terms.reshape(devices, members // devices, cells)
    got = lax.all_to_all(sent, both, split_axis=0, concat_axis=0, tiled=True)
    squares = lax.all_gather(square[:, 0], both, axis=0, tiled=False)
    misfit = jnp.sum(squares, axis=0) / (2.0 * total)
    got = jnp.sum(got.reshape(tiles, owners, members // devices, cells), axis=1)
    lent = (all_borrowed[None, :] == jnp.arange(tiles)[:, None]).astype(jnp.float32)
    gradient = got[:, :, :block_cells] + jnp.sum(
        lent[:, :, None, None] * got[None, :, :, block_cells:], axis=1
    )
    scale = jnp.sqrt(jnp.sum(gradient * gradient, axis=(0, 2)) / ncells + EPSILON)
    step = gradient / scale[None, :, None]
    step = step.reshape(tiles, members // devices, owners, owned).transpose(0, 2, 1, 3)
    step = step.reshape(devices, members // devices, owned)
    back = lax.all_to_all(step, both, split_axis=0, concat_axis=0, tiled=True)
    back = back.reshape(members, owned)
    return (models - (STEP_LENGTH * misfit)[None, :] * back.T, misfit)


def solution(mesh):
    in_specs = (
        P("tile", "freq", None, None, None),
        P(("tile", "freq"), None),
        P("tile", None, "freq"),
        P(),
        P("tile", None),
        P(),
    )
    out_specs = (P(("tile", "freq"), None), P())
    return jax.shard_map(body, mesh=mesh, in_specs=in_specs, out_specs=out_specs, check_vma=False)
```

time: 521 us -> 576 us (1.11)
  waiting for transfers between devices: 377 us -> 178 us
  starting transfers between devices: 27.4 us -> 169 us
  blocking collectives: 5.53 us -> 118 us
  between operations: 14.4 us -> 1.41 us
  other arithmetic: 10.4 us -> 19.7 us
    all_to_all x5 -> x1, waiting for transfers between devices: 271 us -> 6.62 us  [body(): back = lax.all_to_all(step, both, split_axis=0, concat_axis=0, tiled=True)]
    ppermute x0 -> x42, waiting for transfers between devices: none -> 172 us  [swap(): return lax.ppermute(x, axis, [(i, i ^ k) for i in range(size)])]
    ppermute x0 -> x42, starting transfers between devices: none -> 161 us  [swap(): return lax.ppermute(x, axis, [(i, i ^ k) for i in range(size)])]
    all_gather x0 -> x1, blocking collectives: none -> 118 us  [body(): squares = lax.all_gather(square[:, 0], both, axis=0, tiled=False)]
    all_gather x1 -> x0, waiting for transfers between devices: 94.2 us -> none  [body(): all_models = lax.all_gather(models, both, axis=0, tiled=True)]
    all_to_all x5 -> x1, starting transfers between devices: 23.7 us -> 3.74 us  [body(): back = lax.all_to_all(step, both, split_axis=0, concat_axis=0, tiled=True)]
    dynamic_slice x0 -> x4, local copies, waits for them, and re-layouts: none -> 15.5 us  [body(): lax.dynamic_slice_in_dim(source, (my_freq ^ k) * own_soundings + start *...]
    slice x12 -> x14, local copies, waits for them, and re-layouts: 12.9 us -> 0.92 us  [the longest x13 0.92 us: body(): obs[start:start + size]]
  transfers between devices with their start and end apart: 7 -> 44, of which waited for: 6 -> 16; matrix products, arithmetic and copies ran while one was open for 7% -> 9% of each run, Pallas kernels for 6% -> 6%
where the time goes in v1:
time: 576 us; the launch traced here: 575 us
  waiting for transfers between devices  178 us (31%)
  starting transfers between devices  169 us (29%)
  blocking collectives  118 us (20%)
  local copies, waits for them, and re-layouts  48.4 us (8%)
  Pallas kernels  38.5 us (7%)
  other arithmetic  19.7 us (3%)
    ppermute x42, waiting for transfers between devices, swap(): return lax.ppermute(x, axis, [(i, i ^ k) for i in range(size)])  172 us
    ppermute x42, starting transfers between devices, swap(): return lax.ppermute(x, axis, [(i, i ^ k) for i in range(size)])  161 us
    all_gather x1, blocking collectives, body(): squares = lax.all_gather(square[:, 0], both, axis=0, tiled=False)  118 us
    pallas_call x5, Pallas kernels, chunk_step(): pl.pallas_call(functools.partial(chunk_kernel, pieces), grid=(groups,), i...  38.5 us
    dynamic_slice x4, local copies, waits for them, and re-layouts, body(): lax.dynamic_slice_in_dim(source, (my_freq ^ k) * own_soundings + start *...  15.5 us
  transfers between devices with their start and end apart: 44, of which 16 were waited for; matrix products, arithmetic and copies ran while one was open for 9% of the time, Pallas kernels for 6%

profile of v1, /device:TPU:0, one launch (start us, length us, event | category | flops | bytes accessed | tf_op | source)
XLA Modules:
  0.0 575.4 jit_solution(11502022633484018910)
XLA Ops:
  0.8 6.7 %constant_dynamic-slice_fusion.8 = (f32[8,32,512]{2,1,0:T(8,128)}, f32[8,32,512]{2,1,0:T(8,128)}, f32[8,32,512]{2,1,0:T(8,128)}, f32[8,32,512]{2,1,0:T(8,128)}, ...) fusion(f32[8,1024,512]{2,1,0:T(8,128)} %bitcast.52, ...), kind=kLoop, calls=%fused_computation.48 | loop fusion | bytes 16777280 | tf_op jit(solution)/shard_map/dynamic_slice | solution.py:157
  7.5 6.0 %collective-permute-start = (f32[8,32,512]{2,1,0:T(8,128)}, f32[8,32,512]{2,1,0:T(8,128)S(1)}, u32[]{:S(2)}, u32[]{:S(2)}) collective-permute-start(f32[8,32,512]{2,1,0:T(8,128)} %get-tuple-element.108), channel_id=1, source_target_pairs={{0,7},{1,6},{2,5},{3,4},{4,3},{5,2},{6,1},{7,0},{8,15},{9,14},{10,... | collective-permute-start | bytes 1572872 | tf_op jit(solution)/shard_map/ppermute | solution.py:31
  20.0 84.9 %collective-permute-done.21 = f32[32,256]{1,0:T(8,128)S(1)} collective-permute-done((f32[32,256]{1,0:T(8,128)S(1)}, f32[32,256]{1,0:T(8,128)S(1)}, u32[]{:S(2)}, u32[]{:S(2)}) %collective-permute-start.21) | collective-permute-done | bytes 32800 | tf_op jit(solution)/shard_map/ppermute | solution.py:31
  104.9 4.2 collective-permute-done.22
  110.3 5.4 broadcast_multiply_fusion
  118.9 4.3 collective-permute-done.24
  124.7 9.1 %mul.204 = f32[512,320]{0,1:T(8,128)} reshape(f32[64,8,40,8]{1,0,3,2:T(8,128)} %broadcast_multiply_fusion) | data formatting | bytes 1310720 | tf_op jit(solution)/shard_map/mul | solution.py:175
  139.5 3.4 collective-permute-start.26
  150.9 3.5 collective-permute-start.29
  156.8 8.4 %collective-permute-done.26.refs_1_ = f32[8,32,512]{2,1,0:T(8,128)} collective-permute-done((f32[8,32,512]{2,1,0:T(8,128)}, f32[8,32,512]{2,1,0:T(8,128)}, u32[]{:S(2)}, u32[]{:S(2)}) %collective-permute-start.26) | collective-permute-done | bytes 524320 | tf_op jit(solution)/shard_map/ppermute | solution.py:31
  165.2 35.9 %collective-permute-start.31 = (f32[8,32,512]{2,1,0:T(8,128)}, f32[8,32,512]{2,1,0:T(8,128)}, u32[]{:S(2)}, u32[]{:S(2)}) collective-permute-start(f32[8,32,512]{2,1,0:T(8,128)} %get-tuple-element.95), channel_id=1, source_target_pairs={{0,2},{1,3},{2,0},{3,1},{4,6},{5,7},{6,4},{7,5},{8,10},{9,11},{10,... | collective-permute-start | bytes 1572872 | tf_op jit(solution)/shard_map/ppermute | solution.py:31
  206.5 16.1 %collective-permute-done.28.refs_3_ = f32[8,32,512]{2,1,0:T(8,128)} collective-permute-done((f32[8,32,512]{2,1,0:T(8,128)}, f32[8,32,512]{2,1,0:T(8,128)}, u32[]{:S(2)}, u32[]{:S(2)}) %collective-permute-start.28) | collective-permute-done | bytes 524320 | tf_op jit(solution)/shard_map/ppermute | solution.py:31
  222.6 6.3 %collective-permute-done.29.refs_4_ = f32[8,32,512]{2,1,0:T(8,128)} collective-permute-done((f32[8,32,512]{2,1,0:T(8,128)}, f32[8,32,512]{2,1,0:T(8,128)}, u32[]{:S(2)}, u32[]{:S(2)}) %collective-permute-start.29) | collective-permute-done | bytes 524320 | tf_op jit(solution)/shard_map/ppermute | solution.py:31
  230.3 4.1 constant_dynamic-slice_fusion.24
  238.7 3.4 constant_dynamic-slice_fusion
  246.0 3.5 gather_fusion
  261.1 9.9 %chunk_step.5 = (f32[256,512]{1,0:T(8,128)S(1)}, f32[256,128]{1,0:T(8,128)S(1)}) custom-call(f32[8,32,512]{2,1,0:T(8,128)S(1)} %get-tuple-element.58.refs_0_, f32[8,32,512]{2,1,0:T(8,128)S(1)} %collective-permute-done.refs_1_, f32[8,32,512]{2,1,0:T(8,128)S(1)} %copy-done.1, ...), custom_call_target="tpu_custom_call", output_to_operand_aliasing={{0}: (13, {}), {1}: (14, {})} | custom-call | flops 6442450944 | bytes 4194304 | tf_op jit(solution)/shard_map/chunk_step/pallas_call | solution.py:102
  271.1 10.4 %collective-permute-done.12.refs_6_ = f32[8,32,512]{2,1,0:T(8,128)} collective-permute-done((f32[8,32,512]{2,1,0:T(8,128)}, f32[8,32,512]{2,1,0:T(8,128)}, u32[]{:S(2)}, u32[]{:S(2)}) %collective-permute-start.12) | collective-permute-done | bytes 524320 | tf_op jit(solution)/shard_map/ppermute | solution.py:31
  285.0 39.2 %collective-permute-start.35 = (f32[8,24,512]{2,1,0:T(8,128)S(1)}, f32[8,24,512]{2,1,0:T(8,128)S(1)}, u32[]{:S(2)}, u32[]{:S(2)}) collective-permute-start(f32[8,24,512]{2,1,0:T(8,128)S(1)} %copy-done.12), channel_id=1, source_target_pairs={{0,5},{1,4},{2,7},{3,6},{4,1},{5,0},{6,3},{7,2},{8,13},{9,12},{10,... | collective-permute-start | bytes 1179656 | tf_op jit(solution)/shard_map/ppermute | solution.py:31
  324.3 18.7 %collective-permute-start.36 = (f32[8,24,512]{2,1,0:T(8,128)S(1)}, f32[8,24,512]{2,1,0:T(8,128)S(1)}, u32[]{:S(2)}, u32[]{:S(2)}) collective-permute-start(f32[8,24,512]{2,1,0:T(8,128)S(1)} %copy-done.11), channel_id=1, source_target_pairs={{0,4},{1,5},{2,6},{3,7},{4,0},{5,1},{6,2},{7,3},{8,12},{9,13},{10,... | collective-permute-start | bytes 1179656 | tf_op jit(solution)/shard_map/ppermute | solution.py:31
  342.9 10.0 %chunk_step.6 = (f32[256,512]{1,0:T(8,128)S(1)}, f32[256,128]{1,0:T(8,128)S(1)}) custom-call(f32[8,32,512]{2,1,0:T(8,128)S(1)} %get-tuple-element.50.refs_0_, f32[8,32,512]{2,1,0:T(8,128)} %collective-permute-done.26.refs_1_, f32[8,32,512]{2,1,0:T(8,128)} %collective-permute-done.27.refs_2_, ...), custom_call_target="tpu_custom_call", output_to_operand_aliasing={{0}: (13, {}), {1}: (14, {})} | custom-call | flops 6442450944 | bytes 4194304 | tf_op jit(solution)/shard_map/chunk_step/pallas_call | solution.py:102
  352.9 4.8 collective-permute-done.9.refs_3_
  359.0 11.9 %collective-permute-start.38 = (f32[8,24,512]{2,1,0:T(8,128)S(1)}, f32[8,24,512]{2,1,0:T(8,128)S(1)}, u32[]{:S(2)}, u32[]{:S(2)}) collective-permute-start(f32[8,24,512]{2,1,0:T(8,128)S(1)} %copy-done.9), channel_id=1, source_target_pairs={{0,2},{1,3},{2,0},{3,1},{4,6},{5,7},{6,4},{7,5},{8,10},{9,11},{10,... | collective-permute-start | bytes 1179656 | tf_op jit(solution)/shard_map/ppermute | solution.py:31
  373.7 12.7 %collective-permute-done.35.refs_3_ = f32[8,24,512]{2,1,0:T(8,128)S(1)} collective-permute-done((f32[8,24,512]{2,1,0:T(8,128)S(1)}, f32[8,24,512]{2,1,0:T(8,128)S(1)}, u32[]{:S(2)}, u32[]{:S(2)}) %collective-permute-start.35) | collective-permute-done | bytes 393248 | tf_op jit(solution)/shard_map/ppermute | solution.py:31
  389.4 9.4 %collective-permute-done.36.refs_4_ = f32[8,24,512]{2,1,0:T(8,128)S(1)} collective-permute-done((f32[8,24,512]{2,1,0:T(8,128)S(1)}, f32[8,24,512]{2,1,0:T(8,128)S(1)}, u32[]{:S(2)}, u32[]{:S(2)}) %collective-permute-start.36) | collective-permute-done | bytes 393248 | tf_op jit(solution)/shard_map/ppermute | solution.py:31
  399.7 9.8 %chunk_step.7 = (f32[256,512]{1,0:T(8,128)S(1)}, f32[256,128]{1,0:T(8,128)S(1)}) custom-call(f32[8,32,512]{2,1,0:T(8,128)S(1)} %get-tuple-element.42.refs_0_, f32[8,32,512]{2,1,0:T(8,128)} %collective-permute-done.7.refs_1_, f32[8,32,512]{2,1,0:T(8,128)S(1)} %collective-permute-done.8.refs_2_, ...), custom_call_target="tpu_custom_call", output_to_operand_aliasing={{0}: (13, {}), {1}: (14, {})} | custom-call | flops 6442450944 | bytes 4194304 | tf_op jit(solution)/shard_map/chunk_step/pallas_call | solution.py:102
  416.3 6.7 %chunk_step.8 = (f32[256,512]{1,0:T(8,128)S(1)}, f32[256,128]{1,0:T(8,128)S(1)}) custom-call(f32[8,24,512]{2,1,0:T(8,128)S(1)} %get-tuple-element.93.refs_0_, f32[8,24,512]{2,1,0:T(8,128)S(1)} %collective-permute-done.33.refs_1_, f32[8,24,512]{2,1,0:T(8,128)S(1)} %collective-permute-done.34.refs_2_, ...), custom_call_target="tpu_custom_call", output_to_operand_aliasing={{0}: (13, {}), {1}: (14, {})} | custom-call | flops 4831838208 | bytes 3145728 | tf_op jit(solution)/shard_map/chunk_step/pallas_call | solution.py:102
  426.8 4.9 all-to-all-start
  439.8 117.9 %all-gather = f32[8192,1]{1,0:T(8,128)} all-gather(f32[256,1]{1,0:T(8,128)S(1)} %bitcast.51), channel_id=2, replica_groups=mesh['tile'=4,'freq'=8] {'tile','freq'}, dimensions={0}, use_global_device_ids=true | all-gather | bytes 33792 | tf_op jit(solution)/shard_map/all_gather | solution.py:190
  557.8 3.3 reduce
  562.4 3.7 all-to-all-start.1
  566.7 6.6 %all-to-all-done.1 = f32[32,1,256]{2,1,0:T(1,128)S(1)} async-done(((f32[32,1,256]{2,1,0:T(1,128)}), f32[32,1,256]{2,1,0:T(1,128)S(1)}, u32[]{:S(2)}, u32[]{:S(2)}) %all-to-all-start.1) | async-done | bytes 32800 | tf_op jit(solution)/shard_map/all_to_all | solution.py:201
  (178 shorter events, 88.9 us)
Async XLA Ops:
  7.5 128.7 %collective-permute-start = (f32[8,32,512]{2,1,0:T(8,128)}, f32[8,32,512]{2,1,0:T(8,128)S(1)}, u32[]{:S(2)}, u32[]{:S(2)}) collective-permute-start(f32[8,32,512]{2,1,0:T(8,128)} %get-tuple-element.108), channel_id=1, source_target_pairs={{0,7},{1,6},{2,5},{3,4},{4,3},{5,2},{6,1},{7,0},{8,15},{9,14},{10,... | collective-permute-start | bytes 1572872 | tf_op jit(solution)/shard_map/ppermute | solution.py:31
  13.5 124.6 %collective-permute-start.1 = (f32[8,32,512]{2,1,0:T(8,128)}, f32[8,32,512]{2,1,0:T(8,128)S(1)}, u32[]{:S(2)}, u32[]{:S(2)}) collective-permute-start(f32[8,32,512]{2,1,0:T(8,128)} %get-tuple-element.107), channel_id=1, source_target_pairs={{0,6},{1,7},{2,4},{3,5},{4,2},{5,3},{6,0},{7,1},{8,14},{9,15},{10,... | collective-permute-start | bytes 1572872 | tf_op jit(solution)/shard_map/ppermute | solution.py:31
  13.8 125.0 %collective-permute-start.2 = (f32[8,32,512]{2,1,0:T(8,128)}, f32[8,32,512]{2,1,0:T(8,128)S(1)}, u32[]{:S(2)}, u32[]{:S(2)}) collective-permute-start(f32[8,32,512]{2,1,0:T(8,128)} %get-tuple-element.106), channel_id=1, source_target_pairs={{0,5},{1,4},{2,7},{3,6},{4,1},{5,0},{6,3},{7,2},{8,13},{9,12},{10,... | collective-permute-start | bytes 1572872 | tf_op jit(solution)/shard_map/ppermute | solution.py:31
  14.5 128.4 %collective-permute-start.3 = (f32[8,32,512]{2,1,0:T(8,128)}, f32[8,32,512]{2,1,0:T(8,128)S(1)}, u32[]{:S(2)}, u32[]{:S(2)}) collective-permute-start(f32[8,32,512]{2,1,0:T(8,128)} %get-tuple-element.105), channel_id=1, source_target_pairs={{0,4},{1,5},{2,6},{3,7},{4,0},{5,1},{6,2},{7,3},{8,12},{9,13},{10,... | collective-permute-start | bytes 1572872 | tf_op jit(solution)/shard_map/ppermute | solution.py:31
  16.5 88.3 %collective-permute-start.21 = (f32[32,256]{1,0:T(8,128)S(1)}, f32[32,256]{1,0:T(8,128)S(1)}, u32[]{:S(2)}, u32[]{:S(2)}) collective-permute-start(f32[32,256]{1,0:T(8,128)S(1)} %copy-done.6), channel_id=1, source_target_pairs={{0,4},{1,5},{2,6},{3,7},{4,0},{5,1},{6,2},{7,3},{8,12},{9,13},{10,... | collective-permute-start | bytes 98312 | tf_op jit(solution)/shard_map/ppermute | solution.py:31
  123.2 23.2 %collective-permute-start.4 = (f32[8,32,512]{2,1,0:T(8,128)}, f32[8,32,512]{2,1,0:T(8,128)}, u32[]{:S(2)}, u32[]{:S(2)}) collective-permute-start(f32[8,32,512]{2,1,0:T(8,128)} %get-tuple-element.104), channel_id=1, source_target_pairs={{0,3},{1,2},{2,1},{3,0},{4,7},{5,6},{6,5},{7,4},{8,11},{9,10},{10,... | collective-permute-start | bytes 1572872 | tf_op jit(solution)/shard_map/ppermute | solution.py:31
  138.2 16.2 %collective-permute-start.6 = (f32[8,32,512]{2,1,0:T(8,128)}, f32[8,32,512]{2,1,0:T(8,128)}, u32[]{:S(2)}, u32[]{:S(2)}) collective-permute-start(f32[8,32,512]{2,1,0:T(8,128)} %get-tuple-element.102), channel_id=1, source_target_pairs={{0,1},{1,0},{2,3},{3,2},{4,5},{5,4},{6,7},{7,6},{8,9},{9,8},{10,11... | collective-permute-start | bytes 1572872 | tf_op jit(solution)/shard_map/ppermute | solution.py:31
  139.5 25.7 %collective-permute-start.26 = (f32[8,32,512]{2,1,0:T(8,128)}, f32[8,32,512]{2,1,0:T(8,128)}, u32[]{:S(2)}, u32[]{:S(2)}) collective-permute-start(f32[8,32,512]{2,1,0:T(8,128)} %get-tuple-element.100), channel_id=1, source_target_pairs={{0,7},{1,6},{2,5},{3,4},{4,3},{5,2},{6,1},{7,0},{8,15},{9,14},{10,... | collective-permute-start | bytes 1572872 | tf_op jit(solution)/shard_map/ppermute | solution.py:31
  143.7 57.4 %collective-permute-start.27 = (f32[8,32,512]{2,1,0:T(8,128)}, f32[8,32,512]{2,1,0:T(8,128)}, u32[]{:S(2)}, u32[]{:S(2)}) collective-permute-start(f32[8,32,512]{2,1,0:T(8,128)} %get-tuple-element.99), channel_id=1, source_target_pairs={{0,6},{1,7},{2,4},{3,5},{4,2},{5,3},{6,0},{7,1},{8,14},{9,15},{10,... | collective-permute-start | bytes 1572872 | tf_op jit(solution)/shard_map/ppermute | solution.py:31
  146.4 76.3 %collective-permute-start.28 = (f32[8,32,512]{2,1,0:T(8,128)}, f32[8,32,512]{2,1,0:T(8,128)}, u32[]{:S(2)}, u32[]{:S(2)}) collective-permute-start(f32[8,32,512]{2,1,0:T(8,128)} %get-tuple-element.98), channel_id=1, source_target_pairs={{0,5},{1,4},{2,7},{3,6},{4,1},{5,0},{6,3},{7,2},{8,13},{9,12},{10,... | collective-permute-start | bytes 1572872 | tf_op jit(solution)/shard_map/ppermute | solution.py:31
  150.9 78.1 %collective-permute-start.29 = (f32[8,32,512]{2,1,0:T(8,128)}, f32[8,32,512]{2,1,0:T(8,128)}, u32[]{:S(2)}, u32[]{:S(2)}) collective-permute-start(f32[8,32,512]{2,1,0:T(8,128)} %get-tuple-element.97), channel_id=1, source_target_pairs={{0,4},{1,5},{2,6},{3,7},{4,0},{5,1},{6,2},{7,3},{8,12},{9,13},{10,... | collective-permute-start | bytes 1572872 | tf_op jit(solution)/shard_map/ppermute | solution.py:31
  154.4 74.6 %collective-permute-start.30 = (f32[8,32,512]{2,1,0:T(8,128)}, f32[8,32,512]{2,1,0:T(8,128)}, u32[]{:S(2)}, u32[]{:S(2)}) collective-permute-start(f32[8,32,512]{2,1,0:T(8,128)} %get-tuple-element.96), channel_id=1, source_target_pairs={{0,3},{1,2},{2,1},{3,0},{4,7},{5,6},{6,5},{7,4},{8,11},{9,10},{10,... | collective-permute-start | bytes 1572872 | tf_op jit(solution)/shard_map/ppermute | solution.py:31
  165.2 65.1 %collective-permute-start.31 = (f32[8,32,512]{2,1,0:T(8,128)}, f32[8,32,512]{2,1,0:T(8,128)}, u32[]{:S(2)}, u32[]{:S(2)}) collective-permute-start(f32[8,32,512]{2,1,0:T(8,128)} %get-tuple-element.95), channel_id=1, source_target_pairs={{0,2},{1,3},{2,0},{3,1},{4,6},{5,7},{6,4},{7,5},{8,10},{9,11},{10,... | collective-permute-start | bytes 1572872 | tf_op jit(solution)/shard_map/ppermute | solution.py:31
  201.1 29.2 %collective-permute-start.32 = (f32[8,32,512]{2,1,0:T(8,128)}, f32[8,32,512]{2,1,0:T(8,128)}, u32[]{:S(2)}, u32[]{:S(2)}) collective-permute-start(f32[8,32,512]{2,1,0:T(8,128)} %get-tuple-element.94), channel_id=1, source_target_pairs={{0,1},{1,0},{2,3},{3,2},{4,5},{5,4},{6,7},{7,6},{8,9},{9,8},{10,11... | collective-permute-start | bytes 1572872 | tf_op jit(solution)/shard_map/ppermute | solution.py:31
  222.6 19.4 %collective-permute-start.25 = (f32[512,256]{1,0:T(8,128)}, f32[512,256]{1,0:T(8,128)}, u32[]{:S(2)}, u32[]{:S(2)}) collective-permute-start(f32[512,256]{1,0:T(8,128)} %get-tuple-element.130), channel_id=1, source_target_pairs={{0,8},{8,0},{16,24},{24,16},{1,9},{9,1},{17,25},{25,17},{2,10},{10... | collective-permute-start | bytes 1572872 | tf_op jit(solution)/shard_map/ppermute | solution.py:31
  234.4 21.4 %collective-permute-start.10 = (f32[8,32,512]{2,1,0:T(8,128)}, f32[8,32,512]{2,1,0:T(8,128)}, u32[]{:S(2)}, u32[]{:S(2)}) collective-permute-start(f32[8,32,512]{2,1,0:T(8,128)} %get-tuple-element.121), channel_id=1, source_target_pairs={{0,4},{1,5},{2,6},{3,7},{4,0},{5,1},{6,2},{7,3},{8,12},{9,13},{10,... | collective-permute-start | bytes 1572872 | tf_op jit(solution)/shard_map/ppermute | solution.py:31
  234.7 36.3 %collective-permute-start.11 = (f32[8,32,512]{2,1,0:T(8,128)}, f32[8,32,512]{2,1,0:T(8,128)}, u32[]{:S(2)}, u32[]{:S(2)}) collective-permute-start(f32[8,32,512]{2,1,0:T(8,128)} %get-tuple-element.120), channel_id=1, source_target_pairs={{0,3},{1,2},{2,1},{3,0},{4,7},{5,6},{6,5},{7,4},{8,11},{9,10},{10,... | collective-permute-start | bytes 1572872 | tf_op jit(solution)/shard_map/ppermute | solution.py:31
  237.7 43.7 %collective-permute-start.12 = (f32[8,32,512]{2,1,0:T(8,128)}, f32[8,32,512]{2,1,0:T(8,128)}, u32[]{:S(2)}, u32[]{:S(2)}) collective-permute-start(f32[8,32,512]{2,1,0:T(8,128)} %get-tuple-element.119), channel_id=1, source_target_pairs={{0,2},{1,3},{2,0},{3,1},{4,6},{5,7},{6,4},{7,5},{8,10},{9,11},{10,... | collective-permute-start | bytes 1572872 | tf_op jit(solution)/shard_map/ppermute | solution.py:31
  237.7 46.0 %collective-permute-start.13 = (f32[8,32,512]{2,1,0:T(8,128)}, f32[8,32,512]{2,1,0:T(8,128)}, u32[]{:S(2)}, u32[]{:S(2)}) collective-permute-start(f32[8,32,512]{2,1,0:T(8,128)} %get-tuple-element.118), channel_id=1, source_target_pairs={{0,1},{1,0},{2,3},{3,2},{4,5},{5,4},{6,7},{7,6},{8,9},{9,8},{10,11... | collective-permute-start | bytes 1572872 | tf_op jit(solution)/shard_map/ppermute | solution.py:31
  242.1 42.9 %collective-permute-start.7 = (f32[8,32,512]{2,1,0:T(8,128)}, f32[8,32,512]{2,1,0:T(8,128)}, u32[]{:S(2)}, u32[]{:S(2)}) collective-permute-start(f32[8,32,512]{2,1,0:T(8,128)} %get-tuple-element.124), channel_id=1, source_target_pairs={{0,7},{1,6},{2,5},{3,4},{4,3},{5,2},{6,1},{7,0},{8,15},{9,14},{10,... | collective-permute-start | bytes 1572872 | tf_op jit(solution)/shard_map/ppermute | solution.py:31
  255.8 68.4 %collective-permute-start.8 = (f32[8,32,512]{2,1,0:T(8,128)}, f32[8,32,512]{2,1,0:T(8,128)S(1)}, u32[]{:S(2)}, u32[]{:S(2)}) collective-permute-start(f32[8,32,512]{2,1,0:T(8,128)} %get-tuple-element.123), channel_id=1, source_target_pairs={{0,6},{1,7},{2,4},{3,5},{4,2},{5,3},{6,0},{7,1},{8,14},{9,15},{10,... | collective-permute-start | bytes 1572872 | tf_op jit(solution)/shard_map/ppermute | solution.py:31
  271.0 86.6 %collective-permute-start.9 = (f32[8,32,512]{2,1,0:T(8,128)S(1)}, f32[8,32,512]{2,1,0:T(8,128)S(1)}, u32[]{:S(2)}, u32[]{:S(2)}) collective-permute-start(f32[8,32,512]{2,1,0:T(8,128)S(1)} %copy-done.7), channel_id=1, source_target_pairs={{0,5},{1,4},{2,7},{3,6},{4,1},{5,0},{6,3},{7,2},{8,13},{9,12},{10,... | collective-permute-start | bytes 1572872 | tf_op jit(solution)/shard_map/ppermute | solution.py:31
  281.5 77.6 %collective-permute-start.33 = (f32[8,24,512]{2,1,0:T(8,128)S(1)}, f32[8,24,512]{2,1,0:T(8,128)S(1)}, u32[]{:S(2)}, u32[]{:S(2)}) collective-permute-start(f32[8,24,512]{2,1,0:T(8,128)S(1)} %copy-done.14), channel_id=1, source_target_pairs={{0,7},{1,6},{2,5},{3,4},{4,3},{5,2},{6,1},{7,0},{8,15},{9,14},{10,... | collective-permute-start | bytes 1179656 | tf_op jit(solution)/shard_map/ppermute | solution.py:31
  283.7 87.3 %collective-permute-start.34 = (f32[8,24,512]{2,1,0:T(8,128)S(1)}, f32[8,24,512]{2,1,0:T(8,128)S(1)}, u32[]{:S(2)}, u32[]{:S(2)}) collective-permute-start(f32[8,24,512]{2,1,0:T(8,128)S(1)} %copy-done.13), channel_id=1, source_target_pairs={{0,6},{1,7},{2,4},{3,5},{4,2},{5,3},{6,0},{7,1},{8,14},{9,15},{10,... | collective-permute-start | bytes 1179656 | tf_op jit(solution)/shard_map/ppermute | solution.py:31
  285.0 101.3 %collective-permute-start.35 = (f32[8,24,512]{2,1,0:T(8,128)S(1)}, f32[8,24,512]{2,1,0:T(8,128)S(1)}, u32[]{:S(2)}, u32[]{:S(2)}) collective-permute-start(f32[8,24,512]{2,1,0:T(8,128)S(1)} %copy-done.12), channel_id=1, source_target_pairs={{0,5},{1,4},{2,7},{3,6},{4,1},{5,0},{6,3},{7,2},{8,13},{9,12},{10,... | collective-permute-start | bytes 1179656 | tf_op jit(solution)/shard_map/ppermute | solution.py:31
  324.3 74.5 %collective-permute-start.36 = (f32[8,24,512]{2,1,0:T(8,128)S(1)}, f32[8,24,512]{2,1,0:T(8,128)S(1)}, u32[]{:S(2)}, u32[]{:S(2)}) collective-permute-start(f32[8,24,512]{2,1,0:T(8,128)S(1)} %copy-done.11), channel_id=1, source_target_pairs={{0,4},{1,5},{2,6},{3,7},{4,0},{5,1},{6,2},{7,3},{8,12},{9,13},{10,... | collective-permute-start | bytes 1179656 | tf_op jit(solution)/shard_map/ppermute | solution.py:31
  357.6 51.9 %collective-permute-start.37 = (f32[8,24,512]{2,1,0:T(8,128)S(1)}, f32[8,24,512]{2,1,0:T(8,128)S(1)}, u32[]{:S(2)}, u32[]{:S(2)}) collective-permute-start(f32[8,24,512]{2,1,0:T(8,128)S(1)} %copy-done.10), channel_id=1, source_target_pairs={{0,3},{1,2},{2,1},{3,0},{4,7},{5,6},{6,5},{7,4},{8,11},{9,10},{10,... | collective-permute-start | bytes 1179656 | tf_op jit(solution)/shard_map/ppermute | solution.py:31
  359.0 50.6 %collective-permute-start.38 = (f32[8,24,512]{2,1,0:T(8,128)S(1)}, f32[8,24,512]{2,1,0:T(8,128)S(1)}, u32[]{:S(2)}, u32[]{:S(2)}) collective-permute-start(f32[8,24,512]{2,1,0:T(8,128)S(1)} %copy-done.9), channel_id=1, source_target_pairs={{0,2},{1,3},{2,0},{3,1},{4,6},{5,7},{6,4},{7,5},{8,10},{9,11},{10,... | collective-permute-start | bytes 1179656 | tf_op jit(solution)/shard_map/ppermute | solution.py:31
  371.0 41.8 %collective-permute-start.39 = (f32[8,24,512]{2,1,0:T(8,128)S(1)}, f32[8,24,512]{2,1,0:T(8,128)S(1)}, u32[]{:S(2)}, u32[]{:S(2)}) collective-permute-start(f32[8,24,512]{2,1,0:T(8,128)S(1)} %copy-done.8), channel_id=1, source_target_pairs={{0,1},{1,0},{2,3},{3,2},{4,5},{5,4},{6,7},{7,6},{8,9},{9,8},{10,11... | collective-permute-start | bytes 1179656 | tf_op jit(solution)/shard_map/ppermute | solution.py:31
  386.3 27.7 %collective-permute-start.14 = (f32[8,8,512]{2,1,0:T(8,128)S(1)}, f32[8,8,512]{2,1,0:T(8,128)S(1)}, u32[]{:S(2)}, u32[]{:S(2)}) collective-permute-start(f32[8,8,512]{2,1,0:T(8,128)S(1)} %get-tuple-element.116), channel_id=1, source_target_pairs={{0,7},{1,6},{2,5},{3,4},{4,3},{5,2},{6,1},{7,0},{8,15},{9,14},{10,... | collective-permute-start | bytes 393224 | tf_op jit(solution)/shard_map/ppermute | solution.py:31
  398.8 16.7 %collective-permute-start.15 = (f32[8,8,512]{2,1,0:T(8,128)S(1)}, f32[8,8,512]{2,1,0:T(8,128)S(1)}, u32[]{:S(2)}, u32[]{:S(2)}) collective-permute-start(f32[8,8,512]{2,1,0:T(8,128)S(1)} %get-tuple-element.115), channel_id=1, source_target_pairs={{0,6},{1,7},{2,4},{3,5},{4,2},{5,3},{6,0},{7,1},{8,14},{9,15},{10,... | collective-permute-start | bytes 393224 | tf_op jit(solution)/shard_map/ppermute | solution.py:31
  426.8 134.4 %all-to-all-start = ((f32[32,8,512]{2,1,0:T(8,128)}), f32[32,8,512]{2,1,0:T(8,128)S(1)}, u32[]{:S(2)}, u32[]{:S(2)}) async-start(f32[32,8,512]{2,1,0:T(8,128)} %convolution_bitcast_fusion), calls=%async_computation | async-start | bytes 1048576 | tf_op jit(solution)/shard_map/all_to_all | solution.py:189
  (31 other events, 581.7 us)

commit v2 on v1

--- a/solution.py
+++ b/solution.py
@@ -14,34 +14,20 @@
 EPSILON = 1e-06
 GROUP = 8
 LANES = 128
-CHUNKS = 5
-WINDOW = 2
 
 NN = (((1,), (0,)), ((), ()))
 NT = (((1,), (1,)), ((), ()))
 
 
-def bits_of(size):
+def swap(x, axis, k):
+    return lax.ppermute(x, axis, [(i, i ^ k) for i in range(lax.axis_size(axis))])
+
+
+def partner_order(size):
     assert size & (size - 1) == 0
-    return [1 << b for b in reversed(range(size.bit_length() - 1))]
-
-
-def swap(x, axis, k):
-    size = lax.axis_size(axis)
-    return lax.ppermute(x, axis, [(i, i ^ k) for i in range(size)])
-
-
-def gather_doubling(x, axis):
-    for k in bits_of(lax.axis_size(axis)):
-        x = jnp.concatenate([x, swap(x, axis, k)], axis=0)
-    return x
-
-
-def place_of(offset, size):
-    place = 0
-    for b, k in enumerate(bits_of(size)):
-        place = place + jnp.where(offset & k != 0, 1 << b, 0)
-    return place
+    across, near = list(range(size // 2, size))[::-1], list(range(1, size // 2))[::-1]
+    order = [k for pair in zip(across, near + [None]) for k in pair if k is not None]
+    return order
 
 
 def gate_table(owner_order, own_freqs, freqs, waveform, gate_index):
@@ -93,8 +79,8 @@
     terms_ref[...] += three_pass(split(back), sens, NN)
 
 
-def chunk_step(sens, models_t, gates, obs, terms, square):
-    spectra, soundings, cells = sens[0].shape
+def chunk_step(sens, spectra, models_t, gates, obs, terms, square):
+    _, soundings, cells = sens[0].shape
     pieces = len(sens)
     groups = soundings // GROUP
     members = terms.shape[0]
@@ -124,12 +110,12 @@
 
 
 def chunk_groups(groups):
-    count = min(CHUNKS, groups)
-    if count == 1:
-        return [groups]
-    rest = groups - 1
-    base, extra = divmod(rest, count - 1)
-    return [base + (i < extra) for i in range(count - 1)] + [1]
+    if groups < 8:
+        return [1] * groups
+    first, last = groups // 8, [groups // 8, groups // 16 or 1]
+    rest = groups - first - sum(last)
+    middle = -(-rest // (groups // 4))
+    return [first] + [rest // middle + (i < rest % middle) for i in range(middle)] + last
 
 
 def body(sensitivity, models, observed, waveform, cell_index, gate_index):
@@ -137,6 +123,7 @@
     tiles, owners, devices = lax.axis_size("tile"), lax.axis_size("freq"), lax.axis_size(both)
     _, own_freqs, parts, soundings, cells = sensitivity.shape
     freqs = own_freqs * owners
+    spectra = own_freqs * parts
     owned, members = models.shape
     ncells = owned * devices
     gates = gate_index.shape[0]
@@ -145,32 +132,39 @@
     block_cells = owned * owners
     me, my_freq = lax.axis_index("tile"), lax.axis_index("freq")
 
-    block = sensitivity[0].reshape(own_freqs * parts, soundings, cells)
+    block = sensitivity[0].reshape(spectra, soundings, cells)
     sizes = chunk_groups(own_soundings // GROUP)
     starts = [sum(sizes[:i]) for i in range(len(sizes))]
-    distances = sorted(range(1, owners), reverse=True)
+    distances = partner_order(owners)
     received = []
-    source = block
     for i, (start, size) in enumerate(zip(starts, sizes)):
-        if i >= WINDOW:
-            source, received[i - WINDOW] = lax.optimization_barrier((block, received[i - WINDOW]))
-        piece = lambda k: lax.dynamic_slice_in_dim(
-            source, (my_freq ^ k) * own_soundings + start * GROUP, size * GROUP, 1
-        )
-        received.append([piece(0)] + [swap(piece(k), "freq", k) for k in distances])
+        rows = size * GROUP
+        piece = lambda k: lax.dynamic_slice_in_dim(block, (my_freq ^ k) * own_soundings + start * GROUP, rows, 1)
+        if i == 0:
+            slabs = -(-owned * members // (rows * cells))
+            rider = jnp.pad(models.reshape(-1), (0, slabs * rows * cells - owned * members))
+            rider = rider.reshape(slabs, rows, cells)
+            first = [swap(jnp.concatenate([piece(k), rider]), "freq", k) for k in distances]
+            received.append([piece(0)] + first)
+            near = [models] + [
+                r[spectra:].reshape(-1)[: owned * members].reshape(owned, members) for r in first
+            ]
+        else:
+            received.append([piece(0)] + [swap(piece(k), "freq", k) for k in distances])
 
     tile_cells = cell_index[0]
     home = tile_cells // block_cells
     borrowed_from = jnp.max(jnp.where(home == me, -1, home))
-    all_models = gather_doubling(gather_doubling(models, "freq"), "tile")
-    row = tile_cells % owned
-    device = (tile_cells // owned) % owners
-    spot = place_of(home ^ me, tiles) * block_cells + place_of(device ^ my_freq, owners) * owned + row
-    models_t = split_outside(jnp.take(all_models, spot, axis=0).T)
-    all_borrowed = gather_doubling(borrowed_from.reshape(1), "tile")
-    all_borrowed = jnp.take(all_borrowed, place_of(jnp.arange(tiles) ^ me, tiles))
-
-    order = my_freq ^ jnp.array([0] + distances, jnp.int32)
+    near = jnp.concatenate(near + [jnp.full((GROUP, members), borrowed_from, jnp.float32)])
+    far = lax.all_gather(near, "tile", axis=0, tiled=False)
+    all_borrowed = far[:, block_cells, 0].astype(jnp.int32)
+    partners = [0] + distances
+    slot = jnp.array([partners.index(k) for k in range(owners)], jnp.int32)
+    spot = jnp.take(slot, ((tile_cells // owned) % owners) ^ my_freq) * owned + tile_cells % owned
+    spot = home * (block_cells + GROUP) + spot
+    models_t = split_outside(jnp.take(far.reshape(-1, members), spot, axis=0).T)
+
+    order = my_freq ^ jnp.array(partners, jnp.int32)
     table = gate_table(order, own_freqs, freqs, waveform, gate_index).T
     wide = table[:, None, :, None] * jnp.eye(GROUP, dtype=jnp.float32)[None, :, None, :]
     wide = split_outside(wide.reshape(freqs * parts * GROUP, gates * GROUP))
@@ -180,26 +174,31 @@
     terms = jnp.zeros((members, cells), jnp.float32)
     square = jnp.zeros((members, LANES), jnp.float32)
     for i, (start, size) in enumerate(zip(starts, sizes)):
-        terms, square = chunk_step(received[i], models_t, wide, obs[start : start + size], terms, square)
+        terms, square = chunk_step(
+            received[i], spectra, models_t, wide, obs[start : start + size], terms, square
+        )
 
     place = tile_cells % block_cells + jnp.where(home == me, 0, block_cells)
     order = (place[:, None] == jnp.arange(cells)[None, :]).astype(jnp.float32)
     terms = jnp.dot(terms, order, precision=HIGH)
-    sent = terms.reshape(devices, members // devices, cells)
+    slab = members // devices
+    sent = terms.reshape(devices, slab, cells)
     got = lax.all_to_all(sent, both, split_axis=0, concat_axis=0, tiled=True)
-    squares = lax.all_gather(square[:, 0], both, axis=0, tiled=False)
-    misfit = jnp.sum(squares, axis=0) / (2.0 * total)
-    got = jnp.sum(got.reshape(tiles, owners, members // devices, cells), axis=1)
+    got = jnp.sum(got.reshape(tiles, owners, slab, cells), axis=1)
     lent = (all_borrowed[None, :] == jnp.arange(tiles)[:, None]).astype(jnp.float32)
     gradient = got[:, :, :block_cells] + jnp.sum(
         lent[:, :, None, None] * got[None, :, :, block_cells:], axis=1
     )
     scale = jnp.sqrt(jnp.sum(gradient * gradient, axis=(0, 2)) / ncells + EPSILON)
     step = gradient / scale[None, :, None]
-    step = step.reshape(tiles, members // devices, owners, owned).transpose(0, 2, 1, 3)
-    step = step.reshape(devices, members // devices, owned)
-    back = lax.all_to_all(step, both, split_axis=0, concat_axis=0, tiled=True)
-    back = back.reshape(members, owned)
+    step = step.reshape(tiles, slab, owners, owned).transpose(0, 2, 1, 3)
+    step = step.reshape(devices, slab, owned)
+    rider = jnp.broadcast_to(square[:, 0].reshape(1, slab, devices), (devices, slab, devices))
+    back = lax.all_to_all(
+        jnp.concatenate([step, rider], axis=2), both, split_axis=0, concat_axis=0, tiled=True
+    )
+    misfit = jnp.sum(back[:, :, owned:], axis=0).reshape(members) / (2.0 * total)
+    back = back[:, :, :owned].reshape(members, owned)
     return (models - (STEP_LENGTH * misfit)[None, :] * back.T, misfit)
 
 

time: 576 us -> 447 us (0.78)
  blocking collectives: 118 us -> 0 us
  starting transfers between devices: 169 us -> 116 us
  waiting for transfers between devices: 178 us -> 198 us
  between operations: 1.41 us -> 15.9 us
  local copies, waits for them, and re-layouts: 48.4 us -> 60.5 us
    all_gather x1 -> x0, blocking collectives: 118 us -> none  [body(): squares = lax.all_gather(square[:, 0], both, axis=0, tiled=False)]
    ppermute x42, starting transfers between devices: 161 us -> 110 us  [swap(): lax.ppermute(x, axis, [(i, i ^ k) for i in range(lax.axis_size(axis))])]
    all_to_all x1, waiting for transfers between devices: 0.01 us -> 15.3 us  [body(): got = lax.all_to_all(sent, both, split_axis=0, concat_axis=0, tiled=True)]
    unnamed x47 -> x86, local copies, waits for them, and re-layouts: 9.83 us -> 13.3 us
    pallas_call x5 -> x6, Pallas kernels: 38.5 us -> 39.5 us  [chunk_step(): pl.pallas_call(functools.partial(chunk_kernel, pieces), grid=(groups,), i...]
  transfers between devices with their start and end apart: 44 -> 45, of which waited for: 16 -> 15; matrix products, arithmetic and copies ran while one was open for 9% -> 14% of each run, Pallas kernels for 6% -> 8%
where the time goes in v2:
time: 447 us; the launch traced here: 446 us
  waiting for transfers between devices  198 us (44%)
  starting transfers between devices  116 us (26%)
  local copies, waits for them, and re-layouts  60.5 us (14%)
  Pallas kernels  39.5 us (9%)
  between operations  15.9 us (4%)
  other arithmetic  14 us (3%)
    ppermute x42, waiting for transfers between devices, swap(): lax.ppermute(x, axis, [(i, i ^ k) for i in range(lax.axis_size(axis))])  176 us
    ppermute x42, starting transfers between devices, swap(): lax.ppermute(x, axis, [(i, i ^ k) for i in range(lax.axis_size(axis))])  110 us
    pallas_call x6, Pallas kernels, chunk_step(): pl.pallas_call(functools.partial(chunk_kernel, pieces), grid=(groups,), i...  39.5 us
    dynamic_slice x4, local copies, waits for them, and re-layouts, body(): lax.dynamic_slice_in_dim(block, (my_freq ^ k) * own_soundings + start * G...  15.9 us
    all_to_all x1, waiting for transfers between devices, body(): got = lax.all_to_all(sent, both, split_axis=0, concat_axis=0, tiled=True)  15.3 us
    unnamed x86, local copies, waits for them, and re-layouts  13.3 us
    mul x2, local copies, waits for them, and re-layouts, body(): table[:, None, :, None]  11.5 us
  transfers between devices with their start and end apart: 45, of which 15 were waited for; matrix products, arithmetic and copies ran while one was open for 14% of the time, Pallas kernels for 8%

profile of v2, /device:TPU:0, one launch (start us, length us, event | category | flops | bytes accessed | tf_op | source)
XLA Modules:
  0.0 445.7 jit_solution(1038909830272408069)
XLA Ops:
  8.2 3.7 constant_dynamic-slice_fusion
  13.1 6.0 %collective-permute-start.7 = (f32[9,16,512]{2,1,0:T(8,128)S(1)}, f32[9,16,512]{2,1,0:T(8,128)S(1)}, u32[]{:S(2)}, u32[]{:S(2)}) collective-permute-start(f32[9,16,512]{2,1,0:T(8,128)S(1)} %get-tuple-element.102), channel_id=1, source_target_pairs={{0,7},{1,6},{2,5},{3,4},{4,3},{5,2},{6,1},{7,0},{8,15},{9,14},{10,... | collective-permute-start | bytes 884744 | tf_op jit(solution)/shard_map/ppermute | solution.py:23
  30.3 3.4 constant_dynamic-slice_fusion.17
  38.5 6.6 %constant_dynamic-slice_fusion.1 = (f32[8,32,512]{2,1,0:T(8,128)}, f32[8,32,512]{2,1,0:T(8,128)}, f32[8,32,512]{2,1,0:T(8,128)}, f32[8,32,512]{2,1,0:T(8,128)}, ...) fusion(f32[8,1024,512]{2,1,0:T(8,128)} %bitcast.66, ...), kind=kLoop, calls=%fused_computation.46 | loop fusion | bytes 16777280 | tf_op jit(solution)/shard_map/dynamic_slice | solution.py:142
  45.8 3.5 collective-permute-start.21
  52.5 27.9 %collective-permute-done.11.refs_5_ = f32[9,16,512]{2,1,0:T(8,128)} collective-permute-done((f32[9,16,512]{2,1,0:T(8,128)}, f32[9,16,512]{2,1,0:T(8,128)}, u32[]{:S(2)}, u32[]{:S(2)}) %collective-permute-start.11) | collective-permute-done | bytes 294944 | tf_op jit(solution)/shard_map/ppermute | solution.py:23
  81.8 3.2 collective-permute-start
  100.7 5.4 %broadcast_multiply_fusion = f32[64,8,40,8]{1,0,3,2:T(8,128)} fusion(f32[8,8]{0,1:T(8,128)S(1)} %fusion.6, f32[64,40]{0,1:T(8,128)S(1)} %fusion.20), kind=kLoop, calls=%fused_computation.1 | loop fusion | flops 163840 | bytes 665856 | tf_op jit(solution)/shard_map/mul | solution.py:169
  114.4 9.2 %mul.221 = f32[512,320]{0,1:T(8,128)} reshape(f32[64,8,40,8]{1,0,3,2:T(8,128)} %broadcast_multiply_fusion) | data formatting | bytes 1310720 | tf_op jit(solution)/shard_map/mul | solution.py:169
  128.3 3.5 gather_fusion
  133.8 28.4 %collective-permute-done.22.refs_2_ = f32[8,24,512]{2,1,0:T(8,128)} collective-permute-done((f32[8,24,512]{2,1,0:T(8,128)}, f32[8,24,512]{2,1,0:T(8,128)}, u32[]{:S(2)}, u32[]{:S(2)}) %collective-permute-start.22) | collective-permute-done | bytes 393248 | tf_op jit(solution)/shard_map/ppermute | solution.py:23
  173.9 5.5 %chunk_step.6 = (f32[256,512]{1,0:T(8,128)S(1)}, f32[256,128]{1,0:T(8,128)S(1)}) custom-call(f32[8,16,512]{2,1,0:T(8,128)S(1)} %get-tuple-element.40.refs_0_, f32[9,16,512]{2,1,0:T(8,128)S(1)} %collective-permute-done.7.refs_1_, f32[9,16,512]{2,1,0:T(8,128)S(1)} %copy-done.1, ...), custom_call_target="tpu_custom_call", output_to_operand_aliasing={{0}: (13, {}), {1}: (14, {})} | custom-call | flops 3221225472 | bytes 2097152 | tf_op jit(solution)/shard_map/chunk_step/pallas_call | solution.py:88
  179.4 30.7 %collective-permute-done.39.refs_5_ = f32[8,32,512]{2,1,0:T(8,128)S(1)} collective-permute-done((f32[8,32,512]{2,1,0:T(8,128)}, f32[8,32,512]{2,1,0:T(8,128)S(1)}, u32[]{:S(2)}, u32[]{:S(2)}) %collective-permute-start.39) | collective-permute-done | bytes 524320 | tf_op jit(solution)/shard_map/ppermute | solution.py:23
  212.1 20.6 %collective-permute-done.41.refs_7_ = f32[8,32,512]{2,1,0:T(8,128)S(1)} collective-permute-done((f32[8,32,512]{2,1,0:T(8,128)}, f32[8,32,512]{2,1,0:T(8,128)S(1)}, u32[]{:S(2)}, u32[]{:S(2)}) %collective-permute-start.41) | collective-permute-done | bytes 524320 | tf_op jit(solution)/shard_map/ppermute | solution.py:23
  233.8 23.9 %collective-permute-start.34 = (f32[8,32,512]{2,1,0:T(8,128)S(1)}, f32[8,32,512]{2,1,0:T(8,128)S(1)}, u32[]{:S(2)}, u32[]{:S(2)}) collective-permute-start(f32[8,32,512]{2,1,0:T(8,128)S(1)} %copy-done.6), channel_id=1, source_target_pairs={{0,4},{1,5},{2,6},{3,7},{4,0},{5,1},{6,2},{7,3},{8,12},{9,13},{10,... | collective-permute-start | bytes 1572872 | tf_op jit(solution)/shard_map/ppermute | solution.py:23
  257.7 9.9 %chunk_step.7 = (f32[256,512]{1,0:T(8,128)S(1)}, f32[256,128]{1,0:T(8,128)S(1)}) custom-call(f32[8,32,512]{2,1,0:T(8,128)S(1)} %get-tuple-element.63.refs_0_, f32[8,32,512]{2,1,0:T(8,128)} %collective-permute-done.35.refs_1_, f32[8,32,512]{2,1,0:T(8,128)} %collective-permute-done.36.refs_2_, ...), custom_call_target="tpu_custom_call", output_to_operand_aliasing={{0}: (13, {}), {1}: (14, {})} | custom-call | flops 6442450944 | bytes 4194304 | tf_op jit(solution)/shard_map/chunk_step/pallas_call | solution.py:88
  269.6 18.1 %collective-permute-start.24 = (f32[8,24,512]{2,1,0:T(8,128)S(1)}, f32[8,24,512]{2,1,0:T(8,128)S(1)}, u32[]{:S(2)}, u32[]{:S(2)}) collective-permute-start(f32[8,24,512]{2,1,0:T(8,128)S(1)} %copy-done.14), channel_id=1, source_target_pairs={{0,2},{1,3},{2,0},{3,1},{4,6},{5,7},{6,4},{7,5},{8,10},{9,11},{10,... | collective-permute-start | bytes 1179656 | tf_op jit(solution)/shard_map/ppermute | solution.py:23
  287.7 9.7 %collective-permute-done.32.refs_5_ = f32[8,32,512]{2,1,0:T(8,128)S(1)} collective-permute-done((f32[8,32,512]{2,1,0:T(8,128)S(1)}, f32[8,32,512]{2,1,0:T(8,128)S(1)}, u32[]{:S(2)}, u32[]{:S(2)}) %collective-permute-start.32) | collective-permute-done | bytes 524320 | tf_op jit(solution)/shard_map/ppermute | solution.py:23
  299.0 18.1 %collective-permute-done.34.refs_7_ = f32[8,32,512]{2,1,0:T(8,128)S(1)} collective-permute-done((f32[8,32,512]{2,1,0:T(8,128)S(1)}, f32[8,32,512]{2,1,0:T(8,128)S(1)}, u32[]{:S(2)}, u32[]{:S(2)}) %collective-permute-start.34) | collective-permute-done | bytes 524320 | tf_op jit(solution)/shard_map/ppermute | solution.py:23
  317.1 9.1 %chunk_step.8 = (f32[256,512]{1,0:T(8,128)S(1)}, f32[256,128]{1,0:T(8,128)S(1)}) custom-call(f32[8,32,512]{2,1,0:T(8,128)S(1)} %get-tuple-element.71.refs_0_, f32[8,32,512]{2,1,0:T(8,128)S(1)} %collective-permute-done.28.refs_1_, f32[8,32,512]{2,1,0:T(8,128)S(1)} %collective-permute-done.29.refs_2_, ...), custom_call_target="tpu_custom_call", output_to_operand_aliasing={{0}: (13, {}), {1}: (14, {})} | custom-call | flops 6442450944 | bytes 4194304 | tf_op jit(solution)/shard_map/chunk_step/pallas_call | solution.py:88
  328.3 12.8 %collective-permute-start.17 = (f32[8,16,512]{2,1,0:T(8,128)S(1)}, f32[8,16,512]{2,1,0:T(8,128)S(1)}, u32[]{:S(2)}, u32[]{:S(2)}) collective-permute-start(f32[8,16,512]{2,1,0:T(8,128)S(1)} %copy-done.20), channel_id=1, source_target_pairs={{0,2},{1,3},{2,0},{3,1},{4,6},{5,7},{6,4},{7,5},{8,10},{9,11},{10,... | collective-permute-start | bytes 786440 | tf_op jit(solution)/shard_map/ppermute | solution.py:23
  341.1 6.9 %collective-permute-done.25.refs_5_ = f32[8,24,512]{2,1,0:T(8,128)S(1)} collective-permute-done((f32[8,24,512]{2,1,0:T(8,128)S(1)}, f32[8,24,512]{2,1,0:T(8,128)S(1)}, u32[]{:S(2)}, u32[]{:S(2)}) %collective-permute-start.25) | collective-permute-done | bytes 393248 | tf_op jit(solution)/shard_map/ppermute | solution.py:23
  349.6 12.4 %collective-permute-done.27.refs_7_ = f32[8,24,512]{2,1,0:T(8,128)S(1)} collective-permute-done((f32[8,24,512]{2,1,0:T(8,128)S(1)}, f32[8,24,512]{2,1,0:T(8,128)S(1)}, u32[]{:S(2)}, u32[]{:S(2)}) %collective-permute-start.27) | collective-permute-done | bytes 393248 | tf_op jit(solution)/shard_map/ppermute | solution.py:23
  362.0 7.5 %chunk_step.9 = (f32[256,512]{1,0:T(8,128)S(1)}, f32[256,128]{1,0:T(8,128)S(1)}) custom-call(f32[8,24,512]{2,1,0:T(8,128)S(1)} %get-tuple-element.79.refs_0_, f32[8,24,512]{2,1,0:T(8,128)} %collective-permute-done.21.refs_1_, f32[8,24,512]{2,1,0:T(8,128)} %collective-permute-done.22.refs_2_, ...), custom_call_target="tpu_custom_call", output_to_operand_aliasing={{0}: (13, {}), {1}: (14, {})} | custom-call | flops 4831838208 | bytes 3145728 | tf_op jit(solution)/shard_map/chunk_step/pallas_call | solution.py:88
  371.6 3.3 collective-permute-start.3
  374.9 6.9 %collective-permute-done.18.refs_5_ = f32[8,16,512]{2,1,0:T(8,128)S(1)} collective-permute-done((f32[8,16,512]{2,1,0:T(8,128)S(1)}, f32[8,16,512]{2,1,0:T(8,128)S(1)}, u32[]{:S(2)}, u32[]{:S(2)}) %collective-permute-start.18) | collective-permute-done | bytes 262176 | tf_op jit(solution)/shard_map/ppermute | solution.py:23
  383.3 6.8 %collective-permute-done.20.refs_7_ = f32[8,16,512]{2,1,0:T(8,128)S(1)} collective-permute-done((f32[8,16,512]{2,1,0:T(8,128)S(1)}, f32[8,16,512]{2,1,0:T(8,128)S(1)}, u32[]{:S(2)}, u32[]{:S(2)}) %collective-permute-start.20) | collective-permute-done | bytes 262176 | tf_op jit(solution)/shard_map/ppermute | solution.py:23
  390.1 5.3 %chunk_step.10 = (f32[256,512]{1,0:T(8,128)S(1)}, f32[256,128]{1,0:T(8,128)S(1)}) custom-call(f32[8,16,512]{2,1,0:T(8,128)S(1)} %get-tuple-element.48.refs_0_, f32[8,16,512]{2,1,0:T(8,128)} %collective-permute-done.14.refs_1_, f32[8,16,512]{2,1,0:T(8,128)} %collective-permute-done.15.refs_2_, ...), custom_call_target="tpu_custom_call", output_to_operand_aliasing={{0}: (13, {}), {1}: (14, {})} | custom-call | flops 3221225472 | bytes 2097152 | tf_op jit(solution)/shard_map/chunk_step/pallas_call | solution.py:88
  395.5 3.0 collective-permute-done.4.refs_5_
  405.0 3.3 all-to-all-start
  409.3 15.3 %all-to-all-done = f32[32,8,512]{2,1,0:T(8,128)S(1)} async-done(((f32[32,8,512]{2,1,0:T(8,128)}), f32[32,8,512]{2,1,0:T(8,128)S(1)}, u32[]{:S(2)}, u32[]{:S(2)}) %all-to-all-start) | async-done | bytes 524320 | tf_op jit(solution)/shard_map/all_to_all | solution.py:186
  428.7 7.2 %all-to-all-done.1 = f32[32,1,512]{2,1,0:T(1,128)S(1)} async-done(((f32[32,1,512]{2,1,0:T(1,128)}), f32[32,1,512]{2,1,0:T(1,128)S(1)}, u32[]{:S(2)}, u32[]{:S(2)}) %all-to-all-start.1) | async-done | bytes 65568 | tf_op jit(solution)/shard_map/all_to_all | solution.py:197
  (237 shorter events, 92.9 us)
Async XLA Ops:
  7.2 121.0 %all-gather.3.cloned.1.call-start = ((), (), s32[]{:S(2)}) async-start(), calls=%async_computation.2 | async-start | bytes 1351680 | tf_op jit(solution)/shard_map/all_gather | solution.py:159
  20.0 29.9 %collective-permute-start.10 = (f32[9,16,512]{2,1,0:T(8,128)}, f32[9,16,512]{2,1,0:T(8,128)}, u32[]{:S(2)}, u32[]{:S(2)}) collective-permute-start(f32[9,16,512]{2,1,0:T(8,128)} %get-tuple-element.99), channel_id=1, source_target_pairs={{0,2},{1,3},{2,0},{3,1},{4,6},{5,7},{6,4},{7,5},{8,10},{9,11},{10,... | collective-permute-start | bytes 884744 | tf_op jit(solution)/shard_map/ppermute | solution.py:23
  21.1 59.3 %collective-permute-start.11 = (f32[9,16,512]{2,1,0:T(8,128)}, f32[9,16,512]{2,1,0:T(8,128)}, u32[]{:S(2)}, u32[]{:S(2)}) collective-permute-start(f32[9,16,512]{2,1,0:T(8,128)} %get-tuple-element.100), channel_id=1, source_target_pairs={{0,5},{1,4},{2,7},{3,6},{4,1},{5,0},{6,3},{7,2},{8,13},{9,12},{10,... | collective-permute-start | bytes 884744 | tf_op jit(solution)/shard_map/ppermute | solution.py:23
  36.2 45.7 %collective-permute-start.12 = (f32[9,16,512]{2,1,0:T(8,128)}, f32[9,16,512]{2,1,0:T(8,128)}, u32[]{:S(2)}, u32[]{:S(2)}) collective-permute-start(f32[9,16,512]{2,1,0:T(8,128)} %get-tuple-element.101), channel_id=1, source_target_pairs={{0,1},{1,0},{2,3},{3,2},{4,5},{5,4},{6,7},{7,6},{8,9},{9,8},{10,11... | collective-permute-start | bytes 884744 | tf_op jit(solution)/shard_map/ppermute | solution.py:23
  37.2 50.5 %collective-permute-start.13 = (f32[9,16,512]{2,1,0:T(8,128)}, f32[9,16,512]{2,1,0:T(8,128)}, u32[]{:S(2)}, u32[]{:S(2)}) collective-permute-start(f32[9,16,512]{2,1,0:T(8,128)} %get-tuple-element.96), channel_id=1, source_target_pairs={{0,4},{1,5},{2,6},{3,7},{4,0},{5,1},{6,2},{7,3},{8,12},{9,13},{10,... | collective-permute-start | bytes 884744 | tf_op jit(solution)/shard_map/ppermute | solution.py:23
  45.8 66.4 %collective-permute-start.21 = (f32[8,24,512]{2,1,0:T(8,128)}, f32[8,24,512]{2,1,0:T(8,128)}, u32[]{:S(2)}, u32[]{:S(2)}) collective-permute-start(f32[8,24,512]{2,1,0:T(8,128)} %get-tuple-element.78), channel_id=1, source_target_pairs={{0,7},{1,6},{2,5},{3,4},{4,3},{5,2},{6,1},{7,0},{8,15},{9,14},{10,... | collective-permute-start | bytes 1179656 | tf_op jit(solution)/shard_map/ppermute | solution.py:23
  49.9 60.5 %collective-permute-start.14 = (f32[8,16,512]{2,1,0:T(8,128)}, f32[8,16,512]{2,1,0:T(8,128)}, u32[]{:S(2)}, u32[]{:S(2)}) collective-permute-start(f32[8,16,512]{2,1,0:T(8,128)} %get-tuple-element.47), channel_id=1, source_target_pairs={{0,7},{1,6},{2,5},{3,4},{4,3},{5,2},{6,1},{7,0},{8,15},{9,14},{10,... | collective-permute-start | bytes 786440 | tf_op jit(solution)/shard_map/ppermute | solution.py:23
  80.4 31.7 %collective-permute-start.15 = (f32[8,16,512]{2,1,0:T(8,128)}, f32[8,16,512]{2,1,0:T(8,128)}, u32[]{:S(2)}, u32[]{:S(2)}) collective-permute-start(f32[8,16,512]{2,1,0:T(8,128)} %get-tuple-element.46), channel_id=1, source_target_pairs={{0,3},{1,2},{2,1},{3,0},{4,7},{5,6},{6,5},{7,4},{8,11},{9,10},{10,... | collective-permute-start | bytes 786440 | tf_op jit(solution)/shard_map/ppermute | solution.py:23
  106.2 58.7 %collective-permute-start.35 = (f32[8,32,512]{2,1,0:T(8,128)}, f32[8,32,512]{2,1,0:T(8,128)}, u32[]{:S(2)}, u32[]{:S(2)}) collective-permute-start(f32[8,32,512]{2,1,0:T(8,128)} %get-tuple-element.62), channel_id=1, source_target_pairs={{0,7},{1,6},{2,5},{3,4},{4,3},{5,2},{6,1},{7,0},{8,15},{9,14},{10,... | collective-permute-start | bytes 1572872 | tf_op jit(solution)/shard_map/ppermute | solution.py:23
  108.3 58.1 %collective-permute-start.36 = (f32[8,32,512]{2,1,0:T(8,128)}, f32[8,32,512]{2,1,0:T(8,128)}, u32[]{:S(2)}, u32[]{:S(2)}) collective-permute-start(f32[8,32,512]{2,1,0:T(8,128)} %get-tuple-element.61), channel_id=1, source_target_pairs={{0,3},{1,2},{2,1},{3,0},{4,7},{5,6},{6,5},{7,4},{8,11},{9,10},{10,... | collective-permute-start | bytes 1572872 | tf_op jit(solution)/shard_map/ppermute | solution.py:23
  110.3 56.3 %collective-permute-start.37 = (f32[8,32,512]{2,1,0:T(8,128)}, f32[8,32,512]{2,1,0:T(8,128)}, u32[]{:S(2)}, u32[]{:S(2)}) collective-permute-start(f32[8,32,512]{2,1,0:T(8,128)} %get-tuple-element.60), channel_id=1, source_target_pairs={{0,6},{1,7},{2,4},{3,5},{4,2},{5,3},{6,0},{7,1},{8,14},{9,15},{10,... | collective-permute-start | bytes 1572872 | tf_op jit(solution)/shard_map/ppermute | solution.py:23
  112.1 56.4 %collective-permute-start.38 = (f32[8,32,512]{2,1,0:T(8,128)}, f32[8,32,512]{2,1,0:T(8,128)}, u32[]{:S(2)}, u32[]{:S(2)}) collective-permute-start(f32[8,32,512]{2,1,0:T(8,128)} %get-tuple-element.59), channel_id=1, source_target_pairs={{0,2},{1,3},{2,0},{3,1},{4,6},{5,7},{6,4},{7,5},{8,10},{9,11},{10,... | collective-permute-start | bytes 1572872 | tf_op jit(solution)/shard_map/ppermute | solution.py:23
  112.1 50.1 %collective-permute-start.22 = (f32[8,24,512]{2,1,0:T(8,128)}, f32[8,24,512]{2,1,0:T(8,128)}, u32[]{:S(2)}, u32[]{:S(2)}) collective-permute-start(f32[8,24,512]{2,1,0:T(8,128)} %get-tuple-element.77), channel_id=1, source_target_pairs={{0,3},{1,2},{2,1},{3,0},{4,7},{5,6},{6,5},{7,4},{8,11},{9,10},{10,... | collective-permute-start | bytes 1179656 | tf_op jit(solution)/shard_map/ppermute | solution.py:23
  162.2 47.9 %collective-permute-start.39 = (f32[8,32,512]{2,1,0:T(8,128)}, f32[8,32,512]{2,1,0:T(8,128)S(1)}, u32[]{:S(2)}, u32[]{:S(2)}) collective-permute-start(f32[8,32,512]{2,1,0:T(8,128)} %get-tuple-element.58), channel_id=1, source_target_pairs={{0,5},{1,4},{2,7},{3,6},{4,1},{5,0},{6,3},{7,2},{8,13},{9,12},{10,... | collective-permute-start | bytes 1572872 | tf_op jit(solution)/shard_map/ppermute | solution.py:23
  164.8 47.3 %collective-permute-start.40 = (f32[8,32,512]{2,1,0:T(8,128)}, f32[8,32,512]{2,1,0:T(8,128)S(1)}, u32[]{:S(2)}, u32[]{:S(2)}) collective-permute-start(f32[8,32,512]{2,1,0:T(8,128)} %get-tuple-element.57), channel_id=1, source_target_pairs={{0,1},{1,0},{2,3},{3,2},{4,5},{5,4},{6,7},{7,6},{8,9},{9,8},{10,11... | collective-permute-start | bytes 1572872 | tf_op jit(solution)/shard_map/ppermute | solution.py:23
  166.3 66.4 %collective-permute-start.41 = (f32[8,32,512]{2,1,0:T(8,128)}, f32[8,32,512]{2,1,0:T(8,128)S(1)}, u32[]{:S(2)}, u32[]{:S(2)}) collective-permute-start(f32[8,32,512]{2,1,0:T(8,128)} %get-tuple-element.56), channel_id=1, source_target_pairs={{0,4},{1,5},{2,6},{3,7},{4,0},{5,1},{6,2},{7,3},{8,12},{9,13},{10,... | collective-permute-start | bytes 1572872 | tf_op jit(solution)/shard_map/ppermute | solution.py:23
  166.6 66.1 %collective-permute-start.28 = (f32[8,32,512]{2,1,0:T(8,128)}, f32[8,32,512]{2,1,0:T(8,128)S(1)}, u32[]{:S(2)}, u32[]{:S(2)}) collective-permute-start(f32[8,32,512]{2,1,0:T(8,128)} %get-tuple-element.70), channel_id=1, source_target_pairs={{0,7},{1,6},{2,5},{3,4},{4,3},{5,2},{6,1},{7,0},{8,15},{9,14},{10,... | collective-permute-start | bytes 1572872 | tf_op jit(solution)/shard_map/ppermute | solution.py:23
  168.4 65.4 %collective-permute-start.29 = (f32[8,32,512]{2,1,0:T(8,128)}, f32[8,32,512]{2,1,0:T(8,128)S(1)}, u32[]{:S(2)}, u32[]{:S(2)}) collective-permute-start(f32[8,32,512]{2,1,0:T(8,128)} %get-tuple-element.69), channel_id=1, source_target_pairs={{0,3},{1,2},{2,1},{3,0},{4,7},{5,6},{6,5},{7,4},{8,11},{9,10},{10,... | collective-permute-start | bytes 1572872 | tf_op jit(solution)/shard_map/ppermute | solution.py:23
  210.1 57.5 %collective-permute-start.30 = (f32[8,32,512]{2,1,0:T(8,128)S(1)}, f32[8,32,512]{2,1,0:T(8,128)S(1)}, u32[]{:S(2)}, u32[]{:S(2)}) collective-permute-start(f32[8,32,512]{2,1,0:T(8,128)S(1)} %copy-done.10), channel_id=1, source_target_pairs={{0,6},{1,7},{2,4},{3,5},{4,2},{5,3},{6,0},{7,1},{8,14},{9,15},{10,... | collective-permute-start | bytes 1572872 | tf_op jit(solution)/shard_map/ppermute | solution.py:23
  212.1 57.5 %collective-permute-start.31 = (f32[8,32,512]{2,1,0:T(8,128)S(1)}, f32[8,32,512]{2,1,0:T(8,128)S(1)}, u32[]{:S(2)}, u32[]{:S(2)}) collective-permute-start(f32[8,32,512]{2,1,0:T(8,128)S(1)} %copy-done.9), channel_id=1, source_target_pairs={{0,2},{1,3},{2,0},{3,1},{4,6},{5,7},{6,4},{7,5},{8,10},{9,11},{10,... | collective-permute-start | bytes 1572872 | tf_op jit(solution)/shard_map/ppermute | solution.py:23
  232.7 64.6 %collective-permute-start.32 = (f32[8,32,512]{2,1,0:T(8,128)S(1)}, f32[8,32,512]{2,1,0:T(8,128)S(1)}, u32[]{:S(2)}, u32[]{:S(2)}) collective-permute-start(f32[8,32,512]{2,1,0:T(8,128)S(1)} %copy-done.8), channel_id=1, source_target_pairs={{0,5},{1,4},{2,7},{3,6},{4,1},{5,0},{6,3},{7,2},{8,13},{9,12},{10,... | collective-permute-start | bytes 1572872 | tf_op jit(solution)/shard_map/ppermute | solution.py:23
  232.7 64.6 %collective-permute-start.33 = (f32[8,32,512]{2,1,0:T(8,128)S(1)}, f32[8,32,512]{2,1,0:T(8,128)S(1)}, u32[]{:S(2)}, u32[]{:S(2)}) collective-permute-start(f32[8,32,512]{2,1,0:T(8,128)S(1)} %copy-done.7), channel_id=1, source_target_pairs={{0,1},{1,0},{2,3},{3,2},{4,5},{5,4},{6,7},{7,6},{8,9},{9,8},{10,11... | collective-permute-start | bytes 1572872 | tf_op jit(solution)/shard_map/ppermute | solution.py:23
  233.8 83.2 %collective-permute-start.34 = (f32[8,32,512]{2,1,0:T(8,128)S(1)}, f32[8,32,512]{2,1,0:T(8,128)S(1)}, u32[]{:S(2)}, u32[]{:S(2)}) collective-permute-start(f32[8,32,512]{2,1,0:T(8,128)S(1)} %copy-done.6), channel_id=1, source_target_pairs={{0,4},{1,5},{2,6},{3,7},{4,0},{5,1},{6,2},{7,3},{8,12},{9,13},{10,... | collective-permute-start | bytes 1572872 | tf_op jit(solution)/shard_map/ppermute | solution.py:23
  267.6 58.6 %collective-permute-start.23 = (f32[8,24,512]{2,1,0:T(8,128)S(1)}, f32[8,24,512]{2,1,0:T(8,128)S(1)}, u32[]{:S(2)}, u32[]{:S(2)}) collective-permute-start(f32[8,24,512]{2,1,0:T(8,128)S(1)} %copy-done.15), channel_id=1, source_target_pairs={{0,6},{1,7},{2,4},{3,5},{4,2},{5,3},{6,0},{7,1},{8,14},{9,15},{10,... | collective-permute-start | bytes 1179656 | tf_op jit(solution)/shard_map/ppermute | solution.py:23
  269.6 58.7 %collective-permute-start.24 = (f32[8,24,512]{2,1,0:T(8,128)S(1)}, f32[8,24,512]{2,1,0:T(8,128)S(1)}, u32[]{:S(2)}, u32[]{:S(2)}) collective-permute-start(f32[8,24,512]{2,1,0:T(8,128)S(1)} %copy-done.14), channel_id=1, source_target_pairs={{0,2},{1,3},{2,0},{3,1},{4,6},{5,7},{6,4},{7,5},{8,10},{9,11},{10,... | collective-permute-start | bytes 1179656 | tf_op jit(solution)/shard_map/ppermute | solution.py:23
  297.4 50.6 %collective-permute-start.25 = (f32[8,24,512]{2,1,0:T(8,128)S(1)}, f32[8,24,512]{2,1,0:T(8,128)S(1)}, u32[]{:S(2)}, u32[]{:S(2)}) collective-permute-start(f32[8,24,512]{2,1,0:T(8,128)S(1)} %copy-done.13), channel_id=1, source_target_pairs={{0,5},{1,4},{2,7},{3,6},{4,1},{5,0},{6,3},{7,2},{8,13},{9,12},{10,... | collective-permute-start | bytes 1179656 | tf_op jit(solution)/shard_map/ppermute | solution.py:23
  297.4 50.6 %collective-permute-start.26 = (f32[8,24,512]{2,1,0:T(8,128)S(1)}, f32[8,24,512]{2,1,0:T(8,128)S(1)}, u32[]{:S(2)}, u32[]{:S(2)}) collective-permute-start(f32[8,24,512]{2,1,0:T(8,128)S(1)} %copy-done.12), channel_id=1, source_target_pairs={{0,1},{1,0},{2,3},{3,2},{4,5},{5,4},{6,7},{7,6},{8,9},{9,8},{10,11... | collective-permute-start | bytes 1179656 | tf_op jit(solution)/shard_map/ppermute | solution.py:23
  317.0 45.0 %collective-permute-start.27 = (f32[8,24,512]{2,1,0:T(8,128)S(1)}, f32[8,24,512]{2,1,0:T(8,128)S(1)}, u32[]{:S(2)}, u32[]{:S(2)}) collective-permute-start(f32[8,24,512]{2,1,0:T(8,128)S(1)} %copy-done.11), channel_id=1, source_target_pairs={{0,4},{1,5},{2,6},{3,7},{4,0},{5,1},{6,2},{7,3},{8,12},{9,13},{10,... | collective-permute-start | bytes 1179656 | tf_op jit(solution)/shard_map/ppermute | solution.py:23
  326.3 43.3 %collective-permute-start.16 = (f32[8,16,512]{2,1,0:T(8,128)S(1)}, f32[8,16,512]{2,1,0:T(8,128)S(1)}, u32[]{:S(2)}, u32[]{:S(2)}) collective-permute-start(f32[8,16,512]{2,1,0:T(8,128)S(1)} %copy-done.21), channel_id=1, source_target_pairs={{0,6},{1,7},{2,4},{3,5},{4,2},{5,3},{6,0},{7,1},{8,14},{9,15},{10,... | collective-permute-start | bytes 786440 | tf_op jit(solution)/shard_map/ppermute | solution.py:23
  328.3 43.3 %collective-permute-start.17 = (f32[8,16,512]{2,1,0:T(8,128)S(1)}, f32[8,16,512]{2,1,0:T(8,128)S(1)}, u32[]{:S(2)}, u32[]{:S(2)}) collective-permute-start(f32[8,16,512]{2,1,0:T(8,128)S(1)} %copy-done.20), channel_id=1, source_target_pairs={{0,2},{1,3},{2,0},{3,1},{4,6},{5,7},{6,4},{7,5},{8,10},{9,11},{10,... | collective-permute-start | bytes 786440 | tf_op jit(solution)/shard_map/ppermute | solution.py:23
  348.0 33.7 %collective-permute-start.18 = (f32[8,16,512]{2,1,0:T(8,128)S(1)}, f32[8,16,512]{2,1,0:T(8,128)S(1)}, u32[]{:S(2)}, u32[]{:S(2)}) collective-permute-start(f32[8,16,512]{2,1,0:T(8,128)S(1)} %copy-done.19), channel_id=1, source_target_pairs={{0,5},{1,4},{2,7},{3,6},{4,1},{5,0},{6,3},{7,2},{8,13},{9,12},{10,... | collective-permute-start | bytes 786440 | tf_op jit(solution)/shard_map/ppermute | solution.py:23
  348.0 33.7 %collective-permute-start.19 = (f32[8,16,512]{2,1,0:T(8,128)S(1)}, f32[8,16,512]{2,1,0:T(8,128)S(1)}, u32[]{:S(2)}, u32[]{:S(2)}) collective-permute-start(f32[8,16,512]{2,1,0:T(8,128)S(1)} %copy-done.18), channel_id=1, source_target_pairs={{0,1},{1,0},{2,3},{3,2},{4,5},{5,4},{6,7},{7,6},{8,9},{9,8},{10,11... | collective-permute-start | bytes 786440 | tf_op jit(solution)/shard_map/ppermute | solution.py:23
  (49 other events, 1665.3 us)
Sparse Core Ops, SparseCore 0:
  100.8 17.1 all-gather.2

commit v3 on v2

v3 whole, which is shorter than its diff:
```python
import functools
import math

import jax
import jax.numpy as jnp
from jax import lax
from jax.experimental import pallas as pl
from jax.experimental.pallas import tpu as pltpu
from jax.sharding import PartitionSpec as P

HIGH = lax.Precision.HIGHEST
PHASE_RATE = 0.37
STEP_LENGTH = 0.5
EPSILON = 1e-06
GROUP = 8
LANES = 128

NN = (((1,), (0,)), ((), ()))
NT = (((1,), (1,)), ((), ()))


def swap(x, axis, k):
    return lax.ppermute(x, axis, [(i, i ^ k) for i in range(lax.axis_size(axis))])


def partner_order(size):
    assert size & (size - 1) == 0
    across, near = list(range(size // 2, size))[::-1], list(range(1, size // 2))[::-1]
    order = [k for pair in zip(across, near + [None]) for k in pair if k is not None]
    return order


def gate_table(owner_order, own_freqs, freqs, waveform, gate_index):
    samples = waveform.shape[0]
    freq_ids = (owner_order[:, None] * own_freqs + jnp.arange(own_freqs)[None, :]).reshape(freqs)
    freq_col = freq_ids.astype(jnp.float32)[:, None] + 0.5
    time_row = jnp.arange(samples, dtype=jnp.float32)[None, :] + 0.5
    phases = PHASE_RATE * freq_col * time_row
    kernel = jnp.stack([jnp.cos(phases), jnp.sin(phases)], axis=1) / math.sqrt(freqs)
    steps = jnp.arange(samples)
    lag = gate_index[:, None] - steps[None, :]
    picked = jnp.sum(
        jnp.where(lag[:, :, None] == steps[None, None, :], waveform[None, None, :], 0.0), axis=-1
    )
    return jnp.einsum("gk,fpk->gfp", picked, kernel, precision=HIGH).reshape(gate_index.shape[0], freqs * 2)


def split(x):
    high = x.astype(jnp.bfloat16)
    return high, (x - high.astype(jnp.float32)).astype(jnp.bfloat16)


def three_pass(a, b, dims):
    dot = functools.partial(lax.dot_general, dimension_numbers=dims, preferred_element_type=jnp.float32)
    return dot(a[0], b[0]) + (dot(a[0], b[1]) + dot(a[1], b[0]))


def params():
    return pltpu.CompilerParams(vmem_limit_bytes=48 * 1024 * 1024)


def cost(flops, bytes_accessed):
    return pl.CostEstimate(flops=flops, bytes_accessed=bytes_accessed, transcendentals=0)


def whole(a):
    return pl.BlockSpec(a.shape, lambda *_: (0,) * a.ndim)


ANY = pl.BlockSpec(memory_space=pl.ANY)
SCALARS = pl.BlockSpec(memory_space=pltpu.SMEM)


def pack_kernel(distances, own, first, rows, lanes, place_ref, block_ref, models_ref, *refs):
    outs, sems = refs[: len(distances)], refs[len(distances)]
    spectra = block_ref.shape[0]
    copies = []
    for j, k in enumerate(distances):
        row = pl.multiple_of((place_ref[1] ^ k) * own + first, GROUP)
        copies.append((block_ref.at[:, pl.ds(row, rows)], outs[j].at[pl.ds(0, spectra)]))
        owned, members = models_ref.shape
        for lane in range(lanes):
            part = owned // lanes
            target = outs[j].at[spectra, pl.ds(0, part), pl.ds(lane * members, members)]
            copies.append((models_ref.at[pl.ds(lane * part, part)], target))
    copies = [pltpu.make_async_copy(*c, sems.at[n]) for n, c in enumerate(copies)]
    for c in copies:
        c.start()
    for c in copies:
        c.wait()


def pack(place, block, models, distances, own, first, rows, lanes):
    spectra, _, cells = block.shape
    shape = jax.ShapeDtypeStruct((spectra + (lanes > 0), rows, cells), jnp.float32)
    return pl.pallas_call(
        functools.partial(pack_kernel, distances, own, first, rows, lanes),
        in_specs=[SCALARS, ANY, ANY],
        out_specs=[ANY] * len(distances),
        out_shape=[shape] * len(distances),
        scratch_shapes=[pltpu.SemaphoreType.DMA((len(distances) * (1 + lanes),))],
        cost_estimate=cost(0, 8 * len(distances) * spectra * rows * cells),
        name="pack",
    )(place, block, models)


def near_kernel(lanes, place_ref, cells_ref, models_ref, *refs):
    riders, out_ref = refs[:-1], refs[-1]
    owned, members = models_ref.shape
    part = owned // lanes
    out_ref[pl.ds(0, owned), :] = models_ref[...]
    for j, r in enumerate(riders):
        for lane in range(lanes):
            out_ref[pl.ds((j + 1) * owned + lane * part, part), :] = r[
                0, pl.ds(0, part), pl.ds(lane * members, members)
            ]
    block_cells = owned * (len(riders) + 1)
    home = cells_ref[...] // block_cells
    other = jnp.where(home == place_ref[0], -1, home).astype(jnp.float32)
    other = jnp.max(other, axis=1, keepdims=True)
    out_ref[pl.ds(block_cells, GROUP), :] = jnp.broadcast_to(other, (GROUP, members))


def near_models(place, cell_index, models, first, lanes):
    owned, members = models.shape
    slabs, rows, cells = first[0].shape
    rider = pl.BlockSpec((1, rows, cells), lambda i: (slabs - 1, 0, 0))
    return pl.pallas_call(
        functools.partial(near_kernel, lanes),
        grid=(1,),
        in_specs=[SCALARS, whole(cell_index), whole(models)] + [rider] * len(first),
        out_specs=pl.BlockSpec((owned * (len(first) + 1) + GROUP, members), lambda i: (0, 0)),
        out_shape=jax.ShapeDtypeStruct((owned * (len(first) + 1) + GROUP, members), jnp.float32),
        compiler_params=params(),
        cost_estimate=cost(0, 1 << 20),
        name="near_models",
    )(place, cell_index, models, *first)


def tile_models_kernel(owned, partners, place_ref, cells_ref, far_ref, high_ref, low_ref):
    tiles, rows, _ = far_ref.shape
    owners = len(partners)
    block_cells = owned * owners
    cells = cells_ref[...]
    distance = (cells // owned % owners) ^ place_ref[1]
    slot = jnp.zeros_like(cells)
    for n, k in enumerate(partners):
        slot = jnp.where(distance == k, n, slot)
    spot = slot * owned + cells % owned
    home = cells // block_cells
    high, low = None, None
    for t in range(tiles):
        row = lax.broadcasted_iota(jnp.int32, (block_cells, cells.shape[1]), 0)
        pick = jnp.where((row == spot) & (home == t), 1.0, 0.0).astype(jnp.bfloat16)
        h, l = split(far_ref[t, pl.ds(0, block_cells), :].T)
        h = lax.dot_general(h, pick, NN, preferred_element_type=jnp.float32)
        l = lax.dot_general(l, pick, NN, preferred_element_type=jnp.float32)
        high, low = (h, l) if t == 0 else (high + h, low + l)
    high_ref[...] = high.astype(jnp.bfloat16)
    low_ref[...] = low.astype(jnp.bfloat16)


def tile_models(place, cell_index, far, owned, partners):
    shape = jax.ShapeDtypeStruct((far.shape[2], cell_index.shape[1]), jnp.bfloat16)
    return pl.pallas_call(
        functools.partial(tile_models_kernel, owned, partners),
        in_specs=[SCALARS] + [pl.BlockSpec(memory_space=pltpu.VMEM)] * 2,
        out_specs=[pl.BlockSpec(memory_space=pltpu.VMEM)] * 2,
        out_shape=[shape] * 2,
        compiler_params=params(),
        cost_estimate=cost(1 << 30, 2 << 20),
        name="tile_models",
    )(place, cell_index, far)


def wide_kernel(table_ref, high_ref, low_ref):
    fp, gates = table_ref.shape
    rows, columns = high_ref.shape
    iota = lax.broadcasted_iota
    down = (iota(jnp.int32, (rows, fp), 0) // GROUP == iota(jnp.int32, (rows, fp), 1)).astype(jnp.float32)
    across = iota(jnp.int32, (gates, columns), 1) // GROUP == iota(jnp.int32, (gates, columns), 0)
    across = across.astype(jnp.float32).astype(jnp.bfloat16)
    down = down.astype(jnp.bfloat16)
    same = iota(jnp.int32, (rows, columns), 0) % GROUP == iota(jnp.int32, (rows, columns), 1) % GROUP
    for part, ref in zip(split(table_ref[...]), (high_ref, low_ref)):
        tall = lax.dot_general(down, part, NN, preferred_element_type=jnp.float32).astype(jnp.bfloat16)
        full = lax.dot_general(tall, across, NN, preferred_element_type=jnp.float32)
        ref[...] = jnp.where(same, full, 0.0).astype(jnp.bfloat16)


def wide_table(table):
    shape = jax.ShapeDtypeStruct((table.shape[0] * GROUP, table.shape[1] * GROUP), jnp.bfloat16)
    return pl.pallas_call(
        wide_kernel,
        in_specs=[pl.BlockSpec(memory_space=pltpu.VMEM)],
        out_specs=[pl.BlockSpec(memory_space=pltpu.VMEM)] * 2,
        out_shape=[shape] * 2,
        compiler_params=params(),
        cost_estimate=cost(1 << 28, 1 << 20),
        name="wide_table",
    )(table)


def chunk_kernel(pieces, block_cells, last, place_ref, *refs):
    sens_refs = refs[:pieces]
    model_h, model_l, gate_h, gate_l, obs_ref, cells_ref, terms_in, square_in, terms_ref, square_ref = refs[pieces:]

    @pl.when(pl.program_id(0) == 0)
    def _():
        terms_ref[...] = terms_in[...]
        square_ref[...] = square_in[...]

    sens = [split(r[...].reshape(r.shape[0] * r.shape[1], r.shape[2])) for r in sens_refs]
    sens = tuple(jnp.concatenate([s[i] for s in sens], axis=0) for i in range(2))
    gates = (gate_h[...], gate_l[...])
    predicted = three_pass((model_h[...], model_l[...]), sens, NT)
    misfit_rows = three_pass(split(predicted), gates, NN) - obs_ref[0]
    square_ref[...] += jnp.sum(misfit_rows * misfit_rows, axis=1, keepdims=True)
    back = three_pass(split(misfit_rows), gates, NT)
    terms = terms_ref[...] + three_pass(split(back), sens, NN)
    terms_ref[...] = terms

    if last:

        @pl.when(pl.program_id(0) == pl.num_programs(0) - 1)
        def _():
            cells = cells_ref[...]
            spot = cells % block_cells + jnp.where(cells // block_cells == place_ref[0], 0, block_cells)
            size = cells.shape[1]
            row = lax.broadcasted_iota(jnp.int32, (size, size), 0)
            pick = jnp.where(row == spot, 1.0, 0.0).astype(jnp.bfloat16)
            high = terms.astype(jnp.bfloat16)
            middle, low = split(terms - high.astype(jnp.float32))
            dot = functools.partial(lax.dot_general, dimension_numbers=NT, preferred_element_type=jnp.float32)
            terms_ref[...] = dot(high, pick) + (dot(middle, pick) + dot(low, pick))


def chunk_step(place, block, sens, first, models_t, gates, obs, cell_index, terms, square, block_cells, last):
    spectra, soundings, cells = block.shape
    rows = sens[0].shape[1]
    pieces = len(sens) + 1
    members = terms.shape[0]
    own_groups = soundings // (pieces * GROUP)
    return pl.pallas_call(
        functools.partial(chunk_kernel, pieces, block_cells, last),
        grid_spec=pltpu.PrefetchScalarGridSpec(
            num_scalar_prefetch=1,
            grid=(rows // GROUP,),
            in_specs=[
                pl.BlockSpec((spectra, GROUP, cells), lambda i, place: (0, place[1] * own_groups + first + i, 0))
            ]
            + [pl.BlockSpec((spectra, GROUP, cells), lambda i, place: (0, i, 0))] * len(sens)
            + [whole(a) for a in (*models_t, *gates)]
            + [pl.BlockSpec((1, 1, obs.shape[2]), lambda i, place: (first + i, 0, 0)), whole(cell_index)]
            + [whole(terms), whole(square)],
            out_specs=[whole(terms), whole(square)],
        ),
        out_shape=[
            jax.ShapeDtypeStruct(terms.shape, jnp.float32),
            jax.ShapeDtypeStruct(square.shape, jnp.float32),
        ],
        input_output_aliases={pieces + 7: 0, pieces + 8: 1},
        compiler_params=params(),
        cost_estimate=cost(
            12 * pieces * spectra * rows * cells * members * 2, 4 * pieces * spectra * rows * cells
        ),
        name="chunk_step",
    )(place, block, *sens, *models_t, *gates, obs, cell_index, terms, square)


def exact_dot(a, b, dims):
    return lax.dot_general(a, b, dims, precision=HIGH, preferred_element_type=jnp.float32)


def gradient_kernel(tiles, owned, borrowed_ref, got_ref, square_ref, out_ref):
    devices, slab, cells = got_ref.shape
    owners = devices // tiles
    block_cells = owned * owners
    members = square_ref.shape[0]
    sums = []
    for t in range(tiles):
        total = got_ref[t * owners]
        for f in range(1, owners):
            total = total + got_ref[t * owners + f]
        sums.append(total)
    gradient = []
    for b in range(tiles):
        block = sums[b][:, :block_cells]
        for t in range(tiles):
            block = block + jnp.where(borrowed_ref[t] == b, sums[t][:, block_cells:], 0.0)
        gradient.append(block)
    square = sum(jnp.sum(g * g, axis=1, keepdims=True) for g in gradient)
    scale = jnp.sqrt(square / (tiles * block_cells) + EPSILON)
    iota = lax.broadcasted_iota
    per_row = members // slab
    down = (iota(jnp.int32, (slab, members), 1) // per_row == iota(jnp.int32, (slab, members), 0))
    lane = iota(jnp.int32, (members, LANES), 1)
    spread = jnp.where(iota(jnp.int32, (members, LANES), 0) % per_row + owned == lane, square_ref[...], 0.0)
    rider = exact_dot(down.astype(jnp.float32), spread, NN)
    for b in range(tiles):
        step = gradient[b] / scale
        for f in range(owners):
            piece = step[:, f * owned : (f + 1) * owned]
            piece = jnp.concatenate([piece, jnp.zeros((slab, LANES - owned), jnp.float32)], axis=1)
            out_ref[b * owners + f] = piece + rider


def gradient_step(borrowed, got, square, tiles, owned):
    devices, slab, _ = got.shape
    return pl.pallas_call(
        functools.partial(gradient_kernel, tiles, owned),
        in_specs=[SCALARS] + [pl.BlockSpec(memory_space=pltpu.VMEM)] * 2,
        out_specs=pl.BlockSpec(memory_space=pltpu.VMEM),
        out_shape=jax.ShapeDtypeStruct((devices, slab, LANES), jnp.float32),
        compiler_params=params(),
        cost_estimate=cost(1 << 22, 1 << 20),
        name="gradient_step",
    )(borrowed, got, square)


def update_kernel(divisor, models_ref, back_ref, updated_ref, misfit_ref):
    devices, slab, _ = back_ref.shape
    owned, members = models_ref.shape
    per_row = members // slab
    iota = lax.broadcasted_iota
    riders = back_ref[0]
    for d in range(1, devices):
        riders = riders + back_ref[d]
    down = (iota(jnp.int32, (slab, members), 1) // per_row == iota(jnp.int32, (slab, members), 0))
    tall = exact_dot(riders, down.astype(jnp.float32), (((0,), (0,)), ((), ())))
    mine = iota(jnp.int32, (LANES, members), 1) % per_row + owned == iota(jnp.int32, (LANES, members), 0)
    misfit = jnp.sum(jnp.where(mine, tall, 0.0), axis=0, keepdims=True) / divisor
    step = back_ref[...].reshape(members, LANES).T[:owned]
    updated_ref[...] = models_ref[...] - STEP_LENGTH * misfit * step
    misfit_ref[...] = misfit


def update(models, back, divisor):
    return pl.pallas_call(
        functools.partial(update_kernel, divisor),
        in_specs=[pl.BlockSpec(memory_space=pltpu.VMEM)] * 2,
        out_specs=[pl.BlockSpec(memory_space=pltpu.VMEM)] * 2,
        out_shape=[
            jax.ShapeDtypeStruct(models.shape, jnp.float32),
            jax.ShapeDtypeStruct((1, models.shape[1]), jnp.float32),
        ],
        compiler_params=params(),
        cost_estimate=cost(1 << 20, 1 << 18),
        name="update",
    )(models, back)


def chunk_groups(groups, riders):
    if groups < 8:
        return [1] * groups
    first, last = max(groups // 8, riders), [groups // 8, groups // 16 or 1]
    rest = groups - first - sum(last)
    middle = -(-rest // (groups // 4))
    return [first] + [rest // middle + (i < rest % middle) for i in range(middle)] + last


def body(sensitivity, models, observed, waveform, cell_index, gate_index):
    both = ("tile", "freq")
    tiles, owners, devices = lax.axis_size("tile"), lax.axis_size("freq"), lax.axis_size(both)
    _, own_freqs, parts, soundings, cells = sensitivity.shape
    freqs = own_freqs * owners
    spectra = own_freqs * parts
    owned, members = models.shape
    ncells = owned * devices
    gates = gate_index.shape[0]
    divisor = 2.0 * tiles * soundings * gates
    own = soundings // owners
    block_cells = owned * owners
    place = jnp.stack([lax.axis_index("tile"), lax.axis_index("freq")])

    block = sensitivity[0].reshape(spectra, soundings, cells)
    lanes = cells // members if owned % (GROUP * (cells // members)) == 0 else 1
    sizes = chunk_groups(own // GROUP, -(-owned // (lanes * GROUP)))
    starts = [sum(sizes[:i]) for i in range(len(sizes))]
    distances = partner_order(owners)
    partners = [0] + distances
    received = []
    for i, (start, size) in enumerate(zip(starts, sizes)):
        pieces = pack(
            place, block, models, distances, own, start * GROUP, size * GROUP, lanes if i == 0 else 0
        )
        received.append([swap(p, "freq", k) for p, k in zip(pieces, distances)])

    near = near_models(place, cell_index, models, received[0], lanes)
    far = lax.all_gather(near, "tile", axis=0, tiled=False)
    all_borrowed = far[:, block_cells, 0].astype(jnp.int32)
    models_t = tile_models(place, cell_index, far, owned, partners)

    order = place[1] ^ jnp.array(partners, jnp.int32)
    wide = wide_table(gate_table(order, own_freqs, freqs, waveform, gate_index).T)
    obs = observed[0].reshape(gates, own // GROUP, GROUP)
    obs = jnp.swapaxes(obs, 0, 1).reshape(own // GROUP, 1, gates * GROUP)

    terms = jnp.zeros((members, cells), jnp.float32)
    square = jnp.zeros((members, LANES), jnp.float32)
    for i, start in enumerate(starts):
        last = i == len(starts) - 1
        terms, square = chunk_step(
            place, block, received[i], start, models_t, wide, obs, cell_index, terms, square, block_cells, last
        )

    slab = members // devices
    sent = terms.reshape(devices, slab, cells)
    got = lax.all_to_all(sent, both, split_axis=0, concat_axis=0, tiled=True)
    if slab % GROUP == 0 and members // slab + owned <= LANES:
        step = gradient_step(all_borrowed, got, square, tiles, owned)
        back = lax.all_to_all(step, both, split_axis=0, concat_axis=0, tiled=True)
        updated, misfit = update(models, back, divisor)
        return (updated, misfit.reshape(members))

    got = jnp.sum(got.reshape(tiles, owners, slab, cells), axis=1)
    lent = (all_borrowed[None, :] == jnp.arange(tiles)[:, None]).astype(jnp.float32)
    gradient = got[:, :, :block_cells] + jnp.sum(
        lent[:, :, None, None] * got[None, :, :, block_cells:], axis=1
    )
    scale = jnp.sqrt(jnp.sum(gradient * gradient, axis=(0, 2)) / ncells + EPSILON)
    step = gradient / scale[None, :, None]
    step = step.reshape(tiles, slab, owners, owned).transpose(0, 2, 1, 3)
    step = step.reshape(devices, slab, owned)
    rider = jnp.broadcast_to(square[:, 0].reshape(1, slab, devices), (devices, slab, devices))
    back = lax.all_to_all(
        jnp.concatenate([step, rider], axis=2), both, split_axis=0, concat_axis=0, tiled=True
    )
    misfit = jnp.sum(back[:, :, owned:], axis=0).reshape(members) / divisor
    back = back[:, :, :owned].reshape(members, owned)
    return (models - (STEP_LENGTH * misfit)[None, :] * back.T, misfit)


def solution(mesh):
    in_specs = (
        P("tile", "freq", None, None, None),
        P(("tile", "freq"), None),
        P("tile", None, "freq"),
        P(),
        P("tile", None),
        P(),
    )
    out_specs = (P(("tile", "freq"), None), P())
    return jax.shard_map(body, mesh=mesh, in_specs=in_specs, out_specs=out_specs, check_vma=False)
```

time: 447 us -> 835 us (1.87)
  Pallas kernels: 39.5 us -> 519 us
  local copies, waits for them, and re-layouts: 60.5 us -> 3.42 us
  waiting for transfers between devices: 198 us -> 173 us
  other arithmetic: 14 us -> 3.79 us
  blocking collectives: 0 us -> 9.82 us
    pallas_call x6 -> x17, Pallas kernels: 39.5 us -> 519 us  [the longest x6 463 us: pack(): pl.pallas_call(functools.partial(pack_kernel, distances, own, first, rows...]
    ppermute x42, waiting for transfers between devices: 176 us -> 157 us  [swap(): lax.ppermute(x, axis, [(i, i ^ k) for i in range(lax.axis_size(axis))])]
    dynamic_slice x4 -> x0, local copies, waits for them, and re-layouts: 15.9 us -> none  [body(): lax.dynamic_slice_in_dim(block, (my_freq ^ k) * own_soundings + start * G...]
    mul x3 -> x0, local copies, waits for them, and re-layouts: 11.5 us -> none  [the longest x2 11.5 us: body(): table[:, None, :, None]]
    unnamed x86 -> x81, local copies, waits for them, and re-layouts: 13.3 us -> 2.25 us
    all_to_all x0 -> x1, blocking collectives: none -> 9.82 us  [body(): back = lax.all_to_all(step, both, split_axis=0, concat_axis=0, tiled=True)]
  transfers between devices with their start and end apart: 45 -> 44, of which waited for: 15 -> 16; matrix products, arithmetic and copies ran while one was open for 14% -> 1% of each run, Pallas kernels for 8% -> 53%
where the time goes in v3:
time: 835 us
  Pallas kernels  519 us (62%)
  waiting for transfers between devices  173 us (21%)
  starting transfers between devices  111 us (13%)
  between operations  14.6 us (2%)
  blocking collectives  9.82 us (1%)
    pallas_call x6, Pallas kernels, pack(): pl.pallas_call(functools.partial(pack_kernel, distances, own, first, rows...  463 us
    ppermute x42, waiting for transfers between devices, swap(): lax.ppermute(x, axis, [(i, i ^ k) for i in range(lax.axis_size(axis))])  157 us
    ppermute x42, starting transfers between devices, swap(): lax.ppermute(x, axis, [(i, i ^ k) for i in range(lax.axis_size(axis))])  106 us
    pallas_call x6, Pallas kernels, chunk_step(): pl.pallas_call(functools.partial(chunk_kernel, pieces, block_cells, last)...  50.7 us
  transfers between devices with their start and end apart: 44, of which 16 were waited for; matrix products, arithmetic and copies ran while one was open for 1% of the time, Pallas kernels for 53%

profile of v3, /device:TPU:0, one launch (start us, length us, event | category | flops | bytes accessed | tf_op | source)
XLA Modules:
  0.0 834.7 jit_solution(2203076369512078288)
XLA Ops:
  7.8 64.6 %pack.6 = (f32[9,16,512]{2,1,0:T(8,128)}, f32[9,16,512]{2,1,0:T(8,128)}, f32[9,16,512]{2,1,0:T(8,128)}, f32[9,16,512]{2,1,0:T(8,128)}, f32[9,16,512]{2,1,0:T(8,1...) custom-call(s32[2]{0:T(128)} %pad_add_fusion.place_ref, f32[8,1024,512]{2,1,0:T(8,128)} %bitcast.15, f32[32,256]{1,0:T(8,128)} %models_ref.15), custom_call_target="tpu_custom_call" | custom-call | bytes 3670016 | tf_op jit(solution)/shard_map/pack/pallas_call | solution.py:96
  72.4 6.0 collective-permute-start
  88.3 7.6 collective-permute-done.1.refs_1_.refs_2_
  102.3 6.3 collective-permute-done.3.refs_3_.refs_4_
  108.6 17.3 %collective-permute-done.4.refs_4_.refs_5_ = f32[9,16,512]{2,1,0:T(8,128)S(1)} collective-permute-done((f32[9,16,512]{2,1,0:T(8,128)}, f32[9,16,512]{2,1,0:T(8,128)S(1)}, u32[]{:S(2)}, u32[]{:S(2)}) %collective-permute-start.4) | collective-permute-done | bytes 294944 | tf_op jit(solution)/shard_map/ppermute | solution.py:23
  125.9 5.3 collective-permute-done.6.refs_6_.refs_7_
  132.6 85.2 %pack.9 = (f32[8,24,512]{2,1,0:T(8,128)}, f32[8,24,512]{2,1,0:T(8,128)}, f32[8,24,512]{2,1,0:T(8,128)}, f32[8,24,512]{2,1,0:T(8,128)}, f32[8,24,512]{2,1,0:T(8,1...) custom-call(s32[2]{0:T(128)} %pad_add_fusion.place_ref, f32[8,1024,512]{2,1,0:T(8,128)} %bitcast.16, f32[32,256]{1,0:T(8,128)} %models_ref.15), custom_call_target="tpu_custom_call" | custom-call | bytes 5505024 | tf_op jit(solution)/shard_map/pack/pallas_call | solution.py:96
  220.0 57.4 %pack.8 = (f32[8,16,512]{2,1,0:T(8,128)}, f32[8,16,512]{2,1,0:T(8,128)}, f32[8,16,512]{2,1,0:T(8,128)}, f32[8,16,512]{2,1,0:T(8,128)}, f32[8,16,512]{2,1,0:T(8,1...) custom-call(s32[2]{0:T(128)} %pad_add_fusion.place_ref, f32[8,1024,512]{2,1,0:T(8,128)} %bitcast.17, f32[32,256]{1,0:T(8,128)} %models_ref.15), custom_call_target="tpu_custom_call" | custom-call | bytes 3670016 | tf_op jit(solution)/shard_map/pack/pallas_call | solution.py:96
  280.1 29.8 %pack.7 = (f32[8,8,512]{2,1,0:T(8,128)}, f32[8,8,512]{2,1,0:T(8,128)}, f32[8,8,512]{2,1,0:T(8,128)}, f32[8,8,512]{2,1,0:T(8,128)}, f32[8,8,512]{2,1,0:T(8,128)},...) custom-call(s32[2]{0:T(128)} %pad_add_fusion.place_ref, f32[8,1024,512]{2,1,0:T(8,128)} %bitcast.18, f32[32,256]{1,0:T(8,128)} %models_ref.15), custom_call_target="tpu_custom_call" | custom-call | bytes 1835008 | tf_op jit(solution)/shard_map/pack/pallas_call | solution.py:96
  313.6 113.0 %pack.11 = (f32[8,32,512]{2,1,0:T(8,128)}, f32[8,32,512]{2,1,0:T(8,128)}, f32[8,32,512]{2,1,0:T(8,128)}, f32[8,32,512]{2,1,0:T(8,128)}, f32[8,32,512]{2,1,0:T(8,...) custom-call(s32[2]{0:T(128)} %pad_add_fusion.place_ref, f32[8,1024,512]{2,1,0:T(8,128)} %bitcast.19, f32[32,256]{1,0:T(8,128)} %models_ref.15), custom_call_target="tpu_custom_call" | custom-call | bytes 7340032 | tf_op jit(solution)/shard_map/pack/pallas_call | solution.py:96
  432.8 113.1 %pack.10 = (f32[8,32,512]{2,1,0:T(8,128)}, f32[8,32,512]{2,1,0:T(8,128)}, f32[8,32,512]{2,1,0:T(8,128)}, f32[8,32,512]{2,1,0:T(8,128)}, f32[8,32,512]{2,1,0:T(8,...) custom-call(s32[2]{0:T(128)} %pad_add_fusion.place_ref, f32[8,1024,512]{2,1,0:T(8,128)} %bitcast.20, f32[32,256]{1,0:T(8,128)} %models_ref.15), custom_call_target="tpu_custom_call" | custom-call | bytes 7340032 | tf_op jit(solution)/shard_map/pack/pallas_call | solution.py:96
  550.1 4.9 collective-permute-done.22.refs_2_
  568.5 6.9 chunk_step.6
  575.4 26.9 %collective-permute-done.39.refs_5_ = f32[8,32,512]{2,1,0:T(8,128)} collective-permute-done((f32[8,32,512]{2,1,0:T(8,128)}, f32[8,32,512]{2,1,0:T(8,128)}, u32[]{:S(2)}, u32[]{:S(2)}) %collective-permute-start.39) | collective-permute-done | bytes 524320 | tf_op jit(solution)/shard_map/ppermute | solution.py:23
  604.1 19.7 %collective-permute-done.41.refs_7_ = f32[8,32,512]{2,1,0:T(8,128)} collective-permute-done((f32[8,32,512]{2,1,0:T(8,128)}, f32[8,32,512]{2,1,0:T(8,128)}, u32[]{:S(2)}, u32[]{:S(2)}) %collective-permute-start.41) | collective-permute-done | bytes 524320 | tf_op jit(solution)/shard_map/ppermute | solution.py:23
  625.4 23.3 %collective-permute-start.34 = (f32[8,32,512]{2,1,0:T(8,128)S(1)}, f32[8,32,512]{2,1,0:T(8,128)S(1)}, u32[]{:S(2)}, u32[]{:S(2)}) collective-permute-start(f32[8,32,512]{2,1,0:T(8,128)S(1)} %copy-done.19), channel_id=1, source_target_pairs={{0,4},{1,5},{2,6},{3,7},{4,0},{5,1},{6,2},{7,3},{8,12},{9,13},{10,... | collective-permute-start | bytes 1572872 | tf_op jit(solution)/shard_map/ppermute | solution.py:23
  648.8 11.5 %chunk_step.7 = (f32[256,512]{1,0:T(8,128)}, f32[256,128]{1,0:T(8,128)S(1)}) custom-call(s32[2]{0:T(128)S(1)} %copy-done.13, f32[8,1024,512]{2,1,0:T(8,128)} %bitcast.22, f32[8,32,512]{2,1,0:T(8,128)} %collective-permute-done.35.refs_1_, f32[8,32,512]{2,1,0:T(8,128)} %collective-permute-done.36.refs_2_, ...), custom_call_target="tpu_custom_call", output_to_operand_aliasing={{0}: (15, {}), {1}: (16, {})} | custom-call | flops 6442450944 | bytes 4194304 | tf_op jit(solution)/shard_map/chunk_step/pallas_call | solution.py:244
  662.4 16.2 %collective-permute-start.24 = (f32[8,24,512]{2,1,0:T(8,128)S(1)}, f32[8,24,512]{2,1,0:T(8,128)S(1)}, u32[]{:S(2)}, u32[]{:S(2)}) collective-permute-start(f32[8,24,512]{2,1,0:T(8,128)S(1)} %copy-done.27), channel_id=1, source_target_pairs={{0,2},{1,3},{2,0},{3,1},{4,6},{5,7},{6,4},{7,5},{8,10},{9,11},{10,... | collective-permute-start | bytes 1179656 | tf_op jit(solution)/shard_map/ppermute | solution.py:23
  678.6 10.7 %collective-permute-done.32.refs_5_ = f32[8,32,512]{2,1,0:T(8,128)S(1)} collective-permute-done((f32[8,32,512]{2,1,0:T(8,128)S(1)}, f32[8,32,512]{2,1,0:T(8,128)S(1)}, u32[]{:S(2)}, u32[]{:S(2)}) %collective-permute-start.32) | collective-permute-done | bytes 524320 | tf_op jit(solution)/shard_map/ppermute | solution.py:23
  690.0 18.1 %collective-permute-done.34.refs_7_ = f32[8,32,512]{2,1,0:T(8,128)S(1)} collective-permute-done((f32[8,32,512]{2,1,0:T(8,128)S(1)}, f32[8,32,512]{2,1,0:T(8,128)S(1)}, u32[]{:S(2)}, u32[]{:S(2)}) %collective-permute-start.34) | collective-permute-done | bytes 524320 | tf_op jit(solution)/shard_map/ppermute | solution.py:23
  708.1 11.3 %chunk_step.8 = (f32[256,512]{1,0:T(8,128)}, f32[256,128]{1,0:T(8,128)S(1)}) custom-call(s32[2]{0:T(128)S(1)} %copy-done.13, f32[8,1024,512]{2,1,0:T(8,128)} %bitcast.23, f32[8,32,512]{2,1,0:T(8,128)} %collective-permute-done.28.refs_1_, f32[8,32,512]{2,1,0:T(8,128)} %collective-permute-done.29.refs_2_, ...), custom_call_target="tpu_custom_call", output_to_operand_aliasing={{0}: (15, {}), {1}: (16, {})} | custom-call | flops 6442450944 | bytes 4194304 | tf_op jit(solution)/shard_map/chunk_step/pallas_call | solution.py:244
  721.3 10.7 %collective-permute-start.17 = (f32[8,16,512]{2,1,0:T(8,128)S(1)}, f32[8,16,512]{2,1,0:T(8,128)S(1)}, u32[]{:S(2)}, u32[]{:S(2)}) collective-permute-start(f32[8,16,512]{2,1,0:T(8,128)S(1)} %copy-done.32), channel_id=1, source_target_pairs={{0,2},{1,3},{2,0},{3,1},{4,6},{5,7},{6,4},{7,5},{8,10},{9,11},{10,... | collective-permute-start | bytes 786440 | tf_op jit(solution)/shard_map/ppermute | solution.py:23
  732.0 7.9 collective-permute-done.25.refs_5_
  740.6 12.4 %collective-permute-done.27.refs_7_ = f32[8,24,512]{2,1,0:T(8,128)S(1)} collective-permute-done((f32[8,24,512]{2,1,0:T(8,128)S(1)}, f32[8,24,512]{2,1,0:T(8,128)S(1)}, u32[]{:S(2)}, u32[]{:S(2)}) %collective-permute-start.27) | collective-permute-done | bytes 393248 | tf_op jit(solution)/shard_map/ppermute | solution.py:23
  753.1 9.0 %chunk_step.9 = (f32[256,512]{1,0:T(8,128)}, f32[256,128]{1,0:T(8,128)S(1)}) custom-call(s32[2]{0:T(128)S(1)} %copy-done.13, f32[8,1024,512]{2,1,0:T(8,128)} %bitcast.24, f32[8,24,512]{2,1,0:T(8,128)S(1)} %collective-permute-done.21.refs_1_, f32[8,24,512]{2,1,0:T(8,128)S(1)} %copy-done.3, ...), custom_call_target="tpu_custom_call", output_to_operand_aliasing={{0}: (15, {}), {1}: (16, {})} | custom-call | flops 4831838208 | bytes 3145728 | tf_op jit(solution)/shard_map/chunk_step/pallas_call | solution.py:244
  766.7 6.9 collective-permute-done.18.refs_5_
  775.5 5.8 collective-permute-done.20.refs_7_
  783.1 7.0 chunk_step.10
  790.1 5.1 chunk_step.11
  795.2 4.7 all-to-all-start
  800.8 15.5 %all-to-all-done.got_ref = f32[32,8,512]{2,1,0:T(8,128)S(1)} async-done(((f32[32,8,512]{2,1,0:T(8,128)}), f32[32,8,512]{2,1,0:T(8,128)S(1)}, u32[]{:S(2)}, u32[]{:S(2)}) %all-to-all-start) | async-done | bytes 524320 | tf_op jit(solution)/shard_map/all_to_all | solution.py:409
  817.0 9.8 %all_to_all.10.back_ref = f32[32,8,128]{2,1,0:T(8,128)S(1)} all-to-all(f32[32,8,128]{2,1,0:T(8,128)S(1)} %gradient_step.1), channel_id=1, replica_groups=mesh['tile'=4,'freq'=8] {'tile','freq'}, dimensions={0} | all-to-all | bytes 262144 | tf_op jit(solution)/shard_map/all_to_all | solution.py:412
  (172 shorter events, 70.2 us)
Async XLA Ops:
  7.2 557.8 %all-gather.3.cloned.1.call-start = ((), (), s32[]{:S(2)}) async-start(), calls=%async_computation.2 | async-start | bytes 1351680 | tf_op jit(solution)/shard_map/all_gather | solution.py:390
  80.5 45.4 %collective-permute-start.4 = (f32[9,16,512]{2,1,0:T(8,128)}, f32[9,16,512]{2,1,0:T(8,128)S(1)}, u32[]{:S(2)}, u32[]{:S(2)}) collective-permute-start(f32[9,16,512]{2,1,0:T(8,128)} %get-tuple-element.66), channel_id=1, source_target_pairs={{0,5},{1,4},{2,7},{3,6},{4,1},{5,0},{6,3},{7,2},{8,13},{9,12},{10,... | collective-permute-start | bytes 884744 | tf_op jit(solution)/shard_map/ppermute | solution.py:23
  86.6 39.3 %collective-permute-start.5 = (f32[9,16,512]{2,1,0:T(8,128)}, f32[9,16,512]{2,1,0:T(8,128)S(1)}, u32[]{:S(2)}, u32[]{:S(2)}) collective-permute-start(f32[9,16,512]{2,1,0:T(8,128)} %get-tuple-element.67), channel_id=1, source_target_pairs={{0,1},{1,0},{2,3},{3,2},{4,5},{5,4},{6,7},{7,6},{8,9},{9,8},{10,11... | collective-permute-start | bytes 884744 | tf_op jit(solution)/shard_map/ppermute | solution.py:23
  95.9 35.2 %collective-permute-start.6 = (f32[9,16,512]{2,1,0:T(8,128)}, f32[9,16,512]{2,1,0:T(8,128)S(1)}, u32[]{:S(2)}, u32[]{:S(2)}) collective-permute-start(f32[9,16,512]{2,1,0:T(8,128)} %get-tuple-element.68), channel_id=1, source_target_pairs={{0,4},{1,5},{2,6},{3,7},{4,0},{5,1},{6,2},{7,3},{8,12},{9,13},{10,... | collective-permute-start | bytes 884744 | tf_op jit(solution)/shard_map/ppermute | solution.py:23
  217.8 328.3 %collective-permute-start.21 = (f32[8,24,512]{2,1,0:T(8,128)}, f32[8,24,512]{2,1,0:T(8,128)S(1)}, u32[]{:S(2)}, u32[]{:S(2)}) collective-permute-start(f32[8,24,512]{2,1,0:T(8,128)} %get-tuple-element.87), channel_id=1, source_target_pairs={{0,7},{1,6},{2,5},{3,4},{4,3},{5,2},{6,1},{7,0},{8,15},{9,14},{10,... | collective-permute-start | bytes 1179656 | tf_op jit(solution)/shard_map/ppermute | solution.py:23
  277.4 152.9 %collective-permute-start.14 = (f32[8,16,512]{2,1,0:T(8,128)}, f32[8,16,512]{2,1,0:T(8,128)S(1)}, u32[]{:S(2)}, u32[]{:S(2)}) collective-permute-start(f32[8,16,512]{2,1,0:T(8,128)} %get-tuple-element.80), channel_id=1, source_target_pairs={{0,7},{1,6},{2,5},{3,4},{4,3},{5,2},{6,1},{7,0},{8,15},{9,14},{10,... | collective-permute-start | bytes 786440 | tf_op jit(solution)/shard_map/ppermute | solution.py:23
  280.1 152.5 %collective-permute-start.15 = (f32[8,16,512]{2,1,0:T(8,128)}, f32[8,16,512]{2,1,0:T(8,128)S(1)}, u32[]{:S(2)}, u32[]{:S(2)}) collective-permute-start(f32[8,16,512]{2,1,0:T(8,128)} %get-tuple-element.81), channel_id=1, source_target_pairs={{0,3},{1,2},{2,1},{3,0},{4,7},{5,6},{6,5},{7,4},{8,11},{9,10},{10,... | collective-permute-start | bytes 786440 | tf_op jit(solution)/shard_map/ppermute | solution.py:23
  309.8 116.8 %collective-permute-start.10 = (f32[8,8,512]{2,1,0:T(8,128)}, f32[8,8,512]{2,1,0:T(8,128)S(1)}, u32[]{:S(2)}, u32[]{:S(2)}) collective-permute-start(f32[8,8,512]{2,1,0:T(8,128)} %get-tuple-element.72), channel_id=1, source_target_pairs={{0,2},{1,3},{2,0},{3,1},{4,6},{5,7},{6,4},{7,5},{8,10},{9,11},{10,... | collective-permute-start | bytes 393224 | tf_op jit(solution)/shard_map/ppermute | solution.py:23
  311.8 116.6 %collective-permute-start.11 = (f32[8,8,512]{2,1,0:T(8,128)}, f32[8,8,512]{2,1,0:T(8,128)S(1)}, u32[]{:S(2)}, u32[]{:S(2)}) collective-permute-start(f32[8,8,512]{2,1,0:T(8,128)} %get-tuple-element.73), channel_id=1, source_target_pairs={{0,5},{1,4},{2,7},{3,6},{4,1},{5,0},{6,3},{7,2},{8,13},{9,12},{10,... | collective-permute-start | bytes 393224 | tf_op jit(solution)/shard_map/ppermute | solution.py:23
  426.7 131.2 %collective-permute-start.35 = (f32[8,32,512]{2,1,0:T(8,128)}, f32[8,32,512]{2,1,0:T(8,128)}, u32[]{:S(2)}, u32[]{:S(2)}) collective-permute-start(f32[8,32,512]{2,1,0:T(8,128)} %get-tuple-element.101), channel_id=1, source_target_pairs={{0,7},{1,6},{2,5},{3,4},{4,3},{5,2},{6,1},{7,0},{8,15},{9,14},{10,... | collective-permute-start | bytes 1572872 | tf_op jit(solution)/shard_map/ppermute | solution.py:23
  428.4 130.9 %collective-permute-start.36 = (f32[8,32,512]{2,1,0:T(8,128)}, f32[8,32,512]{2,1,0:T(8,128)}, u32[]{:S(2)}, u32[]{:S(2)}) collective-permute-start(f32[8,32,512]{2,1,0:T(8,128)} %get-tuple-element.102), channel_id=1, source_target_pairs={{0,3},{1,2},{2,1},{3,0},{4,7},{5,6},{6,5},{7,4},{8,11},{9,10},{10,... | collective-permute-start | bytes 1572872 | tf_op jit(solution)/shard_map/ppermute | solution.py:23
  430.3 129.8 %collective-permute-start.37 = (f32[8,32,512]{2,1,0:T(8,128)}, f32[8,32,512]{2,1,0:T(8,128)}, u32[]{:S(2)}, u32[]{:S(2)}) collective-permute-start(f32[8,32,512]{2,1,0:T(8,128)} %get-tuple-element.103), channel_id=1, source_target_pairs={{0,6},{1,7},{2,4},{3,5},{4,2},{5,3},{6,0},{7,1},{8,14},{9,15},{10,... | collective-permute-start | bytes 1572872 | tf_op jit(solution)/shard_map/ppermute | solution.py:23
  432.5 129.5 %collective-permute-start.38 = (f32[8,32,512]{2,1,0:T(8,128)}, f32[8,32,512]{2,1,0:T(8,128)}, u32[]{:S(2)}, u32[]{:S(2)}) collective-permute-start(f32[8,32,512]{2,1,0:T(8,128)} %get-tuple-element.104), channel_id=1, source_target_pairs={{0,2},{1,3},{2,0},{3,1},{4,6},{5,7},{6,4},{7,5},{8,10},{9,11},{10,... | collective-permute-start | bytes 1572872 | tf_op jit(solution)/shard_map/ppermute | solution.py:23
  555.8 46.5 %collective-permute-start.39 = (f32[8,32,512]{2,1,0:T(8,128)}, f32[8,32,512]{2,1,0:T(8,128)}, u32[]{:S(2)}, u32[]{:S(2)}) collective-permute-start(f32[8,32,512]{2,1,0:T(8,128)} %get-tuple-element.105), channel_id=1, source_target_pairs={{0,5},{1,4},{2,7},{3,6},{4,1},{5,0},{6,3},{7,2},{8,13},{9,12},{10,... | collective-permute-start | bytes 1572872 | tf_op jit(solution)/shard_map/ppermute | solution.py:23
  557.9 46.2 %collective-permute-start.40 = (f32[8,32,512]{2,1,0:T(8,128)}, f32[8,32,512]{2,1,0:T(8,128)}, u32[]{:S(2)}, u32[]{:S(2)}) collective-permute-start(f32[8,32,512]{2,1,0:T(8,128)} %get-tuple-element.106), channel_id=1, source_target_pairs={{0,1},{1,0},{2,3},{3,2},{4,5},{5,4},{6,7},{7,6},{8,9},{9,8},{10,11... | collective-permute-start | bytes 1572872 | tf_op jit(solution)/shard_map/ppermute | solution.py:23
  559.4 64.5 %collective-permute-start.41 = (f32[8,32,512]{2,1,0:T(8,128)}, f32[8,32,512]{2,1,0:T(8,128)}, u32[]{:S(2)}, u32[]{:S(2)}) collective-permute-start(f32[8,32,512]{2,1,0:T(8,128)} %get-tuple-element.107), channel_id=1, source_target_pairs={{0,4},{1,5},{2,6},{3,7},{4,0},{5,1},{6,2},{7,3},{8,12},{9,13},{10,... | collective-permute-start | bytes 1572872 | tf_op jit(solution)/shard_map/ppermute | solution.py:23
  560.2 64.2 %collective-permute-start.28 = (f32[8,32,512]{2,1,0:T(8,128)}, f32[8,32,512]{2,1,0:T(8,128)}, u32[]{:S(2)}, u32[]{:S(2)}) collective-permute-start(f32[8,32,512]{2,1,0:T(8,128)} %get-tuple-element.94), channel_id=1, source_target_pairs={{0,7},{1,6},{2,5},{3,4},{4,3},{5,2},{6,1},{7,0},{8,15},{9,14},{10,... | collective-permute-start | bytes 1572872 | tf_op jit(solution)/shard_map/ppermute | solution.py:23
  562.1 63.3 %collective-permute-start.29 = (f32[8,32,512]{2,1,0:T(8,128)}, f32[8,32,512]{2,1,0:T(8,128)}, u32[]{:S(2)}, u32[]{:S(2)}) collective-permute-start(f32[8,32,512]{2,1,0:T(8,128)} %get-tuple-element.95), channel_id=1, source_target_pairs={{0,3},{1,2},{2,1},{3,0},{4,7},{5,6},{6,5},{7,4},{8,11},{9,10},{10,... | collective-permute-start | bytes 1572872 | tf_op jit(solution)/shard_map/ppermute | solution.py:23
  602.2 58.0 %collective-permute-start.30 = (f32[8,32,512]{2,1,0:T(8,128)S(1)}, f32[8,32,512]{2,1,0:T(8,128)S(1)}, u32[]{:S(2)}, u32[]{:S(2)}) collective-permute-start(f32[8,32,512]{2,1,0:T(8,128)S(1)} %copy-done.23), channel_id=1, source_target_pairs={{0,6},{1,7},{2,4},{3,5},{4,2},{5,3},{6,0},{7,1},{8,14},{9,15},{10,... | collective-permute-start | bytes 1572872 | tf_op jit(solution)/shard_map/ppermute | solution.py:23
  604.1 58.3 %collective-permute-start.31 = (f32[8,32,512]{2,1,0:T(8,128)S(1)}, f32[8,32,512]{2,1,0:T(8,128)S(1)}, u32[]{:S(2)}, u32[]{:S(2)}) collective-permute-start(f32[8,32,512]{2,1,0:T(8,128)S(1)} %copy-done.22), channel_id=1, source_target_pairs={{0,2},{1,3},{2,0},{3,1},{4,6},{5,7},{6,4},{7,5},{8,10},{9,11},{10,... | collective-permute-start | bytes 1572872 | tf_op jit(solution)/shard_map/ppermute | solution.py:23
  623.9 65.5 %collective-permute-start.32 = (f32[8,32,512]{2,1,0:T(8,128)S(1)}, f32[8,32,512]{2,1,0:T(8,128)S(1)}, u32[]{:S(2)}, u32[]{:S(2)}) collective-permute-start(f32[8,32,512]{2,1,0:T(8,128)S(1)} %copy-done.21), channel_id=1, source_target_pairs={{0,5},{1,4},{2,7},{3,6},{4,1},{5,0},{6,3},{7,2},{8,13},{9,12},{10,... | collective-permute-start | bytes 1572872 | tf_op jit(solution)/shard_map/ppermute | solution.py:23
  624.3 65.1 %collective-permute-start.33 = (f32[8,32,512]{2,1,0:T(8,128)S(1)}, f32[8,32,512]{2,1,0:T(8,128)S(1)}, u32[]{:S(2)}, u32[]{:S(2)}) collective-permute-start(f32[8,32,512]{2,1,0:T(8,128)S(1)} %copy-done.20), channel_id=1, source_target_pairs={{0,1},{1,0},{2,3},{3,2},{4,5},{5,4},{6,7},{7,6},{8,9},{9,8},{10,11... | collective-permute-start | bytes 1572872 | tf_op jit(solution)/shard_map/ppermute | solution.py:23
  625.4 82.7 %collective-permute-start.34 = (f32[8,32,512]{2,1,0:T(8,128)S(1)}, f32[8,32,512]{2,1,0:T(8,128)S(1)}, u32[]{:S(2)}, u32[]{:S(2)}) collective-permute-start(f32[8,32,512]{2,1,0:T(8,128)S(1)} %copy-done.19), channel_id=1, source_target_pairs={{0,4},{1,5},{2,6},{3,7},{4,0},{5,1},{6,2},{7,3},{8,12},{9,13},{10,... | collective-permute-start | bytes 1572872 | tf_op jit(solution)/shard_map/ppermute | solution.py:23
  660.3 59.1 %collective-permute-start.23 = (f32[8,24,512]{2,1,0:T(8,128)S(1)}, f32[8,24,512]{2,1,0:T(8,128)S(1)}, u32[]{:S(2)}, u32[]{:S(2)}) collective-permute-start(f32[8,24,512]{2,1,0:T(8,128)S(1)} %copy-done.28), channel_id=1, source_target_pairs={{0,6},{1,7},{2,4},{3,5},{4,2},{5,3},{6,0},{7,1},{8,14},{9,15},{10,... | collective-permute-start | bytes 1179656 | tf_op jit(solution)/shard_map/ppermute | solution.py:23
  662.4 58.9 %collective-permute-start.24 = (f32[8,24,512]{2,1,0:T(8,128)S(1)}, f32[8,24,512]{2,1,0:T(8,128)S(1)}, u32[]{:S(2)}, u32[]{:S(2)}) collective-permute-start(f32[8,24,512]{2,1,0:T(8,128)S(1)} %copy-done.27), channel_id=1, source_target_pairs={{0,2},{1,3},{2,0},{3,1},{4,6},{5,7},{6,4},{7,5},{8,10},{9,11},{10,... | collective-permute-start | bytes 1179656 | tf_op jit(solution)/shard_map/ppermute | solution.py:23
  689.4 50.6 %collective-permute-start.25 = (f32[8,24,512]{2,1,0:T(8,128)S(1)}, f32[8,24,512]{2,1,0:T(8,128)S(1)}, u32[]{:S(2)}, u32[]{:S(2)}) collective-permute-start(f32[8,24,512]{2,1,0:T(8,128)S(1)} %copy-done.26), channel_id=1, source_target_pairs={{0,5},{1,4},{2,7},{3,6},{4,1},{5,0},{6,3},{7,2},{8,13},{9,12},{10,... | collective-permute-start | bytes 1179656 | tf_op jit(solution)/shard_map/ppermute | solution.py:23
  689.4 50.6 %collective-permute-start.26 = (f32[8,24,512]{2,1,0:T(8,128)S(1)}, f32[8,24,512]{2,1,0:T(8,128)S(1)}, u32[]{:S(2)}, u32[]{:S(2)}) collective-permute-start(f32[8,24,512]{2,1,0:T(8,128)S(1)} %copy-done.25), channel_id=1, source_target_pairs={{0,1},{1,0},{2,3},{3,2},{4,5},{5,4},{6,7},{7,6},{8,9},{9,8},{10,11... | collective-permute-start | bytes 1179656 | tf_op jit(solution)/shard_map/ppermute | solution.py:23
  708.1 45.0 %collective-permute-start.27 = (f32[8,24,512]{2,1,0:T(8,128)S(1)}, f32[8,24,512]{2,1,0:T(8,128)S(1)}, u32[]{:S(2)}, u32[]{:S(2)}) collective-permute-start(f32[8,24,512]{2,1,0:T(8,128)S(1)} %copy-done.24), channel_id=1, source_target_pairs={{0,4},{1,5},{2,6},{3,7},{4,0},{5,1},{6,2},{7,3},{8,12},{9,13},{10,... | collective-permute-start | bytes 1179656 | tf_op jit(solution)/shard_map/ppermute | solution.py:23
  719.4 42.7 %collective-permute-start.16 = (f32[8,16,512]{2,1,0:T(8,128)S(1)}, f32[8,16,512]{2,1,0:T(8,128)S(1)}, u32[]{:S(2)}, u32[]{:S(2)}) collective-permute-start(f32[8,16,512]{2,1,0:T(8,128)S(1)} %copy-done.33), channel_id=1, source_target_pairs={{0,6},{1,7},{2,4},{3,5},{4,2},{5,3},{6,0},{7,1},{8,14},{9,15},{10,... | collective-permute-start | bytes 786440 | tf_op jit(solution)/shard_map/ppermute | solution.py:23
  721.3 42.3 %collective-permute-start.17 = (f32[8,16,512]{2,1,0:T(8,128)S(1)}, f32[8,16,512]{2,1,0:T(8,128)S(1)}, u32[]{:S(2)}, u32[]{:S(2)}) collective-permute-start(f32[8,16,512]{2,1,0:T(8,128)S(1)} %copy-done.32), channel_id=1, source_target_pairs={{0,2},{1,3},{2,0},{3,1},{4,6},{5,7},{6,4},{7,5},{8,10},{9,11},{10,... | collective-permute-start | bytes 786440 | tf_op jit(solution)/shard_map/ppermute | solution.py:23
  740.0 33.6 %collective-permute-start.18 = (f32[8,16,512]{2,1,0:T(8,128)S(1)}, f32[8,16,512]{2,1,0:T(8,128)S(1)}, u32[]{:S(2)}, u32[]{:S(2)}) collective-permute-start(f32[8,16,512]{2,1,0:T(8,128)S(1)} %copy-done.31), channel_id=1, source_target_pairs={{0,5},{1,4},{2,7},{3,6},{4,1},{5,0},{6,3},{7,2},{8,13},{9,12},{10,... | collective-permute-start | bytes 786440 | tf_op jit(solution)/shard_map/ppermute | solution.py:23
  740.0 35.5 %collective-permute-start.19 = (f32[8,16,512]{2,1,0:T(8,128)S(1)}, f32[8,16,512]{2,1,0:T(8,128)S(1)}, u32[]{:S(2)}, u32[]{:S(2)}) collective-permute-start(f32[8,16,512]{2,1,0:T(8,128)S(1)} %copy-done.30), channel_id=1, source_target_pairs={{0,1},{1,0},{2,3},{3,2},{4,5},{5,4},{6,7},{7,6},{8,9},{9,8},{10,11... | collective-permute-start | bytes 786440 | tf_op jit(solution)/shard_map/ppermute | solution.py:23
  (52 other events, 2385.7 us)
Sparse Core Ops, SparseCore 0:
  132.7 15.8 all-gather.2

commit v4 on v3

--- a/solution.py
+++ b/solution.py
@@ -55,8 +55,8 @@
     return dot(a[0], b[0]) + (dot(a[0], b[1]) + dot(a[1], b[0]))
 
 
-def params():
-    return pltpu.CompilerParams(vmem_limit_bytes=48 * 1024 * 1024)
+def params(mebibytes):
+    return pltpu.CompilerParams(vmem_limit_bytes=mebibytes * 1024 * 1024)
 
 
 def cost(flops, bytes_accessed):
@@ -67,39 +67,48 @@
     return pl.BlockSpec(a.shape, lambda *_: (0,) * a.ndim)
 
 
-ANY = pl.BlockSpec(memory_space=pl.ANY)
+HBM = pl.BlockSpec(memory_space=pltpu.HBM)
 SCALARS = pl.BlockSpec(memory_space=pltpu.SMEM)
 
 
-def pack_kernel(distances, own, first, rows, lanes, place_ref, block_ref, models_ref, *refs):
-    outs, sems = refs[: len(distances)], refs[len(distances)]
-    spectra = block_ref.shape[0]
-    copies = []
+def pack_kernel(distances, own, first, lanes, place_ref, block_ref, models_ref, *refs):
+    outs, (held, in_sems, out_sems) = refs[: len(distances)], refs[len(distances) :]
+    spectra, rows = block_ref.shape[0], held.shape[2]
+    owned, members = models_ref.shape
+    arrivals, departures = [], []
     for j, k in enumerate(distances):
         row = pl.multiple_of((place_ref[1] ^ k) * own + first, GROUP)
-        copies.append((block_ref.at[:, pl.ds(row, rows)], outs[j].at[pl.ds(0, spectra)]))
-        owned, members = models_ref.shape
+        source, target = block_ref.at[:, pl.ds(row, rows)], held.at[j, pl.ds(0, spectra)]
+        arrivals.append(pltpu.make_async_copy(source, target, in_sems.at[j]))
+        departures.append(pltpu.make_async_copy(held.at[j], outs[j], out_sems.at[j]))
+        arrivals[j].start()
+    for j in range(len(distances)):
         for lane in range(lanes):
             part = owned // lanes
-            target = outs[j].at[spectra, pl.ds(0, part), pl.ds(lane * members, members)]
-            copies.append((models_ref.at[pl.ds(lane * part, part)], target))
-    copies = [pltpu.make_async_copy(*c, sems.at[n]) for n, c in enumerate(copies)]
-    for c in copies:
-        c.start()
-    for c in copies:
-        c.wait()
+            held[j, spectra, pl.ds(0, part), pl.ds(lane * members, members)] = models_ref[pl.ds(lane * part, part), :]
+    for arrival, departure in zip(arrivals, departures):
+        arrival.wait()
+        departure.start()
+    for departure in departures:
+        departure.wait()
 
 
 def pack(place, block, models, distances, own, first, rows, lanes):
     spectra, _, cells = block.shape
-    shape = jax.ShapeDtypeStruct((spectra + (lanes > 0), rows, cells), jnp.float32)
-    return pl.pallas_call(
-        functools.partial(pack_kernel, distances, own, first, rows, lanes),
-        in_specs=[SCALARS, ANY, ANY],
-        out_specs=[ANY] * len(distances),
-        out_shape=[shape] * len(distances),
-        scratch_shapes=[pltpu.SemaphoreType.DMA((len(distances) * (1 + lanes),))],
-        cost_estimate=cost(0, 8 * len(distances) * spectra * rows * cells),
+    count = len(distances)
+    shape = (spectra + (lanes > 0), rows, cells)
+    return pl.pallas_call(
+        functools.partial(pack_kernel, distances, own, first, lanes),
+        in_specs=[SCALARS, HBM, pl.BlockSpec(memory_space=pltpu.VMEM)],
+        out_specs=[HBM] * count,
+        out_shape=[jax.ShapeDtypeStruct(shape, jnp.float32)] * count,
+        scratch_shapes=[
+            pltpu.VMEM((count, *shape), jnp.float32),
+            pltpu.SemaphoreType.DMA((count,)),
+            pltpu.SemaphoreType.DMA((count,)),
+        ],
+        compiler_params=params(48),
+        cost_estimate=cost(0, 8 * count * spectra * rows * cells),
         name="pack",
     )(place, block, models)
 
@@ -131,46 +140,45 @@
         in_specs=[SCALARS, whole(cell_index), whole(models)] + [rider] * len(first),
         out_specs=pl.BlockSpec((owned * (len(first) + 1) + GROUP, members), lambda i: (0, 0)),
         out_shape=jax.ShapeDtypeStruct((owned * (len(first) + 1) + GROUP, members), jnp.float32),
-        compiler_params=params(),
+        compiler_params=params(16),
         cost_estimate=cost(0, 1 << 20),
         name="near_models",
     )(place, cell_index, models, *first)
 
 
-def tile_models_kernel(owned, partners, place_ref, cells_ref, far_ref, high_ref, low_ref):
-    tiles, rows, _ = far_ref.shape
-    owners = len(partners)
-    block_cells = owned * owners
+def tile_models_kernel(owned, partners, place_ref, cells_ref, *refs):
+    tile_refs, (high_ref, low_ref) = refs[:-2], refs[-2:]
+    block_cells = owned * len(partners)
     cells = cells_ref[...]
-    distance = (cells // owned % owners) ^ place_ref[1]
+    distance = (cells // owned % len(partners)) ^ place_ref[1]
     slot = jnp.zeros_like(cells)
     for n, k in enumerate(partners):
         slot = jnp.where(distance == k, n, slot)
     spot = slot * owned + cells % owned
-    home = cells // block_cells
+    away = (cells // block_cells) ^ place_ref[0]
     high, low = None, None
-    for t in range(tiles):
+    for k, ref in enumerate(tile_refs):
         row = lax.broadcasted_iota(jnp.int32, (block_cells, cells.shape[1]), 0)
-        pick = jnp.where((row == spot) & (home == t), 1.0, 0.0).astype(jnp.bfloat16)
-        h, l = split(far_ref[t, pl.ds(0, block_cells), :].T)
+        pick = jnp.where((row == spot) & (away == k), 1.0, 0.0).astype(jnp.bfloat16)
+        h, l = split(ref[pl.ds(0, block_cells), :].T)
         h = lax.dot_general(h, pick, NN, preferred_element_type=jnp.float32)
         l = lax.dot_general(l, pick, NN, preferred_element_type=jnp.float32)
-        high, low = (h, l) if t == 0 else (high + h, low + l)
+        high, low = (h, l) if k == 0 else (high + h, low + l)
     high_ref[...] = high.astype(jnp.bfloat16)
     low_ref[...] = low.astype(jnp.bfloat16)
 
 
-def tile_models(place, cell_index, far, owned, partners):
-    shape = jax.ShapeDtypeStruct((far.shape[2], cell_index.shape[1]), jnp.bfloat16)
+def tile_models(place, cell_index, tiles, owned, partners):
+    shape = jax.ShapeDtypeStruct((tiles[0].shape[1], cell_index.shape[1]), jnp.bfloat16)
     return pl.pallas_call(
         functools.partial(tile_models_kernel, owned, partners),
-        in_specs=[SCALARS] + [pl.BlockSpec(memory_space=pltpu.VMEM)] * 2,
+        in_specs=[SCALARS] + [pl.BlockSpec(memory_space=pltpu.VMEM)] * (1 + len(tiles)),
         out_specs=[pl.BlockSpec(memory_space=pltpu.VMEM)] * 2,
         out_shape=[shape] * 2,
-        compiler_params=params(),
+        compiler_params=params(16),
         cost_estimate=cost(1 << 30, 2 << 20),
         name="tile_models",
-    )(place, cell_index, far)
+    )(place, cell_index, *tiles)
 
 
 def wide_kernel(table_ref, high_ref, low_ref):
@@ -195,7 +203,7 @@
         in_specs=[pl.BlockSpec(memory_space=pltpu.VMEM)],
         out_specs=[pl.BlockSpec(memory_space=pltpu.VMEM)] * 2,
         out_shape=[shape] * 2,
-        compiler_params=params(),
+        compiler_params=params(16),
         cost_estimate=cost(1 << 28, 1 << 20),
         name="wide_table",
     )(table)
@@ -260,7 +268,7 @@
             jax.ShapeDtypeStruct(square.shape, jnp.float32),
         ],
         input_output_aliases={pieces + 7: 0, pieces + 8: 1},
-        compiler_params=params(),
+        compiler_params=params(40),
         cost_estimate=cost(
             12 * pieces * spectra * rows * cells * members * 2, 4 * pieces * spectra * rows * cells
         ),
@@ -272,7 +280,7 @@
     return lax.dot_general(a, b, dims, precision=HIGH, preferred_element_type=jnp.float32)
 
 
-def gradient_kernel(tiles, owned, borrowed_ref, got_ref, square_ref, out_ref):
+def gradient_kernel(tiles, owned, place_ref, borrowed_ref, got_ref, square_ref, out_ref):
     devices, slab, cells = got_ref.shape
     owners = devices // tiles
     block_cells = owned * owners
@@ -287,7 +295,7 @@
     for b in range(tiles):
         block = sums[b][:, :block_cells]
         for t in range(tiles):
-            block = block + jnp.where(borrowed_ref[t] == b, sums[t][:, block_cells:], 0.0)
+            block = block + jnp.where(borrowed_ref[place_ref[0] ^ t] == b, sums[t][:, block_cells:], 0.0)
         gradient.append(block)
     square = sum(jnp.sum(g * g, axis=1, keepdims=True) for g in gradient)
     scale = jnp.sqrt(square / (tiles * block_cells) + EPSILON)
@@ -305,17 +313,17 @@
             out_ref[b * owners + f] = piece + rider
 
 
-def gradient_step(borrowed, got, square, tiles, owned):
+def gradient_step(place, borrowed, got, square, tiles, owned):
     devices, slab, _ = got.shape
     return pl.pallas_call(
         functools.partial(gradient_kernel, tiles, owned),
-        in_specs=[SCALARS] + [pl.BlockSpec(memory_space=pltpu.VMEM)] * 2,
+        in_specs=[SCALARS] * 2 + [pl.BlockSpec(memory_space=pltpu.VMEM)] * 2,
         out_specs=pl.BlockSpec(memory_space=pltpu.VMEM),
         out_shape=jax.ShapeDtypeStruct((devices, slab, LANES), jnp.float32),
-        compiler_params=params(),
+        compiler_params=params(16),
         cost_estimate=cost(1 << 22, 1 << 20),
         name="gradient_step",
-    )(borrowed, got, square)
+    )(place, borrowed, got, square)
 
 
 def update_kernel(divisor, models_ref, back_ref, updated_ref, misfit_ref):
@@ -344,7 +352,7 @@
             jax.ShapeDtypeStruct(models.shape, jnp.float32),
             jax.ShapeDtypeStruct((1, models.shape[1]), jnp.float32),
         ],
-        compiler_params=params(),
+        compiler_params=params(16),
         cost_estimate=cost(1 << 20, 1 << 18),
         name="update",
     )(models, back)
@@ -387,9 +395,9 @@
         received.append([swap(p, "freq", k) for p, k in zip(pieces, distances)])
 
     near = near_models(place, cell_index, models, received[0], lanes)
-    far = lax.all_gather(near, "tile", axis=0, tiled=False)
-    all_borrowed = far[:, block_cells, 0].astype(jnp.int32)
-    models_t = tile_models(place, cell_index, far, owned, partners)
+    blocks = [near] + [swap(near, "tile", k) for k in range(1, tiles)]
+    borrowed = jnp.stack([b[block_cells, 0] for b in blocks]).astype(jnp.int32)
+    models_t = tile_models(place, cell_index, blocks, owned, partners)
 
     order = place[1] ^ jnp.array(partners, jnp.int32)
     wide = wide_table(gate_table(order, own_freqs, freqs, waveform, gate_index).T)
@@ -408,13 +416,14 @@
     sent = terms.reshape(devices, slab, cells)
     got = lax.all_to_all(sent, both, split_axis=0, concat_axis=0, tiled=True)
     if slab % GROUP == 0 and members // slab + owned <= LANES:
-        step = gradient_step(all_borrowed, got, square, tiles, owned)
+        step = gradient_step(place, borrowed, got, square, tiles, owned)
         back = lax.all_to_all(step, both, split_axis=0, concat_axis=0, tiled=True)
         updated, misfit = update(models, back, divisor)
         return (updated, misfit.reshape(members))
 
     got = jnp.sum(got.reshape(tiles, owners, slab, cells), axis=1)
-    lent = (all_borrowed[None, :] == jnp.arange(tiles)[:, None]).astype(jnp.float32)
+    tile_ids = jnp.arange(tiles)
+    lent = (jnp.take(borrowed, tile_ids ^ place[0])[None, :] == tile_ids[:, None]).astype(jnp.float32)
     gradient = got[:, :, :block_cells] + jnp.sum(
         lent[:, :, None, None] * got[None, :, :, block_cells:], axis=1
     )

time: 835 us -> 428 us (0.51)
  Pallas kernels: 519 us -> 70.9 us
  starting transfers between devices: 111 us -> 151 us
  local copies, waits for them, and re-layouts: 3.42 us -> 32.2 us
  waiting for transfers between devices: 173 us -> 156 us
  between operations: 14.6 us -> 1.18 us
    pallas_call x6, Pallas kernels: 463 us -> 15.6 us  [pack(): pl.pallas_call(functools.partial(pack_kernel, distances, own, first, lane...]
    ppermute x42 -> x45, starting transfers between devices: 106 us -> 148 us  [swap(): lax.ppermute(x, axis, [(i, i ^ k) for i in range(lax.axis_size(axis))])]
    unnamed x81 -> x129, local copies, waits for them, and re-layouts: 2.25 us -> 25.3 us
    ppermute x42 -> x45, waiting for transfers between devices: 157 us -> 147 us  [swap(): lax.ppermute(x, axis, [(i, i ^ k) for i in range(lax.axis_size(axis))])]
  transfers between devices with their start and end apart: 44 -> 46, of which waited for: 16 -> 17; matrix products, arithmetic and copies ran while one was open for 1% -> 3% of each run, Pallas kernels for 53% -> 14%
where the time goes in v4:
time: 428 us; the launch traced here: 427 us
  waiting for transfers between devices  156 us (36%)
  starting transfers between devices  151 us (35%)
  Pallas kernels  70.9 us (17%)
  local copies, waits for them, and re-layouts  32.2 us (8%)
  blocking collectives  9.82 us (2%)
  other arithmetic  4.85 us (1%)
    ppermute x45, starting transfers between devices, swap(): lax.ppermute(x, axis, [(i, i ^ k) for i in range(lax.axis_size(axis))])  148 us
    ppermute x45, waiting for transfers between devices, swap(): lax.ppermute(x, axis, [(i, i ^ k) for i in range(lax.axis_size(axis))])  147 us
    pallas_call x6, Pallas kernels, chunk_step(): pl.pallas_call(functools.partial(chunk_kernel, pieces, block_cells, last)...  50.8 us
    unnamed x129, local copies, waits for them, and re-layouts  25.3 us
    pallas_call x6, Pallas kernels, pack(): pl.pallas_call(functools.partial(pack_kernel, distances, own, first, lane...  15.6 us
    all_to_all x1, blocking collectives, body(): back = lax.all_to_all(step, both, split_axis=0, concat_axis=0, tiled=True)  9.82 us
    all_to_all x1, waiting for transfers between devices, body(): got = lax.all_to_all(sent, both, split_axis=0, concat_axis=0, tiled=True)  9.59 us
  transfers between devices with their start and end apart: 46, of which 17 were waited for; matrix products, arithmetic and copies ran while one was open for 3% of the time, Pallas kernels for 14%

profile of v4, /device:TPU:0, one launch (start us, length us, event | category | flops | bytes accessed | tf_op | source)
XLA Modules:
  0.0 426.8 jit_solution(4082715153643154320)
XLA Ops:
  3.6 6.0 %collective-permute-start = (f32[9,16,512]{2,1,0:T(8,128)S(1)}, f32[9,16,512]{2,1,0:T(8,128)S(1)}, u32[]{:S(2)}, u32[]{:S(2)}) collective-permute-start(f32[9,16,512]{2,1,0:T(8,128)S(1)} %get-tuple-element.62), channel_id=1, source_target_pairs={{0,7},{1,6},{2,5},{3,4},{4,3},{5,2},{6,1},{7,0},{8,15},{9,14},{10,... | collective-permute-start | bytes 884744 | tf_op jit(solution)/shard_map/ppermute | solution.py:23
  20.8 3.8 collective-permute-start.10
  26.7 9.5 %collective-permute-done.10.refs_1_ = f32[8,8,512]{2,1,0:T(8,128)S(1)} collective-permute-done((f32[8,8,512]{2,1,0:T(8,128)S(1)}, f32[8,8,512]{2,1,0:T(8,128)S(1)}, u32[]{:S(2)}, u32[]{:S(2)}) %collective-permute-start.10) | collective-permute-done | bytes 131104 | tf_op jit(solution)/shard_map/ppermute | solution.py:23
  36.2 8.7 %collective-permute-start.1 = (f32[9,16,512]{2,1,0:T(8,128)S(1)}, f32[9,16,512]{2,1,0:T(8,128)S(1)}, u32[]{:S(2)}, u32[]{:S(2)}) collective-permute-start(f32[9,16,512]{2,1,0:T(8,128)S(1)} %get-tuple-element.63), channel_id=1, source_target_pairs={{0,3},{1,2},{2,1},{3,0},{4,7},{5,6},{6,5},{7,4},{8,11},{9,10},{10,... | collective-permute-start | bytes 884744 | tf_op jit(solution)/shard_map/ppermute | solution.py:23
  71.4 27.8 %collective-permute-done.4.refs_4_.refs_5_ = f32[9,16,512]{2,1,0:T(8,128)S(1)} collective-permute-done((f32[9,16,512]{2,1,0:T(8,128)S(1)}, f32[9,16,512]{2,1,0:T(8,128)S(1)}, u32[]{:S(2)}, u32[]{:S(2)}) %collective-permute-start.4) | collective-permute-done | bytes 294944 | tf_op jit(solution)/shard_map/ppermute | solution.py:23
  103.7 3.8 collective-permute-start.40
  107.5 16.6 %collective-permute-start.41 = (f32[8,32,512]{2,1,0:T(8,128)}, f32[8,32,512]{2,1,0:T(8,128)}, u32[]{:S(2)}, u32[]{:S(2)}) collective-permute-start(f32[8,32,512]{2,1,0:T(8,128)} %get-tuple-element.104), channel_id=1, source_target_pairs={{0,2},{1,3},{2,0},{3,1},{4,6},{5,7},{6,4},{7,5},{8,10},{9,11},{10,... | collective-permute-start | bytes 1572872 | tf_op jit(solution)/shard_map/ppermute | solution.py:23
  137.4 4.7 %collective-permute-done.40.refs_3_ = f32[8,32,512]{2,1,0:T(8,128)} collective-permute-done((f32[8,32,512]{2,1,0:T(8,128)}, f32[8,32,512]{2,1,0:T(8,128)}, u32[]{:S(2)}, u32[]{:S(2)}) %collective-permute-start.40) | collective-permute-done | bytes 524320 | tf_op jit(solution)/shard_map/ppermute | solution.py:23
  142.1 12.1 %collective-permute-start.42 = (f32[8,32,512]{2,1,0:T(8,128)}, f32[8,32,512]{2,1,0:T(8,128)}, u32[]{:S(2)}, u32[]{:S(2)}) collective-permute-start(f32[8,32,512]{2,1,0:T(8,128)} %copy-done.21), channel_id=1, source_target_pairs={{0,5},{1,4},{2,7},{3,6},{4,1},{5,0},{6,3},{7,2},{8,13},{9,12},{10,... | collective-permute-start | bytes 1572872 | tf_op jit(solution)/shard_map/ppermute | solution.py:23
  170.4 6.9 %chunk_step.6 = (f32[256,512]{1,0:T(8,128)}, f32[256,128]{1,0:T(8,128)S(1)}) custom-call(s32[2]{0:T(128)S(1)} %pad_add_fusion.place_ref, f32[8,1024,512]{2,1,0:T(8,128)} %bitcast.22, f32[9,16,512]{2,1,0:T(8,128)S(1)} %collective-permute-done.refs_0_.refs_1_, ...), custom_call_target="tpu_custom_call", output_to_operand_aliasing={{0}: (15, {}), {1}: (16, {})} | custom-call | flops 3221225472 | bytes 2097152 | tf_op jit(solution)/shard_map/chunk_step/pallas_call | solution.py:252
  177.3 23.8 %collective-permute-done.42.refs_5_ = f32[8,32,512]{2,1,0:T(8,128)} collective-permute-done((f32[8,32,512]{2,1,0:T(8,128)}, f32[8,32,512]{2,1,0:T(8,128)}, u32[]{:S(2)}, u32[]{:S(2)}) %collective-permute-start.42) | collective-permute-done | bytes 524320 | tf_op jit(solution)/shard_map/ppermute | solution.py:23
  203.4 20.1 %collective-permute-done.44.refs_7_ = f32[8,32,512]{2,1,0:T(8,128)} collective-permute-done((f32[8,32,512]{2,1,0:T(8,128)}, f32[8,32,512]{2,1,0:T(8,128)}, u32[]{:S(2)}, u32[]{:S(2)}) %collective-permute-start.44) | collective-permute-done | bytes 524320 | tf_op jit(solution)/shard_map/ppermute | solution.py:23
  224.5 23.5 %collective-permute-start.37 = (f32[8,32,512]{2,1,0:T(8,128)S(1)}, f32[8,32,512]{2,1,0:T(8,128)S(1)}, u32[]{:S(2)}, u32[]{:S(2)}) collective-permute-start(f32[8,32,512]{2,1,0:T(8,128)S(1)} %copy-done.10), channel_id=1, source_target_pairs={{0,4},{1,5},{2,6},{3,7},{4,0},{5,1},{6,2},{7,3},{8,12},{9,13},{10,... | collective-permute-start | bytes 1572872 | tf_op jit(solution)/shard_map/ppermute | solution.py:23
  248.0 11.5 %chunk_step.7 = (f32[256,512]{1,0:T(8,128)}, f32[256,128]{1,0:T(8,128)S(1)}) custom-call(s32[2]{0:T(128)S(1)} %pad_add_fusion.place_ref, f32[8,1024,512]{2,1,0:T(8,128)} %bitcast.23, f32[8,32,512]{2,1,0:T(8,128)} %collective-permute-done.38.refs_1_, f32[8,32,512]{2,1,0:T(8,128)} %collective-permute-done.39.refs_2_, ...), custom_call_target="tpu_custom_call", output_to_operand_aliasing={{0}: (15, {}), {1}: (16, {})} | custom-call | flops 6442450944 | bytes 4194304 | tf_op jit(solution)/shard_map/chunk_step/pallas_call | solution.py:252
  262.0 15.9 %collective-permute-start.27 = (f32[8,24,512]{2,1,0:T(8,128)S(1)}, f32[8,24,512]{2,1,0:T(8,128)S(1)}, u32[]{:S(2)}, u32[]{:S(2)}) collective-permute-start(f32[8,24,512]{2,1,0:T(8,128)S(1)} %copy-done.31), channel_id=1, source_target_pairs={{0,2},{1,3},{2,0},{3,1},{4,6},{5,7},{6,4},{7,5},{8,10},{9,11},{10,... | collective-permute-start | bytes 1179656 | tf_op jit(solution)/shard_map/ppermute | solution.py:23
  277.9 10.3 %collective-permute-done.35.refs_5_ = f32[8,32,512]{2,1,0:T(8,128)S(1)} collective-permute-done((f32[8,32,512]{2,1,0:T(8,128)S(1)}, f32[8,32,512]{2,1,0:T(8,128)S(1)}, u32[]{:S(2)}, u32[]{:S(2)}) %collective-permute-start.35) | collective-permute-done | bytes 524320 | tf_op jit(solution)/shard_map/ppermute | solution.py:23
  288.2 5.6 %collective-permute-start.29 = (f32[8,24,512]{2,1,0:T(8,128)S(1)}, f32[8,24,512]{2,1,0:T(8,128)S(1)}, u32[]{:S(2)}, u32[]{:S(2)}) collective-permute-start(f32[8,24,512]{2,1,0:T(8,128)S(1)} %copy-done.27), channel_id=1, source_target_pairs={{0,1},{1,0},{2,3},{3,2},{4,5},{5,4},{6,7},{7,6},{8,9},{9,8},{10,11... | collective-permute-start | bytes 1179656 | tf_op jit(solution)/shard_map/ppermute | solution.py:23
  293.8 13.8 %collective-permute-done.37.refs_7_ = f32[8,32,512]{2,1,0:T(8,128)S(1)} collective-permute-done((f32[8,32,512]{2,1,0:T(8,128)S(1)}, f32[8,32,512]{2,1,0:T(8,128)S(1)}, u32[]{:S(2)}, u32[]{:S(2)}) %collective-permute-start.37) | collective-permute-done | bytes 524320 | tf_op jit(solution)/shard_map/ppermute | solution.py:23
  307.7 11.3 %chunk_step.8 = (f32[256,512]{1,0:T(8,128)}, f32[256,128]{1,0:T(8,128)S(1)}) custom-call(s32[2]{0:T(128)S(1)} %pad_add_fusion.place_ref, f32[8,1024,512]{2,1,0:T(8,128)} %bitcast.24, f32[8,32,512]{2,1,0:T(8,128)} %collective-permute-done.31.refs_1_, f32[8,32,512]{2,1,0:T(8,128)} %collective-permute-done.32.refs_2_, ...), custom_call_target="tpu_custom_call", output_to_operand_aliasing={{0}: (15, {}), {1}: (16, {})} | custom-call | flops 6442450944 | bytes 4194304 | tf_op jit(solution)/shard_map/chunk_step/pallas_call | solution.py:252
  319.1 9.9 %collective-permute-start.19 = (f32[8,16,512]{2,1,0:T(8,128)S(1)}, f32[8,16,512]{2,1,0:T(8,128)S(1)}, u32[]{:S(2)}, u32[]{:S(2)}) collective-permute-start(f32[8,16,512]{2,1,0:T(8,128)S(1)} %copy-done.49), channel_id=1, source_target_pairs={{0,6},{1,7},{2,4},{3,5},{4,2},{5,3},{6,0},{7,1},{8,14},{9,15},{10,... | collective-permute-start | bytes 786440 | tf_op jit(solution)/shard_map/ppermute | solution.py:23
  329.7 9.1 %collective-permute-done.28.refs_5_ = f32[8,24,512]{2,1,0:T(8,128)S(1)} collective-permute-done((f32[8,24,512]{2,1,0:T(8,128)S(1)}, f32[8,24,512]{2,1,0:T(8,128)S(1)}, u32[]{:S(2)}, u32[]{:S(2)}) %collective-permute-start.28) | collective-permute-done | bytes 393248 | tf_op jit(solution)/shard_map/ppermute | solution.py:23
  338.8 4.2 collective-permute-start.22
  343.0 9.6 %collective-permute-done.30.refs_7_ = f32[8,24,512]{2,1,0:T(8,128)S(1)} collective-permute-done((f32[8,24,512]{2,1,0:T(8,128)S(1)}, f32[8,24,512]{2,1,0:T(8,128)S(1)}, u32[]{:S(2)}, u32[]{:S(2)}) %collective-permute-start.30) | collective-permute-done | bytes 393248 | tf_op jit(solution)/shard_map/ppermute | solution.py:23
  352.7 9.2 %chunk_step.9 = (f32[256,512]{1,0:T(8,128)}, f32[256,128]{1,0:T(8,128)S(1)}) custom-call(s32[2]{0:T(128)S(1)} %pad_add_fusion.place_ref, f32[8,1024,512]{2,1,0:T(8,128)} %bitcast.25, f32[8,24,512]{2,1,0:T(8,128)S(1)} %collective-permute-done.24.refs_1_, ...), custom_call_target="tpu_custom_call", output_to_operand_aliasing={{0}: (15, {}), {1}: (16, {})} | custom-call | flops 4831838208 | bytes 3145728 | tf_op jit(solution)/shard_map/chunk_step/pallas_call | solution.py:252
  361.9 4.3 %collective-permute-start.12 = (f32[8,8,512]{2,1,0:T(8,128)S(1)}, f32[8,8,512]{2,1,0:T(8,128)S(1)}, u32[]{:S(2)}, u32[]{:S(2)}) collective-permute-start(f32[8,8,512]{2,1,0:T(8,128)S(1)} %copy-done.59), channel_id=1, source_target_pairs={{0,6},{1,7},{2,4},{3,5},{4,2},{5,3},{6,0},{7,1},{8,14},{9,15},{10,... | collective-permute-start | bytes 393224 | tf_op jit(solution)/shard_map/ppermute | solution.py:23
  366.8 5.9 %collective-permute-done.21.refs_5_ = f32[8,16,512]{2,1,0:T(8,128)S(1)} collective-permute-done((f32[8,16,512]{2,1,0:T(8,128)S(1)}, f32[8,16,512]{2,1,0:T(8,128)S(1)}, u32[]{:S(2)}, u32[]{:S(2)}) %collective-permute-start.21) | collective-permute-done | bytes 262176 | tf_op jit(solution)/shard_map/ppermute | solution.py:23
  375.4 5.4 %collective-permute-done.23.refs_7_ = f32[8,16,512]{2,1,0:T(8,128)S(1)} collective-permute-done((f32[8,16,512]{2,1,0:T(8,128)S(1)}, f32[8,16,512]{2,1,0:T(8,128)S(1)}, u32[]{:S(2)}, u32[]{:S(2)}) %collective-permute-start.23) | collective-permute-done | bytes 262176 | tf_op jit(solution)/shard_map/ppermute | solution.py:23
  380.8 6.8 %chunk_step.10 = (f32[256,512]{1,0:T(8,128)}, f32[256,128]{1,0:T(8,128)S(1)}) custom-call(s32[2]{0:T(128)S(1)} %pad_add_fusion.place_ref, f32[8,1024,512]{2,1,0:T(8,128)} %bitcast.26, f32[8,16,512]{2,1,0:T(8,128)S(1)} %copy-done.3, f32[8,16,512]{2,1,0:T(8,128)S(1)} %copy-done.5, ...), custom_call_target="tpu_custom_call", output_to_operand_aliasing={{0}: (15, {}), {1}: (16, {})} | custom-call | flops 3221225472 | bytes 2097152 | tf_op jit(solution)/shard_map/chunk_step/pallas_call | solution.py:252
  389.9 5.1 %chunk_step.11 = (f32[256,512]{1,0:T(8,128)}, f32[256,128]{1,0:T(8,128)S(1)}) custom-call(s32[2]{0:T(128)S(1)} %pad_add_fusion.place_ref, f32[8,1024,512]{2,1,0:T(8,128)} %bitcast.27, f32[8,8,512]{2,1,0:T(8,128)S(1)} %collective-permute-done.10.refs_1_, f32[8,8,512]{2,1,0:T(8,128)S(1)} %copy-done.7, ...), custom_call_target="tpu_custom_call", output_to_operand_aliasing={{0}: (15, {}), {1}: (16, {})} | custom-call | flops 1610612736 | bytes 1048576 | tf_op jit(solution)/shard_map/chunk_step/pallas_call | solution.py:252
  395.0 3.9 all-to-all-start
  405.6 9.6 %all-to-all-done.got_ref = f32[32,8,512]{2,1,0:T(8,128)S(1)} async-done(((f32[32,8,512]{2,1,0:T(8,128)}), f32[32,8,512]{2,1,0:T(8,128)S(1)}, u32[]{:S(2)}, u32[]{:S(2)}) %all-to-all-start) | async-done | bytes 524320 | tf_op jit(solution)/shard_map/all_to_all | solution.py:417
  416.0 9.8 %all_to_all.10.back_ref = f32[32,8,128]{2,1,0:T(8,128)S(1)} all-to-all(f32[32,8,128]{2,1,0:T(8,128)S(1)} %gradient_step.1), channel_id=1, replica_groups=mesh['tile'=4,'freq'=8] {'tile','freq'}, dimensions={0} | all-to-all | bytes 262144 | tf_op jit(solution)/shard_map/all_to_all | solution.py:420
  (227 shorter events, 96.8 us)
Async XLA Ops:
  3.6 47.2 %collective-permute-start = (f32[9,16,512]{2,1,0:T(8,128)S(1)}, f32[9,16,512]{2,1,0:T(8,128)S(1)}, u32[]{:S(2)}, u32[]{:S(2)}) collective-permute-start(f32[9,16,512]{2,1,0:T(8,128)S(1)} %get-tuple-element.62), channel_id=1, source_target_pairs={{0,7},{1,6},{2,5},{3,4},{4,3},{5,2},{6,1},{7,0},{8,15},{9,14},{10,... | collective-permute-start | bytes 884744 | tf_op jit(solution)/shard_map/ppermute | solution.py:23
  13.9 33.6 %collective-permute-start.17 = (f32[8,16,512]{2,1,0:T(8,128)S(1)}, f32[8,16,512]{2,1,0:T(8,128)S(1)}, u32[]{:S(2)}, u32[]{:S(2)}) collective-permute-start(f32[8,16,512]{2,1,0:T(8,128)S(1)} %get-tuple-element.80), channel_id=1, source_target_pairs={{0,7},{1,6},{2,5},{3,4},{4,3},{5,2},{6,1},{7,0},{8,15},{9,14},{10,... | collective-permute-start | bytes 786440 | tf_op jit(solution)/shard_map/ppermute | solution.py:23
  13.9 34.3 %collective-permute-start.18 = (f32[8,16,512]{2,1,0:T(8,128)S(1)}, f32[8,16,512]{2,1,0:T(8,128)S(1)}, u32[]{:S(2)}, u32[]{:S(2)}) collective-permute-start(f32[8,16,512]{2,1,0:T(8,128)S(1)} %get-tuple-element.81), channel_id=1, source_target_pairs={{0,3},{1,2},{2,1},{3,0},{4,7},{5,6},{6,5},{7,4},{8,11},{9,10},{10,... | collective-permute-start | bytes 786440 | tf_op jit(solution)/shard_map/ppermute | solution.py:23
  48.9 50.3 %collective-permute-start.4 = (f32[9,16,512]{2,1,0:T(8,128)S(1)}, f32[9,16,512]{2,1,0:T(8,128)S(1)}, u32[]{:S(2)}, u32[]{:S(2)}) collective-permute-start(f32[9,16,512]{2,1,0:T(8,128)S(1)} %get-tuple-element.66), channel_id=1, source_target_pairs={{0,5},{1,4},{2,7},{3,6},{4,1},{5,0},{6,3},{7,2},{8,13},{9,12},{10,... | collective-permute-start | bytes 884744 | tf_op jit(solution)/shard_map/ppermute | solution.py:23
  50.8 48.4 %collective-permute-start.5 = (f32[9,16,512]{2,1,0:T(8,128)S(1)}, f32[9,16,512]{2,1,0:T(8,128)S(1)}, u32[]{:S(2)}, u32[]{:S(2)}) collective-permute-start(f32[9,16,512]{2,1,0:T(8,128)S(1)} %get-tuple-element.67), channel_id=1, source_target_pairs={{0,1},{1,0},{2,3},{3,2},{4,5},{5,4},{6,7},{7,6},{8,9},{9,8},{10,11... | collective-permute-start | bytes 884744 | tf_op jit(solution)/shard_map/ppermute | solution.py:23
  59.6 44.2 %collective-permute-start.6 = (f32[9,16,512]{2,1,0:T(8,128)S(1)}, f32[9,16,512]{2,1,0:T(8,128)S(1)}, u32[]{:S(2)}, u32[]{:S(2)}) collective-permute-start(f32[9,16,512]{2,1,0:T(8,128)S(1)} %get-tuple-element.68), channel_id=1, source_target_pairs={{0,4},{1,5},{2,6},{3,7},{4,0},{5,1},{6,2},{7,3},{8,12},{9,13},{10,... | collective-permute-start | bytes 884744 | tf_op jit(solution)/shard_map/ppermute | solution.py:23
  61.1 46.4 %collective-permute-start.24 = (f32[8,24,512]{2,1,0:T(8,128)S(1)}, f32[8,24,512]{2,1,0:T(8,128)S(1)}, u32[]{:S(2)}, u32[]{:S(2)}) collective-permute-start(f32[8,24,512]{2,1,0:T(8,128)S(1)} %get-tuple-element.87), channel_id=1, source_target_pairs={{0,7},{1,6},{2,5},{3,4},{4,3},{5,2},{6,1},{7,0},{8,15},{9,14},{10,... | collective-permute-start | bytes 1179656 | tf_op jit(solution)/shard_map/ppermute | solution.py:23
  69.7 63.9 %collective-permute-start.38 = (f32[8,32,512]{2,1,0:T(8,128)}, f32[8,32,512]{2,1,0:T(8,128)}, u32[]{:S(2)}, u32[]{:S(2)}) collective-permute-start(f32[8,32,512]{2,1,0:T(8,128)} %get-tuple-element.101), channel_id=1, source_target_pairs={{0,7},{1,6},{2,5},{3,4},{4,3},{5,2},{6,1},{7,0},{8,15},{9,14},{10,... | collective-permute-start | bytes 1572872 | tf_op jit(solution)/shard_map/ppermute | solution.py:23
  99.2 36.0 %collective-permute-start.39 = (f32[8,32,512]{2,1,0:T(8,128)}, f32[8,32,512]{2,1,0:T(8,128)}, u32[]{:S(2)}, u32[]{:S(2)}) collective-permute-start(f32[8,32,512]{2,1,0:T(8,128)} %get-tuple-element.102), channel_id=1, source_target_pairs={{0,3},{1,2},{2,1},{3,0},{4,7},{5,6},{6,5},{7,4},{8,11},{9,10},{10,... | collective-permute-start | bytes 1572872 | tf_op jit(solution)/shard_map/ppermute | solution.py:23
  99.2 34.4 %collective-permute-start.25 = (f32[8,24,512]{2,1,0:T(8,128)}, f32[8,24,512]{2,1,0:T(8,128)S(1)}, u32[]{:S(2)}, u32[]{:S(2)}) collective-permute-start(f32[8,24,512]{2,1,0:T(8,128)} %get-tuple-element.88), channel_id=1, source_target_pairs={{0,3},{1,2},{2,1},{3,0},{4,7},{5,6},{6,5},{7,4},{8,11},{9,10},{10,... | collective-permute-start | bytes 1179656 | tf_op jit(solution)/shard_map/ppermute | solution.py:23
  103.7 38.4 %collective-permute-start.40 = (f32[8,32,512]{2,1,0:T(8,128)}, f32[8,32,512]{2,1,0:T(8,128)}, u32[]{:S(2)}, u32[]{:S(2)}) collective-permute-start(f32[8,32,512]{2,1,0:T(8,128)} %get-tuple-element.103), channel_id=1, source_target_pairs={{0,6},{1,7},{2,4},{3,5},{4,2},{5,3},{6,0},{7,1},{8,14},{9,15},{10,... | collective-permute-start | bytes 1572872 | tf_op jit(solution)/shard_map/ppermute | solution.py:23
  107.5 46.7 %collective-permute-start.41 = (f32[8,32,512]{2,1,0:T(8,128)}, f32[8,32,512]{2,1,0:T(8,128)}, u32[]{:S(2)}, u32[]{:S(2)}) collective-permute-start(f32[8,32,512]{2,1,0:T(8,128)} %get-tuple-element.104), channel_id=1, source_target_pairs={{0,2},{1,3},{2,0},{3,1},{4,6},{5,7},{6,4},{7,5},{8,10},{9,11},{10,... | collective-permute-start | bytes 1572872 | tf_op jit(solution)/shard_map/ppermute | solution.py:23
  142.1 59.0 %collective-permute-start.42 = (f32[8,32,512]{2,1,0:T(8,128)}, f32[8,32,512]{2,1,0:T(8,128)}, u32[]{:S(2)}, u32[]{:S(2)}) collective-permute-start(f32[8,32,512]{2,1,0:T(8,128)} %copy-done.21), channel_id=1, source_target_pairs={{0,5},{1,4},{2,7},{3,6},{4,1},{5,0},{6,3},{7,2},{8,13},{9,12},{10,... | collective-permute-start | bytes 1572872 | tf_op jit(solution)/shard_map/ppermute | solution.py:23
  154.2 49.2 %collective-permute-start.43 = (f32[8,32,512]{2,1,0:T(8,128)}, f32[8,32,512]{2,1,0:T(8,128)}, u32[]{:S(2)}, u32[]{:S(2)}) collective-permute-start(f32[8,32,512]{2,1,0:T(8,128)} %copy-done.18), channel_id=1, source_target_pairs={{0,1},{1,0},{2,3},{3,2},{4,5},{5,4},{6,7},{7,6},{8,9},{9,8},{10,11... | collective-permute-start | bytes 1572872 | tf_op jit(solution)/shard_map/ppermute | solution.py:23
  156.7 66.8 %collective-permute-start.44 = (f32[8,32,512]{2,1,0:T(8,128)}, f32[8,32,512]{2,1,0:T(8,128)}, u32[]{:S(2)}, u32[]{:S(2)}) collective-permute-start(f32[8,32,512]{2,1,0:T(8,128)} %copy-done.15), channel_id=1, source_target_pairs={{0,4},{1,5},{2,6},{3,7},{4,0},{5,1},{6,2},{7,3},{8,12},{9,13},{10,... | collective-permute-start | bytes 1572872 | tf_op jit(solution)/shard_map/ppermute | solution.py:23
  157.4 66.1 %collective-permute-start.31 = (f32[8,32,512]{2,1,0:T(8,128)}, f32[8,32,512]{2,1,0:T(8,128)}, u32[]{:S(2)}, u32[]{:S(2)}) collective-permute-start(f32[8,32,512]{2,1,0:T(8,128)} %copy-done.23), channel_id=1, source_target_pairs={{0,7},{1,6},{2,5},{3,4},{4,3},{5,2},{6,1},{7,0},{8,15},{9,14},{10,... | collective-permute-start | bytes 1572872 | tf_op jit(solution)/shard_map/ppermute | solution.py:23
  160.1 64.3 %collective-permute-start.32 = (f32[8,32,512]{2,1,0:T(8,128)}, f32[8,32,512]{2,1,0:T(8,128)}, u32[]{:S(2)}, u32[]{:S(2)}) collective-permute-start(f32[8,32,512]{2,1,0:T(8,128)} %copy-done.22), channel_id=1, source_target_pairs={{0,3},{1,2},{2,1},{3,0},{4,7},{5,6},{6,5},{7,4},{8,11},{9,10},{10,... | collective-permute-start | bytes 1572872 | tf_op jit(solution)/shard_map/ppermute | solution.py:23
  201.1 58.5 %collective-permute-start.33 = (f32[8,32,512]{2,1,0:T(8,128)S(1)}, f32[8,32,512]{2,1,0:T(8,128)S(1)}, u32[]{:S(2)}, u32[]{:S(2)}) collective-permute-start(f32[8,32,512]{2,1,0:T(8,128)S(1)} %copy-done.20), channel_id=1, source_target_pairs={{0,6},{1,7},{2,4},{3,5},{4,2},{5,3},{6,0},{7,1},{8,14},{9,15},{10,... | collective-permute-start | bytes 1572872 | tf_op jit(solution)/shard_map/ppermute | solution.py:23
  203.4 58.6 %collective-permute-start.34 = (f32[8,32,512]{2,1,0:T(8,128)S(1)}, f32[8,32,512]{2,1,0:T(8,128)S(1)}, u32[]{:S(2)}, u32[]{:S(2)}) collective-permute-start(f32[8,32,512]{2,1,0:T(8,128)S(1)} %copy-done.17), channel_id=1, source_target_pairs={{0,2},{1,3},{2,0},{3,1},{4,6},{5,7},{6,4},{7,5},{8,10},{9,11},{10,... | collective-permute-start | bytes 1572872 | tf_op jit(solution)/shard_map/ppermute | solution.py:23
  223.4 64.7 %collective-permute-start.35 = (f32[8,32,512]{2,1,0:T(8,128)S(1)}, f32[8,32,512]{2,1,0:T(8,128)S(1)}, u32[]{:S(2)}, u32[]{:S(2)}) collective-permute-start(f32[8,32,512]{2,1,0:T(8,128)S(1)} %copy-done.14), channel_id=1, source_target_pairs={{0,5},{1,4},{2,7},{3,6},{4,1},{5,0},{6,3},{7,2},{8,13},{9,12},{10,... | collective-permute-start | bytes 1572872 | tf_op jit(solution)/shard_map/ppermute | solution.py:23
  223.5 64.7 %collective-permute-start.36 = (f32[8,32,512]{2,1,0:T(8,128)S(1)}, f32[8,32,512]{2,1,0:T(8,128)S(1)}, u32[]{:S(2)}, u32[]{:S(2)}) collective-permute-start(f32[8,32,512]{2,1,0:T(8,128)S(1)} %copy-done.12), channel_id=1, source_target_pairs={{0,1},{1,0},{2,3},{3,2},{4,5},{5,4},{6,7},{7,6},{8,9},{9,8},{10,11... | collective-permute-start | bytes 1572872 | tf_op jit(solution)/shard_map/ppermute | solution.py:23
  224.5 83.2 %collective-permute-start.37 = (f32[8,32,512]{2,1,0:T(8,128)S(1)}, f32[8,32,512]{2,1,0:T(8,128)S(1)}, u32[]{:S(2)}, u32[]{:S(2)}) collective-permute-start(f32[8,32,512]{2,1,0:T(8,128)S(1)} %copy-done.10), channel_id=1, source_target_pairs={{0,4},{1,5},{2,6},{3,7},{4,0},{5,1},{6,2},{7,3},{8,12},{9,13},{10,... | collective-permute-start | bytes 1572872 | tf_op jit(solution)/shard_map/ppermute | solution.py:23
  259.6 59.5 %collective-permute-start.26 = (f32[8,24,512]{2,1,0:T(8,128)S(1)}, f32[8,24,512]{2,1,0:T(8,128)S(1)}, u32[]{:S(2)}, u32[]{:S(2)}) collective-permute-start(f32[8,24,512]{2,1,0:T(8,128)S(1)} %copy-done.33), channel_id=1, source_target_pairs={{0,6},{1,7},{2,4},{3,5},{4,2},{5,3},{6,0},{7,1},{8,14},{9,15},{10,... | collective-permute-start | bytes 1179656 | tf_op jit(solution)/shard_map/ppermute | solution.py:23
  262.0 67.0 %collective-permute-start.27 = (f32[8,24,512]{2,1,0:T(8,128)S(1)}, f32[8,24,512]{2,1,0:T(8,128)S(1)}, u32[]{:S(2)}, u32[]{:S(2)}) collective-permute-start(f32[8,24,512]{2,1,0:T(8,128)S(1)} %copy-done.31), channel_id=1, source_target_pairs={{0,2},{1,3},{2,0},{3,1},{4,6},{5,7},{6,4},{7,5},{8,10},{9,11},{10,... | collective-permute-start | bytes 1179656 | tf_op jit(solution)/shard_map/ppermute | solution.py:23
  288.2 50.6 %collective-permute-start.28 = (f32[8,24,512]{2,1,0:T(8,128)S(1)}, f32[8,24,512]{2,1,0:T(8,128)S(1)}, u32[]{:S(2)}, u32[]{:S(2)}) collective-permute-start(f32[8,24,512]{2,1,0:T(8,128)S(1)} %copy-done.29), channel_id=1, source_target_pairs={{0,5},{1,4},{2,7},{3,6},{4,1},{5,0},{6,3},{7,2},{8,13},{9,12},{10,... | collective-permute-start | bytes 1179656 | tf_op jit(solution)/shard_map/ppermute | solution.py:23
  288.2 50.6 %collective-permute-start.29 = (f32[8,24,512]{2,1,0:T(8,128)S(1)}, f32[8,24,512]{2,1,0:T(8,128)S(1)}, u32[]{:S(2)}, u32[]{:S(2)}) collective-permute-start(f32[8,24,512]{2,1,0:T(8,128)S(1)} %copy-done.27), channel_id=1, source_target_pairs={{0,1},{1,0},{2,3},{3,2},{4,5},{5,4},{6,7},{7,6},{8,9},{9,8},{10,11... | collective-permute-start | bytes 1179656 | tf_op jit(solution)/shard_map/ppermute | solution.py:23
  307.7 45.0 %collective-permute-start.30 = (f32[8,24,512]{2,1,0:T(8,128)S(1)}, f32[8,24,512]{2,1,0:T(8,128)S(1)}, u32[]{:S(2)}, u32[]{:S(2)}) collective-permute-start(f32[8,24,512]{2,1,0:T(8,128)S(1)} %copy-done.25), channel_id=1, source_target_pairs={{0,4},{1,5},{2,6},{3,7},{4,0},{5,1},{6,2},{7,3},{8,12},{9,13},{10,... | collective-permute-start | bytes 1179656 | tf_op jit(solution)/shard_map/ppermute | solution.py:23
  319.1 42.8 %collective-permute-start.19 = (f32[8,16,512]{2,1,0:T(8,128)S(1)}, f32[8,16,512]{2,1,0:T(8,128)S(1)}, u32[]{:S(2)}, u32[]{:S(2)}) collective-permute-start(f32[8,16,512]{2,1,0:T(8,128)S(1)} %copy-done.49), channel_id=1, source_target_pairs={{0,6},{1,7},{2,4},{3,5},{4,2},{5,3},{6,0},{7,1},{8,14},{9,15},{10,... | collective-permute-start | bytes 786440 | tf_op jit(solution)/shard_map/ppermute | solution.py:23
  329.0 37.2 %collective-permute-start.20 = (f32[8,16,512]{2,1,0:T(8,128)S(1)}, f32[8,16,512]{2,1,0:T(8,128)S(1)}, u32[]{:S(2)}, u32[]{:S(2)}) collective-permute-start(f32[8,16,512]{2,1,0:T(8,128)S(1)} %copy-done.47), channel_id=1, source_target_pairs={{0,2},{1,3},{2,0},{3,1},{4,6},{5,7},{6,4},{7,5},{8,10},{9,11},{10,... | collective-permute-start | bytes 786440 | tf_op jit(solution)/shard_map/ppermute | solution.py:23
  338.8 34.0 %collective-permute-start.21 = (f32[8,16,512]{2,1,0:T(8,128)S(1)}, f32[8,16,512]{2,1,0:T(8,128)S(1)}, u32[]{:S(2)}, u32[]{:S(2)}) collective-permute-start(f32[8,16,512]{2,1,0:T(8,128)S(1)} %copy-done.45), channel_id=1, source_target_pairs={{0,5},{1,4},{2,7},{3,6},{4,1},{5,0},{6,3},{7,2},{8,13},{9,12},{10,... | collective-permute-start | bytes 786440 | tf_op jit(solution)/shard_map/ppermute | solution.py:23
  338.8 34.0 %collective-permute-start.22 = (f32[8,16,512]{2,1,0:T(8,128)S(1)}, f32[8,16,512]{2,1,0:T(8,128)S(1)}, u32[]{:S(2)}, u32[]{:S(2)}) collective-permute-start(f32[8,16,512]{2,1,0:T(8,128)S(1)} %copy-done.43), channel_id=1, source_target_pairs={{0,1},{1,0},{2,3},{3,2},{4,5},{5,4},{6,7},{7,6},{8,9},{9,8},{10,11... | collective-permute-start | bytes 786440 | tf_op jit(solution)/shard_map/ppermute | solution.py:23
  352.7 28.1 %collective-permute-start.23 = (f32[8,16,512]{2,1,0:T(8,128)S(1)}, f32[8,16,512]{2,1,0:T(8,128)S(1)}, u32[]{:S(2)}, u32[]{:S(2)}) collective-permute-start(f32[8,16,512]{2,1,0:T(8,128)S(1)} %copy-done.41), channel_id=1, source_target_pairs={{0,4},{1,5},{2,6},{3,7},{4,0},{5,1},{6,2},{7,3},{8,12},{9,13},{10,... | collective-permute-start | bytes 786440 | tf_op jit(solution)/shard_map/ppermute | solution.py:23
  (78 other events, 1098.8 us)

commit v5 on v4

--- a/solution.py
+++ b/solution.py
@@ -25,9 +25,7 @@
 
 def partner_order(size):
     assert size & (size - 1) == 0
-    across, near = list(range(size // 2, size))[::-1], list(range(1, size // 2))[::-1]
-    order = [k for pair in zip(across, near + [None]) for k in pair if k is not None]
-    return order
+    return list(range(1, size))[::-1]
 
 
 def gate_table(owner_order, own_freqs, freqs, waveform, gate_index):
@@ -71,21 +69,15 @@
 SCALARS = pl.BlockSpec(memory_space=pltpu.SMEM)
 
 
-def pack_kernel(distances, own, first, lanes, place_ref, block_ref, models_ref, *refs):
-    outs, (held, in_sems, out_sems) = refs[: len(distances)], refs[len(distances) :]
-    spectra, rows = block_ref.shape[0], held.shape[2]
-    owned, members = models_ref.shape
+def pack_kernel(distances, own, first, place_ref, block_ref, *refs):
+    outs, (held, in_sems, out_sems) = refs[-len(distances) - 3 : -3], refs[-3:]
+    rows = held.shape[2]
     arrivals, departures = [], []
     for j, k in enumerate(distances):
         row = pl.multiple_of((place_ref[1] ^ k) * own + first, GROUP)
-        source, target = block_ref.at[:, pl.ds(row, rows)], held.at[j, pl.ds(0, spectra)]
-        arrivals.append(pltpu.make_async_copy(source, target, in_sems.at[j]))
+        arrivals.append(pltpu.make_async_copy(block_ref.at[:, pl.ds(row, rows)], held.at[j], in_sems.at[j]))
         departures.append(pltpu.make_async_copy(held.at[j], outs[j], out_sems.at[j]))
         arrivals[j].start()
-    for j in range(len(distances)):
-        for lane in range(lanes):
-            part = owned // lanes
-            held[j, spectra, pl.ds(0, part), pl.ds(lane * members, members)] = models_ref[pl.ds(lane * part, part), :]
     for arrival, departure in zip(arrivals, departures):
         arrival.wait()
         departure.start()
@@ -93,13 +85,13 @@
         departure.wait()
 
 
-def pack(place, block, models, distances, own, first, rows, lanes):
+def pack(place, block, after, distances, own, first, rows):
     spectra, _, cells = block.shape
     count = len(distances)
-    shape = (spectra + (lanes > 0), rows, cells)
-    return pl.pallas_call(
-        functools.partial(pack_kernel, distances, own, first, lanes),
-        in_specs=[SCALARS, HBM, pl.BlockSpec(memory_space=pltpu.VMEM)],
+    shape = (spectra, rows, cells)
+    return pl.pallas_call(
+        functools.partial(pack_kernel, distances, own, first),
+        in_specs=[SCALARS, HBM] + [HBM] * len(after),
         out_specs=[HBM] * count,
         out_shape=[jax.ShapeDtypeStruct(shape, jnp.float32)] * count,
         scratch_shapes=[
@@ -110,40 +102,31 @@
         compiler_params=params(48),
         cost_estimate=cost(0, 8 * count * spectra * rows * cells),
         name="pack",
-    )(place, block, models)
-
-
-def near_kernel(lanes, place_ref, cells_ref, models_ref, *refs):
-    riders, out_ref = refs[:-1], refs[-1]
-    owned, members = models_ref.shape
-    part = owned // lanes
-    out_ref[pl.ds(0, owned), :] = models_ref[...]
-    for j, r in enumerate(riders):
-        for lane in range(lanes):
-            out_ref[pl.ds((j + 1) * owned + lane * part, part), :] = r[
-                0, pl.ds(0, part), pl.ds(lane * members, members)
-            ]
-    block_cells = owned * (len(riders) + 1)
+    )(place, block, *after)
+
+
+def near_kernel(block_cells, place_ref, cells_ref, *refs):
+    parts, out_ref = refs[:-1], refs[-1]
+    row = 0
+    for part in parts:
+        out_ref[pl.ds(row, part.shape[0]), :] = part[...]
+        row += part.shape[0]
     home = cells_ref[...] // block_cells
     other = jnp.where(home == place_ref[0], -1, home).astype(jnp.float32)
     other = jnp.max(other, axis=1, keepdims=True)
-    out_ref[pl.ds(block_cells, GROUP), :] = jnp.broadcast_to(other, (GROUP, members))
-
-
-def near_models(place, cell_index, models, first, lanes):
-    owned, members = models.shape
-    slabs, rows, cells = first[0].shape
-    rider = pl.BlockSpec((1, rows, cells), lambda i: (slabs - 1, 0, 0))
-    return pl.pallas_call(
-        functools.partial(near_kernel, lanes),
-        grid=(1,),
-        in_specs=[SCALARS, whole(cell_index), whole(models)] + [rider] * len(first),
-        out_specs=pl.BlockSpec((owned * (len(first) + 1) + GROUP, members), lambda i: (0, 0)),
-        out_shape=jax.ShapeDtypeStruct((owned * (len(first) + 1) + GROUP, members), jnp.float32),
+    out_ref[pl.ds(block_cells, GROUP), :] = jnp.broadcast_to(other, (GROUP, out_ref.shape[1]))
+
+
+def near_models(place, cell_index, parts, block_cells):
+    return pl.pallas_call(
+        functools.partial(near_kernel, block_cells),
+        in_specs=[SCALARS] + [pl.BlockSpec(memory_space=pltpu.VMEM)] * (1 + len(parts)),
+        out_specs=pl.BlockSpec(memory_space=pltpu.VMEM),
+        out_shape=jax.ShapeDtypeStruct((block_cells + GROUP, parts[0].shape[1]), jnp.float32),
         compiler_params=params(16),
         cost_estimate=cost(0, 1 << 20),
         name="near_models",
-    )(place, cell_index, models, *first)
+    )(place, cell_index, *parts)
 
 
 def tile_models_kernel(owned, partners, place_ref, cells_ref, *refs):
@@ -358,13 +341,12 @@
     )(models, back)
 
 
-def chunk_groups(groups, riders):
-    if groups < 8:
+def chunk_groups(groups):
+    if groups < 16:
         return [1] * groups
-    first, last = max(groups // 8, riders), [groups // 8, groups // 16 or 1]
+    first, last = groups // 8, [groups * 3 // 16, groups // 16]
     rest = groups - first - sum(last)
-    middle = -(-rest // (groups // 4))
-    return [first] + [rest // middle + (i < rest % middle) for i in range(middle)] + last
+    return [first, rest - rest // 2, rest // 2] + last
 
 
 def body(sensitivity, models, observed, waveform, cell_index, gate_index):
@@ -382,22 +364,24 @@
     place = jnp.stack([lax.axis_index("tile"), lax.axis_index("freq")])
 
     block = sensitivity[0].reshape(spectra, soundings, cells)
-    lanes = cells // members if owned % (GROUP * (cells // members)) == 0 else 1
-    sizes = chunk_groups(own // GROUP, -(-owned // (lanes * GROUP)))
+    sizes = chunk_groups(own // GROUP)
     starts = [sum(sizes[:i]) for i in range(len(sizes))]
     distances = partner_order(owners)
     partners = [0] + distances
+    half = owners // 2
+    pair = jnp.concatenate([models, swap(models, "freq", half)])
+    parts_near = [pair] + [swap(pair, "freq", k) for k in range(1, half)]
+    slots = [k ^ j for k in range(half) for j in (0, half)]
     received = []
     for i, (start, size) in enumerate(zip(starts, sizes)):
-        pieces = pack(
-            place, block, models, distances, own, start * GROUP, size * GROUP, lanes if i == 0 else 0
-        )
+        after = received[i - 1][:1] if i else []
+        pieces = pack(place, block, after, distances, own, start * GROUP, size * GROUP)
         received.append([swap(p, "freq", k) for p, k in zip(pieces, distances)])
 
-    near = near_models(place, cell_index, models, received[0], lanes)
+    near = near_models(place, cell_index, parts_near, block_cells)
     blocks = [near] + [swap(near, "tile", k) for k in range(1, tiles)]
     borrowed = jnp.stack([b[block_cells, 0] for b in blocks]).astype(jnp.int32)
-    models_t = tile_models(place, cell_index, blocks, owned, partners)
+    models_t = tile_models(place, cell_index, blocks, owned, slots)
 
     order = place[1] ^ jnp.array(partners, jnp.int32)
     wide = wide_table(gate_table(order, own_freqs, freqs, waveform, gate_index).T)

time: 428 us -> 431 us (level)
  waiting for transfers between devices: 156 us -> 179 us
  local copies, waits for them, and re-layouts: 32.2 us -> 12.2 us
    ppermute x45 -> x42, waiting for transfers between devices: 147 us -> 169 us  [swap(): lax.ppermute(x, axis, [(i, i ^ k) for i in range(lax.axis_size(axis))])]
    unnamed x129 -> x54, local copies, waits for them, and re-layouts: 25.3 us -> 6.83 us
    ppermute x45 -> x42, starting transfers between devices: 148 us -> 150 us  [swap(): lax.ppermute(x, axis, [(i, i ^ k) for i in range(lax.axis_size(axis))])]
    pallas_call x6 -> x5, Pallas kernels: 50.8 us -> 48.8 us  [chunk_step(): pl.pallas_call(functools.partial(chunk_kernel, pieces, block_cells, last)...]
    pallas_call x7 -> x6, Pallas kernels: 16.3 us -> 16 us  [the longest x5 15.3 us: pack(): pl.pallas_call(functools.partial(pack_kernel, distances, own, first), in_...]
  transfers between devices with their start and end apart: 46 -> 43, of which waited for: 17 -> 15; matrix products, arithmetic and copies ran while one was open for 3% -> 2% of each run, Pallas kernels for 14% -> 14%
where the time goes in v5:
time: 431 us; the launch traced here: 430 us
  waiting for transfers between devices  179 us (42%)
  starting transfers between devices  154 us (36%)
  Pallas kernels  69 us (16%)
  local copies, waits for them, and re-layouts  12.2 us (3%)
  blocking collectives  9.82 us (2%)
  other arithmetic  4.85 us (1%)
    ppermute x42, waiting for transfers between devices, swap(): lax.ppermute(x, axis, [(i, i ^ k) for i in range(lax.axis_size(axis))])  169 us
    ppermute x42, starting transfers between devices, swap(): lax.ppermute(x, axis, [(i, i ^ k) for i in range(lax.axis_size(axis))])  150 us
    pallas_call x5, Pallas kernels, chunk_step(): pl.pallas_call(functools.partial(chunk_kernel, pieces, block_cells, last)...  48.8 us
    pallas_call x5, Pallas kernels, pack(): pl.pallas_call(functools.partial(pack_kernel, distances, own, first), in_...  15.3 us
    all_to_all x1, blocking collectives, body(): back = lax.all_to_all(step, both, split_axis=0, concat_axis=0, tiled=True)  9.82 us
    all_to_all x1, waiting for transfers between devices, body(): got = lax.all_to_all(sent, both, split_axis=0, concat_axis=0, tiled=True)  9.59 us
  transfers between devices with their start and end apart: 43, of which 15 were waited for; matrix products, arithmetic and copies ran while one was open for 2% of the time, Pallas kernels for 14%

profile of v5, /device:TPU:0, one launch (start us, length us, event | category | flops | bytes accessed | tf_op | source)
XLA Modules:
  0.0 430.3 jit_solution(18300033917641471335)
XLA Ops:
  2.8 6.0 %collective-permute-start.7 = (f32[8,16,512]{2,1,0:T(8,128)S(1)}, f32[8,16,512]{2,1,0:T(8,128)S(1)}, u32[]{:S(2)}, u32[]{:S(2)}) collective-permute-start(f32[8,16,512]{2,1,0:T(8,128)S(1)} %get-tuple-element.53), channel_id=1, source_target_pairs={{0,7},{1,6},{2,5},{3,4},{4,3},{5,2},{6,1},{7,0},{8,15},{9,14},{10,... | collective-permute-start | bytes 786440 | tf_op jit(solution)/shard_map/ppermute | solution.py:23
  16.1 4.0 pack.6
  21.8 4.7 %collective-permute-start.8 = (f32[8,40,512]{2,1,0:T(8,128)S(1)}, f32[8,40,512]{2,1,0:T(8,128)S(1)}, u32[]{:S(2)}, u32[]{:S(2)}) collective-permute-start(f32[8,40,512]{2,1,0:T(8,128)S(1)} %get-tuple-element.54), channel_id=1, source_target_pairs={{0,7},{1,6},{2,5},{3,4},{4,3},{5,2},{6,1},{7,0},{8,15},{9,14},{10,... | collective-permute-start | bytes 1966088 | tf_op jit(solution)/shard_map/ppermute | solution.py:23
  26.5 26.6 %collective-permute-done = f32[32,256]{1,0:T(8,128)S(1)} collective-permute-done((f32[32,256]{1,0:T(8,128)S(1)}, f32[32,256]{1,0:T(8,128)S(1)}, u32[]{:S(2)}, u32[]{:S(2)}) %collective-permute-start) | collective-permute-done | bytes 32800 | tf_op jit(solution)/shard_map/ppermute | solution.py:23
  53.2 8.3 %collective-permute-start.3 = (f32[64,256]{1,0:T(8,128)S(1)}, f32[64,256]{1,0:T(8,128)S(1)}, u32[]{:S(2)}, u32[]{:S(2)}) collective-permute-start(f32[64,256]{1,0:T(8,128)S(1)} %constant_dynamic-update-slice_fusion.refs_0_), channel_id=1, source_target_pairs={{0,3},{1,2},{2,1},{3,0},{4,7},{5,6},{6,5},{7,4},{8,11},{9,10},{10,... | collective-permute-start | bytes 196616 | tf_op jit(solution)/shard_map/ppermute | solution.py:23
  61.5 9.0 %collective-permute-done.3.refs_3_ = f32[64,256]{1,0:T(8,128)S(1)} collective-permute-done((f32[64,256]{1,0:T(8,128)S(1)}, f32[64,256]{1,0:T(8,128)S(1)}, u32[]{:S(2)}, u32[]{:S(2)}) %collective-permute-start.3) | collective-permute-done | bytes 65568 | tf_op jit(solution)/shard_map/ppermute | solution.py:23
  70.5 4.3 collective-permute-done.2.refs_2_
  79.0 7.0 %collective-permute-start.39 = (f32[8,16,512]{2,1,0:T(8,128)S(1)}, f32[8,16,512]{2,1,0:T(8,128)S(1)}, u32[]{:S(2)}, u32[]{:S(2)}) collective-permute-start(f32[8,16,512]{2,1,0:T(8,128)S(1)} %get-tuple-element.89), channel_id=1, source_target_pairs={{0,3},{1,2},{2,1},{3,0},{4,7},{5,6},{6,5},{7,4},{8,11},{9,10},{10,... | collective-permute-start | bytes 786440 | tf_op jit(solution)/shard_map/ppermute | solution.py:23
  89.8 3.4 collective-permute-done.39.refs_5_
  93.2 5.2 %collective-permute-done.40.refs_6_ = f32[8,16,512]{2,1,0:T(8,128)S(1)} collective-permute-done((f32[8,16,512]{2,1,0:T(8,128)S(1)}, f32[8,16,512]{2,1,0:T(8,128)S(1)}, u32[]{:S(2)}, u32[]{:S(2)}) %collective-permute-start.40) | collective-permute-done | bytes 262176 | tf_op jit(solution)/shard_map/ppermute | solution.py:23
  100.0 3.5 collective-permute-start.31
  103.7 3.5 pack.7
  118.9 44.3 %collective-permute-done.31.refs_3_ = f32[8,40,512]{2,1,0:T(8,128)} collective-permute-done((f32[8,40,512]{2,1,0:T(8,128)}, f32[8,40,512]{2,1,0:T(8,128)}, u32[]{:S(2)}, u32[]{:S(2)}) %collective-permute-start.31) | collective-permute-done | bytes 655392 | tf_op jit(solution)/shard_map/ppermute | solution.py:23
  163.9 26.4 %collective-permute-done.32.refs_4_ = f32[8,40,512]{2,1,0:T(8,128)S(1)} collective-permute-done((f32[8,40,512]{2,1,0:T(8,128)S(1)}, f32[8,40,512]{2,1,0:T(8,128)S(1)}, u32[]{:S(2)}, u32[]{:S(2)}) %collective-permute-start.32) | collective-permute-done | bytes 655392 | tf_op jit(solution)/shard_map/ppermute | solution.py:23
  195.3 3.8 collective-permute-start.26
  199.1 48.8 %collective-permute-start.27 = (f32[8,40,512]{2,1,0:T(8,128)}, f32[8,40,512]{2,1,0:T(8,128)}, u32[]{:S(2)}, u32[]{:S(2)}) collective-permute-start(f32[8,40,512]{2,1,0:T(8,128)} %get-tuple-element.77), channel_id=1, source_target_pairs={{0,3},{1,2},{2,1},{3,0},{4,7},{5,6},{6,5},{7,4},{8,11},{9,10},{10,... | collective-permute-start | bytes 1966088 | tf_op jit(solution)/shard_map/ppermute | solution.py:23
  252.1 3.5 collective-permute-start.10
  258.3 7.2 %chunk_step.5 = (f32[256,512]{1,0:T(8,128)}, f32[256,128]{1,0:T(8,128)S(1)}) custom-call(s32[2]{0:T(128)S(1)} %pad_add_fusion.place_ref, f32[8,1024,512]{2,1,0:T(8,128)} %bitcast.20, f32[8,16,512]{2,1,0:T(8,128)S(1)} %collective-permute-done.7.refs_0_.refs_1_, ...), custom_call_target="tpu_custom_call", output_to_operand_aliasing={{0}: (15, {}), {1}: (16, {})} | custom-call | flops 3221225472 | bytes 2097152 | tf_op jit(solution)/shard_map/chunk_step/pallas_call | solution.py:235
  265.5 18.5 %collective-permute-done.25.refs_3_ = f32[8,40,512]{2,1,0:T(8,128)} collective-permute-done((f32[8,40,512]{2,1,0:T(8,128)}, f32[8,40,512]{2,1,0:T(8,128)}, u32[]{:S(2)}, u32[]{:S(2)}) %collective-permute-start.25) | collective-permute-done | bytes 655392 | tf_op jit(solution)/shard_map/ppermute | solution.py:23
  284.5 12.6 %collective-permute-done.26.refs_4_ = f32[8,40,512]{2,1,0:T(8,128)} collective-permute-done((f32[8,40,512]{2,1,0:T(8,128)}, f32[8,40,512]{2,1,0:T(8,128)}, u32[]{:S(2)}, u32[]{:S(2)}) %collective-permute-start.26) | collective-permute-done | bytes 655392 | tf_op jit(solution)/shard_map/ppermute | solution.py:23
  299.6 29.4 %collective-permute-start.20 = (f32[8,24,512]{2,1,0:T(8,128)S(1)}, f32[8,24,512]{2,1,0:T(8,128)S(1)}, u32[]{:S(2)}, u32[]{:S(2)}) collective-permute-start(f32[8,24,512]{2,1,0:T(8,128)S(1)} %get-tuple-element.70), channel_id=1, source_target_pairs={{0,4},{1,5},{2,6},{3,7},{4,0},{5,1},{6,2},{7,3},{8,12},{9,13},{10,... | collective-permute-start | bytes 1179656 | tf_op jit(solution)/shard_map/ppermute | solution.py:23
  329.0 13.6 %chunk_step.6 = (f32[256,512]{1,0:T(8,128)}, f32[256,128]{1,0:T(8,128)S(1)}) custom-call(s32[2]{0:T(128)S(1)} %pad_add_fusion.place_ref, f32[8,1024,512]{2,1,0:T(8,128)} %bitcast.21, f32[8,40,512]{2,1,0:T(8,128)S(1)} %collective-permute-done.8.refs_0_.refs_1_, ...), custom_call_target="tpu_custom_call", output_to_operand_aliasing={{0}: (15, {}), {1}: (16, {})} | custom-call | flops 8053063680 | bytes 5242880 | tf_op jit(solution)/shard_map/chunk_step/pallas_call | solution.py:235
  345.5 3.4 collective-permute-start.23
  351.0 6.4 %collective-permute-done.20.refs_4_ = f32[8,24,512]{2,1,0:T(8,128)S(1)} collective-permute-done((f32[8,24,512]{2,1,0:T(8,128)S(1)}, f32[8,24,512]{2,1,0:T(8,128)S(1)}, u32[]{:S(2)}, u32[]{:S(2)}) %collective-permute-start.20) | collective-permute-done | bytes 393248 | tf_op jit(solution)/shard_map/ppermute | solution.py:23
  359.9 13.6 %chunk_step.7 = (f32[256,512]{1,0:T(8,128)}, f32[256,128]{1,0:T(8,128)S(1)}) custom-call(s32[2]{0:T(128)S(1)} %pad_add_fusion.place_ref, f32[8,1024,512]{2,1,0:T(8,128)} %bitcast.23, f32[8,40,512]{2,1,0:T(8,128)S(1)} %collective-permute-done.9.refs_0_.refs_1_, ...), custom_call_target="tpu_custom_call", output_to_operand_aliasing={{0}: (15, {}), {1}: (16, {})} | custom-call | flops 8053063680 | bytes 5242880 | tf_op jit(solution)/shard_map/chunk_step/pallas_call | solution.py:235
  373.6 4.5 %collective-permute-done.22.refs_6_ = f32[8,24,512]{2,1,0:T(8,128)S(1)} collective-permute-done((f32[8,24,512]{2,1,0:T(8,128)S(1)}, f32[8,24,512]{2,1,0:T(8,128)S(1)}, u32[]{:S(2)}, u32[]{:S(2)}) %collective-permute-start.22) | collective-permute-done | bytes 393248 | tf_op jit(solution)/shard_map/ppermute | solution.py:23
  380.2 3.0 collective-permute-start.15
  383.8 9.3 %chunk_step.8 = (f32[256,512]{1,0:T(8,128)}, f32[256,128]{1,0:T(8,128)S(1)}) custom-call(s32[2]{0:T(128)S(1)} %pad_add_fusion.place_ref, f32[8,1024,512]{2,1,0:T(8,128)} %bitcast.24, f32[8,24,512]{2,1,0:T(8,128)S(1)} %collective-permute-done.10.refs_0_.refs_1_, ...), custom_call_target="tpu_custom_call", output_to_operand_aliasing={{0}: (15, {}), {1}: (16, {})} | custom-call | flops 4831838208 | bytes 3145728 | tf_op jit(solution)/shard_map/chunk_step/pallas_call | solution.py:235
  393.1 5.1 %chunk_step.9 = (f32[256,512]{1,0:T(8,128)}, f32[256,128]{1,0:T(8,128)S(1)}) custom-call(s32[2]{0:T(128)S(1)} %pad_add_fusion.place_ref, f32[8,1024,512]{2,1,0:T(8,128)} %bitcast.25, f32[8,8,512]{2,1,0:T(8,128)S(1)} %collective-permute-done.11.refs_1_, ...), custom_call_target="tpu_custom_call", output_to_operand_aliasing={{0}: (15, {}), {1}: (16, {})} | custom-call | flops 1610612736 | bytes 1048576 | tf_op jit(solution)/shard_map/chunk_step/pallas_call | solution.py:235
  398.2 4.2 all-to-all-start
  409.2 9.6 %all-to-all-done.got_ref = f32[32,8,512]{2,1,0:T(8,128)S(1)} async-done(((f32[32,8,512]{2,1,0:T(8,128)}), f32[32,8,512]{2,1,0:T(8,128)S(1)}, u32[]{:S(2)}, u32[]{:S(2)}) %all-to-all-start) | async-done | bytes 524320 | tf_op jit(solution)/shard_map/all_to_all | solution.py:401
  419.6 9.8 %all_to_all.10.back_ref = f32[32,8,128]{2,1,0:T(8,128)S(1)} all-to-all(f32[32,8,128]{2,1,0:T(8,128)S(1)} %gradient_step.1), channel_id=1, replica_groups=mesh['tile'=4,'freq'=8] {'tile','freq'}, dimensions={0} | all-to-all | bytes 262144 | tf_op jit(solution)/shard_map/all_to_all | solution.py:404
  (145 shorter events, 66.9 us)
Async XLA Ops:
  8.9 44.3 %collective-permute-start = (f32[32,256]{1,0:T(8,128)S(1)}, f32[32,256]{1,0:T(8,128)S(1)}, u32[]{:S(2)}, u32[]{:S(2)}) collective-permute-start(f32[32,256]{1,0:T(8,128)S(1)} %copy-done.2), channel_id=1, source_target_pairs={{0,4},{1,5},{2,6},{3,7},{4,0},{5,1},{6,2},{7,3},{8,12},{9,13},{10,... | collective-permute-start | bytes 98312 | tf_op jit(solution)/shard_map/ppermute | solution.py:23
  8.9 77.2 %collective-permute-start.36 = (f32[8,16,512]{2,1,0:T(8,128)S(1)}, f32[8,16,512]{2,1,0:T(8,128)S(1)}, u32[]{:S(2)}, u32[]{:S(2)}) collective-permute-start(f32[8,16,512]{2,1,0:T(8,128)S(1)} %get-tuple-element.86), channel_id=1, source_target_pairs={{0,6},{1,7},{2,4},{3,5},{4,2},{5,3},{6,0},{7,1},{8,14},{9,15},{10,... | collective-permute-start | bytes 786440 | tf_op jit(solution)/shard_map/ppermute | solution.py:23
  10.8 75.3 %collective-permute-start.37 = (f32[8,16,512]{2,1,0:T(8,128)S(1)}, f32[8,16,512]{2,1,0:T(8,128)S(1)}, u32[]{:S(2)}, u32[]{:S(2)}) collective-permute-start(f32[8,16,512]{2,1,0:T(8,128)S(1)} %get-tuple-element.87), channel_id=1, source_target_pairs={{0,5},{1,4},{2,7},{3,6},{4,1},{5,0},{6,3},{7,2},{8,13},{9,12},{10,... | collective-permute-start | bytes 786440 | tf_op jit(solution)/shard_map/ppermute | solution.py:23
  11.8 74.9 %collective-permute-start.38 = (f32[8,16,512]{2,1,0:T(8,128)S(1)}, f32[8,16,512]{2,1,0:T(8,128)S(1)}, u32[]{:S(2)}, u32[]{:S(2)}) collective-permute-start(f32[8,16,512]{2,1,0:T(8,128)S(1)} %get-tuple-element.88), channel_id=1, source_target_pairs={{0,4},{1,5},{2,6},{3,7},{4,0},{5,1},{6,2},{7,3},{8,12},{9,13},{10,... | collective-permute-start | bytes 786440 | tf_op jit(solution)/shard_map/ppermute | solution.py:23
  21.8 78.1 %collective-permute-start.8 = (f32[8,40,512]{2,1,0:T(8,128)S(1)}, f32[8,40,512]{2,1,0:T(8,128)S(1)}, u32[]{:S(2)}, u32[]{:S(2)}) collective-permute-start(f32[8,40,512]{2,1,0:T(8,128)S(1)} %get-tuple-element.54), channel_id=1, source_target_pairs={{0,7},{1,6},{2,5},{3,4},{4,3},{5,2},{6,1},{7,0},{8,15},{9,14},{10,... | collective-permute-start | bytes 1966088 | tf_op jit(solution)/shard_map/ppermute | solution.py:23
  53.2 17.3 %collective-permute-start.3 = (f32[64,256]{1,0:T(8,128)S(1)}, f32[64,256]{1,0:T(8,128)S(1)}, u32[]{:S(2)}, u32[]{:S(2)}) collective-permute-start(f32[64,256]{1,0:T(8,128)S(1)} %constant_dynamic-update-slice_fusion.refs_0_), channel_id=1, source_target_pairs={{0,3},{1,2},{2,1},{3,0},{4,7},{5,6},{6,5},{7,4},{8,11},{9,10},{10,... | collective-permute-start | bytes 196616 | tf_op jit(solution)/shard_map/ppermute | solution.py:23
  86.7 28.9 %collective-permute-start.30 = (f32[8,40,512]{2,1,0:T(8,128)}, f32[8,40,512]{2,1,0:T(8,128)}, u32[]{:S(2)}, u32[]{:S(2)}) collective-permute-start(f32[8,40,512]{2,1,0:T(8,128)} %get-tuple-element.80), channel_id=1, source_target_pairs={{0,6},{1,7},{2,4},{3,5},{4,2},{5,3},{6,0},{7,1},{8,14},{9,15},{10,... | collective-permute-start | bytes 1966088 | tf_op jit(solution)/shard_map/ppermute | solution.py:23
  93.2 15.7 %collective-permute-start.6 = (f32[264,256]{1,0:T(8,128)S(1)}, f32[264,256]{1,0:T(8,128)S(1)}, u32[]{:S(2)}, u32[]{:S(2)}) collective-permute-start(f32[264,256]{1,0:T(8,128)S(1)} %near_models.1.refs_0_), channel_id=1, source_target_pairs={{0,24},{8,16},{16,8},{24,0},{1,25},{9,17},{17,9},{25,1},{2,26},{10... | collective-permute-start | bytes 811016 | tf_op jit(solution)/shard_map/ppermute | solution.py:23
  100.0 63.2 %collective-permute-start.31 = (f32[8,40,512]{2,1,0:T(8,128)}, f32[8,40,512]{2,1,0:T(8,128)}, u32[]{:S(2)}, u32[]{:S(2)}) collective-permute-start(f32[8,40,512]{2,1,0:T(8,128)} %get-tuple-element.81), channel_id=1, source_target_pairs={{0,5},{1,4},{2,7},{3,6},{4,1},{5,0},{6,3},{7,2},{8,13},{9,12},{10,... | collective-permute-start | bytes 1966088 | tf_op jit(solution)/shard_map/ppermute | solution.py:23
  109.7 80.5 %collective-permute-start.32 = (f32[8,40,512]{2,1,0:T(8,128)S(1)}, f32[8,40,512]{2,1,0:T(8,128)S(1)}, u32[]{:S(2)}, u32[]{:S(2)}) collective-permute-start(f32[8,40,512]{2,1,0:T(8,128)S(1)} %copy-done.17), channel_id=1, source_target_pairs={{0,4},{1,5},{2,6},{3,7},{4,0},{5,1},{6,2},{7,3},{8,12},{9,13},{10,... | collective-permute-start | bytes 1966088 | tf_op jit(solution)/shard_map/ppermute | solution.py:23
  109.7 83.8 %collective-permute-start.33 = (f32[8,40,512]{2,1,0:T(8,128)S(1)}, f32[8,40,512]{2,1,0:T(8,128)S(1)}, u32[]{:S(2)}, u32[]{:S(2)}) collective-permute-start(f32[8,40,512]{2,1,0:T(8,128)S(1)} %copy-done.13), channel_id=1, source_target_pairs={{0,3},{1,2},{2,1},{3,0},{4,7},{5,6},{6,5},{7,4},{8,11},{9,10},{10,... | collective-permute-start | bytes 1966088 | tf_op jit(solution)/shard_map/ppermute | solution.py:23
  112.5 81.9 %collective-permute-start.34 = (f32[8,40,512]{2,1,0:T(8,128)S(1)}, f32[8,40,512]{2,1,0:T(8,128)S(1)}, u32[]{:S(2)}, u32[]{:S(2)}) collective-permute-start(f32[8,40,512]{2,1,0:T(8,128)S(1)} %copy-done.9), channel_id=1, source_target_pairs={{0,2},{1,3},{2,0},{3,1},{4,6},{5,7},{6,4},{7,5},{8,10},{9,11},{10,... | collective-permute-start | bytes 1966088 | tf_op jit(solution)/shard_map/ppermute | solution.py:23
  115.6 83.5 %collective-permute-start.9 = (f32[8,40,512]{2,1,0:T(8,128)S(1)}, f32[8,40,512]{2,1,0:T(8,128)S(1)}, u32[]{:S(2)}, u32[]{:S(2)}) collective-permute-start(f32[8,40,512]{2,1,0:T(8,128)S(1)} %get-tuple-element.55), channel_id=1, source_target_pairs={{0,7},{1,6},{2,5},{3,4},{4,3},{5,2},{6,1},{7,0},{8,15},{9,14},{10,... | collective-permute-start | bytes 1966088 | tf_op jit(solution)/shard_map/ppermute | solution.py:23
  163.2 89.0 %collective-permute-start.35 = (f32[8,40,512]{2,1,0:T(8,128)}, f32[8,40,512]{2,1,0:T(8,128)}, u32[]{:S(2)}, u32[]{:S(2)}) collective-permute-start(f32[8,40,512]{2,1,0:T(8,128)} %get-tuple-element.85), channel_id=1, source_target_pairs={{0,1},{1,0},{2,3},{3,2},{4,5},{5,4},{6,7},{7,6},{8,9},{9,8},{10,11... | collective-permute-start | bytes 1966088 | tf_op jit(solution)/shard_map/ppermute | solution.py:23
  191.1 74.4 %collective-permute-start.24 = (f32[8,40,512]{2,1,0:T(8,128)}, f32[8,40,512]{2,1,0:T(8,128)}, u32[]{:S(2)}, u32[]{:S(2)}) collective-permute-start(f32[8,40,512]{2,1,0:T(8,128)} %get-tuple-element.74), channel_id=1, source_target_pairs={{0,6},{1,7},{2,4},{3,5},{4,2},{5,3},{6,0},{7,1},{8,14},{9,15},{10,... | collective-permute-start | bytes 1966088 | tf_op jit(solution)/shard_map/ppermute | solution.py:23
  194.4 89.6 %collective-permute-start.25 = (f32[8,40,512]{2,1,0:T(8,128)}, f32[8,40,512]{2,1,0:T(8,128)}, u32[]{:S(2)}, u32[]{:S(2)}) collective-permute-start(f32[8,40,512]{2,1,0:T(8,128)} %get-tuple-element.75), channel_id=1, source_target_pairs={{0,5},{1,4},{2,7},{3,6},{4,1},{5,0},{6,3},{7,2},{8,13},{9,12},{10,... | collective-permute-start | bytes 1966088 | tf_op jit(solution)/shard_map/ppermute | solution.py:23
  195.3 101.8 %collective-permute-start.26 = (f32[8,40,512]{2,1,0:T(8,128)}, f32[8,40,512]{2,1,0:T(8,128)}, u32[]{:S(2)}, u32[]{:S(2)}) collective-permute-start(f32[8,40,512]{2,1,0:T(8,128)} %get-tuple-element.76), channel_id=1, source_target_pairs={{0,4},{1,5},{2,6},{3,7},{4,0},{5,1},{6,2},{7,3},{8,12},{9,13},{10,... | collective-permute-start | bytes 1966088 | tf_op jit(solution)/shard_map/ppermute | solution.py:23
  199.1 100.4 %collective-permute-start.27 = (f32[8,40,512]{2,1,0:T(8,128)}, f32[8,40,512]{2,1,0:T(8,128)}, u32[]{:S(2)}, u32[]{:S(2)}) collective-permute-start(f32[8,40,512]{2,1,0:T(8,128)} %get-tuple-element.77), channel_id=1, source_target_pairs={{0,3},{1,2},{2,1},{3,0},{4,7},{5,6},{6,5},{7,4},{8,11},{9,10},{10,... | collective-permute-start | bytes 1966088 | tf_op jit(solution)/shard_map/ppermute | solution.py:23
  252.1 47.4 %collective-permute-start.10 = (f32[8,24,512]{2,1,0:T(8,128)S(1)}, f32[8,24,512]{2,1,0:T(8,128)S(1)}, u32[]{:S(2)}, u32[]{:S(2)}) collective-permute-start(f32[8,24,512]{2,1,0:T(8,128)S(1)} %get-tuple-element.56), channel_id=1, source_target_pairs={{0,7},{1,6},{2,5},{3,4},{4,3},{5,2},{6,1},{7,0},{8,15},{9,14},{10,... | collective-permute-start | bytes 1179656 | tf_op jit(solution)/shard_map/ppermute | solution.py:23
  265.5 79.8 %collective-permute-start.28 = (f32[8,40,512]{2,1,0:T(8,128)S(1)}, f32[8,40,512]{2,1,0:T(8,128)S(1)}, u32[]{:S(2)}, u32[]{:S(2)}) collective-permute-start(f32[8,40,512]{2,1,0:T(8,128)S(1)} %copy-done.7), channel_id=1, source_target_pairs={{0,2},{1,3},{2,0},{3,1},{4,6},{5,7},{6,4},{7,5},{8,10},{9,11},{10,... | collective-permute-start | bytes 1966088 | tf_op jit(solution)/shard_map/ppermute | solution.py:23
  284.0 61.4 %collective-permute-start.29 = (f32[8,40,512]{2,1,0:T(8,128)S(1)}, f32[8,40,512]{2,1,0:T(8,128)S(1)}, u32[]{:S(2)}, u32[]{:S(2)}) collective-permute-start(f32[8,40,512]{2,1,0:T(8,128)S(1)} %copy-done.5), channel_id=1, source_target_pairs={{0,1},{1,0},{2,3},{3,2},{4,5},{5,4},{6,7},{7,6},{8,9},{9,8},{10,11... | collective-permute-start | bytes 1966088 | tf_op jit(solution)/shard_map/ppermute | solution.py:23
  297.1 48.4 %collective-permute-start.18 = (f32[8,24,512]{2,1,0:T(8,128)S(1)}, f32[8,24,512]{2,1,0:T(8,128)S(1)}, u32[]{:S(2)}, u32[]{:S(2)}) collective-permute-start(f32[8,24,512]{2,1,0:T(8,128)S(1)} %get-tuple-element.68), channel_id=1, source_target_pairs={{0,6},{1,7},{2,4},{3,5},{4,2},{5,3},{6,0},{7,1},{8,14},{9,15},{10,... | collective-permute-start | bytes 1179656 | tf_op jit(solution)/shard_map/ppermute | solution.py:23
  299.6 49.3 %collective-permute-start.19 = (f32[8,24,512]{2,1,0:T(8,128)S(1)}, f32[8,24,512]{2,1,0:T(8,128)S(1)}, u32[]{:S(2)}, u32[]{:S(2)}) collective-permute-start(f32[8,24,512]{2,1,0:T(8,128)S(1)} %get-tuple-element.69), channel_id=1, source_target_pairs={{0,5},{1,4},{2,7},{3,6},{4,1},{5,0},{6,3},{7,2},{8,13},{9,12},{10,... | collective-permute-start | bytes 1179656 | tf_op jit(solution)/shard_map/ppermute | solution.py:23
  299.6 57.9 %collective-permute-start.20 = (f32[8,24,512]{2,1,0:T(8,128)S(1)}, f32[8,24,512]{2,1,0:T(8,128)S(1)}, u32[]{:S(2)}, u32[]{:S(2)}) collective-permute-start(f32[8,24,512]{2,1,0:T(8,128)S(1)} %get-tuple-element.70), channel_id=1, source_target_pairs={{0,4},{1,5},{2,6},{3,7},{4,0},{5,1},{6,2},{7,3},{8,12},{9,13},{10,... | collective-permute-start | bytes 1179656 | tf_op jit(solution)/shard_map/ppermute | solution.py:23
  345.3 28.2 %collective-permute-start.21 = (f32[8,24,512]{2,1,0:T(8,128)S(1)}, f32[8,24,512]{2,1,0:T(8,128)S(1)}, u32[]{:S(2)}, u32[]{:S(2)}) collective-permute-start(f32[8,24,512]{2,1,0:T(8,128)S(1)} %get-tuple-element.71), channel_id=1, source_target_pairs={{0,3},{1,2},{2,1},{3,0},{4,7},{5,6},{6,5},{7,4},{8,11},{9,10},{10,... | collective-permute-start | bytes 1179656 | tf_op jit(solution)/shard_map/ppermute | solution.py:23
  345.4 32.6 %collective-permute-start.22 = (f32[8,24,512]{2,1,0:T(8,128)S(1)}, f32[8,24,512]{2,1,0:T(8,128)S(1)}, u32[]{:S(2)}, u32[]{:S(2)}) collective-permute-start(f32[8,24,512]{2,1,0:T(8,128)S(1)} %get-tuple-element.72), channel_id=1, source_target_pairs={{0,2},{1,3},{2,0},{3,1},{4,6},{5,7},{6,4},{7,5},{8,10},{9,11},{10,... | collective-permute-start | bytes 1179656 | tf_op jit(solution)/shard_map/ppermute | solution.py:23
  345.5 34.7 %collective-permute-start.23 = (f32[8,24,512]{2,1,0:T(8,128)S(1)}, f32[8,24,512]{2,1,0:T(8,128)S(1)}, u32[]{:S(2)}, u32[]{:S(2)}) collective-permute-start(f32[8,24,512]{2,1,0:T(8,128)S(1)} %get-tuple-element.73), channel_id=1, source_target_pairs={{0,1},{1,0},{2,3},{3,2},{4,5},{5,4},{6,7},{7,6},{8,9},{9,8},{10,11... | collective-permute-start | bytes 1179656 | tf_op jit(solution)/shard_map/ppermute | solution.py:23
  348.9 34.3 %collective-permute-start.11 = (f32[8,8,512]{2,1,0:T(8,128)S(1)}, f32[8,8,512]{2,1,0:T(8,128)S(1)}, u32[]{:S(2)}, u32[]{:S(2)}) collective-permute-start(f32[8,8,512]{2,1,0:T(8,128)S(1)} %get-tuple-element.57), channel_id=1, source_target_pairs={{0,7},{1,6},{2,5},{3,4},{4,3},{5,2},{6,1},{7,0},{8,15},{9,14},{10,... | collective-permute-start | bytes 393224 | tf_op jit(solution)/shard_map/ppermute | solution.py:23
  357.4 25.8 %collective-permute-start.12 = (f32[8,8,512]{2,1,0:T(8,128)S(1)}, f32[8,8,512]{2,1,0:T(8,128)S(1)}, u32[]{:S(2)}, u32[]{:S(2)}) collective-permute-start(f32[8,8,512]{2,1,0:T(8,128)S(1)} %get-tuple-element.58), channel_id=1, source_target_pairs={{0,6},{1,7},{2,4},{3,5},{4,2},{5,3},{6,0},{7,1},{8,14},{9,15},{10,... | collective-permute-start | bytes 393224 | tf_op jit(solution)/shard_map/ppermute | solution.py:23
  373.6 19.6 %collective-permute-start.13 = (f32[8,8,512]{2,1,0:T(8,128)S(1)}, f32[8,8,512]{2,1,0:T(8,128)S(1)}, u32[]{:S(2)}, u32[]{:S(2)}) collective-permute-start(f32[8,8,512]{2,1,0:T(8,128)S(1)} %get-tuple-element.59), channel_id=1, source_target_pairs={{0,5},{1,4},{2,7},{3,6},{4,1},{5,0},{6,3},{7,2},{8,13},{9,12},{10,... | collective-permute-start | bytes 393224 | tf_op jit(solution)/shard_map/ppermute | solution.py:23
  378.1 15.1 %collective-permute-start.14 = (f32[8,8,512]{2,1,0:T(8,128)S(1)}, f32[8,8,512]{2,1,0:T(8,128)S(1)}, u32[]{:S(2)}, u32[]{:S(2)}) collective-permute-start(f32[8,8,512]{2,1,0:T(8,128)S(1)} %get-tuple-element.60), channel_id=1, source_target_pairs={{0,4},{1,5},{2,6},{3,7},{4,0},{5,1},{6,2},{7,3},{8,12},{9,13},{10,... | collective-permute-start | bytes 393224 | tf_op jit(solution)/shard_map/ppermute | solution.py:23
  398.2 20.5 %all-to-all-start = ((f32[32,8,512]{2,1,0:T(8,128)}), f32[32,8,512]{2,1,0:T(8,128)S(1)}, u32[]{:S(2)}, u32[]{:S(2)}) async-start(f32[32,8,512]{2,1,0:T(8,128)} %bitcast.11), calls=%async_computation | async-start | bytes 1048576 | tf_op jit(solution)/shard_map/all_to_all | solution.py:401
  (37 other events, 837.4 us)

commit v6 on v4

--- a/solution.py
+++ b/solution.py
@@ -17,17 +17,6 @@
 
 NN = (((1,), (0,)), ((), ()))
 NT = (((1,), (1,)), ((), ()))
-
-
-def swap(x, axis, k):
-    return lax.ppermute(x, axis, [(i, i ^ k) for i in range(lax.axis_size(axis))])
-
-
-def partner_order(size):
-    assert size & (size - 1) == 0
-    across, near = list(range(size // 2, size))[::-1], list(range(1, size // 2))[::-1]
-    order = [k for pair in zip(across, near + [None]) for k in pair if k is not None]
-    return order
 
 
 def gate_table(owner_order, own_freqs, freqs, waveform, gate_index):
@@ -71,18 +60,20 @@
 SCALARS = pl.BlockSpec(memory_space=pltpu.SMEM)
 
 
-def pack_kernel(distances, own, first, lanes, place_ref, block_ref, models_ref, *refs):
-    outs, (held, in_sems, out_sems) = refs[: len(distances)], refs[len(distances) :]
-    spectra, rows = block_ref.shape[0], held.shape[2]
+def pack_kernel(owners_of, own, first, rows, lanes, joined, place_ref, block_ref, models_ref, *refs):
+    held, in_sems, out_sems = refs[-3:]
+    count = held.shape[0]
+    outs = [refs[-4].at[j] for j in range(count)] if joined else refs[-3 - count : -3]
+    spectra = block_ref.shape[0]
     owned, members = models_ref.shape
     arrivals, departures = [], []
-    for j, k in enumerate(distances):
-        row = pl.multiple_of((place_ref[1] ^ k) * own + first, GROUP)
+    for j in range(count):
+        row = pl.multiple_of(owners_of(place_ref[1], j) * own + first, GROUP)
         source, target = block_ref.at[:, pl.ds(row, rows)], held.at[j, pl.ds(0, spectra)]
         arrivals.append(pltpu.make_async_copy(source, target, in_sems.at[j]))
         departures.append(pltpu.make_async_copy(held.at[j], outs[j], out_sems.at[j]))
         arrivals[j].start()
-    for j in range(len(distances)):
+    for j in range(count):
         for lane in range(lanes):
             part = owned // lanes
             held[j, spectra, pl.ds(0, part), pl.ds(lane * members, members)] = models_ref[pl.ds(lane * part, part), :]
@@ -93,15 +84,18 @@
         departure.wait()
 
 
-def pack(place, block, models, distances, own, first, rows, lanes):
+def pack(place, block, models, after, count, owners_of, own, first, rows, lanes, joined):
     spectra, _, cells = block.shape
-    count = len(distances)
     shape = (spectra + (lanes > 0), rows, cells)
-    return pl.pallas_call(
-        functools.partial(pack_kernel, distances, own, first, lanes),
-        in_specs=[SCALARS, HBM, pl.BlockSpec(memory_space=pltpu.VMEM)],
-        out_specs=[HBM] * count,
-        out_shape=[jax.ShapeDtypeStruct(shape, jnp.float32)] * count,
+    if joined:
+        out_shape = [jax.ShapeDtypeStruct((count, *shape), jnp.float32)]
+    else:
+        out_shape = [jax.ShapeDtypeStruct(shape, jnp.float32)] * count
+    return pl.pallas_call(
+        functools.partial(pack_kernel, owners_of, own, first, rows, lanes, joined),
+        in_specs=[SCALARS, HBM, pl.BlockSpec(memory_space=pltpu.VMEM)] + [HBM] * len(after),
+        out_specs=[HBM] * len(out_shape),
+        out_shape=out_shape,
         scratch_shapes=[
             pltpu.VMEM((count, *shape), jnp.float32),
             pltpu.SemaphoreType.DMA((count,)),
@@ -109,51 +103,50 @@
         ],
         compiler_params=params(48),
         cost_estimate=cost(0, 8 * count * spectra * rows * cells),
-        name="pack",
-    )(place, block, models)
-
-
-def near_kernel(lanes, place_ref, cells_ref, models_ref, *refs):
+        name="pack_near" if joined else "pack_across",
+    )(place, block, models, *after)
+
+
+def block_kernel(block_cells, owned, lanes, place_ref, cells_ref, near_ref, *refs):
     riders, out_ref = refs[:-1], refs[-1]
-    owned, members = models_ref.shape
+    members = out_ref.shape[1]
     part = owned // lanes
-    out_ref[pl.ds(0, owned), :] = models_ref[...]
-    for j, r in enumerate(riders):
+    sources = [near_ref.at[r, 0] for r in range(near_ref.shape[0])] + [r.at[0] for r in riders]
+    for n, source in enumerate(sources):
         for lane in range(lanes):
-            out_ref[pl.ds((j + 1) * owned + lane * part, part), :] = r[
-                0, pl.ds(0, part), pl.ds(lane * members, members)
-            ]
-    block_cells = owned * (len(riders) + 1)
+            out_ref[pl.ds(n * owned + lane * part, part), :] = source[pl.ds(0, part), pl.ds(lane * members, members)]
     home = cells_ref[...] // block_cells
     other = jnp.where(home == place_ref[0], -1, home).astype(jnp.float32)
     other = jnp.max(other, axis=1, keepdims=True)
     out_ref[pl.ds(block_cells, GROUP), :] = jnp.broadcast_to(other, (GROUP, members))
 
 
-def near_models(place, cell_index, models, first, lanes):
-    owned, members = models.shape
-    slabs, rows, cells = first[0].shape
-    rider = pl.BlockSpec((1, rows, cells), lambda i: (slabs - 1, 0, 0))
-    return pl.pallas_call(
-        functools.partial(near_kernel, lanes),
+def block_models(place, cell_index, near, across, block_cells, owned, members, lanes):
+    count, slabs, near_rows, cells = near.shape
+    rows = across[0].shape[1]
+    out = jax.ShapeDtypeStruct((block_cells + GROUP, members), jnp.float32)
+    return pl.pallas_call(
+        functools.partial(block_kernel, block_cells, owned, lanes),
         grid=(1,),
-        in_specs=[SCALARS, whole(cell_index), whole(models)] + [rider] * len(first),
-        out_specs=pl.BlockSpec((owned * (len(first) + 1) + GROUP, members), lambda i: (0, 0)),
-        out_shape=jax.ShapeDtypeStruct((owned * (len(first) + 1) + GROUP, members), jnp.float32),
+        in_specs=[SCALARS, whole(cell_index), pl.BlockSpec((count, 1, rows, cells), lambda i: (0, slabs - 1, 0, 0))]
+        + [pl.BlockSpec((1, rows, cells), lambda i: (slabs - 1, 0, 0))] * len(across),
+        out_specs=whole(out),
+        out_shape=out,
         compiler_params=params(16),
         cost_estimate=cost(0, 1 << 20),
-        name="near_models",
-    )(place, cell_index, models, *first)
-
-
-def tile_models_kernel(owned, partners, place_ref, cells_ref, *refs):
+        name="block_models",
+    )(place, cell_index, near, *across)
+
+
+def tile_models_kernel(owned, across, place_ref, cells_ref, *refs):
     tile_refs, (high_ref, low_ref) = refs[:-2], refs[-2:]
-    block_cells = owned * len(partners)
+    half = len(across)
+    block_cells = owned * 2 * half
     cells = cells_ref[...]
-    distance = (cells // owned % len(partners)) ^ place_ref[1]
-    slot = jnp.zeros_like(cells)
-    for n, k in enumerate(partners):
-        slot = jnp.where(distance == k, n, slot)
+    owner = cells // owned % (2 * half)
+    slot = owner % half
+    for n, k in enumerate(across):
+        slot = jnp.where(owner ^ place_ref[1] == k, half + n, slot)
     spot = slot * owned + cells % owned
     away = (cells // block_cells) ^ place_ref[0]
     high, low = None, None
@@ -168,10 +161,10 @@
     low_ref[...] = low.astype(jnp.bfloat16)
 
 
-def tile_models(place, cell_index, tiles, owned, partners):
+def tile_models(place, cell_index, tiles, owned, across):
     shape = jax.ShapeDtypeStruct((tiles[0].shape[1], cell_index.shape[1]), jnp.bfloat16)
     return pl.pallas_call(
-        functools.partial(tile_models_kernel, owned, partners),
+        functools.partial(tile_models_kernel, owned, across),
         in_specs=[SCALARS] + [pl.BlockSpec(memory_space=pltpu.VMEM)] * (1 + len(tiles)),
         out_specs=[pl.BlockSpec(memory_space=pltpu.VMEM)] * 2,
         out_shape=[shape] * 2,
@@ -218,7 +211,7 @@
         terms_ref[...] = terms_in[...]
         square_ref[...] = square_in[...]
 
-    sens = [split(r[...].reshape(r.shape[0] * r.shape[1], r.shape[2])) for r in sens_refs]
+    sens = [split(r[...].reshape(-1, r.shape[-1])) for r in sens_refs]
     sens = tuple(jnp.concatenate([s[i] for s in sens], axis=0) for i in range(2))
     gates = (gate_h[...], gate_l[...])
     predicted = three_pass((model_h[...], model_l[...]), sens, NT)
@@ -243,37 +236,31 @@
             terms_ref[...] = dot(high, pick) + (dot(middle, pick) + dot(low, pick))
 
 
-def chunk_step(place, block, sens, first, models_t, gates, obs, cell_index, terms, square, block_cells, last):
-    spectra, soundings, cells = block.shape
-    rows = sens[0].shape[1]
-    pieces = len(sens) + 1
+def chunk_step(place, near, near_first, across, first, models_t, gates, obs, cell_index, terms, square, block_cells, last):
+    half, rows, cells = near.shape[0], across[0].shape[1], across[0].shape[2]
     members = terms.shape[0]
-    own_groups = soundings // (pieces * GROUP)
+    spectra = gates[0].shape[0] // (2 * half * GROUP)
+    pieces = 1 + len(across)
+    work = 2 * half * spectra * rows * cells
     return pl.pallas_call(
         functools.partial(chunk_kernel, pieces, block_cells, last),
-        grid_spec=pltpu.PrefetchScalarGridSpec(
-            num_scalar_prefetch=1,
-            grid=(rows // GROUP,),
-            in_specs=[
-                pl.BlockSpec((spectra, GROUP, cells), lambda i, place: (0, place[1] * own_groups + first + i, 0))
-            ]
-            + [pl.BlockSpec((spectra, GROUP, cells), lambda i, place: (0, i, 0))] * len(sens)
-            + [whole(a) for a in (*models_t, *gates)]
-            + [pl.BlockSpec((1, 1, obs.shape[2]), lambda i, place: (first + i, 0, 0)), whole(cell_index)]
-            + [whole(terms), whole(square)],
-            out_specs=[whole(terms), whole(square)],
-        ),
+        grid=(rows // GROUP,),
+        in_specs=[SCALARS]
+        + [pl.BlockSpec((half, spectra, GROUP, cells), lambda i: (0, 0, near_first + i, 0))]
+        + [pl.BlockSpec((spectra, GROUP, cells), lambda i: (0, i, 0))] * len(across)
+        + [whole(a) for a in (*models_t, *gates)]
+        + [pl.BlockSpec((1, 1, obs.shape[2]), lambda i: (first + i, 0, 0)), whole(cell_index)]
+        + [whole(terms), whole(square)],
+        out_specs=[whole(terms), whole(square)],
         out_shape=[
             jax.ShapeDtypeStruct(terms.shape, jnp.float32),
             jax.ShapeDtypeStruct(square.shape, jnp.float32),
         ],
         input_output_aliases={pieces + 7: 0, pieces + 8: 1},
         compiler_params=params(40),
-        cost_estimate=cost(
-            12 * pieces * spectra * rows * cells * members * 2, 4 * pieces * spectra * rows * cells
-        ),
+        cost_estimate=cost(12 * work * members * 2, 4 * work),
         name="chunk_step",
-    )(place, block, *sens, *models_t, *gates, obs, cell_index, terms, square)
+    )(place, near, *across, *models_t, *gates, obs, cell_index, terms, square)
 
 
 def exact_dot(a, b, dims):
@@ -358,13 +345,12 @@
     )(models, back)
 
 
-def chunk_groups(groups, riders):
-    if groups < 8:
+def chunk_groups(groups):
+    if groups < 16:
         return [1] * groups
-    first, last = max(groups // 8, riders), [groups // 8, groups // 16 or 1]
-    rest = groups - first - sum(last)
-    middle = -(-rest // (groups // 4))
-    return [first] + [rest // middle + (i < rest % middle) for i in range(middle)] + last
+    ends = [groups // 8, groups * 3 // 16, groups // 8, groups // 16]
+    rest = groups - sum(ends)
+    return [ends[0], rest - rest // 2, rest // 2] + ends[1:]
 
 
 def body(sensitivity, models, observed, waveform, cell_index, gate_index):
@@ -382,35 +368,61 @@
     place = jnp.stack([lax.axis_index("tile"), lax.axis_index("freq")])
 
     block = sensitivity[0].reshape(spectra, soundings, cells)
+    half = owners // 2
     lanes = cells // members if owned % (GROUP * (cells // members)) == 0 else 1
-    sizes = chunk_groups(own // GROUP, -(-owned // (lanes * GROUP)))
+    sizes = chunk_groups(own // GROUP)
     starts = [sum(sizes[:i]) for i in range(len(sizes))]
-    distances = partner_order(owners)
-    partners = [0] + distances
-    received = []
-    for i, (start, size) in enumerate(zip(starts, sizes)):
+    across_by = list(range(half, owners))[::-1]
+    in_halves = [[h * half + r for r in range(half)] for h in range(2)]
+
+    def send_across(i, after):
         pieces = pack(
-            place, block, models, distances, own, start * GROUP, size * GROUP, lanes if i == 0 else 0
+            place, block, models, after, half, lambda f, j: f ^ across_by[j],
+            own, starts[i] * GROUP, sizes[i] * GROUP, lanes if i == 0 else 0, False,
         )
-        received.append([swap(p, "freq", k) for p, k in zip(pieces, distances)])
-
-    near = near_models(place, cell_index, models, received[0], lanes)
-    blocks = [near] + [swap(near, "tile", k) for k in range(1, tiles)]
+        return [
+            lax.ppermute(p, "freq", [(f, f ^ k) for f in range(owners)]) for p, k in zip(pieces, across_by)
+        ]
+
+    def send_near(first, groups, after, lanes):
+        [pieces] = pack(
+            place, block, models, after, half, lambda f, j: f // half * half + j,
+            own, first * GROUP, groups * GROUP, lanes, True,
+        )
+        return lax.all_to_all(
+            pieces, "freq", split_axis=0, concat_axis=0, axis_index_groups=in_halves, tiled=True
+        )
+
+    split_at = starts[2]
+    across = [send_across(0, [])]
+    near = [send_near(0, split_at, [], lanes)]
+    across.append(send_across(1, across[0][:1]))
+    near.append(send_near(split_at, own // GROUP - split_at, across[0][-1:], 0))
+
+    mine = block_models(place, cell_index, near[0], across[0], block_cells, owned, members, lanes)
+    blocks = [mine] + [
+        lax.ppermute(mine, "tile", [(t, t ^ k) for t in range(tiles)]) for k in range(1, tiles)
+    ]
     borrowed = jnp.stack([b[block_cells, 0] for b in blocks]).astype(jnp.int32)
-    models_t = tile_models(place, cell_index, blocks, owned, partners)
-
-    order = place[1] ^ jnp.array(partners, jnp.int32)
+    models_t = tile_models(place, cell_index, blocks, owned, across_by)
+
+    order = jnp.concatenate([place[1] // half * half + jnp.arange(half), place[1] ^ jnp.array(across_by)])
     wide = wide_table(gate_table(order, own_freqs, freqs, waveform, gate_index).T)
     obs = observed[0].reshape(gates, own // GROUP, GROUP)
     obs = jnp.swapaxes(obs, 0, 1).reshape(own // GROUP, 1, gates * GROUP)
 
     terms = jnp.zeros((members, cells), jnp.float32)
     square = jnp.zeros((members, LANES), jnp.float32)
+    done = []
     for i, start in enumerate(starts):
-        last = i == len(starts) - 1
+        if i >= 2:
+            across.append(send_across(i, across[i - 1][:1] + done[: i - 2][-1:]))
+        part, offset = (near[0], start) if start < split_at else (near[1], start - split_at)
         terms, square = chunk_step(
-            place, block, received[i], start, models_t, wide, obs, cell_index, terms, square, block_cells, last
+            place, part, offset, across[i], start, models_t, wide, obs, cell_index, terms, square, block_cells,
+            i == len(starts) - 1,
         )
+        done.append(square)
 
     slab = members // devices
     sent = terms.reshape(devices, slab, cells)

time: 428 us -> 505 us (1.18)
  starting transfers between devices: 151 us -> 201 us
  waiting for transfers between devices: 156 us -> 173 us
    ppermute x45 -> x27, starting transfers between devices: 148 us -> 183 us  [the longest x24 181 us: send_across(): lax.ppermute(p, 'freq', [(f, f ^ k) for f in range(owners)])]
    ppermute x45 -> x27, waiting for transfers between devices: 147 us -> 164 us  [the longest x24 164 us: send_across(): lax.ppermute(p, 'freq', [(f, f ^ k) for f in range(owners)])]
    all_to_all x0 -> x2, starting transfers between devices: none -> 12.5 us  [send_near(): lax.all_to_all(pieces, 'freq', split_axis=0, concat_axis=0, axis_index_gr...]
    pallas_call x8 -> x10, Pallas kernels: 17.6 us -> 23.9 us  [the longest x8 20.4 us: pack(): pl.pallas_call(functools.partial(pack_kernel, owners_of, own, first, rows...]
    unnamed x129 -> x107, local copies, waits for them, and re-layouts: 25.3 us -> 27.7 us
  transfers between devices with their start and end apart: 46 -> 30, of which waited for: 17 -> 13; matrix products, arithmetic and copies ran while one was open for 3% -> 4% of each run, Pallas kernels for 14% -> 13%
where the time goes in v6:
time: 505 us; the launch traced here: 504 us
  starting transfers between devices  201 us (40%)
  waiting for transfers between devices  173 us (34%)
  Pallas kernels  74 us (15%)
  local copies, waits for them, and re-layouts  36.9 us (7%)
  blocking collectives  9.82 us (2%)
  other arithmetic  7.41 us (1%)
    ppermute x24, starting transfers between devices, send_across(): lax.ppermute(p, 'freq', [(f, f ^ k) for f in range(owners)])  181 us
    ppermute x24, waiting for transfers between devices, send_across(): lax.ppermute(p, 'freq', [(f, f ^ k) for f in range(owners)])  164 us
    pallas_call x6, Pallas kernels, chunk_step(): pl.pallas_call(functools.partial(chunk_kernel, pieces, block_cells, last)...  47.7 us
    unnamed x107, local copies, waits for them, and re-layouts  27.7 us
    pallas_call x8, Pallas kernels, pack(): pl.pallas_call(functools.partial(pack_kernel, owners_of, own, first, rows...  20.4 us
    all_to_all x2, starting transfers between devices, send_near(): lax.all_to_all(pieces, 'freq', split_axis=0, concat_axis=0, axis_index_gr...  12.5 us
  transfers between devices with their start and end apart: 30, of which 13 were waited for; matrix products, arithmetic and copies ran while one was open for 4% of the time, Pallas kernels for 13%

profile of v6, /device:TPU:0, one launch (start us, length us, event | category | flops | bytes accessed | tf_op | source)
XLA Modules:
  0.0 503.8 jit_solution(2351873237076778417)
XLA Ops:
  5.9 5.2 %all-to-all-start = ((f32[4,9,48,512]{3,2,1,0:T(8,128)}), f32[4,9,48,512]{3,2,1,0:T(8,128)S(1)}, u32[]{:S(2)}, u32[]{:S(2)}) async-start(f32[4,9,48,512]{3,2,1,0:T(8,128)} %copy-done.1), calls=%async_computation | async-start | bytes 7077888 | tf_op jit(solution)/shard_map/all_to_all | solution.py:392
  18.4 37.1 %collective-permute-done.3.refs_3_.refs_0_.refs_4_ = f32[9,16,512]{2,1,0:T(8,128)S(1)} collective-permute-done((f32[9,16,512]{2,1,0:T(8,128)S(1)}, f32[9,16,512]{2,1,0:T(8,128)S(1)}, u32[]{:S(2)}, u32[]{:S(2)}) %collective-permute-start.3) | collective-permute-done | bytes 294944 | tf_op jit(solution)/shard_map/ppermute | solution.py:384
  55.5 3.2 pack_near.3
  61.8 7.3 %all-to-all-start.1 = ((f32[4,8,80,512]{3,2,1,0:T(8,128)}), f32[4,8,80,512]{3,2,1,0:T(8,128)}, u32[]{:S(2)}, u32[]{:S(2)}) async-start(f32[4,8,80,512]{3,2,1,0:T(8,128)} %copy-done), calls=%async_computation.1 | async-start | bytes 10485760 | tf_op jit(solution)/shard_map/all_to_all | solution.py:392
  69.1 3.6 collective-permute-start
  75.4 75.9 %collective-permute-done.refs_0_.refs_1_ = f32[9,16,512]{2,1,0:T(8,128)} collective-permute-done((f32[9,16,512]{2,1,0:T(8,128)}, f32[9,16,512]{2,1,0:T(8,128)}, u32[]{:S(2)}, u32[]{:S(2)}) %collective-permute-start) | collective-permute-done | bytes 294944 | tf_op jit(solution)/shard_map/ppermute | solution.py:384
  152.1 3.0 pack_across.7
  164.8 5.8 %collective-permute-start.10 = (f32[8,32,512]{2,1,0:T(8,128)}, f32[8,32,512]{2,1,0:T(8,128)}, u32[]{:S(2)}, u32[]{:S(2)}) collective-permute-start(f32[8,32,512]{2,1,0:T(8,128)} %get-tuple-element.56), channel_id=1, source_target_pairs={{0,6},{1,7},{2,4},{3,5},{4,2},{5,3},{6,0},{7,1},{8,14},{9,15},{10,... | collective-permute-start | bytes 1572872 | tf_op jit(solution)/shard_map/ppermute | solution.py:384
  170.5 2.8 collective-permute-done.7.refs_0_.refs_1_
  179.5 2.9 collective-permute-start.12
  190.3 4.0 collective-permute-start.14
  199.0 6.5 %chunk_step.6 = (f32[256,512]{1,0:T(8,128)}, f32[256,128]{1,0:T(8,128)S(1)}) custom-call(s32[2]{0:T(128)S(1)} %pad_add_fusion.place_ref, f32[4,9,48,512]{3,2,1,0:T(8,128)S(1)} %all-to-all-done.near_ref.refs_0_, f32[9,16,512]{2,1,0:T(8,128)} %collective-permute-done.refs_0_.refs_1_, ...), custom_call_target="tpu_custom_call", output_to_operand_aliasing={{0}: (12, {}), {1}: (13, {})} | custom-call | flops 3221225472 | bytes 2097152 | tf_op jit(solution)/shard_map/chunk_step/pallas_call | solution.py:245
  205.6 12.8 %collective-permute-done.8.refs_0_.refs_1_ = f32[8,32,512]{2,1,0:T(8,128)} collective-permute-done((f32[8,32,512]{2,1,0:T(8,128)}, f32[8,32,512]{2,1,0:T(8,128)}, u32[]{:S(2)}, u32[]{:S(2)}) %collective-permute-start.8) | collective-permute-done | bytes 524320 | tf_op jit(solution)/shard_map/ppermute | solution.py:384
  218.4 58.5 %collective-permute-start.15 = (f32[8,32,512]{2,1,0:T(8,128)S(1)}, f32[8,32,512]{2,1,0:T(8,128)S(1)}, u32[]{:S(2)}, u32[]{:S(2)}) collective-permute-start(f32[8,32,512]{2,1,0:T(8,128)S(1)} %copy-done.35), channel_id=1, source_target_pairs={{0,5},{1,4},{2,7},{3,6},{4,1},{5,0},{6,3},{7,2},{8,13},{9,12},{10,... | collective-permute-start | bytes 1572872 | tf_op jit(solution)/shard_map/ppermute | solution.py:384
  276.8 2.8 pack_across.9
  281.2 3.4 collective-permute-start.24
  284.6 11.0 %chunk_step.7 = (f32[256,512]{1,0:T(8,128)}, f32[256,128]{1,0:T(8,128)S(1)}) custom-call(s32[2]{0:T(128)S(1)} %pad_add_fusion.place_ref, f32[4,9,48,512]{3,2,1,0:T(8,128)S(1)} %all-to-all-done.near_ref.refs_0_, f32[8,32,512]{2,1,0:T(8,128)} %collective-permute-done.7.refs_0_.refs_1_, ...), custom_call_target="tpu_custom_call", output_to_operand_aliasing={{0}: (12, {}), {1}: (13, {})} | custom-call | flops 6442450944 | bytes 4194304 | tf_op jit(solution)/shard_map/chunk_step/pallas_call | solution.py:245
  295.6 15.1 %collective-permute-done.9.refs_0_.refs_1_ = f32[8,24,512]{2,1,0:T(8,128)S(1)} collective-permute-done((f32[8,24,512]{2,1,0:T(8,128)S(1)}, f32[8,24,512]{2,1,0:T(8,128)S(1)}, u32[]{:S(2)}, u32[]{:S(2)}) %collective-permute-start.9) | collective-permute-done | bytes 393248 | tf_op jit(solution)/shard_map/ppermute | solution.py:384
  310.7 47.5 %collective-permute-start.25 = (f32[8,24,512]{2,1,0:T(8,128)}, f32[8,24,512]{2,1,0:T(8,128)S(1)}, u32[]{:S(2)}, u32[]{:S(2)}) collective-permute-start(f32[8,24,512]{2,1,0:T(8,128)} %get-tuple-element.75), channel_id=1, source_target_pairs={{0,5},{1,4},{2,7},{3,6},{4,1},{5,0},{6,3},{7,2},{8,13},{9,12},{10,... | collective-permute-start | bytes 1179656 | tf_op jit(solution)/shard_map/ppermute | solution.py:384
  364.2 3.4 collective-permute-start.21
  371.7 10.7 %chunk_step.8 = (f32[256,512]{1,0:T(8,128)}, f32[256,128]{1,0:T(8,128)S(1)}) custom-call(s32[2]{0:T(128)S(1)} %pad_add_fusion.place_ref, f32[4,8,80,512]{3,2,1,0:T(8,128)} %all-to-all-done.1.refs_0_, f32[8,32,512]{2,1,0:T(8,128)} %collective-permute-done.8.refs_0_.refs_1_, ...), custom_call_target="tpu_custom_call", output_to_operand_aliasing={{0}: (12, {}), {1}: (13, {})} | custom-call | flops 6442450944 | bytes 4194304 | tf_op jit(solution)/shard_map/chunk_step/pallas_call | solution.py:245
  383.8 33.4 %collective-permute-start.22 = (f32[8,16,512]{2,1,0:T(8,128)S(1)}, f32[8,16,512]{2,1,0:T(8,128)S(1)}, u32[]{:S(2)}, u32[]{:S(2)}) collective-permute-start(f32[8,16,512]{2,1,0:T(8,128)S(1)} %get-tuple-element.72), channel_id=1, source_target_pairs={{0,5},{1,4},{2,7},{3,6},{4,1},{5,0},{6,3},{7,2},{8,13},{9,12},{10,... | collective-permute-start | bytes 786440 | tf_op jit(solution)/shard_map/ppermute | solution.py:384
  421.7 3.4 collective-permute-start.18
  425.1 8.5 %chunk_step.9 = (f32[256,512]{1,0:T(8,128)}, f32[256,128]{1,0:T(8,128)S(1)}) custom-call(s32[2]{0:T(128)S(1)} %pad_add_fusion.place_ref, f32[4,8,80,512]{3,2,1,0:T(8,128)} %all-to-all-done.1.refs_0_, f32[8,24,512]{2,1,0:T(8,128)S(1)} %copy-done.23, f32[8,24,512]{2,1,0:T(8,128)} %collective-permute-done.24.refs_2_, ...), custom_call_target="tpu_custom_call", output_to_operand_aliasing={{0}: (12, {}), {1}: (13, {})} | custom-call | flops 4831838208 | bytes 3145728 | tf_op jit(solution)/shard_map/chunk_step/pallas_call | solution.py:245
  433.7 6.0 %collective-permute-start.19 = (f32[8,8,512]{2,1,0:T(8,128)S(1)}, f32[8,8,512]{2,1,0:T(8,128)S(1)}, u32[]{:S(2)}, u32[]{:S(2)}) collective-permute-start(f32[8,8,512]{2,1,0:T(8,128)S(1)} %get-tuple-element.69), channel_id=1, source_target_pairs={{0,5},{1,4},{2,7},{3,6},{4,1},{5,0},{6,3},{7,2},{8,13},{9,12},{10,... | collective-permute-start | bytes 393224 | tf_op jit(solution)/shard_map/ppermute | solution.py:384
  439.6 5.9 %collective-permute-done.22.refs_3_ = f32[8,16,512]{2,1,0:T(8,128)S(1)} collective-permute-done((f32[8,16,512]{2,1,0:T(8,128)S(1)}, f32[8,16,512]{2,1,0:T(8,128)S(1)}, u32[]{:S(2)}, u32[]{:S(2)}) %collective-permute-start.22) | collective-permute-done | bytes 262176 | tf_op jit(solution)/shard_map/ppermute | solution.py:384
  445.6 7.8 %collective-permute-done.23.refs_4_ = f32[8,16,512]{2,1,0:T(8,128)S(1)} collective-permute-done((f32[8,16,512]{2,1,0:T(8,128)S(1)}, f32[8,16,512]{2,1,0:T(8,128)S(1)}, u32[]{:S(2)}, u32[]{:S(2)}) %collective-permute-start.23) | collective-permute-done | bytes 262176 | tf_op jit(solution)/shard_map/ppermute | solution.py:384
  453.4 6.3 %chunk_step.10 = (f32[256,512]{1,0:T(8,128)}, f32[256,128]{1,0:T(8,128)S(1)}) custom-call(s32[2]{0:T(128)S(1)} %pad_add_fusion.place_ref, f32[4,8,80,512]{3,2,1,0:T(8,128)} %all-to-all-done.1.refs_0_, f32[8,16,512]{2,1,0:T(8,128)S(1)} %collective-permute-done.13.refs_0_.refs_1_, ...), custom_call_target="tpu_custom_call", output_to_operand_aliasing={{0}: (12, {}), {1}: (13, {})} | custom-call | flops 3221225472 | bytes 2097152 | tf_op jit(solution)/shard_map/chunk_step/pallas_call | solution.py:245
  464.6 4.7 chunk_step.11
  470.0 5.0 all-to-all-start.2
  482.5 8.8 %all-to-all-done.2.got_ref = f32[32,8,512]{2,1,0:T(8,128)S(1)} async-done(((f32[32,8,512]{2,1,0:T(8,128)}), f32[32,8,512]{2,1,0:T(8,128)S(1)}, u32[]{:S(2)}, u32[]{:S(2)}) %all-to-all-start.2) | async-done | bytes 524320 | tf_op jit(solution)/shard_map/all_to_all | solution.py:429
  493.0 9.8 %all_to_all.20.back_ref = f32[32,8,128]{2,1,0:T(8,128)S(1)} all-to-all(f32[32,8,128]{2,1,0:T(8,128)S(1)} %gradient_step.1), channel_id=1, replica_groups=mesh['tile'=4,'freq'=8] {'tile','freq'}, dimensions={0} | all-to-all | bytes 262144 | tf_op jit(solution)/shard_map/all_to_all | solution.py:432
  (176 shorter events, 80.8 us)
Async XLA Ops:
  5.9 56.0 %all-to-all-start = ((f32[4,9,48,512]{3,2,1,0:T(8,128)}), f32[4,9,48,512]{3,2,1,0:T(8,128)S(1)}, u32[]{:S(2)}, u32[]{:S(2)}) async-start(f32[4,9,48,512]{3,2,1,0:T(8,128)} %copy-done.1), calls=%async_computation | async-start | bytes 7077888 | tf_op jit(solution)/shard_map/all_to_all | solution.py:392
  15.9 39.7 %collective-permute-start.3 = (f32[9,16,512]{2,1,0:T(8,128)S(1)}, f32[9,16,512]{2,1,0:T(8,128)S(1)}, u32[]{:S(2)}, u32[]{:S(2)}) collective-permute-start(f32[9,16,512]{2,1,0:T(8,128)S(1)} %get-tuple-element.47), channel_id=1, source_target_pairs={{0,4},{1,5},{2,6},{3,7},{4,0},{5,1},{6,2},{7,3},{8,12},{9,13},{10,... | collective-permute-start | bytes 884744 | tf_op jit(solution)/shard_map/ppermute | solution.py:384
  61.8 305.8 %all-to-all-start.1 = ((f32[4,8,80,512]{3,2,1,0:T(8,128)}), f32[4,8,80,512]{3,2,1,0:T(8,128)}, u32[]{:S(2)}, u32[]{:S(2)}) async-start(f32[4,8,80,512]{3,2,1,0:T(8,128)} %copy-done), calls=%async_computation.1 | async-start | bytes 10485760 | tf_op jit(solution)/shard_map/all_to_all | solution.py:392
  69.1 82.2 %collective-permute-start = (f32[9,16,512]{2,1,0:T(8,128)}, f32[9,16,512]{2,1,0:T(8,128)}, u32[]{:S(2)}, u32[]{:S(2)}) collective-permute-start(f32[9,16,512]{2,1,0:T(8,128)} %copy-done.45), channel_id=1, source_target_pairs={{0,7},{1,6},{2,5},{3,4},{4,3},{5,2},{6,1},{7,0},{8,15},{9,14},{10,... | collective-permute-start | bytes 884744 | tf_op jit(solution)/shard_map/ppermute | solution.py:384
  72.7 84.4 %collective-permute-start.1 = (f32[9,16,512]{2,1,0:T(8,128)}, f32[9,16,512]{2,1,0:T(8,128)}, u32[]{:S(2)}, u32[]{:S(2)}) collective-permute-start(f32[9,16,512]{2,1,0:T(8,128)} %copy-done.44), channel_id=1, source_target_pairs={{0,6},{1,7},{2,4},{3,5},{4,2},{5,3},{6,0},{7,1},{8,14},{9,15},{10,... | collective-permute-start | bytes 884744 | tf_op jit(solution)/shard_map/ppermute | solution.py:384
  74.4 83.3 %collective-permute-start.2 = (f32[9,16,512]{2,1,0:T(8,128)}, f32[9,16,512]{2,1,0:T(8,128)}, u32[]{:S(2)}, u32[]{:S(2)}) collective-permute-start(f32[9,16,512]{2,1,0:T(8,128)} %copy-done.43), channel_id=1, source_target_pairs={{0,5},{1,4},{2,7},{3,6},{4,1},{5,0},{6,3},{7,2},{8,13},{9,12},{10,... | collective-permute-start | bytes 884744 | tf_op jit(solution)/shard_map/ppermute | solution.py:384
  155.0 18.3 %collective-permute-start.7 = (f32[8,32,512]{2,1,0:T(8,128)}, f32[8,32,512]{2,1,0:T(8,128)}, u32[]{:S(2)}, u32[]{:S(2)}) collective-permute-start(f32[8,32,512]{2,1,0:T(8,128)} %get-tuple-element.48), channel_id=1, source_target_pairs={{0,7},{1,6},{2,5},{3,4},{4,3},{5,2},{6,1},{7,0},{8,15},{9,14},{10,... | collective-permute-start | bytes 1572872 | tf_op jit(solution)/shard_map/ppermute | solution.py:384
  160.3 18.5 %collective-permute-start.6 = (f32[264,256]{1,0:T(8,128)}, f32[264,256]{1,0:T(8,128)S(1)}, u32[]{:S(2)}, u32[]{:S(2)}) collective-permute-start(f32[264,256]{1,0:T(8,128)} %block_models.1.refs_0_), channel_id=1, source_target_pairs={{0,24},{8,16},{16,8},{24,0},{1,25},{9,17},{17,9},{25,1},{2,26},{10... | collective-permute-start | bytes 811016 | tf_op jit(solution)/shard_map/ppermute | solution.py:404
  160.3 22.1 %collective-permute-start.5 = (f32[264,256]{1,0:T(8,128)}, f32[264,256]{1,0:T(8,128)S(1)}, u32[]{:S(2)}, u32[]{:S(2)}) collective-permute-start(f32[264,256]{1,0:T(8,128)} %block_models.1.refs_0_), channel_id=1, source_target_pairs={{0,16},{8,24},{16,0},{24,8},{1,17},{9,25},{17,1},{25,9},{2,18},{10... | collective-permute-start | bytes 811016 | tf_op jit(solution)/shard_map/ppermute | solution.py:404
  164.4 25.9 %collective-permute-start.4 = (f32[264,256]{1,0:T(8,128)}, f32[264,256]{1,0:T(8,128)}, u32[]{:S(2)}, u32[]{:S(2)}) collective-permute-start(f32[264,256]{1,0:T(8,128)} %block_models.1.refs_0_), channel_id=1, source_target_pairs={{0,8},{8,0},{16,24},{24,16},{1,9},{9,1},{17,25},{25,17},{2,10},{10... | collective-permute-start | bytes 811016 | tf_op jit(solution)/shard_map/ppermute | solution.py:404
  164.8 114.9 %collective-permute-start.10 = (f32[8,32,512]{2,1,0:T(8,128)}, f32[8,32,512]{2,1,0:T(8,128)}, u32[]{:S(2)}, u32[]{:S(2)}) collective-permute-start(f32[8,32,512]{2,1,0:T(8,128)} %get-tuple-element.56), channel_id=1, source_target_pairs={{0,6},{1,7},{2,4},{3,5},{4,2},{5,3},{6,0},{7,1},{8,14},{9,15},{10,... | collective-permute-start | bytes 1572872 | tf_op jit(solution)/shard_map/ppermute | solution.py:384
  173.3 106.5 %collective-permute-start.11 = (f32[8,32,512]{2,1,0:T(8,128)}, f32[8,32,512]{2,1,0:T(8,128)}, u32[]{:S(2)}, u32[]{:S(2)}) collective-permute-start(f32[8,32,512]{2,1,0:T(8,128)} %get-tuple-element.57), channel_id=1, source_target_pairs={{0,5},{1,4},{2,7},{3,6},{4,1},{5,0},{6,3},{7,2},{8,13},{9,12},{10,... | collective-permute-start | bytes 1572872 | tf_op jit(solution)/shard_map/ppermute | solution.py:384
  179.5 101.6 %collective-permute-start.12 = (f32[8,32,512]{2,1,0:T(8,128)}, f32[8,32,512]{2,1,0:T(8,128)}, u32[]{:S(2)}, u32[]{:S(2)}) collective-permute-start(f32[8,32,512]{2,1,0:T(8,128)} %get-tuple-element.58), channel_id=1, source_target_pairs={{0,4},{1,5},{2,6},{3,7},{4,0},{5,1},{6,2},{7,3},{8,12},{9,13},{10,... | collective-permute-start | bytes 1572872 | tf_op jit(solution)/shard_map/ppermute | solution.py:384
  183.1 35.2 %collective-permute-start.8 = (f32[8,32,512]{2,1,0:T(8,128)}, f32[8,32,512]{2,1,0:T(8,128)}, u32[]{:S(2)}, u32[]{:S(2)}) collective-permute-start(f32[8,32,512]{2,1,0:T(8,128)} %get-tuple-element.49), channel_id=1, source_target_pairs={{0,7},{1,6},{2,5},{3,4},{4,3},{5,2},{6,1},{7,0},{8,15},{9,14},{10,... | collective-permute-start | bytes 1572872 | tf_op jit(solution)/shard_map/ppermute | solution.py:384
  190.3 94.3 %copy-start.18 = (bf16[512,320]{1,0:T(8,128)(2,1)}, bf16[512,320]{1,0:T(8,128)(2,1)S(1)}, u32[]{:S(2)}) copy-start(bf16[512,320]{1,0:T(8,128)(2,1)S(1)} %get-tuple-element.52.refs_7_) | copy-start | bytes 983044
  190.3 94.3 %copy-start.20 = (bf16[512,320]{1,0:T(8,128)(2,1)}, bf16[512,320]{1,0:T(8,128)(2,1)S(1)}, u32[]{:S(2)}) copy-start(bf16[512,320]{1,0:T(8,128)(2,1)S(1)} %get-tuple-element.53.refs_8_) | copy-start | bytes 983044
  190.3 170.2 %collective-permute-start.14 = (f32[8,32,512]{2,1,0:T(8,128)}, f32[8,32,512]{2,1,0:T(8,128)S(1)}, u32[]{:S(2)}, u32[]{:S(2)}) collective-permute-start(f32[8,32,512]{2,1,0:T(8,128)} %copy-done.36), channel_id=1, source_target_pairs={{0,6},{1,7},{2,4},{3,5},{4,2},{5,3},{6,0},{7,1},{8,14},{9,15},{10,... | collective-permute-start | bytes 1572872 | tf_op jit(solution)/shard_map/ppermute | solution.py:384
  218.4 143.0 %collective-permute-start.15 = (f32[8,32,512]{2,1,0:T(8,128)S(1)}, f32[8,32,512]{2,1,0:T(8,128)S(1)}, u32[]{:S(2)}, u32[]{:S(2)}) collective-permute-start(f32[8,32,512]{2,1,0:T(8,128)S(1)} %copy-done.35), channel_id=1, source_target_pairs={{0,5},{1,4},{2,7},{3,6},{4,1},{5,0},{6,3},{7,2},{8,13},{9,12},{10,... | collective-permute-start | bytes 1572872 | tf_op jit(solution)/shard_map/ppermute | solution.py:384
  279.7 83.7 %collective-permute-start.16 = (f32[8,32,512]{2,1,0:T(8,128)S(1)}, f32[8,32,512]{2,1,0:T(8,128)S(1)}, u32[]{:S(2)}, u32[]{:S(2)}) collective-permute-start(f32[8,32,512]{2,1,0:T(8,128)S(1)} %copy-done.33), channel_id=1, source_target_pairs={{0,4},{1,5},{2,6},{3,7},{4,0},{5,1},{6,2},{7,3},{8,12},{9,13},{10,... | collective-permute-start | bytes 1572872 | tf_op jit(solution)/shard_map/ppermute | solution.py:384
  279.8 30.9 %collective-permute-start.9 = (f32[8,24,512]{2,1,0:T(8,128)S(1)}, f32[8,24,512]{2,1,0:T(8,128)S(1)}, u32[]{:S(2)}, u32[]{:S(2)}) collective-permute-start(f32[8,24,512]{2,1,0:T(8,128)S(1)} %get-tuple-element.55), channel_id=1, source_target_pairs={{0,7},{1,6},{2,5},{3,4},{4,3},{5,2},{6,1},{7,0},{8,15},{9,14},{10,... | collective-permute-start | bytes 1179656 | tf_op jit(solution)/shard_map/ppermute | solution.py:384
  281.2 139.1 %collective-permute-start.24 = (f32[8,24,512]{2,1,0:T(8,128)}, f32[8,24,512]{2,1,0:T(8,128)}, u32[]{:S(2)}, u32[]{:S(2)}) collective-permute-start(f32[8,24,512]{2,1,0:T(8,128)} %get-tuple-element.74), channel_id=1, source_target_pairs={{0,6},{1,7},{2,4},{3,5},{4,2},{5,3},{6,0},{7,1},{8,14},{9,15},{10,... | collective-permute-start | bytes 1179656 | tf_op jit(solution)/shard_map/ppermute | solution.py:384
  310.7 109.7 %collective-permute-start.25 = (f32[8,24,512]{2,1,0:T(8,128)}, f32[8,24,512]{2,1,0:T(8,128)S(1)}, u32[]{:S(2)}, u32[]{:S(2)}) collective-permute-start(f32[8,24,512]{2,1,0:T(8,128)} %get-tuple-element.75), channel_id=1, source_target_pairs={{0,5},{1,4},{2,7},{3,6},{4,1},{5,0},{6,3},{7,2},{8,13},{9,12},{10,... | collective-permute-start | bytes 1179656 | tf_op jit(solution)/shard_map/ppermute | solution.py:384
  361.3 60.4 %collective-permute-start.26 = (f32[8,24,512]{2,1,0:T(8,128)}, f32[8,24,512]{2,1,0:T(8,128)S(1)}, u32[]{:S(2)}, u32[]{:S(2)}) collective-permute-start(f32[8,24,512]{2,1,0:T(8,128)} %get-tuple-element.76), channel_id=1, source_target_pairs={{0,4},{1,5},{2,6},{3,7},{4,0},{5,1},{6,2},{7,3},{8,12},{9,13},{10,... | collective-permute-start | bytes 1179656 | tf_op jit(solution)/shard_map/ppermute | solution.py:384
  362.1 21.7 %collective-permute-start.13 = (f32[8,16,512]{2,1,0:T(8,128)}, f32[8,16,512]{2,1,0:T(8,128)S(1)}, u32[]{:S(2)}, u32[]{:S(2)}) collective-permute-start(f32[8,16,512]{2,1,0:T(8,128)} %get-tuple-element.61), channel_id=1, source_target_pairs={{0,7},{1,6},{2,5},{3,4},{4,3},{5,2},{6,1},{7,0},{8,15},{9,14},{10,... | collective-permute-start | bytes 786440 | tf_op jit(solution)/shard_map/ppermute | solution.py:384
  364.2 69.4 %collective-permute-start.21 = (f32[8,16,512]{2,1,0:T(8,128)S(1)}, f32[8,16,512]{2,1,0:T(8,128)S(1)}, u32[]{:S(2)}, u32[]{:S(2)}) collective-permute-start(f32[8,16,512]{2,1,0:T(8,128)S(1)} %get-tuple-element.71), channel_id=1, source_target_pairs={{0,6},{1,7},{2,4},{3,5},{4,2},{5,3},{6,0},{7,1},{8,14},{9,15},{10,... | collective-permute-start | bytes 786440 | tf_op jit(solution)/shard_map/ppermute | solution.py:384
  383.8 61.8 %collective-permute-start.22 = (f32[8,16,512]{2,1,0:T(8,128)S(1)}, f32[8,16,512]{2,1,0:T(8,128)S(1)}, u32[]{:S(2)}, u32[]{:S(2)}) collective-permute-start(f32[8,16,512]{2,1,0:T(8,128)S(1)} %get-tuple-element.72), channel_id=1, source_target_pairs={{0,5},{1,4},{2,7},{3,6},{4,1},{5,0},{6,3},{7,2},{8,13},{9,12},{10,... | collective-permute-start | bytes 786440 | tf_op jit(solution)/shard_map/ppermute | solution.py:384
  420.3 33.2 %collective-permute-start.23 = (f32[8,16,512]{2,1,0:T(8,128)S(1)}, f32[8,16,512]{2,1,0:T(8,128)S(1)}, u32[]{:S(2)}, u32[]{:S(2)}) collective-permute-start(f32[8,16,512]{2,1,0:T(8,128)S(1)} %get-tuple-element.73), channel_id=1, source_target_pairs={{0,4},{1,5},{2,6},{3,7},{4,0},{5,1},{6,2},{7,3},{8,12},{9,13},{10,... | collective-permute-start | bytes 786440 | tf_op jit(solution)/shard_map/ppermute | solution.py:384
  420.3 39.4 %collective-permute-start.17 = (f32[8,8,512]{2,1,0:T(8,128)S(1)}, f32[8,8,512]{2,1,0:T(8,128)S(1)}, u32[]{:S(2)}, u32[]{:S(2)}) collective-permute-start(f32[8,8,512]{2,1,0:T(8,128)S(1)} %get-tuple-element.67), channel_id=1, source_target_pairs={{0,7},{1,6},{2,5},{3,4},{4,3},{5,2},{6,1},{7,0},{8,15},{9,14},{10,... | collective-permute-start | bytes 393224 | tf_op jit(solution)/shard_map/ppermute | solution.py:384
  421.7 38.0 %collective-permute-start.18 = (f32[8,8,512]{2,1,0:T(8,128)S(1)}, f32[8,8,512]{2,1,0:T(8,128)S(1)}, u32[]{:S(2)}, u32[]{:S(2)}) collective-permute-start(f32[8,8,512]{2,1,0:T(8,128)S(1)} %get-tuple-element.68), channel_id=1, source_target_pairs={{0,6},{1,7},{2,4},{3,5},{4,2},{5,3},{6,0},{7,1},{8,14},{9,15},{10,... | collective-permute-start | bytes 393224 | tf_op jit(solution)/shard_map/ppermute | solution.py:384
  433.7 28.8 %collective-permute-start.19 = (f32[8,8,512]{2,1,0:T(8,128)S(1)}, f32[8,8,512]{2,1,0:T(8,128)S(1)}, u32[]{:S(2)}, u32[]{:S(2)}) collective-permute-start(f32[8,8,512]{2,1,0:T(8,128)S(1)} %get-tuple-element.69), channel_id=1, source_target_pairs={{0,5},{1,4},{2,7},{3,6},{4,1},{5,0},{6,3},{7,2},{8,13},{9,12},{10,... | collective-permute-start | bytes 393224 | tf_op jit(solution)/shard_map/ppermute | solution.py:384
  445.6 19.0 %collective-permute-start.20 = (f32[8,8,512]{2,1,0:T(8,128)S(1)}, f32[8,8,512]{2,1,0:T(8,128)S(1)}, u32[]{:S(2)}, u32[]{:S(2)}) collective-permute-start(f32[8,8,512]{2,1,0:T(8,128)S(1)} %get-tuple-element.70), channel_id=1, source_target_pairs={{0,4},{1,5},{2,6},{3,7},{4,0},{5,1},{6,2},{7,3},{8,12},{9,13},{10,... | collective-permute-start | bytes 393224 | tf_op jit(solution)/shard_map/ppermute | solution.py:384
  470.0 21.3 %all-to-all-start.2 = ((f32[32,8,512]{2,1,0:T(8,128)}), f32[32,8,512]{2,1,0:T(8,128)S(1)}, u32[]{:S(2)}, u32[]{:S(2)}) async-start(f32[32,8,512]{2,1,0:T(8,128)} %bitcast.11), calls=%async_computation.2 | async-start | bytes 1048576 | tf_op jit(solution)/shard_map/all_to_all | solution.py:429
  (51 other events, 629.1 us)

commit v7 on v4

--- a/solution.py
+++ b/solution.py
@@ -25,9 +25,7 @@
 
 def partner_order(size):
     assert size & (size - 1) == 0
-    across, near = list(range(size // 2, size))[::-1], list(range(1, size // 2))[::-1]
-    order = [k for pair in zip(across, near + [None]) for k in pair if k is not None]
-    return order
+    return list(range(1, size))[::-1]
 
 
 def gate_table(owner_order, own_freqs, freqs, waveform, gate_index):
@@ -71,9 +69,9 @@
 SCALARS = pl.BlockSpec(memory_space=pltpu.SMEM)
 
 
-def pack_kernel(distances, own, first, lanes, place_ref, block_ref, models_ref, *refs):
-    outs, (held, in_sems, out_sems) = refs[: len(distances)], refs[len(distances) :]
-    spectra, rows = block_ref.shape[0], held.shape[2]
+def pack_kernel(distances, own, first, rows, lanes, place_ref, block_ref, models_ref, *refs):
+    outs, (held, in_sems, out_sems) = refs[-len(distances) - 3 : -3], refs[-3:]
+    spectra = block_ref.shape[0]
     owned, members = models_ref.shape
     arrivals, departures = [], []
     for j, k in enumerate(distances):
@@ -93,13 +91,13 @@
         departure.wait()
 
 
-def pack(place, block, models, distances, own, first, rows, lanes):
+def pack(place, block, models, after, distances, own, first, rows, lanes):
     spectra, _, cells = block.shape
     count = len(distances)
     shape = (spectra + (lanes > 0), rows, cells)
     return pl.pallas_call(
-        functools.partial(pack_kernel, distances, own, first, lanes),
-        in_specs=[SCALARS, HBM, pl.BlockSpec(memory_space=pltpu.VMEM)],
+        functools.partial(pack_kernel, distances, own, first, rows, lanes),
+        in_specs=[SCALARS, HBM, pl.BlockSpec(memory_space=pltpu.VMEM)] + [HBM] * len(after),
         out_specs=[HBM] * count,
         out_shape=[jax.ShapeDtypeStruct(shape, jnp.float32)] * count,
         scratch_shapes=[
@@ -110,7 +108,7 @@
         compiler_params=params(48),
         cost_estimate=cost(0, 8 * count * spectra * rows * cells),
         name="pack",
-    )(place, block, models)
+    )(place, block, models, *after)
 
 
 def near_kernel(lanes, place_ref, cells_ref, models_ref, *refs):
@@ -358,13 +356,12 @@
     )(models, back)
 
 
-def chunk_groups(groups, riders):
-    if groups < 8:
+def chunk_groups(groups):
+    if groups < 16:
         return [1] * groups
-    first, last = max(groups // 8, riders), [groups // 8, groups // 16 or 1]
-    rest = groups - first - sum(last)
-    middle = -(-rest // (groups // 4))
-    return [first] + [rest // middle + (i < rest % middle) for i in range(middle)] + last
+    ends = [groups // 8, groups * 3 // 16, groups // 8, groups // 16]
+    rest = groups - sum(ends)
+    return [ends[0], rest - rest // 2, rest // 2] + ends[1:]
 
 
 def body(sensitivity, models, observed, waveform, cell_index, gate_index):
@@ -383,17 +380,23 @@
 
     block = sensitivity[0].reshape(spectra, soundings, cells)
     lanes = cells // members if owned % (GROUP * (cells // members)) == 0 else 1
-    sizes = chunk_groups(own // GROUP, -(-owned // (lanes * GROUP)))
+    sizes = chunk_groups(own // GROUP)
     starts = [sum(sizes[:i]) for i in range(len(sizes))]
     distances = partner_order(owners)
     partners = [0] + distances
-    received = []
-    for i, (start, size) in enumerate(zip(starts, sizes)):
+    received, done = [], []
+
+    def send(i):
+        after = received[i - 1][:1] if i else []
+        if i > 2:
+            after = after + done[i - 3 : i - 2]
         pieces = pack(
-            place, block, models, distances, own, start * GROUP, size * GROUP, lanes if i == 0 else 0
+            place, block, models, after, distances, own, starts[i] * GROUP, sizes[i] * GROUP, 0 if i else lanes
         )
         received.append([swap(p, "freq", k) for p, k in zip(pieces, distances)])
 
+    send(0)
+    send(1)
     near = near_models(place, cell_index, models, received[0], lanes)
     blocks = [near] + [swap(near, "tile", k) for k in range(1, tiles)]
     borrowed = jnp.stack([b[block_cells, 0] for b in blocks]).astype(jnp.int32)
@@ -407,10 +410,13 @@
     terms = jnp.zeros((members, cells), jnp.float32)
     square = jnp.zeros((members, LANES), jnp.float32)
     for i, start in enumerate(starts):
+        if i > 1:
+            send(i)
         last = i == len(starts) - 1
         terms, square = chunk_step(
             place, block, received[i], start, models_t, wide, obs, cell_index, terms, square, block_cells, last
         )
+        done.append(square)
 
     slab = members // devices
     sent = terms.reshape(devices, slab, cells)

time: 428 us -> 423 us (0.988)
  starting transfers between devices: 151 us -> 172 us
  local copies, waits for them, and re-layouts: 32.2 us -> 17.7 us
  waiting for transfers between devices: 156 us -> 144 us
    ppermute x45, starting transfers between devices: 148 us -> 169 us  [swap(): lax.ppermute(x, axis, [(i, i ^ k) for i in range(lax.axis_size(axis))])]
    unnamed x129 -> x65, local copies, waits for them, and re-layouts: 25.3 us -> 11.8 us
    ppermute x45, waiting for transfers between devices: 147 us -> 135 us  [swap(): lax.ppermute(x, axis, [(i, i ^ k) for i in range(lax.axis_size(axis))])]
  transfers between devices with their start and end apart: 46 -> 46, of which waited for: 17 -> 17; matrix products, arithmetic and copies ran while one was open for 3% -> 3% of each run, Pallas kernels for 14% -> 15%
where the time goes in v7:
time: 423 us
  starting transfers between devices  172 us (41%)
  waiting for transfers between devices  144 us (34%)
  Pallas kernels  72.3 us (17%)
  local copies, waits for them, and re-layouts  17.7 us (4%)
  blocking collectives  9.82 us (2%)
  other arithmetic  4.77 us (1%)
    ppermute x45, starting transfers between devices, swap(): lax.ppermute(x, axis, [(i, i ^ k) for i in range(lax.axis_size(axis))])  169 us
    ppermute x45, waiting for transfers between devices, swap(): lax.ppermute(x, axis, [(i, i ^ k) for i in range(lax.axis_size(axis))])  135 us
    pallas_call x6, Pallas kernels, chunk_step(): pl.pallas_call(functools.partial(chunk_kernel, pieces, block_cells, last)...  51 us
    pallas_call x6, Pallas kernels, pack(): pl.pallas_call(functools.partial(pack_kernel, distances, own, first, rows...  16.5 us
    unnamed x65, local copies, waits for them, and re-layouts  11.8 us
    all_to_all x1, blocking collectives, body(): back = lax.all_to_all(step, both, split_axis=0, concat_axis=0, tiled=True)  9.82 us
    all_to_all x1, waiting for transfers between devices, body(): got = lax.all_to_all(sent, both, split_axis=0, concat_axis=0, tiled=True)  9.01 us
  transfers between devices with their start and end apart: 46, of which 17 were waited for; matrix products, arithmetic and copies ran while one was open for 3% of the time, Pallas kernels for 15%

profile of v7, /device:TPU:0, one launch (start us, length us, event | category | flops | bytes accessed | tf_op | source)
XLA Modules:
  0.0 422.7 jit_solution(17450251191064668605)
XLA Ops:
  3.6 6.0 %collective-permute-start = (f32[9,16,512]{2,1,0:T(8,128)S(1)}, f32[9,16,512]{2,1,0:T(8,128)S(1)}, u32[]{:S(2)}, u32[]{:S(2)}) collective-permute-start(f32[9,16,512]{2,1,0:T(8,128)S(1)} %get-tuple-element.62), channel_id=1, source_target_pairs={{0,7},{1,6},{2,5},{3,4},{4,3},{5,2},{6,1},{7,0},{8,15},{9,14},{10,... | collective-permute-start | bytes 884744 | tf_op jit(solution)/shard_map/ppermute | solution.py:23
  17.7 28.1 %collective-permute-start.5 = (f32[9,16,512]{2,1,0:T(8,128)S(1)}, f32[9,16,512]{2,1,0:T(8,128)S(1)}, u32[]{:S(2)}, u32[]{:S(2)}) collective-permute-start(f32[9,16,512]{2,1,0:T(8,128)S(1)} %get-tuple-element.67), channel_id=1, source_target_pairs={{0,2},{1,3},{2,0},{3,1},{4,6},{5,7},{6,4},{7,5},{8,10},{9,11},{10,... | collective-permute-start | bytes 884744 | tf_op jit(solution)/shard_map/ppermute | solution.py:23
  47.1 3.6 pack.7
  50.8 6.2 %collective-permute-done.2.refs_2_.refs_3_ = f32[9,16,512]{2,1,0:T(8,128)S(1)} collective-permute-done((f32[9,16,512]{2,1,0:T(8,128)S(1)}, f32[9,16,512]{2,1,0:T(8,128)S(1)}, u32[]{:S(2)}, u32[]{:S(2)}) %collective-permute-start.2) | collective-permute-done | bytes 294944 | tf_op jit(solution)/shard_map/ppermute | solution.py:23
  57.0 3.2 collective-permute-start.10
  60.2 14.1 %collective-permute-done.3.refs_3_.refs_4_ = f32[9,16,512]{2,1,0:T(8,128)S(1)} collective-permute-done((f32[9,16,512]{2,1,0:T(8,128)S(1)}, f32[9,16,512]{2,1,0:T(8,128)S(1)}, u32[]{:S(2)}, u32[]{:S(2)}) %collective-permute-start.3) | collective-permute-done | bytes 294944 | tf_op jit(solution)/shard_map/ppermute | solution.py:23
  77.6 3.7 collective-permute-start.15
  93.2 35.3 %collective-permute-start.16 = (f32[8,32,512]{2,1,0:T(8,128)}, f32[8,32,512]{2,1,0:T(8,128)}, u32[]{:S(2)}, u32[]{:S(2)}) collective-permute-start(f32[8,32,512]{2,1,0:T(8,128)} %get-tuple-element.80), channel_id=1, source_target_pairs={{0,3},{1,2},{2,1},{3,0},{4,7},{5,6},{6,5},{7,4},{8,11},{9,10},{10,... | collective-permute-start | bytes 1572872 | tf_op jit(solution)/shard_map/ppermute | solution.py:23
  130.7 11.3 %collective-permute-done.14.refs_3_ = f32[8,32,512]{2,1,0:T(8,128)S(1)} collective-permute-done((f32[8,32,512]{2,1,0:T(8,128)}, f32[8,32,512]{2,1,0:T(8,128)S(1)}, u32[]{:S(2)}, u32[]{:S(2)}) %collective-permute-start.14) | collective-permute-done | bytes 524320 | tf_op jit(solution)/shard_map/ppermute | solution.py:23
  142.9 3.2 collective-permute-start.11
  147.9 5.2 %collective-permute-done.15.refs_4_ = f32[8,32,512]{2,1,0:T(8,128)S(1)} collective-permute-done((f32[8,32,512]{2,1,0:T(8,128)}, f32[8,32,512]{2,1,0:T(8,128)S(1)}, u32[]{:S(2)}, u32[]{:S(2)}) %collective-permute-start.15) | collective-permute-done | bytes 524320 | tf_op jit(solution)/shard_map/ppermute | solution.py:23
  162.3 23.5 %collective-permute-done.16.refs_5_ = f32[8,32,512]{2,1,0:T(8,128)} collective-permute-done((f32[8,32,512]{2,1,0:T(8,128)}, f32[8,32,512]{2,1,0:T(8,128)}, u32[]{:S(2)}, u32[]{:S(2)}) %collective-permute-start.16) | collective-permute-done | bytes 524320 | tf_op jit(solution)/shard_map/ppermute | solution.py:23
  186.0 10.5 %collective-permute-done.17.refs_6_ = f32[8,32,512]{2,1,0:T(8,128)} collective-permute-done((f32[8,32,512]{2,1,0:T(8,128)}, f32[8,32,512]{2,1,0:T(8,128)}, u32[]{:S(2)}, u32[]{:S(2)}) %collective-permute-start.17) | collective-permute-done | bytes 524320 | tf_op jit(solution)/shard_map/ppermute | solution.py:23
  196.7 2.9 collective-permute-start.23
  200.6 6.9 %chunk_step.6 = (f32[256,512]{1,0:T(8,128)}, f32[256,128]{1,0:T(8,128)S(1)}) custom-call(s32[2]{0:T(128)S(1)} %pad_add_fusion.place_ref, f32[8,1024,512]{2,1,0:T(8,128)} %bitcast.19, f32[9,16,512]{2,1,0:T(8,128)S(1)} %collective-permute-done.refs_0_.refs_1_, ...), custom_call_target="tpu_custom_call", output_to_operand_aliasing={{0}: (15, {}), {1}: (16, {})} | custom-call | flops 3221225472 | bytes 2097152 | tf_op jit(solution)/shard_map/chunk_step/pallas_call | solution.py:250
  207.4 3.1 pack.9
  212.8 19.2 %collective-permute-done.21.refs_3_ = f32[8,32,512]{2,1,0:T(8,128)S(1)} collective-permute-done((f32[8,32,512]{2,1,0:T(8,128)S(1)}, f32[8,32,512]{2,1,0:T(8,128)S(1)}, u32[]{:S(2)}, u32[]{:S(2)}) %collective-permute-start.21) | collective-permute-done | bytes 524320 | tf_op jit(solution)/shard_map/ppermute | solution.py:23
  233.3 18.1 %collective-permute-done.22.refs_4_ = f32[8,32,512]{2,1,0:T(8,128)S(1)} collective-permute-done((f32[8,32,512]{2,1,0:T(8,128)S(1)}, f32[8,32,512]{2,1,0:T(8,128)S(1)}, u32[]{:S(2)}, u32[]{:S(2)}) %collective-permute-start.22) | collective-permute-done | bytes 524320 | tf_op jit(solution)/shard_map/ppermute | solution.py:23
  253.8 2.9 collective-permute-start.41
  256.7 29.9 %collective-permute-start.42 = (f32[8,24,512]{2,1,0:T(8,128)S(1)}, f32[8,24,512]{2,1,0:T(8,128)S(1)}, u32[]{:S(2)}, u32[]{:S(2)}) collective-permute-start(f32[8,24,512]{2,1,0:T(8,128)S(1)} %get-tuple-element.110), channel_id=1, source_target_pairs={{0,3},{1,2},{2,1},{3,0},{4,7},{5,6},{6,5},{7,4},{8,11},{9,10},{10,... | collective-permute-start | bytes 1179656 | tf_op jit(solution)/shard_map/ppermute | solution.py:23
  286.7 11.5 %chunk_step.7 = (f32[256,512]{1,0:T(8,128)}, f32[256,128]{1,0:T(8,128)S(1)}) custom-call(s32[2]{0:T(128)S(1)} %pad_add_fusion.place_ref, f32[8,1024,512]{2,1,0:T(8,128)} %bitcast.21, f32[8,32,512]{2,1,0:T(8,128)S(1)} %collective-permute-done.10.refs_0_.refs_1_, f32[8,32,512]{2,1,0:T(8,128)S(1)} %copy-done.6, ...), custom_call_target="tpu_custom_call", output_to_operand_aliasing={{0}: (15, {}), {1}: (16, {})} | custom-call | flops 6442450944 | bytes 4194304 | tf_op jit(solution)/shard_map/chunk_step/pallas_call | solution.py:250
  304.2 11.9 %collective-permute-done.41.refs_4_ = f32[8,24,512]{2,1,0:T(8,128)S(1)} collective-permute-done((f32[8,24,512]{2,1,0:T(8,128)S(1)}, f32[8,24,512]{2,1,0:T(8,128)S(1)}, u32[]{:S(2)}, u32[]{:S(2)}) %collective-permute-start.41) | collective-permute-done | bytes 393248 | tf_op jit(solution)/shard_map/ppermute | solution.py:23
  318.5 15.9 %collective-permute-start.35 = (f32[8,16,512]{2,1,0:T(8,128)S(1)}, f32[8,16,512]{2,1,0:T(8,128)S(1)}, u32[]{:S(2)}, u32[]{:S(2)}) collective-permute-start(f32[8,16,512]{2,1,0:T(8,128)S(1)} %get-tuple-element.103), channel_id=1, source_target_pairs={{0,4},{1,5},{2,6},{3,7},{4,0},{5,1},{6,2},{7,3},{8,12},{9,13},{10,... | collective-permute-start | bytes 786440 | tf_op jit(solution)/shard_map/ppermute | solution.py:23
  334.4 11.4 %chunk_step.8 = (f32[256,512]{1,0:T(8,128)}, f32[256,128]{1,0:T(8,128)S(1)}) custom-call(s32[2]{0:T(128)S(1)} %pad_add_fusion.place_ref, f32[8,1024,512]{2,1,0:T(8,128)} %bitcast.23, f32[8,32,512]{2,1,0:T(8,128)S(1)} %collective-permute-done.11.refs_0_.refs_1_, ...), custom_call_target="tpu_custom_call", output_to_operand_aliasing={{0}: (15, {}), {1}: (16, {})} | custom-call | flops 6442450944 | bytes 4194304 | tf_op jit(solution)/shard_map/chunk_step/pallas_call | solution.py:250
  348.7 2.9 collective-permute-start.37
  357.9 9.3 %chunk_step.9 = (f32[256,512]{1,0:T(8,128)}, f32[256,128]{1,0:T(8,128)S(1)}) custom-call(s32[2]{0:T(128)S(1)} %pad_add_fusion.place_ref, f32[8,1024,512]{2,1,0:T(8,128)} %bitcast.25, f32[8,24,512]{2,1,0:T(8,128)S(1)} %collective-permute-done.12.refs_0_.refs_1_, ...), custom_call_target="tpu_custom_call", output_to_operand_aliasing={{0}: (15, {}), {1}: (16, {})} | custom-call | flops 4831838208 | bytes 3145728 | tf_op jit(solution)/shard_map/chunk_step/pallas_call | solution.py:250
  367.2 7.1 %collective-permute-done.37.refs_6_ = f32[8,16,512]{2,1,0:T(8,128)S(1)} collective-permute-done((f32[8,16,512]{2,1,0:T(8,128)S(1)}, f32[8,16,512]{2,1,0:T(8,128)S(1)}, u32[]{:S(2)}, u32[]{:S(2)}) %collective-permute-start.37) | collective-permute-done | bytes 262176 | tf_op jit(solution)/shard_map/ppermute | solution.py:23
  378.5 6.9 %chunk_step.10 = (f32[256,512]{1,0:T(8,128)}, f32[256,128]{1,0:T(8,128)S(1)}) custom-call(s32[2]{0:T(128)S(1)} %pad_add_fusion.place_ref, f32[8,1024,512]{2,1,0:T(8,128)} %bitcast.26, f32[8,16,512]{2,1,0:T(8,128)S(1)} %collective-permute-done.19.refs_0_.refs_1_, ...), custom_call_target="tpu_custom_call", output_to_operand_aliasing={{0}: (15, {}), {1}: (16, {})} | custom-call | flops 3221225472 | bytes 2097152 | tf_op jit(solution)/shard_map/chunk_step/pallas_call | solution.py:250
  386.0 5.1 %chunk_step.11 = (f32[256,512]{1,0:T(8,128)}, f32[256,128]{1,0:T(8,128)S(1)}) custom-call(s32[2]{0:T(128)S(1)} %pad_add_fusion.place_ref, f32[8,1024,512]{2,1,0:T(8,128)} %bitcast.27, f32[8,8,512]{2,1,0:T(8,128)S(1)} %collective-permute-done.26.refs_1_, ...), custom_call_target="tpu_custom_call", output_to_operand_aliasing={{0}: (15, {}), {1}: (16, {})} | custom-call | flops 1610612736 | bytes 1048576 | tf_op jit(solution)/shard_map/chunk_step/pallas_call | solution.py:250
  391.1 3.7 all-to-all-start
  402.1 9.0 %all-to-all-done.got_ref = f32[32,8,512]{2,1,0:T(8,128)S(1)} async-done(((f32[32,8,512]{2,1,0:T(8,128)}), f32[32,8,512]{2,1,0:T(8,128)S(1)}, u32[]{:S(2)}, u32[]{:S(2)}) %all-to-all-start) | async-done | bytes 524320 | tf_op jit(solution)/shard_map/all_to_all | solution.py:423
  411.9 9.8 %all_to_all.10.back_ref = f32[32,8,128]{2,1,0:T(8,128)S(1)} all-to-all(f32[32,8,128]{2,1,0:T(8,128)S(1)} %gradient_step.1), channel_id=1, replica_groups=mesh['tile'=4,'freq'=8] {'tile','freq'}, dimensions={0} | all-to-all | bytes 262144 | tf_op jit(solution)/shard_map/all_to_all | solution.py:426
  (163 shorter events, 80.4 us)
Async XLA Ops:
  9.7 36.1 %collective-permute-start.1 = (f32[9,16,512]{2,1,0:T(8,128)S(1)}, f32[9,16,512]{2,1,0:T(8,128)S(1)}, u32[]{:S(2)}, u32[]{:S(2)}) collective-permute-start(f32[9,16,512]{2,1,0:T(8,128)S(1)} %get-tuple-element.63), channel_id=1, source_target_pairs={{0,6},{1,7},{2,4},{3,5},{4,2},{5,3},{6,0},{7,1},{8,14},{9,15},{10,... | collective-permute-start | bytes 884744 | tf_op jit(solution)/shard_map/ppermute | solution.py:23
  9.9 47.1 %collective-permute-start.2 = (f32[9,16,512]{2,1,0:T(8,128)S(1)}, f32[9,16,512]{2,1,0:T(8,128)S(1)}, u32[]{:S(2)}, u32[]{:S(2)}) collective-permute-start(f32[9,16,512]{2,1,0:T(8,128)S(1)} %get-tuple-element.64), channel_id=1, source_target_pairs={{0,5},{1,4},{2,7},{3,6},{4,1},{5,0},{6,3},{7,2},{8,13},{9,12},{10,... | collective-permute-start | bytes 884744 | tf_op jit(solution)/shard_map/ppermute | solution.py:23
  10.7 63.7 %collective-permute-start.3 = (f32[9,16,512]{2,1,0:T(8,128)S(1)}, f32[9,16,512]{2,1,0:T(8,128)S(1)}, u32[]{:S(2)}, u32[]{:S(2)}) collective-permute-start(f32[9,16,512]{2,1,0:T(8,128)S(1)} %get-tuple-element.65), channel_id=1, source_target_pairs={{0,4},{1,5},{2,6},{3,7},{4,0},{5,1},{6,2},{7,3},{8,12},{9,13},{10,... | collective-permute-start | bytes 884744 | tf_op jit(solution)/shard_map/ppermute | solution.py:23
  12.7 61.7 %collective-permute-start.4 = (f32[9,16,512]{2,1,0:T(8,128)S(1)}, f32[9,16,512]{2,1,0:T(8,128)S(1)}, u32[]{:S(2)}, u32[]{:S(2)}) collective-permute-start(f32[9,16,512]{2,1,0:T(8,128)S(1)} %get-tuple-element.66), channel_id=1, source_target_pairs={{0,3},{1,2},{2,1},{3,0},{4,7},{5,6},{6,5},{7,4},{8,11},{9,10},{10,... | collective-permute-start | bytes 884744 | tf_op jit(solution)/shard_map/ppermute | solution.py:23
  17.7 56.9 %collective-permute-start.5 = (f32[9,16,512]{2,1,0:T(8,128)S(1)}, f32[9,16,512]{2,1,0:T(8,128)S(1)}, u32[]{:S(2)}, u32[]{:S(2)}) collective-permute-start(f32[9,16,512]{2,1,0:T(8,128)S(1)} %get-tuple-element.67), channel_id=1, source_target_pairs={{0,2},{1,3},{2,0},{3,1},{4,6},{5,7},{6,4},{7,5},{8,10},{9,11},{10,... | collective-permute-start | bytes 884744 | tf_op jit(solution)/shard_map/ppermute | solution.py:23
  45.8 28.8 %collective-permute-start.6 = (f32[9,16,512]{2,1,0:T(8,128)S(1)}, f32[9,16,512]{2,1,0:T(8,128)S(1)}, u32[]{:S(2)}, u32[]{:S(2)}) collective-permute-start(f32[9,16,512]{2,1,0:T(8,128)S(1)} %get-tuple-element.68), channel_id=1, source_target_pairs={{0,1},{1,0},{2,3},{3,2},{4,5},{5,4},{6,7},{7,6},{8,9},{9,8},{10,11... | collective-permute-start | bytes 884744 | tf_op jit(solution)/shard_map/ppermute | solution.py:23
  57.0 27.8 %collective-permute-start.10 = (f32[8,32,512]{2,1,0:T(8,128)}, f32[8,32,512]{2,1,0:T(8,128)S(1)}, u32[]{:S(2)}, u32[]{:S(2)}) collective-permute-start(f32[8,32,512]{2,1,0:T(8,128)} %get-tuple-element.69), channel_id=1, source_target_pairs={{0,7},{1,6},{2,5},{3,4},{4,3},{5,2},{6,1},{7,0},{8,15},{9,14},{10,... | collective-permute-start | bytes 1572872 | tf_op jit(solution)/shard_map/ppermute | solution.py:23
  75.4 53.8 %collective-permute-start.13 = (f32[8,32,512]{2,1,0:T(8,128)}, f32[8,32,512]{2,1,0:T(8,128)S(1)}, u32[]{:S(2)}, u32[]{:S(2)}) collective-permute-start(f32[8,32,512]{2,1,0:T(8,128)} %copy-done.23), channel_id=1, source_target_pairs={{0,6},{1,7},{2,4},{3,5},{4,2},{5,3},{6,0},{7,1},{8,14},{9,15},{10,... | collective-permute-start | bytes 1572872 | tf_op jit(solution)/shard_map/ppermute | solution.py:23
  77.6 64.5 %collective-permute-start.14 = (f32[8,32,512]{2,1,0:T(8,128)}, f32[8,32,512]{2,1,0:T(8,128)S(1)}, u32[]{:S(2)}, u32[]{:S(2)}) collective-permute-start(f32[8,32,512]{2,1,0:T(8,128)} %copy-done.22), channel_id=1, source_target_pairs={{0,5},{1,4},{2,7},{3,6},{4,1},{5,0},{6,3},{7,2},{8,13},{9,12},{10,... | collective-permute-start | bytes 1572872 | tf_op jit(solution)/shard_map/ppermute | solution.py:23
  77.6 75.5 %collective-permute-start.15 = (f32[8,32,512]{2,1,0:T(8,128)}, f32[8,32,512]{2,1,0:T(8,128)S(1)}, u32[]{:S(2)}, u32[]{:S(2)}) collective-permute-start(f32[8,32,512]{2,1,0:T(8,128)} %copy-done.21), channel_id=1, source_target_pairs={{0,4},{1,5},{2,6},{3,7},{4,0},{5,1},{6,2},{7,3},{8,12},{9,13},{10,... | collective-permute-start | bytes 1572872 | tf_op jit(solution)/shard_map/ppermute | solution.py:23
  84.8 43.7 %collective-permute-start.7 = (f32[264,256]{1,0:T(8,128)S(1)}, f32[264,256]{1,0:T(8,128)S(1)}, u32[]{:S(2)}, u32[]{:S(2)}) collective-permute-start(f32[264,256]{1,0:T(8,128)S(1)} %near_models.1.refs_0_), channel_id=1, source_target_pairs={{0,8},{8,0},{16,24},{24,16},{1,9},{9,1},{17,25},{25,17},{2,10},{10... | collective-permute-start | bytes 811016 | tf_op jit(solution)/shard_map/ppermute | solution.py:23
  93.2 92.6 %collective-permute-start.16 = (f32[8,32,512]{2,1,0:T(8,128)}, f32[8,32,512]{2,1,0:T(8,128)}, u32[]{:S(2)}, u32[]{:S(2)}) collective-permute-start(f32[8,32,512]{2,1,0:T(8,128)} %get-tuple-element.80), channel_id=1, source_target_pairs={{0,3},{1,2},{2,1},{3,0},{4,7},{5,6},{6,5},{7,4},{8,11},{9,10},{10,... | collective-permute-start | bytes 1572872 | tf_op jit(solution)/shard_map/ppermute | solution.py:23
  129.2 67.4 %collective-permute-start.17 = (f32[8,32,512]{2,1,0:T(8,128)}, f32[8,32,512]{2,1,0:T(8,128)}, u32[]{:S(2)}, u32[]{:S(2)}) collective-permute-start(f32[8,32,512]{2,1,0:T(8,128)} %get-tuple-element.81), channel_id=1, source_target_pairs={{0,2},{1,3},{2,0},{3,1},{4,6},{5,7},{6,4},{7,5},{8,10},{9,11},{10,... | collective-permute-start | bytes 1572872 | tf_op jit(solution)/shard_map/ppermute | solution.py:23
  130.0 66.7 %collective-permute-start.18 = (f32[8,32,512]{2,1,0:T(8,128)}, f32[8,32,512]{2,1,0:T(8,128)}, u32[]{:S(2)}, u32[]{:S(2)}) collective-permute-start(f32[8,32,512]{2,1,0:T(8,128)} %get-tuple-element.82), channel_id=1, source_target_pairs={{0,1},{1,0},{2,3},{3,2},{4,5},{5,4},{6,7},{7,6},{8,9},{9,8},{10,11... | collective-permute-start | bytes 1572872 | tf_op jit(solution)/shard_map/ppermute | solution.py:23
  142.9 56.8 %collective-permute-start.11 = (f32[8,32,512]{2,1,0:T(8,128)}, f32[8,32,512]{2,1,0:T(8,128)S(1)}, u32[]{:S(2)}, u32[]{:S(2)}) collective-permute-start(f32[8,32,512]{2,1,0:T(8,128)} %get-tuple-element.70), channel_id=1, source_target_pairs={{0,7},{1,6},{2,5},{3,4},{4,3},{5,2},{6,1},{7,0},{8,15},{9,14},{10,... | collective-permute-start | bytes 1572872 | tf_op jit(solution)/shard_map/ppermute | solution.py:23
  153.9 56.6 %collective-permute-start.20 = (f32[8,32,512]{2,1,0:T(8,128)}, f32[8,32,512]{2,1,0:T(8,128)}, u32[]{:S(2)}, u32[]{:S(2)}) collective-permute-start(f32[8,32,512]{2,1,0:T(8,128)} %get-tuple-element.86), channel_id=1, source_target_pairs={{0,6},{1,7},{2,4},{3,5},{4,2},{5,3},{6,0},{7,1},{8,14},{9,15},{10,... | collective-permute-start | bytes 1572872 | tf_op jit(solution)/shard_map/ppermute | solution.py:23
  185.8 46.2 %collective-permute-start.21 = (f32[8,32,512]{2,1,0:T(8,128)S(1)}, f32[8,32,512]{2,1,0:T(8,128)S(1)}, u32[]{:S(2)}, u32[]{:S(2)}) collective-permute-start(f32[8,32,512]{2,1,0:T(8,128)S(1)} %copy-done.20), channel_id=1, source_target_pairs={{0,5},{1,4},{2,7},{3,6},{4,1},{5,0},{6,3},{7,2},{8,13},{9,12},{10,... | collective-permute-start | bytes 1572872 | tf_op jit(solution)/shard_map/ppermute | solution.py:23
  196.6 54.9 %collective-permute-start.22 = (f32[8,32,512]{2,1,0:T(8,128)S(1)}, f32[8,32,512]{2,1,0:T(8,128)S(1)}, u32[]{:S(2)}, u32[]{:S(2)}) collective-permute-start(f32[8,32,512]{2,1,0:T(8,128)S(1)} %copy-done.18), channel_id=1, source_target_pairs={{0,4},{1,5},{2,6},{3,7},{4,0},{5,1},{6,2},{7,3},{8,12},{9,13},{10,... | collective-permute-start | bytes 1572872 | tf_op jit(solution)/shard_map/ppermute | solution.py:23
  196.7 57.1 %collective-permute-start.23 = (f32[8,32,512]{2,1,0:T(8,128)S(1)}, f32[8,32,512]{2,1,0:T(8,128)S(1)}, u32[]{:S(2)}, u32[]{:S(2)}) collective-permute-start(f32[8,32,512]{2,1,0:T(8,128)S(1)} %copy-done.16), channel_id=1, source_target_pairs={{0,3},{1,2},{2,1},{3,0},{4,7},{5,6},{6,5},{7,4},{8,11},{9,10},{10,... | collective-permute-start | bytes 1572872 | tf_op jit(solution)/shard_map/ppermute | solution.py:23
  199.7 54.2 %collective-permute-start.24 = (f32[8,32,512]{2,1,0:T(8,128)S(1)}, f32[8,32,512]{2,1,0:T(8,128)S(1)}, u32[]{:S(2)}, u32[]{:S(2)}) collective-permute-start(f32[8,32,512]{2,1,0:T(8,128)S(1)} %copy-done.14), channel_id=1, source_target_pairs={{0,2},{1,3},{2,0},{3,1},{4,6},{5,7},{6,4},{7,5},{8,10},{9,11},{10,... | collective-permute-start | bytes 1572872 | tf_op jit(solution)/shard_map/ppermute | solution.py:23
  210.5 46.2 %collective-permute-start.12 = (f32[8,24,512]{2,1,0:T(8,128)S(1)}, f32[8,24,512]{2,1,0:T(8,128)S(1)}, u32[]{:S(2)}, u32[]{:S(2)}) collective-permute-start(f32[8,24,512]{2,1,0:T(8,128)S(1)} %get-tuple-element.76), channel_id=1, source_target_pairs={{0,7},{1,6},{2,5},{3,4},{4,3},{5,2},{6,1},{7,0},{8,15},{9,14},{10,... | collective-permute-start | bytes 1179656 | tf_op jit(solution)/shard_map/ppermute | solution.py:23
  232.0 68.3 %collective-permute-start.25 = (f32[8,32,512]{2,1,0:T(8,128)S(1)}, f32[8,32,512]{2,1,0:T(8,128)S(1)}, u32[]{:S(2)}, u32[]{:S(2)}) collective-permute-start(f32[8,32,512]{2,1,0:T(8,128)S(1)} %copy-done.12), channel_id=1, source_target_pairs={{0,1},{1,0},{2,3},{3,2},{4,5},{5,4},{6,7},{7,6},{8,9},{9,8},{10,11... | collective-permute-start | bytes 1572872 | tf_op jit(solution)/shard_map/ppermute | solution.py:23
  251.5 51.2 %collective-permute-start.39 = (f32[8,24,512]{2,1,0:T(8,128)S(1)}, f32[8,24,512]{2,1,0:T(8,128)S(1)}, u32[]{:S(2)}, u32[]{:S(2)}) collective-permute-start(f32[8,24,512]{2,1,0:T(8,128)S(1)} %get-tuple-element.107), channel_id=1, source_target_pairs={{0,6},{1,7},{2,4},{3,5},{4,2},{5,3},{6,0},{7,1},{8,14},{9,15},{10,... | collective-permute-start | bytes 1179656 | tf_op jit(solution)/shard_map/ppermute | solution.py:23
  253.8 48.8 %collective-permute-start.40 = (f32[8,24,512]{2,1,0:T(8,128)S(1)}, f32[8,24,512]{2,1,0:T(8,128)S(1)}, u32[]{:S(2)}, u32[]{:S(2)}) collective-permute-start(f32[8,24,512]{2,1,0:T(8,128)S(1)} %get-tuple-element.108), channel_id=1, source_target_pairs={{0,5},{1,4},{2,7},{3,6},{4,1},{5,0},{6,3},{7,2},{8,13},{9,12},{10,... | collective-permute-start | bytes 1179656 | tf_op jit(solution)/shard_map/ppermute | solution.py:23
  253.8 62.3 %collective-permute-start.41 = (f32[8,24,512]{2,1,0:T(8,128)S(1)}, f32[8,24,512]{2,1,0:T(8,128)S(1)}, u32[]{:S(2)}, u32[]{:S(2)}) collective-permute-start(f32[8,24,512]{2,1,0:T(8,128)S(1)} %get-tuple-element.109), channel_id=1, source_target_pairs={{0,4},{1,5},{2,6},{3,7},{4,0},{5,1},{6,2},{7,3},{8,12},{9,13},{10,... | collective-permute-start | bytes 1179656 | tf_op jit(solution)/shard_map/ppermute | solution.py:23
  256.7 61.8 %collective-permute-start.42 = (f32[8,24,512]{2,1,0:T(8,128)S(1)}, f32[8,24,512]{2,1,0:T(8,128)S(1)}, u32[]{:S(2)}, u32[]{:S(2)}) collective-permute-start(f32[8,24,512]{2,1,0:T(8,128)S(1)} %get-tuple-element.110), channel_id=1, source_target_pairs={{0,3},{1,2},{2,1},{3,0},{4,7},{5,6},{6,5},{7,4},{8,11},{9,10},{10,... | collective-permute-start | bytes 1179656 | tf_op jit(solution)/shard_map/ppermute | solution.py:23
  302.7 45.8 %collective-permute-start.43 = (f32[8,24,512]{2,1,0:T(8,128)S(1)}, f32[8,24,512]{2,1,0:T(8,128)S(1)}, u32[]{:S(2)}, u32[]{:S(2)}) collective-permute-start(f32[8,24,512]{2,1,0:T(8,128)S(1)} %get-tuple-element.111), channel_id=1, source_target_pairs={{0,2},{1,3},{2,0},{3,1},{4,6},{5,7},{6,4},{7,5},{8,10},{9,11},{10,... | collective-permute-start | bytes 1179656 | tf_op jit(solution)/shard_map/ppermute | solution.py:23
  302.7 46.0 %collective-permute-start.44 = (f32[8,24,512]{2,1,0:T(8,128)S(1)}, f32[8,24,512]{2,1,0:T(8,128)S(1)}, u32[]{:S(2)}, u32[]{:S(2)}) collective-permute-start(f32[8,24,512]{2,1,0:T(8,128)S(1)} %get-tuple-element.112), channel_id=1, source_target_pairs={{0,1},{1,0},{2,3},{3,2},{4,5},{5,4},{6,7},{7,6},{8,9},{9,8},{10,11... | collective-permute-start | bytes 1179656 | tf_op jit(solution)/shard_map/ppermute | solution.py:23
  316.2 35.4 %collective-permute-start.33 = (f32[8,16,512]{2,1,0:T(8,128)S(1)}, f32[8,16,512]{2,1,0:T(8,128)S(1)}, u32[]{:S(2)}, u32[]{:S(2)}) collective-permute-start(f32[8,16,512]{2,1,0:T(8,128)S(1)} %get-tuple-element.101), channel_id=1, source_target_pairs={{0,6},{1,7},{2,4},{3,5},{4,2},{5,3},{6,0},{7,1},{8,14},{9,15},{10,... | collective-permute-start | bytes 786440 | tf_op jit(solution)/shard_map/ppermute | solution.py:23
  318.5 33.6 %collective-permute-start.34 = (f32[8,16,512]{2,1,0:T(8,128)S(1)}, f32[8,16,512]{2,1,0:T(8,128)S(1)}, u32[]{:S(2)}, u32[]{:S(2)}) collective-permute-start(f32[8,16,512]{2,1,0:T(8,128)S(1)} %get-tuple-element.102), channel_id=1, source_target_pairs={{0,5},{1,4},{2,7},{3,6},{4,1},{5,0},{6,3},{7,2},{8,13},{9,12},{10,... | collective-permute-start | bytes 786440 | tf_op jit(solution)/shard_map/ppermute | solution.py:23
  318.5 37.0 %collective-permute-start.35 = (f32[8,16,512]{2,1,0:T(8,128)S(1)}, f32[8,16,512]{2,1,0:T(8,128)S(1)}, u32[]{:S(2)}, u32[]{:S(2)}) collective-permute-start(f32[8,16,512]{2,1,0:T(8,128)S(1)} %get-tuple-element.103), channel_id=1, source_target_pairs={{0,4},{1,5},{2,6},{3,7},{4,0},{5,1},{6,2},{7,3},{8,12},{9,13},{10,... | collective-permute-start | bytes 786440 | tf_op jit(solution)/shard_map/ppermute | solution.py:23
  348.7 25.6 %collective-permute-start.37 = (f32[8,16,512]{2,1,0:T(8,128)S(1)}, f32[8,16,512]{2,1,0:T(8,128)S(1)}, u32[]{:S(2)}, u32[]{:S(2)}) collective-permute-start(f32[8,16,512]{2,1,0:T(8,128)S(1)} %get-tuple-element.105), channel_id=1, source_target_pairs={{0,2},{1,3},{2,0},{3,1},{4,6},{5,7},{6,4},{7,5},{8,10},{9,11},{10,... | collective-permute-start | bytes 786440 | tf_op jit(solution)/shard_map/ppermute | solution.py:23
  (46 other events, 997.7 us)

commit v8 on v7

--- a/solution.py
+++ b/solution.py
@@ -25,7 +25,9 @@
 
 def partner_order(size):
     assert size & (size - 1) == 0
-    return list(range(1, size))[::-1]
+    across, near = list(range(size // 2, size)), list(range(1, size // 2))[::-1]
+    across = across[:1] + across[1:][::-1]
+    return [k for pair in zip(across, near + [None]) for k in pair if k is not None]
 
 
 def gate_table(owner_order, own_freqs, freqs, waveform, gate_index):

time: 423 us -> 422 us (level)
  starting transfers between devices: 172 us -> 152 us
  waiting for transfers between devices: 144 us -> 164 us
    ppermute x45, starting transfers between devices: 169 us -> 147 us  [swap(): lax.ppermute(x, axis, [(i, i ^ k) for i in range(lax.axis_size(axis))])]
    ppermute x45, waiting for transfers between devices: 135 us -> 155 us  [swap(): lax.ppermute(x, axis, [(i, i ^ k) for i in range(lax.axis_size(axis))])]
where the time goes in v8:
time: 422 us; the launch traced here: 421 us
  waiting for transfers between devices  164 us (39%)
  starting transfers between devices  152 us (36%)
  Pallas kernels  72.3 us (17%)
  local copies, waits for them, and re-layouts  17.7 us (4%)
  blocking collectives  9.82 us (2%)
  other arithmetic  4.77 us (1%)
    ppermute x45, waiting for transfers between devices, swap(): lax.ppermute(x, axis, [(i, i ^ k) for i in range(lax.axis_size(axis))])  155 us
    ppermute x45, starting transfers between devices, swap(): lax.ppermute(x, axis, [(i, i ^ k) for i in range(lax.axis_size(axis))])  147 us
    pallas_call x6, Pallas kernels, chunk_step(): pl.pallas_call(functools.partial(chunk_kernel, pieces, block_cells, last)...  50.9 us
    pallas_call x6, Pallas kernels, pack(): pl.pallas_call(functools.partial(pack_kernel, distances, own, first, rows...  16.5 us
    unnamed x65, local copies, waits for them, and re-layouts  11.8 us
    all_to_all x1, blocking collectives, body(): back = lax.all_to_all(step, both, split_axis=0, concat_axis=0, tiled=True)  9.82 us
    all_to_all x1, waiting for transfers between devices, body(): got = lax.all_to_all(sent, both, split_axis=0, concat_axis=0, tiled=True)  9.01 us
  transfers between devices with their start and end apart: 46, of which 17 were waited for; matrix products, arithmetic and copies ran while one was open for 3% of the time, Pallas kernels for 15%

profile of v8, /device:TPU:0, one launch (start us, length us, event | category | flops | bytes accessed | tf_op | source)
XLA Modules:
  0.0 421.2 jit_solution(13730563422027425195)
XLA Ops:
  3.6 4.1 collective-permute-start
  14.0 8.8 %collective-permute-done.refs_0_.refs_1_ = f32[9,16,512]{2,1,0:T(8,128)S(1)} collective-permute-done((f32[9,16,512]{2,1,0:T(8,128)S(1)}, f32[9,16,512]{2,1,0:T(8,128)S(1)}, u32[]{:S(2)}, u32[]{:S(2)}) %collective-permute-start) | collective-permute-done | bytes 294944 | tf_op jit(solution)/shard_map/ppermute | solution.py:23
  22.8 6.3 %collective-permute-start.5 = (f32[9,16,512]{2,1,0:T(8,128)S(1)}, f32[9,16,512]{2,1,0:T(8,128)S(1)}, u32[]{:S(2)}, u32[]{:S(2)}) collective-permute-start(f32[9,16,512]{2,1,0:T(8,128)S(1)} %get-tuple-element.67), channel_id=1, source_target_pairs={{0,1},{1,0},{2,3},{3,2},{4,5},{5,4},{6,7},{7,6},{8,9},{9,8},{10,11... | collective-permute-start | bytes 884744 | tf_op jit(solution)/shard_map/ppermute | solution.py:23
  29.7 3.6 pack.7
  33.3 5.3 %collective-permute-start.10 = (f32[8,32,512]{2,1,0:T(8,128)}, f32[8,32,512]{2,1,0:T(8,128)S(1)}, u32[]{:S(2)}, u32[]{:S(2)}) collective-permute-start(f32[8,32,512]{2,1,0:T(8,128)} %get-tuple-element.69), channel_id=1, source_target_pairs={{0,4},{1,5},{2,6},{3,7},{4,0},{5,1},{6,2},{7,3},{8,12},{9,13},{10,... | collective-permute-start | bytes 1572872 | tf_op jit(solution)/shard_map/ppermute | solution.py:23
  38.6 3.7 collective-permute-done.4.refs_4_.refs_5_
  42.4 30.0 %collective-permute-done.6.refs_6_.refs_7_ = f32[9,16,512]{2,1,0:T(8,128)S(1)} collective-permute-done((f32[9,16,512]{2,1,0:T(8,128)S(1)}, f32[9,16,512]{2,1,0:T(8,128)S(1)}, u32[]{:S(2)}, u32[]{:S(2)}) %collective-permute-start.6) | collective-permute-done | bytes 294944 | tf_op jit(solution)/shard_map/ppermute | solution.py:23
  95.1 9.9 %collective-permute-done.13.refs_2_ = f32[8,32,512]{2,1,0:T(8,128)S(1)} collective-permute-done((f32[8,32,512]{2,1,0:T(8,128)}, f32[8,32,512]{2,1,0:T(8,128)S(1)}, u32[]{:S(2)}, u32[]{:S(2)}) %collective-permute-start.13) | collective-permute-done | bytes 524320 | tf_op jit(solution)/shard_map/ppermute | solution.py:23
  108.4 4.3 %collective-permute-start.11 = (f32[8,32,512]{2,1,0:T(8,128)}, f32[8,32,512]{2,1,0:T(8,128)S(1)}, u32[]{:S(2)}, u32[]{:S(2)}) collective-permute-start(f32[8,32,512]{2,1,0:T(8,128)} %get-tuple-element.70), channel_id=1, source_target_pairs={{0,4},{1,5},{2,6},{3,7},{4,0},{5,1},{6,2},{7,3},{8,12},{9,13},{10,... | collective-permute-start | bytes 1572872 | tf_op jit(solution)/shard_map/ppermute | solution.py:23
  122.6 5.8 %collective-permute-done.16.refs_5_ = f32[8,32,512]{2,1,0:T(8,128)} collective-permute-done((f32[8,32,512]{2,1,0:T(8,128)}, f32[8,32,512]{2,1,0:T(8,128)}, u32[]{:S(2)}, u32[]{:S(2)}) %collective-permute-start.16) | collective-permute-done | bytes 524320 | tf_op jit(solution)/shard_map/ppermute | solution.py:23
  128.4 9.4 %collective-permute-start.21 = (f32[8,32,512]{2,1,0:T(8,128)S(1)}, f32[8,32,512]{2,1,0:T(8,128)S(1)}, u32[]{:S(2)}, u32[]{:S(2)}) collective-permute-start(f32[8,32,512]{2,1,0:T(8,128)S(1)} %copy-done.20), channel_id=1, source_target_pairs={{0,7},{1,6},{2,5},{3,4},{4,3},{5,2},{6,1},{7,0},{8,15},{9,14},{10,... | collective-permute-start | bytes 1572872 | tf_op jit(solution)/shard_map/ppermute | solution.py:23
  137.8 19.5 %collective-permute-start.22 = (f32[8,32,512]{2,1,0:T(8,128)S(1)}, f32[8,32,512]{2,1,0:T(8,128)S(1)}, u32[]{:S(2)}, u32[]{:S(2)}) collective-permute-start(f32[8,32,512]{2,1,0:T(8,128)S(1)} %copy-done.18), channel_id=1, source_target_pairs={{0,2},{1,3},{2,0},{3,1},{4,6},{5,7},{6,4},{7,5},{8,10},{9,11},{10,... | collective-permute-start | bytes 1572872 | tf_op jit(solution)/shard_map/ppermute | solution.py:23
  157.4 21.0 %collective-permute-done.18.refs_7_ = f32[8,32,512]{2,1,0:T(8,128)} collective-permute-done((f32[8,32,512]{2,1,0:T(8,128)}, f32[8,32,512]{2,1,0:T(8,128)}, u32[]{:S(2)}, u32[]{:S(2)}) %collective-permute-start.18) | collective-permute-done | bytes 524320 | tf_op jit(solution)/shard_map/ppermute | solution.py:23
  180.3 20.2 %collective-permute-done.11.refs_0_.refs_1_ = f32[8,32,512]{2,1,0:T(8,128)S(1)} collective-permute-done((f32[8,32,512]{2,1,0:T(8,128)}, f32[8,32,512]{2,1,0:T(8,128)S(1)}, u32[]{:S(2)}, u32[]{:S(2)}) %collective-permute-start.11) | collective-permute-done | bytes 524320 | tf_op jit(solution)/shard_map/ppermute | solution.py:23
  202.2 6.9 %chunk_step.6 = (f32[256,512]{1,0:T(8,128)}, f32[256,128]{1,0:T(8,128)S(1)}) custom-call(s32[2]{0:T(128)S(1)} %pad_add_fusion.place_ref, f32[8,1024,512]{2,1,0:T(8,128)} %bitcast.19, f32[9,16,512]{2,1,0:T(8,128)S(1)} %collective-permute-done.refs_0_.refs_1_, ...), custom_call_target="tpu_custom_call", output_to_operand_aliasing={{0}: (15, {}), {1}: (16, {})} | custom-call | flops 3221225472 | bytes 2097152 | tf_op jit(solution)/shard_map/chunk_step/pallas_call | solution.py:252
  212.2 3.6 collective-permute-start.25
  218.3 27.5 %collective-permute-start.41 = (f32[8,24,512]{2,1,0:T(8,128)S(1)}, f32[8,24,512]{2,1,0:T(8,128)S(1)}, u32[]{:S(2)}, u32[]{:S(2)}) collective-permute-start(f32[8,24,512]{2,1,0:T(8,128)S(1)} %get-tuple-element.109), channel_id=1, source_target_pairs={{0,2},{1,3},{2,0},{3,1},{4,6},{5,7},{6,4},{7,5},{8,10},{9,11},{10,... | collective-permute-start | bytes 1179656 | tf_op jit(solution)/shard_map/ppermute | solution.py:23
  245.8 13.8 %collective-permute-done.12.refs_0_.refs_1_ = f32[8,24,512]{2,1,0:T(8,128)S(1)} collective-permute-done((f32[8,24,512]{2,1,0:T(8,128)S(1)}, f32[8,24,512]{2,1,0:T(8,128)S(1)}, u32[]{:S(2)}, u32[]{:S(2)}) %collective-permute-start.12) | collective-permute-done | bytes 393248 | tf_op jit(solution)/shard_map/ppermute | solution.py:23
  261.7 11.5 %chunk_step.7 = (f32[256,512]{1,0:T(8,128)}, f32[256,128]{1,0:T(8,128)S(1)}) custom-call(s32[2]{0:T(128)S(1)} %pad_add_fusion.place_ref, f32[8,1024,512]{2,1,0:T(8,128)} %bitcast.21, f32[8,32,512]{2,1,0:T(8,128)S(1)} %collective-permute-done.10.refs_0_.refs_1_, f32[8,32,512]{2,1,0:T(8,128)S(1)} %copy-done.6, ...), custom_call_target="tpu_custom_call", output_to_operand_aliasing={{0}: (15, {}), {1}: (16, {})} | custom-call | flops 6442450944 | bytes 4194304 | tf_op jit(solution)/shard_map/chunk_step/pallas_call | solution.py:252
  275.3 4.2 collective-permute-done.25.refs_7_
  280.7 14.7 %collective-permute-start.44 = (f32[8,24,512]{2,1,0:T(8,128)S(1)}, f32[8,24,512]{2,1,0:T(8,128)S(1)}, u32[]{:S(2)}, u32[]{:S(2)}) collective-permute-start(f32[8,24,512]{2,1,0:T(8,128)S(1)} %get-tuple-element.112), channel_id=1, source_target_pairs={{0,5},{1,4},{2,7},{3,6},{4,1},{5,0},{6,3},{7,2},{8,13},{9,12},{10,... | collective-permute-start | bytes 1179656 | tf_op jit(solution)/shard_map/ppermute | solution.py:23
  297.5 23.9 %collective-permute-done.19.refs_0_.refs_1_ = f32[8,16,512]{2,1,0:T(8,128)S(1)} collective-permute-done((f32[8,16,512]{2,1,0:T(8,128)S(1)}, f32[8,16,512]{2,1,0:T(8,128)S(1)}, u32[]{:S(2)}, u32[]{:S(2)}) %collective-permute-start.19) | collective-permute-done | bytes 262176 | tf_op jit(solution)/shard_map/ppermute | solution.py:23
  321.4 11.4 %chunk_step.8 = (f32[256,512]{1,0:T(8,128)}, f32[256,128]{1,0:T(8,128)S(1)}) custom-call(s32[2]{0:T(128)S(1)} %pad_add_fusion.place_ref, f32[8,1024,512]{2,1,0:T(8,128)} %bitcast.23, f32[8,32,512]{2,1,0:T(8,128)S(1)} %collective-permute-done.11.refs_0_.refs_1_, ...), custom_call_target="tpu_custom_call", output_to_operand_aliasing={{0}: (15, {}), {1}: (16, {})} | custom-call | flops 6442450944 | bytes 4194304 | tf_op jit(solution)/shard_map/chunk_step/pallas_call | solution.py:252
  343.2 9.3 %chunk_step.9 = (f32[256,512]{1,0:T(8,128)}, f32[256,128]{1,0:T(8,128)S(1)}) custom-call(s32[2]{0:T(128)S(1)} %pad_add_fusion.place_ref, f32[8,1024,512]{2,1,0:T(8,128)} %bitcast.25, f32[8,24,512]{2,1,0:T(8,128)S(1)} %collective-permute-done.12.refs_0_.refs_1_, ...), custom_call_target="tpu_custom_call", output_to_operand_aliasing={{0}: (15, {}), {1}: (16, {})} | custom-call | flops 4831838208 | bytes 3145728 | tf_op jit(solution)/shard_map/chunk_step/pallas_call | solution.py:252
  355.1 9.2 %collective-permute-start.29 = (f32[8,8,512]{2,1,0:T(8,128)S(1)}, f32[8,8,512]{2,1,0:T(8,128)S(1)}, u32[]{:S(2)}, u32[]{:S(2)}) collective-permute-start(f32[8,8,512]{2,1,0:T(8,128)S(1)} %get-tuple-element.97), channel_id=1, source_target_pairs={{0,2},{1,3},{2,0},{3,1},{4,6},{5,7},{6,4},{7,5},{8,10},{9,11},{10,... | collective-permute-start | bytes 393224 | tf_op jit(solution)/shard_map/ppermute | solution.py:23
  367.2 3.1 collective-permute-start.30
  371.8 6.9 %chunk_step.10 = (f32[256,512]{1,0:T(8,128)}, f32[256,128]{1,0:T(8,128)S(1)}) custom-call(s32[2]{0:T(128)S(1)} %pad_add_fusion.place_ref, f32[8,1024,512]{2,1,0:T(8,128)} %bitcast.26, f32[8,16,512]{2,1,0:T(8,128)S(1)} %collective-permute-done.19.refs_0_.refs_1_, ...), custom_call_target="tpu_custom_call", output_to_operand_aliasing={{0}: (15, {}), {1}: (16, {})} | custom-call | flops 3221225472 | bytes 2097152 | tf_op jit(solution)/shard_map/chunk_step/pallas_call | solution.py:252
  378.7 5.0 %collective-permute-done.32.refs_7_ = f32[8,8,512]{2,1,0:T(8,128)S(1)} collective-permute-done((f32[8,8,512]{2,1,0:T(8,128)S(1)}, f32[8,8,512]{2,1,0:T(8,128)S(1)}, u32[]{:S(2)}, u32[]{:S(2)}) %collective-permute-start.32) | collective-permute-done | bytes 131104 | tf_op jit(solution)/shard_map/ppermute | solution.py:23
  383.7 5.1 %chunk_step.11 = (f32[256,512]{1,0:T(8,128)}, f32[256,128]{1,0:T(8,128)S(1)}) custom-call(s32[2]{0:T(128)S(1)} %pad_add_fusion.place_ref, f32[8,1024,512]{2,1,0:T(8,128)} %bitcast.27, f32[8,8,512]{2,1,0:T(8,128)S(1)} %collective-permute-done.26.refs_1_, ...), custom_call_target="tpu_custom_call", output_to_operand_aliasing={{0}: (15, {}), {1}: (16, {})} | custom-call | flops 1610612736 | bytes 1048576 | tf_op jit(solution)/shard_map/chunk_step/pallas_call | solution.py:252
  388.8 4.5 %all-to-all-start = ((f32[32,8,512]{2,1,0:T(8,128)}), f32[32,8,512]{2,1,0:T(8,128)S(1)}, u32[]{:S(2)}, u32[]{:S(2)}) async-start(f32[32,8,512]{2,1,0:T(8,128)} %bitcast.11), calls=%async_computation | async-start | bytes 1048576 | tf_op jit(solution)/shard_map/all_to_all | solution.py:425
  400.6 9.0 %all-to-all-done.got_ref = f32[32,8,512]{2,1,0:T(8,128)S(1)} async-done(((f32[32,8,512]{2,1,0:T(8,128)}), f32[32,8,512]{2,1,0:T(8,128)S(1)}, u32[]{:S(2)}, u32[]{:S(2)}) %all-to-all-start) | async-done | bytes 524320 | tf_op jit(solution)/shard_map/all_to_all | solution.py:425
  410.5 9.8 %all_to_all.10.back_ref = f32[32,8,128]{2,1,0:T(8,128)S(1)} all-to-all(f32[32,8,128]{2,1,0:T(8,128)S(1)} %gradient_step.1), channel_id=1, replica_groups=mesh['tile'=4,'freq'=8] {'tile','freq'}, dimensions={0} | all-to-all | bytes 262144 | tf_op jit(solution)/shard_map/all_to_all | solution.py:428
  (163 shorter events, 89.0 us)
Async XLA Ops:
  10.2 23.0 %collective-permute-start.2 = (f32[9,16,512]{2,1,0:T(8,128)S(1)}, f32[9,16,512]{2,1,0:T(8,128)S(1)}, u32[]{:S(2)}, u32[]{:S(2)}) collective-permute-start(f32[9,16,512]{2,1,0:T(8,128)S(1)} %get-tuple-element.64), channel_id=1, source_target_pairs={{0,7},{1,6},{2,5},{3,4},{4,3},{5,2},{6,1},{7,0},{8,15},{9,14},{10,... | collective-permute-start | bytes 884744 | tf_op jit(solution)/shard_map/ppermute | solution.py:23
  10.2 28.4 %collective-permute-start.3 = (f32[9,16,512]{2,1,0:T(8,128)S(1)}, f32[9,16,512]{2,1,0:T(8,128)S(1)}, u32[]{:S(2)}, u32[]{:S(2)}) collective-permute-start(f32[9,16,512]{2,1,0:T(8,128)S(1)} %get-tuple-element.65), channel_id=1, source_target_pairs={{0,2},{1,3},{2,0},{3,1},{4,6},{5,7},{6,4},{7,5},{8,10},{9,11},{10,... | collective-permute-start | bytes 884744 | tf_op jit(solution)/shard_map/ppermute | solution.py:23
  11.1 31.3 %collective-permute-start.4 = (f32[9,16,512]{2,1,0:T(8,128)S(1)}, f32[9,16,512]{2,1,0:T(8,128)S(1)}, u32[]{:S(2)}, u32[]{:S(2)}) collective-permute-start(f32[9,16,512]{2,1,0:T(8,128)S(1)} %get-tuple-element.66), channel_id=1, source_target_pairs={{0,6},{1,7},{2,4},{3,5},{4,2},{5,3},{6,0},{7,1},{8,14},{9,15},{10,... | collective-permute-start | bytes 884744 | tf_op jit(solution)/shard_map/ppermute | solution.py:23
  29.6 42.8 %collective-permute-start.6 = (f32[9,16,512]{2,1,0:T(8,128)S(1)}, f32[9,16,512]{2,1,0:T(8,128)S(1)}, u32[]{:S(2)}, u32[]{:S(2)}) collective-permute-start(f32[9,16,512]{2,1,0:T(8,128)S(1)} %get-tuple-element.68), channel_id=1, source_target_pairs={{0,5},{1,4},{2,7},{3,6},{4,1},{5,0},{6,3},{7,2},{8,13},{9,12},{10,... | collective-permute-start | bytes 884744 | tf_op jit(solution)/shard_map/ppermute | solution.py:23
  33.3 49.3 %collective-permute-start.10 = (f32[8,32,512]{2,1,0:T(8,128)}, f32[8,32,512]{2,1,0:T(8,128)S(1)}, u32[]{:S(2)}, u32[]{:S(2)}) collective-permute-start(f32[8,32,512]{2,1,0:T(8,128)} %get-tuple-element.69), channel_id=1, source_target_pairs={{0,4},{1,5},{2,6},{3,7},{4,0},{5,1},{6,2},{7,3},{8,12},{9,13},{10,... | collective-permute-start | bytes 1572872 | tf_op jit(solution)/shard_map/ppermute | solution.py:23
  73.2 31.8 %collective-permute-start.13 = (f32[8,32,512]{2,1,0:T(8,128)}, f32[8,32,512]{2,1,0:T(8,128)S(1)}, u32[]{:S(2)}, u32[]{:S(2)}) collective-permute-start(f32[8,32,512]{2,1,0:T(8,128)} %copy-done.23), channel_id=1, source_target_pairs={{0,3},{1,2},{2,1},{3,0},{4,7},{5,6},{6,5},{7,4},{8,11},{9,10},{10,... | collective-permute-start | bytes 1572872 | tf_op jit(solution)/shard_map/ppermute | solution.py:23
  73.8 33.7 %collective-permute-start.14 = (f32[8,32,512]{2,1,0:T(8,128)}, f32[8,32,512]{2,1,0:T(8,128)S(1)}, u32[]{:S(2)}, u32[]{:S(2)}) collective-permute-start(f32[8,32,512]{2,1,0:T(8,128)} %copy-done.22), channel_id=1, source_target_pairs={{0,7},{1,6},{2,5},{3,4},{4,3},{5,2},{6,1},{7,0},{8,15},{9,14},{10,... | collective-permute-start | bytes 1572872 | tf_op jit(solution)/shard_map/ppermute | solution.py:23
  76.7 38.5 %collective-permute-start.15 = (f32[8,32,512]{2,1,0:T(8,128)}, f32[8,32,512]{2,1,0:T(8,128)S(1)}, u32[]{:S(2)}, u32[]{:S(2)}) collective-permute-start(f32[8,32,512]{2,1,0:T(8,128)} %copy-done.21), channel_id=1, source_target_pairs={{0,2},{1,3},{2,0},{3,1},{4,6},{5,7},{6,4},{7,5},{8,10},{9,11},{10,... | collective-permute-start | bytes 1572872 | tf_op jit(solution)/shard_map/ppermute | solution.py:23
  91.1 37.3 %collective-permute-start.16 = (f32[8,32,512]{2,1,0:T(8,128)}, f32[8,32,512]{2,1,0:T(8,128)}, u32[]{:S(2)}, u32[]{:S(2)}) collective-permute-start(f32[8,32,512]{2,1,0:T(8,128)} %get-tuple-element.80), channel_id=1, source_target_pairs={{0,6},{1,7},{2,4},{3,5},{4,2},{5,3},{6,0},{7,1},{8,14},{9,15},{10,... | collective-permute-start | bytes 1572872 | tf_op jit(solution)/shard_map/ppermute | solution.py:23
  94.2 43.6 %collective-permute-start.17 = (f32[8,32,512]{2,1,0:T(8,128)}, f32[8,32,512]{2,1,0:T(8,128)}, u32[]{:S(2)}, u32[]{:S(2)}) collective-permute-start(f32[8,32,512]{2,1,0:T(8,128)} %get-tuple-element.81), channel_id=1, source_target_pairs={{0,1},{1,0},{2,3},{3,2},{4,5},{5,4},{6,7},{7,6},{8,9},{9,8},{10,11... | collective-permute-start | bytes 1572872 | tf_op jit(solution)/shard_map/ppermute | solution.py:23
  105.8 72.6 %collective-permute-start.18 = (f32[8,32,512]{2,1,0:T(8,128)}, f32[8,32,512]{2,1,0:T(8,128)}, u32[]{:S(2)}, u32[]{:S(2)}) collective-permute-start(f32[8,32,512]{2,1,0:T(8,128)} %get-tuple-element.82), channel_id=1, source_target_pairs={{0,5},{1,4},{2,7},{3,6},{4,1},{5,0},{6,3},{7,2},{8,13},{9,12},{10,... | collective-permute-start | bytes 1572872 | tf_op jit(solution)/shard_map/ppermute | solution.py:23
  108.4 92.1 %collective-permute-start.11 = (f32[8,32,512]{2,1,0:T(8,128)}, f32[8,32,512]{2,1,0:T(8,128)S(1)}, u32[]{:S(2)}, u32[]{:S(2)}) collective-permute-start(f32[8,32,512]{2,1,0:T(8,128)} %get-tuple-element.70), channel_id=1, source_target_pairs={{0,4},{1,5},{2,6},{3,7},{4,0},{5,1},{6,2},{7,3},{8,12},{9,13},{10,... | collective-permute-start | bytes 1572872 | tf_op jit(solution)/shard_map/ppermute | solution.py:23
  116.0 96.1 %collective-permute-start.20 = (f32[8,32,512]{2,1,0:T(8,128)}, f32[8,32,512]{2,1,0:T(8,128)}, u32[]{:S(2)}, u32[]{:S(2)}) collective-permute-start(f32[8,32,512]{2,1,0:T(8,128)} %get-tuple-element.86), channel_id=1, source_target_pairs={{0,3},{1,2},{2,1},{3,0},{4,7},{5,6},{6,5},{7,4},{8,11},{9,10},{10,... | collective-permute-start | bytes 1572872 | tf_op jit(solution)/shard_map/ppermute | solution.py:23
  128.4 83.8 %collective-permute-start.21 = (f32[8,32,512]{2,1,0:T(8,128)S(1)}, f32[8,32,512]{2,1,0:T(8,128)S(1)}, u32[]{:S(2)}, u32[]{:S(2)}) collective-permute-start(f32[8,32,512]{2,1,0:T(8,128)S(1)} %copy-done.20), channel_id=1, source_target_pairs={{0,7},{1,6},{2,5},{3,4},{4,3},{5,2},{6,1},{7,0},{8,15},{9,14},{10,... | collective-permute-start | bytes 1572872 | tf_op jit(solution)/shard_map/ppermute | solution.py:23
  137.8 78.0 %collective-permute-start.22 = (f32[8,32,512]{2,1,0:T(8,128)S(1)}, f32[8,32,512]{2,1,0:T(8,128)S(1)}, u32[]{:S(2)}, u32[]{:S(2)}) collective-permute-start(f32[8,32,512]{2,1,0:T(8,128)S(1)} %copy-done.18), channel_id=1, source_target_pairs={{0,2},{1,3},{2,0},{3,1},{4,6},{5,7},{6,4},{7,5},{8,10},{9,11},{10,... | collective-permute-start | bytes 1572872 | tf_op jit(solution)/shard_map/ppermute | solution.py:23
  178.4 37.4 %collective-permute-start.23 = (f32[8,32,512]{2,1,0:T(8,128)S(1)}, f32[8,32,512]{2,1,0:T(8,128)S(1)}, u32[]{:S(2)}, u32[]{:S(2)}) collective-permute-start(f32[8,32,512]{2,1,0:T(8,128)S(1)} %copy-done.16), channel_id=1, source_target_pairs={{0,6},{1,7},{2,4},{3,5},{4,2},{5,3},{6,0},{7,1},{8,14},{9,15},{10,... | collective-permute-start | bytes 1572872 | tf_op jit(solution)/shard_map/ppermute | solution.py:23
  212.1 47.5 %collective-permute-start.12 = (f32[8,24,512]{2,1,0:T(8,128)S(1)}, f32[8,24,512]{2,1,0:T(8,128)S(1)}, u32[]{:S(2)}, u32[]{:S(2)}) collective-permute-start(f32[8,24,512]{2,1,0:T(8,128)S(1)} %get-tuple-element.76), channel_id=1, source_target_pairs={{0,4},{1,5},{2,6},{3,7},{4,0},{5,1},{6,2},{7,3},{8,12},{9,13},{10,... | collective-permute-start | bytes 1179656 | tf_op jit(solution)/shard_map/ppermute | solution.py:23
  212.2 67.2 %collective-permute-start.25 = (f32[8,32,512]{2,1,0:T(8,128)S(1)}, f32[8,32,512]{2,1,0:T(8,128)S(1)}, u32[]{:S(2)}, u32[]{:S(2)}) collective-permute-start(f32[8,32,512]{2,1,0:T(8,128)S(1)} %copy-done.12), channel_id=1, source_target_pairs={{0,5},{1,4},{2,7},{3,6},{4,1},{5,0},{6,3},{7,2},{8,13},{9,12},{10,... | collective-permute-start | bytes 1572872 | tf_op jit(solution)/shard_map/ppermute | solution.py:23
  215.8 63.7 %collective-permute-start.39 = (f32[8,24,512]{2,1,0:T(8,128)S(1)}, f32[8,24,512]{2,1,0:T(8,128)S(1)}, u32[]{:S(2)}, u32[]{:S(2)}) collective-permute-start(f32[8,24,512]{2,1,0:T(8,128)S(1)} %get-tuple-element.107), channel_id=1, source_target_pairs={{0,3},{1,2},{2,1},{3,0},{4,7},{5,6},{6,5},{7,4},{8,11},{9,10},{10,... | collective-permute-start | bytes 1179656 | tf_op jit(solution)/shard_map/ppermute | solution.py:23
  215.8 64.9 %collective-permute-start.40 = (f32[8,24,512]{2,1,0:T(8,128)S(1)}, f32[8,24,512]{2,1,0:T(8,128)S(1)}, u32[]{:S(2)}, u32[]{:S(2)}) collective-permute-start(f32[8,24,512]{2,1,0:T(8,128)S(1)} %get-tuple-element.108), channel_id=1, source_target_pairs={{0,7},{1,6},{2,5},{3,4},{4,3},{5,2},{6,1},{7,0},{8,15},{9,14},{10,... | collective-permute-start | bytes 1179656 | tf_op jit(solution)/shard_map/ppermute | solution.py:23
  218.3 77.2 %collective-permute-start.41 = (f32[8,24,512]{2,1,0:T(8,128)S(1)}, f32[8,24,512]{2,1,0:T(8,128)S(1)}, u32[]{:S(2)}, u32[]{:S(2)}) collective-permute-start(f32[8,24,512]{2,1,0:T(8,128)S(1)} %get-tuple-element.109), channel_id=1, source_target_pairs={{0,2},{1,3},{2,0},{3,1},{4,6},{5,7},{6,4},{7,5},{8,10},{9,11},{10,... | collective-permute-start | bytes 1179656 | tf_op jit(solution)/shard_map/ppermute | solution.py:23
  259.6 35.8 %collective-permute-start.42 = (f32[8,24,512]{2,1,0:T(8,128)S(1)}, f32[8,24,512]{2,1,0:T(8,128)S(1)}, u32[]{:S(2)}, u32[]{:S(2)}) collective-permute-start(f32[8,24,512]{2,1,0:T(8,128)S(1)} %get-tuple-element.110), channel_id=1, source_target_pairs={{0,6},{1,7},{2,4},{3,5},{4,2},{5,3},{6,0},{7,1},{8,14},{9,15},{10,... | collective-permute-start | bytes 1179656 | tf_op jit(solution)/shard_map/ppermute | solution.py:23
  279.5 41.9 %collective-permute-start.19 = (f32[8,16,512]{2,1,0:T(8,128)S(1)}, f32[8,16,512]{2,1,0:T(8,128)S(1)}, u32[]{:S(2)}, u32[]{:S(2)}) collective-permute-start(f32[8,16,512]{2,1,0:T(8,128)S(1)} %get-tuple-element.85), channel_id=1, source_target_pairs={{0,4},{1,5},{2,6},{3,7},{4,0},{5,1},{6,2},{7,3},{8,12},{9,13},{10,... | collective-permute-start | bytes 786440 | tf_op jit(solution)/shard_map/ppermute | solution.py:23
  279.5 56.0 %collective-permute-start.43 = (f32[8,24,512]{2,1,0:T(8,128)S(1)}, f32[8,24,512]{2,1,0:T(8,128)S(1)}, u32[]{:S(2)}, u32[]{:S(2)}) collective-permute-start(f32[8,24,512]{2,1,0:T(8,128)S(1)} %get-tuple-element.111), channel_id=1, source_target_pairs={{0,1},{1,0},{2,3},{3,2},{4,5},{5,4},{6,7},{7,6},{8,9},{9,8},{10,11... | collective-permute-start | bytes 1179656 | tf_op jit(solution)/shard_map/ppermute | solution.py:23
  280.7 57.0 %collective-permute-start.44 = (f32[8,24,512]{2,1,0:T(8,128)S(1)}, f32[8,24,512]{2,1,0:T(8,128)S(1)}, u32[]{:S(2)}, u32[]{:S(2)}) collective-permute-start(f32[8,24,512]{2,1,0:T(8,128)S(1)} %get-tuple-element.112), channel_id=1, source_target_pairs={{0,5},{1,4},{2,7},{3,6},{4,1},{5,0},{6,3},{7,2},{8,13},{9,12},{10,... | collective-permute-start | bytes 1179656 | tf_op jit(solution)/shard_map/ppermute | solution.py:23
  295.4 42.8 %collective-permute-start.33 = (f32[8,16,512]{2,1,0:T(8,128)S(1)}, f32[8,16,512]{2,1,0:T(8,128)S(1)}, u32[]{:S(2)}, u32[]{:S(2)}) collective-permute-start(f32[8,16,512]{2,1,0:T(8,128)S(1)} %get-tuple-element.101), channel_id=1, source_target_pairs={{0,3},{1,2},{2,1},{3,0},{4,7},{5,6},{6,5},{7,4},{8,11},{9,10},{10,... | collective-permute-start | bytes 786440 | tf_op jit(solution)/shard_map/ppermute | solution.py:23
  295.4 45.1 %collective-permute-start.34 = (f32[8,16,512]{2,1,0:T(8,128)S(1)}, f32[8,16,512]{2,1,0:T(8,128)S(1)}, u32[]{:S(2)}, u32[]{:S(2)}) collective-permute-start(f32[8,16,512]{2,1,0:T(8,128)S(1)} %get-tuple-element.102), channel_id=1, source_target_pairs={{0,7},{1,6},{2,5},{3,4},{4,3},{5,2},{6,1},{7,0},{8,15},{9,14},{10,... | collective-permute-start | bytes 786440 | tf_op jit(solution)/shard_map/ppermute | solution.py:23
  338.3 28.9 %collective-permute-start.38 = (f32[8,16,512]{2,1,0:T(8,128)S(1)}, f32[8,16,512]{2,1,0:T(8,128)S(1)}, u32[]{:S(2)}, u32[]{:S(2)}) collective-permute-start(f32[8,16,512]{2,1,0:T(8,128)S(1)} %get-tuple-element.106), channel_id=1, source_target_pairs={{0,5},{1,4},{2,7},{3,6},{4,1},{5,0},{6,3},{7,2},{8,13},{9,12},{10,... | collective-permute-start | bytes 786440 | tf_op jit(solution)/shard_map/ppermute | solution.py:23
  340.6 29.8 %collective-permute-start.26 = (f32[8,8,512]{2,1,0:T(8,128)S(1)}, f32[8,8,512]{2,1,0:T(8,128)S(1)}, u32[]{:S(2)}, u32[]{:S(2)}) collective-permute-start(f32[8,8,512]{2,1,0:T(8,128)S(1)} %get-tuple-element.94), channel_id=1, source_target_pairs={{0,4},{1,5},{2,6},{3,7},{4,0},{5,1},{6,2},{7,3},{8,12},{9,13},{10,... | collective-permute-start | bytes 393224 | tf_op jit(solution)/shard_map/ppermute | solution.py:23
  342.1 29.7 %collective-permute-start.27 = (f32[8,8,512]{2,1,0:T(8,128)S(1)}, f32[8,8,512]{2,1,0:T(8,128)S(1)}, u32[]{:S(2)}, u32[]{:S(2)}) collective-permute-start(f32[8,8,512]{2,1,0:T(8,128)S(1)} %get-tuple-element.95), channel_id=1, source_target_pairs={{0,3},{1,2},{2,1},{3,0},{4,7},{5,6},{6,5},{7,4},{8,11},{9,10},{10,... | collective-permute-start | bytes 393224 | tf_op jit(solution)/shard_map/ppermute | solution.py:23
  352.5 26.2 %collective-permute-start.28 = (f32[8,8,512]{2,1,0:T(8,128)S(1)}, f32[8,8,512]{2,1,0:T(8,128)S(1)}, u32[]{:S(2)}, u32[]{:S(2)}) collective-permute-start(f32[8,8,512]{2,1,0:T(8,128)S(1)} %get-tuple-element.96), channel_id=1, source_target_pairs={{0,7},{1,6},{2,5},{3,4},{4,3},{5,2},{6,1},{7,0},{8,15},{9,14},{10,... | collective-permute-start | bytes 393224 | tf_op jit(solution)/shard_map/ppermute | solution.py:23
  355.1 23.6 %collective-permute-start.29 = (f32[8,8,512]{2,1,0:T(8,128)S(1)}, f32[8,8,512]{2,1,0:T(8,128)S(1)}, u32[]{:S(2)}, u32[]{:S(2)}) collective-permute-start(f32[8,8,512]{2,1,0:T(8,128)S(1)} %get-tuple-element.97), channel_id=1, source_target_pairs={{0,2},{1,3},{2,0},{3,1},{4,6},{5,7},{6,4},{7,5},{8,10},{9,11},{10,... | collective-permute-start | bytes 393224 | tf_op jit(solution)/shard_map/ppermute | solution.py:23
  (46 other events, 925.9 us)

commit v9 on v8

--- a/solution.py
+++ b/solution.py
@@ -71,21 +71,22 @@
 SCALARS = pl.BlockSpec(memory_space=pltpu.SMEM)
 
 
-def pack_kernel(distances, own, first, rows, lanes, place_ref, block_ref, models_ref, *refs):
-    outs, (held, in_sems, out_sems) = refs[-len(distances) - 3 : -3], refs[-3:]
+def pack_kernel(parts, own, lanes, place_ref, block_ref, models_ref, *refs):
+    outs, held = refs[-2 * len(parts) - 2 : -len(parts) - 2], refs[-len(parts) - 2 : -2]
+    in_sems, out_sems = refs[-2:]
     spectra = block_ref.shape[0]
     owned, members = models_ref.shape
     arrivals, departures = [], []
-    for j, k in enumerate(distances):
+    for j, (k, first, rows) in enumerate(parts):
         row = pl.multiple_of((place_ref[1] ^ k) * own + first, GROUP)
-        source, target = block_ref.at[:, pl.ds(row, rows)], held.at[j, pl.ds(0, spectra)]
+        source, target = block_ref.at[:, pl.ds(row, rows)], held[j].at[pl.ds(0, spectra)]
         arrivals.append(pltpu.make_async_copy(source, target, in_sems.at[j]))
-        departures.append(pltpu.make_async_copy(held.at[j], outs[j], out_sems.at[j]))
+        departures.append(pltpu.make_async_copy(held[j], outs[j], out_sems.at[j]))
         arrivals[j].start()
-    for j in range(len(distances)):
+    for j in range(len(parts)):
         for lane in range(lanes):
             part = owned // lanes
-            held[j, spectra, pl.ds(0, part), pl.ds(lane * members, members)] = models_ref[pl.ds(lane * part, part), :]
+            held[j][spectra, pl.ds(0, part), pl.ds(lane * members, members)] = models_ref[pl.ds(lane * part, part), :]
     for arrival, departure in zip(arrivals, departures):
         arrival.wait()
         departure.start()
@@ -93,28 +94,24 @@
         departure.wait()
 
 
-def pack(place, block, models, after, distances, own, first, rows, lanes):
+def pack(place, block, models, after, parts, own, lanes):
     spectra, _, cells = block.shape
-    count = len(distances)
-    shape = (spectra + (lanes > 0), rows, cells)
-    return pl.pallas_call(
-        functools.partial(pack_kernel, distances, own, first, rows, lanes),
+    shapes = [(spectra + (lanes > 0), rows, cells) for _, _, rows in parts]
+    return pl.pallas_call(
+        functools.partial(pack_kernel, parts, own, lanes),
         in_specs=[SCALARS, HBM, pl.BlockSpec(memory_space=pltpu.VMEM)] + [HBM] * len(after),
-        out_specs=[HBM] * count,
-        out_shape=[jax.ShapeDtypeStruct(shape, jnp.float32)] * count,
-        scratch_shapes=[
-            pltpu.VMEM((count, *shape), jnp.float32),
-            pltpu.SemaphoreType.DMA((count,)),
-            pltpu.SemaphoreType.DMA((count,)),
-        ],
+        out_specs=[HBM] * len(parts),
+        out_shape=[jax.ShapeDtypeStruct(shape, jnp.float32) for shape in shapes],
+        scratch_shapes=[pltpu.VMEM(shape, jnp.float32) for shape in shapes]
+        + [pltpu.SemaphoreType.DMA((len(parts),)), pltpu.SemaphoreType.DMA((len(parts),))],
         compiler_params=params(48),
-        cost_estimate=cost(0, 8 * count * spectra * rows * cells),
+        cost_estimate=cost(0, 8 * spectra * cells * sum(rows for _, _, rows in parts)),
         name="pack",
     )(place, block, models, *after)
 
 
 def near_kernel(lanes, place_ref, cells_ref, models_ref, *refs):
-    riders, out_ref = refs[:-1], refs[-1]
+    riders, out_ref = refs[:-2], refs[-1]
     owned, members = models_ref.shape
     part = owned // lanes
     out_ref[pl.ds(0, owned), :] = models_ref[...]
@@ -130,20 +127,20 @@
     out_ref[pl.ds(block_cells, GROUP), :] = jnp.broadcast_to(other, (GROUP, members))
 
 
-def near_models(place, cell_index, models, first, lanes):
+def near_models(place, cell_index, models, first, after, rows, lanes):
     owned, members = models.shape
-    slabs, rows, cells = first[0].shape
+    slabs, _, cells = first[0].shape
     rider = pl.BlockSpec((1, rows, cells), lambda i: (slabs - 1, 0, 0))
     return pl.pallas_call(
         functools.partial(near_kernel, lanes),
         grid=(1,),
-        in_specs=[SCALARS, whole(cell_index), whole(models)] + [rider] * len(first),
+        in_specs=[SCALARS, whole(cell_index), whole(models)] + [rider] * len(first) + [HBM],
         out_specs=pl.BlockSpec((owned * (len(first) + 1) + GROUP, members), lambda i: (0, 0)),
         out_shape=jax.ShapeDtypeStruct((owned * (len(first) + 1) + GROUP, members), jnp.float32),
         compiler_params=params(16),
         cost_estimate=cost(0, 1 << 20),
         name="near_models",
-    )(place, cell_index, models, *first)
+    )(place, cell_index, models, *first, after)
 
 
 def tile_models_kernel(owned, partners, place_ref, cells_ref, *refs):
@@ -243,9 +240,8 @@
             terms_ref[...] = dot(high, pick) + (dot(middle, pick) + dot(low, pick))
 
 
-def chunk_step(place, block, sens, first, models_t, gates, obs, cell_index, terms, square, block_cells, last):
+def chunk_step(place, block, sens, offsets, first, rows, models_t, gates, obs, cell_index, terms, square, block_cells, last):
     spectra, soundings, cells = block.shape
-    rows = sens[0].shape[1]
     pieces = len(sens) + 1
     members = terms.shape[0]
     own_groups = soundings // (pieces * GROUP)
@@ -257,7 +253,10 @@
             in_specs=[
                 pl.BlockSpec((spectra, GROUP, cells), lambda i, place: (0, place[1] * own_groups + first + i, 0))
             ]
-            + [pl.BlockSpec((spectra, GROUP, cells), lambda i, place: (0, i, 0))] * len(sens)
+            + [
+                pl.BlockSpec((spectra, GROUP, cells), lambda i, place, offset=offset: (0, offset + i, 0))
+                for offset in offsets
+            ]
             + [whole(a) for a in (*models_t, *gates)]
             + [pl.BlockSpec((1, 1, obs.shape[2]), lambda i, place: (first + i, 0, 0)), whole(cell_index)]
             + [whole(terms), whole(square)],
@@ -386,20 +385,33 @@
     starts = [sum(sizes[:i]) for i in range(len(sizes))]
     distances = partner_order(owners)
     partners = [0] + distances
-    received, done = [], []
+    received, offsets, done = [], [], []
+    batches = [i for i in (0, 1, 3) if i < len(sizes)]
+    near_by = {}
 
     def send(i):
-        after = received[i - 1][:1] if i else []
+        after = [received[i - 1][distances[0]]] if i else []
         if i > 2:
             after = after + done[i - 3 : i - 2]
-        pieces = pack(
-            place, block, models, after, distances, own, starts[i] * GROUP, sizes[i] * GROUP, 0 if i else lanes
-        )
-        received.append([swap(p, "freq", k) for p, k in zip(pieces, distances)])
+        batch = max(b for b in batches if b <= i)
+        end = starts[min([b for b in batches if b > i] + [len(starts)])] if batch != batches[-1] else own // GROUP
+        parts = []
+        for k in distances:
+            if k >= owners // 2:
+                parts.append((k, starts[i] * GROUP, sizes[i] * GROUP))
+            elif batch == i:
+                parts.append((k, starts[i] * GROUP, (end - starts[i]) * GROUP))
+        pieces = pack(place, block, models, after, parts, own, 0 if i else lanes)
+        got = {k: swap(p, "freq", k) for p, (k, _, _) in zip(pieces, parts)}
+        near_by.update({k: p for k, p in got.items() if k < owners // 2})
+        received.append({k: got.get(k, near_by.get(k)) for k in distances})
+        offsets.append([0 if k >= owners // 2 else starts[i] - starts[batch] for k in distances])
 
     send(0)
     send(1)
-    near = near_models(place, cell_index, models, received[0], lanes)
+    near = near_models(
+        place, cell_index, models, [received[0][k] for k in distances], received[1][distances[2]], sizes[0] * GROUP, lanes
+    )
     blocks = [near] + [swap(near, "tile", k) for k in range(1, tiles)]
     borrowed = jnp.stack([b[block_cells, 0] for b in blocks]).astype(jnp.int32)
     models_t = tile_models(place, cell_index, blocks, owned, partners)
@@ -416,7 +428,8 @@
             send(i)
         last = i == len(starts) - 1
         terms, square = chunk_step(
-            place, block, received[i], start, models_t, wide, obs, cell_index, terms, square, block_cells, last
+            place, block, [received[i][k] for k in distances], offsets[i], start, sizes[i] * GROUP,
+            models_t, wide, obs, cell_index, terms, square, block_cells, last,
         )
         done.append(square)
 

time: 422 us -> 427 us (1.012)
  waiting for transfers between devices: 164 us -> 223 us
  starting transfers between devices: 152 us -> 98.2 us
    ppermute x45 -> x36, waiting for transfers between devices: 155 us -> 214 us  [swap(): lax.ppermute(x, axis, [(i, i ^ k) for i in range(lax.axis_size(axis))])]
    ppermute x45 -> x36, starting transfers between devices: 147 us -> 90.5 us  [swap(): lax.ppermute(x, axis, [(i, i ^ k) for i in range(lax.axis_size(axis))])]
    unnamed x65 -> x91, local copies, waits for them, and re-layouts: 11.8 us -> 11.5 us
  transfers between devices with their start and end apart: 46 -> 37, of which waited for: 17 -> 15; matrix products, arithmetic and copies ran while one was open for 3% -> 3% of each run, Pallas kernels for 15% -> 15%
where the time goes in v9:
time: 427 us; the launch traced here: 426 us
  waiting for transfers between devices  223 us (52%)
  starting transfers between devices  98.2 us (23%)
  Pallas kernels  72 us (17%)
  local copies, waits for them, and re-layouts  17.4 us (4%)
  blocking collectives  9.82 us (2%)
  other arithmetic  4.82 us (1%)
    ppermute x36, waiting for transfers between devices, swap(): lax.ppermute(x, axis, [(i, i ^ k) for i in range(lax.axis_size(axis))])  214 us
    ppermute x36, starting transfers between devices, swap(): lax.ppermute(x, axis, [(i, i ^ k) for i in range(lax.axis_size(axis))])  90.5 us
    pallas_call x6, Pallas kernels, chunk_step(): pl.pallas_call(functools.partial(chunk_kernel, pieces, block_cells, last)...  50.7 us
    pallas_call x6, Pallas kernels, pack(): pl.pallas_call(functools.partial(pack_kernel, parts, own, lanes), in_spec...  15.8 us
    unnamed x91, local copies, waits for them, and re-layouts  11.5 us
    all_to_all x1, blocking collectives, body(): back = lax.all_to_all(step, both, split_axis=0, concat_axis=0, tiled=True)  9.82 us
    all_to_all x1, waiting for transfers between devices, body(): got = lax.all_to_all(sent, both, split_axis=0, concat_axis=0, tiled=True)  8.99 us
  transfers between devices with their start and end apart: 37, of which 15 were waited for; matrix products, arithmetic and copies ran while one was open for 3% of the time, Pallas kernels for 15%

profile of v9, /device:TPU:0, one launch (start us, length us, event | category | flops | bytes accessed | tf_op | source)
XLA Modules:
  0.0 426.3 jit_solution(9509349158083946318)
XLA Ops:
  3.6 4.1 collective-permute-start
  11.1 11.7 %collective-permute-done.refs_0_.refs_1_ = f32[9,16,512]{2,1,0:T(8,128)S(1)} collective-permute-done((f32[9,16,512]{2,1,0:T(8,128)S(1)}, f32[9,16,512]{2,1,0:T(8,128)S(1)}, u32[]{:S(2)}, u32[]{:S(2)}) %collective-permute-start) | collective-permute-done | bytes 294944 | tf_op jit(solution)/shard_map/ppermute | solution.py:23
  22.8 4.4 %pack.7 = (f32[8,32,512]{2,1,0:T(8,128)S(1)}, f32[8,64,512]{2,1,0:T(8,128)}, f32[8,32,512]{2,1,0:T(8,128)S(1)}, f32[8,64,512]{2,1,0:T(8,128)}, f32[8,32,512]{2,1...) custom-call(s32[2]{0:T(128)S(1)} %pad_add_fusion.place_ref, f32[8,1024,512]{2,1,0:T(8,128)} %bitcast.17, ...), custom_call_target="tpu_custom_call" | custom-call | bytes 10485760 | tf_op jit(solution)/shard_map/pack/pallas_call | solution.py:100
  27.2 4.1 collective-permute-start.7
  31.3 5.5 %collective-permute-start.4 = (f32[9,16,512]{2,1,0:T(8,128)S(1)}, f32[9,16,512]{2,1,0:T(8,128)S(1)}, u32[]{:S(2)}, u32[]{:S(2)}) collective-permute-start(f32[9,16,512]{2,1,0:T(8,128)S(1)} %get-tuple-element.57), channel_id=1, source_target_pairs={{0,6},{1,7},{2,4},{3,5},{4,2},{5,3},{6,0},{7,1},{8,14},{9,15},{10,... | collective-permute-start | bytes 884744 | tf_op jit(solution)/shard_map/ppermute | solution.py:23
  41.3 14.7 %collective-permute-done.4.refs_4_.refs_5_ = f32[9,16,512]{2,1,0:T(8,128)S(1)} collective-permute-done((f32[9,16,512]{2,1,0:T(8,128)S(1)}, f32[9,16,512]{2,1,0:T(8,128)S(1)}, u32[]{:S(2)}, u32[]{:S(2)}) %collective-permute-start.4) | collective-permute-done | bytes 294944 | tf_op jit(solution)/shard_map/ppermute | solution.py:23
  56.0 38.9 %collective-permute-done.6.refs_6_.refs_7_ = f32[9,16,512]{2,1,0:T(8,128)S(1)} collective-permute-done((f32[9,16,512]{2,1,0:T(8,128)S(1)}, f32[9,16,512]{2,1,0:T(8,128)S(1)}, u32[]{:S(2)}, u32[]{:S(2)}) %collective-permute-start.6) | collective-permute-done | bytes 294944 | tf_op jit(solution)/shard_map/ppermute | solution.py:23
  98.0 6.0 %collective-permute-done.11.refs_0_.refs_1_ = f32[8,32,512]{2,1,0:T(8,128)S(1)} collective-permute-done((f32[8,32,512]{2,1,0:T(8,128)S(1)}, f32[8,32,512]{2,1,0:T(8,128)S(1)}, u32[]{:S(2)}, u32[]{:S(2)}) %collective-permute-start.11) | collective-permute-done | bytes 524320 | tf_op jit(solution)/shard_map/ppermute | solution.py:23
  108.9 5.1 %collective-permute-start.14 = (f32[8,64,512]{2,1,0:T(8,128)}, f32[8,64,512]{2,1,0:T(8,128)S(1)}, u32[]{:S(2)}, u32[]{:S(2)}) collective-permute-start(f32[8,64,512]{2,1,0:T(8,128)} %get-tuple-element.69), channel_id=1, source_target_pairs={{0,3},{1,2},{2,1},{3,0},{4,7},{5,6},{6,5},{7,4},{8,11},{9,10},{10,... | collective-permute-start | bytes 3145736 | tf_op jit(solution)/shard_map/ppermute | solution.py:23
  120.1 15.6 %collective-permute-done.12.refs_0_.refs_1_ = f32[8,32,512]{2,1,0:T(8,128)S(1)} collective-permute-done((f32[8,32,512]{2,1,0:T(8,128)S(1)}, f32[8,32,512]{2,1,0:T(8,128)S(1)}, u32[]{:S(2)}, u32[]{:S(2)}) %collective-permute-start.12) | collective-permute-done | bytes 524320 | tf_op jit(solution)/shard_map/ppermute | solution.py:23
  143.9 6.8 %chunk_step.6 = (f32[256,512]{1,0:T(8,128)}, f32[256,128]{1,0:T(8,128)S(1)}) custom-call(s32[2]{0:T(128)S(1)} %pad_add_fusion.place_ref, f32[8,1024,512]{2,1,0:T(8,128)} %bitcast.19, f32[9,16,512]{2,1,0:T(8,128)S(1)} %copy-done.1, f32[9,16,512]{2,1,0:T(8,128)S(1)} %copy-done.11, ...), custom_call_target="tpu_custom_call", output_to_operand_aliasing={{0}: (15, {}), {1}: (16, {})} | custom-call | flops 3221225472 | bytes 2097152 | tf_op jit(solution)/shard_map/chunk_step/pallas_call | solution.py:248
  153.9 27.5 %collective-permute-done.16.refs_5_ = f32[8,32,512]{2,1,0:T(8,128)} collective-permute-done((f32[8,32,512]{2,1,0:T(8,128)}, f32[8,32,512]{2,1,0:T(8,128)}, u32[]{:S(2)}, u32[]{:S(2)}) %collective-permute-start.16) | collective-permute-done | bytes 524320 | tf_op jit(solution)/shard_map/ppermute | solution.py:23
  182.8 5.9 %collective-permute-done.18.refs_7_ = f32[8,32,512]{2,1,0:T(8,128)} collective-permute-done((f32[8,32,512]{2,1,0:T(8,128)}, f32[8,32,512]{2,1,0:T(8,128)}, u32[]{:S(2)}, u32[]{:S(2)}) %collective-permute-start.18) | collective-permute-done | bytes 524320 | tf_op jit(solution)/shard_map/ppermute | solution.py:23
  188.7 3.4 collective-permute-start.21
  192.2 3.4 collective-permute-start.22
  195.6 20.0 %collective-permute-start.13 = (f32[8,24,512]{2,1,0:T(8,128)S(1)}, f32[8,24,512]{2,1,0:T(8,128)S(1)}, u32[]{:S(2)}, u32[]{:S(2)}) collective-permute-start(f32[8,24,512]{2,1,0:T(8,128)S(1)} %get-tuple-element.68), channel_id=1, source_target_pairs={{0,4},{1,5},{2,6},{3,7},{4,0},{5,1},{6,2},{7,3},{8,12},{9,13},{10,... | collective-permute-start | bytes 1179656 | tf_op jit(solution)/shard_map/ppermute | solution.py:23
  217.4 11.4 %chunk_step.7 = (f32[256,512]{1,0:T(8,128)}, f32[256,128]{1,0:T(8,128)S(1)}) custom-call(s32[2]{0:T(128)S(1)} %pad_add_fusion.place_ref, f32[8,1024,512]{2,1,0:T(8,128)} %bitcast.21, f32[8,32,512]{2,1,0:T(8,128)S(1)} %copy-done.7, f32[8,64,512]{2,1,0:T(8,128)S(1)} %collective-permute-done.14.refs_2_, ...), custom_call_target="tpu_custom_call", output_to_operand_aliasing={{0}: (15, {}), {1}: (16, {})} | custom-call | flops 6442450944 | bytes 4194304 | tf_op jit(solution)/shard_map/chunk_step/pallas_call | solution.py:248
  228.8 44.7 %collective-permute-done.13.refs_0_.refs_1_ = f32[8,24,512]{2,1,0:T(8,128)S(1)} collective-permute-done((f32[8,24,512]{2,1,0:T(8,128)S(1)}, f32[8,24,512]{2,1,0:T(8,128)S(1)}, u32[]{:S(2)}, u32[]{:S(2)}) %collective-permute-start.13) | collective-permute-done | bytes 393248 | tf_op jit(solution)/shard_map/ppermute | solution.py:23
  283.5 11.1 %collective-permute-done.19.refs_0_.refs_1_ = f32[8,16,512]{2,1,0:T(8,128)S(1)} collective-permute-done((f32[8,16,512]{2,1,0:T(8,128)S(1)}, f32[8,16,512]{2,1,0:T(8,128)S(1)}, u32[]{:S(2)}, u32[]{:S(2)}) %collective-permute-start.19) | collective-permute-done | bytes 262176 | tf_op jit(solution)/shard_map/ppermute | solution.py:23
  295.1 11.3 %chunk_step.8 = (f32[256,512]{1,0:T(8,128)}, f32[256,128]{1,0:T(8,128)S(1)}) custom-call(s32[2]{0:T(128)S(1)} %pad_add_fusion.place_ref, f32[8,1024,512]{2,1,0:T(8,128)} %bitcast.23, f32[8,32,512]{2,1,0:T(8,128)S(1)} %copy-done.5, f32[8,64,512]{2,1,0:T(8,128)S(1)} %collective-permute-done.14.refs_2_, ...), custom_call_target="tpu_custom_call", output_to_operand_aliasing={{0}: (15, {}), {1}: (16, {})} | custom-call | flops 6442450944 | bytes 4194304 | tf_op jit(solution)/shard_map/chunk_step/pallas_call | solution.py:248
  308.5 19.9 %collective-permute-done.34.refs_5_ = f32[8,24,512]{2,1,0:T(8,128)S(1)} collective-permute-done((f32[8,24,512]{2,1,0:T(8,128)S(1)}, f32[8,24,512]{2,1,0:T(8,128)S(1)}, u32[]{:S(2)}, u32[]{:S(2)}) %collective-permute-start.34) | collective-permute-done | bytes 393248 | tf_op jit(solution)/shard_map/ppermute | solution.py:23
  328.4 5.2 %collective-permute-start.30 = (f32[8,16,512]{2,1,0:T(8,128)S(1)}, f32[8,16,512]{2,1,0:T(8,128)S(1)}, u32[]{:S(2)}, u32[]{:S(2)}) collective-permute-start(f32[8,16,512]{2,1,0:T(8,128)S(1)} %copy-done.40), channel_id=1, source_target_pairs={{0,7},{1,6},{2,5},{3,4},{4,3},{5,2},{6,1},{7,0},{8,15},{9,14},{10,... | collective-permute-start | bytes 786440 | tf_op jit(solution)/shard_map/ppermute | solution.py:23
  336.9 4.4 %collective-permute-start.32 = (f32[8,16,512]{2,1,0:T(8,128)S(1)}, f32[8,16,512]{2,1,0:T(8,128)S(1)}, u32[]{:S(2)}, u32[]{:S(2)}) collective-permute-start(f32[8,16,512]{2,1,0:T(8,128)S(1)} %copy-done.36), channel_id=1, source_target_pairs={{0,5},{1,4},{2,7},{3,6},{4,1},{5,0},{6,3},{7,2},{8,13},{9,12},{10,... | collective-permute-start | bytes 786440 | tf_op jit(solution)/shard_map/ppermute | solution.py:23
  341.3 7.2 %collective-permute-done.26.refs_4_ = f32[8,48,512]{2,1,0:T(8,128)S(1)} collective-permute-done((f32[8,48,512]{2,1,0:T(8,128)S(1)}, f32[8,48,512]{2,1,0:T(8,128)S(1)}, u32[]{:S(2)}, u32[]{:S(2)}) %collective-permute-start.26) | collective-permute-done | bytes 786464 | tf_op jit(solution)/shard_map/ppermute | solution.py:23
  349.8 9.2 %chunk_step.9 = (f32[256,512]{1,0:T(8,128)}, f32[256,128]{1,0:T(8,128)S(1)}) custom-call(s32[2]{0:T(128)S(1)} %pad_add_fusion.place_ref, f32[8,1024,512]{2,1,0:T(8,128)} %bitcast.25, f32[8,24,512]{2,1,0:T(8,128)S(1)} %collective-permute-done.13.refs_0_.refs_1_, ...), custom_call_target="tpu_custom_call", output_to_operand_aliasing={{0}: (15, {}), {1}: (16, {})} | custom-call | flops 4831838208 | bytes 3145728 | tf_op jit(solution)/shard_map/chunk_step/pallas_call | solution.py:248
  361.1 10.4 %collective-permute-start.29 = (f32[8,8,512]{2,1,0:T(8,128)S(1)}, f32[8,8,512]{2,1,0:T(8,128)S(1)}, u32[]{:S(2)}, u32[]{:S(2)}) collective-permute-start(f32[8,8,512]{2,1,0:T(8,128)S(1)} %get-tuple-element.88), channel_id=1, source_target_pairs={{0,5},{1,4},{2,7},{3,6},{4,1},{5,0},{6,3},{7,2},{8,13},{9,12},{10,... | collective-permute-start | bytes 393224 | tf_op jit(solution)/shard_map/ppermute | solution.py:23
  371.8 6.8 %chunk_step.10 = (f32[256,512]{1,0:T(8,128)}, f32[256,128]{1,0:T(8,128)S(1)}) custom-call(s32[2]{0:T(128)S(1)} %pad_add_fusion.place_ref, f32[8,1024,512]{2,1,0:T(8,128)} %bitcast.26, f32[8,16,512]{2,1,0:T(8,128)S(1)} %collective-permute-done.19.refs_0_.refs_1_, ...), custom_call_target="tpu_custom_call", output_to_operand_aliasing={{0}: (15, {}), {1}: (16, {})} | custom-call | flops 3221225472 | bytes 2097152 | tf_op jit(solution)/shard_map/chunk_step/pallas_call | solution.py:248
  378.6 7.0 %collective-permute-done.29.refs_7_ = f32[8,8,512]{2,1,0:T(8,128)S(1)} collective-permute-done((f32[8,8,512]{2,1,0:T(8,128)S(1)}, f32[8,8,512]{2,1,0:T(8,128)S(1)}, u32[]{:S(2)}, u32[]{:S(2)}) %collective-permute-start.29) | collective-permute-done | bytes 131104 | tf_op jit(solution)/shard_map/ppermute | solution.py:23
  385.6 5.1 %chunk_step.11 = (f32[256,512]{1,0:T(8,128)}, f32[256,128]{1,0:T(8,128)S(1)}) custom-call(s32[2]{0:T(128)S(1)} %pad_add_fusion.place_ref, f32[8,1024,512]{2,1,0:T(8,128)} %bitcast.27, f32[8,8,512]{2,1,0:T(8,128)S(1)} %collective-permute-done.23.refs_1_, ...), custom_call_target="tpu_custom_call", output_to_operand_aliasing={{0}: (15, {}), {1}: (16, {})} | custom-call | flops 1610612736 | bytes 1048576 | tf_op jit(solution)/shard_map/chunk_step/pallas_call | solution.py:248
  390.7 7.7 %all-to-all-start = ((f32[32,8,512]{2,1,0:T(8,128)}), f32[32,8,512]{2,1,0:T(8,128)S(1)}, u32[]{:S(2)}, u32[]{:S(2)}) async-start(f32[32,8,512]{2,1,0:T(8,128)} %bitcast.11), calls=%async_computation | async-start | bytes 1048576 | tf_op jit(solution)/shard_map/all_to_all | solution.py:438
  405.8 9.0 %all-to-all-done.got_ref = f32[32,8,512]{2,1,0:T(8,128)S(1)} async-done(((f32[32,8,512]{2,1,0:T(8,128)}), f32[32,8,512]{2,1,0:T(8,128)S(1)}, u32[]{:S(2)}, u32[]{:S(2)}) %all-to-all-start) | async-done | bytes 524320 | tf_op jit(solution)/shard_map/all_to_all | solution.py:438
  415.6 9.8 %all_to_all.10.back_ref = f32[32,8,128]{2,1,0:T(8,128)S(1)} all-to-all(f32[32,8,128]{2,1,0:T(8,128)S(1)} %gradient_step.1), channel_id=1, replica_groups=mesh['tile'=4,'freq'=8] {'tile','freq'}, dimensions={0} | all-to-all | bytes 262144 | tf_op jit(solution)/shard_map/all_to_all | solution.py:441
  (171 shorter events, 67.7 us)
Async XLA Ops:
  7.7 29.0 %collective-permute-start.1 = (f32[9,16,512]{2,1,0:T(8,128)S(1)}, f32[9,16,512]{2,1,0:T(8,128)S(1)}, u32[]{:S(2)}, u32[]{:S(2)}) collective-permute-start(f32[9,16,512]{2,1,0:T(8,128)S(1)} %get-tuple-element.54), channel_id=1, source_target_pairs={{0,3},{1,2},{2,1},{3,0},{4,7},{5,6},{6,5},{7,4},{8,11},{9,10},{10,... | collective-permute-start | bytes 884744 | tf_op jit(solution)/shard_map/ppermute | solution.py:23
  10.2 26.5 %collective-permute-start.2 = (f32[9,16,512]{2,1,0:T(8,128)S(1)}, f32[9,16,512]{2,1,0:T(8,128)S(1)}, u32[]{:S(2)}, u32[]{:S(2)}) collective-permute-start(f32[9,16,512]{2,1,0:T(8,128)S(1)} %get-tuple-element.55), channel_id=1, source_target_pairs={{0,7},{1,6},{2,5},{3,4},{4,3},{5,2},{6,1},{7,0},{8,15},{9,14},{10,... | collective-permute-start | bytes 884744 | tf_op jit(solution)/shard_map/ppermute | solution.py:23
  10.3 28.3 %collective-permute-start.3 = (f32[9,16,512]{2,1,0:T(8,128)S(1)}, f32[9,16,512]{2,1,0:T(8,128)S(1)}, u32[]{:S(2)}, u32[]{:S(2)}) collective-permute-start(f32[9,16,512]{2,1,0:T(8,128)S(1)} %get-tuple-element.56), channel_id=1, source_target_pairs={{0,2},{1,3},{2,0},{3,1},{4,6},{5,7},{6,4},{7,5},{8,10},{9,11},{10,... | collective-permute-start | bytes 884744 | tf_op jit(solution)/shard_map/ppermute | solution.py:23
  27.2 67.7 %collective-permute-start.7 = (f32[8,32,512]{2,1,0:T(8,128)S(1)}, f32[8,32,512]{2,1,0:T(8,128)S(1)}, u32[]{:S(2)}, u32[]{:S(2)}) collective-permute-start(f32[8,32,512]{2,1,0:T(8,128)S(1)} %get-tuple-element.60), channel_id=1, source_target_pairs={{0,7},{1,6},{2,5},{3,4},{4,3},{5,2},{6,1},{7,0},{8,15},{9,14},{10,... | collective-permute-start | bytes 1572872 | tf_op jit(solution)/shard_map/ppermute | solution.py:23
  31.3 24.7 %collective-permute-start.4 = (f32[9,16,512]{2,1,0:T(8,128)S(1)}, f32[9,16,512]{2,1,0:T(8,128)S(1)}, u32[]{:S(2)}, u32[]{:S(2)}) collective-permute-start(f32[9,16,512]{2,1,0:T(8,128)S(1)} %get-tuple-element.57), channel_id=1, source_target_pairs={{0,6},{1,7},{2,4},{3,5},{4,2},{5,3},{6,0},{7,1},{8,14},{9,15},{10,... | collective-permute-start | bytes 884744 | tf_op jit(solution)/shard_map/ppermute | solution.py:23
  36.8 19.2 %collective-permute-start.5 = (f32[9,16,512]{2,1,0:T(8,128)S(1)}, f32[9,16,512]{2,1,0:T(8,128)S(1)}, u32[]{:S(2)}, u32[]{:S(2)}) collective-permute-start(f32[9,16,512]{2,1,0:T(8,128)S(1)} %get-tuple-element.58), channel_id=1, source_target_pairs={{0,1},{1,0},{2,3},{3,2},{4,5},{5,4},{6,7},{7,6},{8,9},{9,8},{10,11... | collective-permute-start | bytes 884744 | tf_op jit(solution)/shard_map/ppermute | solution.py:23
  36.8 58.1 %collective-permute-start.6 = (f32[9,16,512]{2,1,0:T(8,128)S(1)}, f32[9,16,512]{2,1,0:T(8,128)S(1)}, u32[]{:S(2)}, u32[]{:S(2)}) collective-permute-start(f32[9,16,512]{2,1,0:T(8,128)S(1)} %get-tuple-element.59), channel_id=1, source_target_pairs={{0,5},{1,4},{2,7},{3,6},{4,1},{5,0},{6,3},{7,2},{8,13},{9,12},{10,... | collective-permute-start | bytes 884744 | tf_op jit(solution)/shard_map/ppermute | solution.py:23
  38.6 65.4 %collective-permute-start.11 = (f32[8,32,512]{2,1,0:T(8,128)S(1)}, f32[8,32,512]{2,1,0:T(8,128)S(1)}, u32[]{:S(2)}, u32[]{:S(2)}) collective-permute-start(f32[8,32,512]{2,1,0:T(8,128)S(1)} %get-tuple-element.61), channel_id=1, source_target_pairs={{0,4},{1,5},{2,6},{3,7},{4,0},{5,1},{6,2},{7,3},{8,12},{9,13},{10,... | collective-permute-start | bytes 1572872 | tf_op jit(solution)/shard_map/ppermute | solution.py:23
  108.7 27.0 %collective-permute-start.12 = (f32[8,32,512]{2,1,0:T(8,128)S(1)}, f32[8,32,512]{2,1,0:T(8,128)S(1)}, u32[]{:S(2)}, u32[]{:S(2)}) collective-permute-start(f32[8,32,512]{2,1,0:T(8,128)S(1)} %get-tuple-element.62), channel_id=1, source_target_pairs={{0,4},{1,5},{2,6},{3,7},{4,0},{5,1},{6,2},{7,3},{8,12},{9,13},{10,... | collective-permute-start | bytes 1572872 | tf_op jit(solution)/shard_map/ppermute | solution.py:23
  108.9 83.3 %collective-permute-start.14 = (f32[8,64,512]{2,1,0:T(8,128)}, f32[8,64,512]{2,1,0:T(8,128)S(1)}, u32[]{:S(2)}, u32[]{:S(2)}) collective-permute-start(f32[8,64,512]{2,1,0:T(8,128)} %get-tuple-element.69), channel_id=1, source_target_pairs={{0,3},{1,2},{2,1},{3,0},{4,7},{5,6},{6,5},{7,4},{8,11},{9,10},{10,... | collective-permute-start | bytes 3145736 | tf_op jit(solution)/shard_map/ppermute | solution.py:23
  114.0 81.6 %collective-permute-start.15 = (f32[8,64,512]{2,1,0:T(8,128)}, f32[8,64,512]{2,1,0:T(8,128)S(1)}, u32[]{:S(2)}, u32[]{:S(2)}) collective-permute-start(f32[8,64,512]{2,1,0:T(8,128)} %get-tuple-element.70), channel_id=1, source_target_pairs={{0,2},{1,3},{2,0},{3,1},{4,6},{5,7},{6,4},{7,5},{8,10},{9,11},{10,... | collective-permute-start | bytes 3145736 | tf_op jit(solution)/shard_map/ppermute | solution.py:23
  114.7 100.9 %collective-permute-start.17 = (f32[8,64,512]{2,1,0:T(8,128)}, f32[8,64,512]{2,1,0:T(8,128)S(1)}, u32[]{:S(2)}, u32[]{:S(2)}) collective-permute-start(f32[8,64,512]{2,1,0:T(8,128)} %get-tuple-element.72), channel_id=1, source_target_pairs={{0,1},{1,0},{2,3},{3,2},{4,5},{5,4},{6,7},{7,6},{8,9},{9,8},{10,11... | collective-permute-start | bytes 3145736 | tf_op jit(solution)/shard_map/ppermute | solution.py:23
  118.8 62.6 %collective-permute-start.16 = (f32[8,32,512]{2,1,0:T(8,128)}, f32[8,32,512]{2,1,0:T(8,128)}, u32[]{:S(2)}, u32[]{:S(2)}) collective-permute-start(f32[8,32,512]{2,1,0:T(8,128)} %get-tuple-element.71), channel_id=1, source_target_pairs={{0,6},{1,7},{2,4},{3,5},{4,2},{5,3},{6,0},{7,1},{8,14},{9,15},{10,... | collective-permute-start | bytes 1572872 | tf_op jit(solution)/shard_map/ppermute | solution.py:23
  136.6 52.1 %collective-permute-start.18 = (f32[8,32,512]{2,1,0:T(8,128)}, f32[8,32,512]{2,1,0:T(8,128)}, u32[]{:S(2)}, u32[]{:S(2)}) collective-permute-start(f32[8,32,512]{2,1,0:T(8,128)} %get-tuple-element.73), channel_id=1, source_target_pairs={{0,5},{1,4},{2,7},{3,6},{4,1},{5,0},{6,3},{7,2},{8,13},{9,12},{10,... | collective-permute-start | bytes 1572872 | tf_op jit(solution)/shard_map/ppermute | solution.py:23
  181.4 96.1 %collective-permute-start.20 = (f32[8,32,512]{2,1,0:T(8,128)S(1)}, f32[8,32,512]{2,1,0:T(8,128)S(1)}, u32[]{:S(2)}, u32[]{:S(2)}) collective-permute-start(f32[8,32,512]{2,1,0:T(8,128)S(1)} %copy-done.28), channel_id=1, source_target_pairs={{0,7},{1,6},{2,5},{3,4},{4,3},{5,2},{6,1},{7,0},{8,15},{9,14},{10,... | collective-permute-start | bytes 1572872 | tf_op jit(solution)/shard_map/ppermute | solution.py:23
  188.7 89.6 %collective-permute-start.21 = (f32[8,32,512]{2,1,0:T(8,128)S(1)}, f32[8,32,512]{2,1,0:T(8,128)S(1)}, u32[]{:S(2)}, u32[]{:S(2)}) collective-permute-start(f32[8,32,512]{2,1,0:T(8,128)S(1)} %copy-done.26), channel_id=1, source_target_pairs={{0,6},{1,7},{2,4},{3,5},{4,2},{5,3},{6,0},{7,1},{8,14},{9,15},{10,... | collective-permute-start | bytes 1572872 | tf_op jit(solution)/shard_map/ppermute | solution.py:23
  192.2 88.3 %collective-permute-start.22 = (f32[8,32,512]{2,1,0:T(8,128)S(1)}, f32[8,32,512]{2,1,0:T(8,128)S(1)}, u32[]{:S(2)}, u32[]{:S(2)}) collective-permute-start(f32[8,32,512]{2,1,0:T(8,128)S(1)} %copy-done.24), channel_id=1, source_target_pairs={{0,5},{1,4},{2,7},{3,6},{4,1},{5,0},{6,3},{7,2},{8,13},{9,12},{10,... | collective-permute-start | bytes 1572872 | tf_op jit(solution)/shard_map/ppermute | solution.py:23
  195.6 77.9 %collective-permute-start.13 = (f32[8,24,512]{2,1,0:T(8,128)S(1)}, f32[8,24,512]{2,1,0:T(8,128)S(1)}, u32[]{:S(2)}, u32[]{:S(2)}) collective-permute-start(f32[8,24,512]{2,1,0:T(8,128)S(1)} %get-tuple-element.68), channel_id=1, source_target_pairs={{0,4},{1,5},{2,6},{3,7},{4,0},{5,1},{6,2},{7,3},{8,12},{9,13},{10,... | collective-permute-start | bytes 1179656 | tf_op jit(solution)/shard_map/ppermute | solution.py:23
  215.6 65.4 %collective-permute-start.33 = (f32[8,24,512]{2,1,0:T(8,128)S(1)}, f32[8,24,512]{2,1,0:T(8,128)S(1)}, u32[]{:S(2)}, u32[]{:S(2)}) collective-permute-start(f32[8,24,512]{2,1,0:T(8,128)S(1)} %get-tuple-element.92), channel_id=1, source_target_pairs={{0,7},{1,6},{2,5},{3,4},{4,3},{5,2},{6,1},{7,0},{8,15},{9,14},{10,... | collective-permute-start | bytes 1179656 | tf_op jit(solution)/shard_map/ppermute | solution.py:23
  277.5 59.4 %collective-permute-start.24 = (f32[8,48,512]{2,1,0:T(8,128)S(1)}, f32[8,48,512]{2,1,0:T(8,128)S(1)}, u32[]{:S(2)}, u32[]{:S(2)}) collective-permute-start(f32[8,48,512]{2,1,0:T(8,128)S(1)} %get-tuple-element.83), channel_id=1, source_target_pairs={{0,3},{1,2},{2,1},{3,0},{4,7},{5,6},{6,5},{7,4},{8,11},{9,10},{10,... | collective-permute-start | bytes 2359304 | tf_op jit(solution)/shard_map/ppermute | solution.py:23
  278.3 70.1 %collective-permute-start.26 = (f32[8,48,512]{2,1,0:T(8,128)S(1)}, f32[8,48,512]{2,1,0:T(8,128)S(1)}, u32[]{:S(2)}, u32[]{:S(2)}) collective-permute-start(f32[8,48,512]{2,1,0:T(8,128)S(1)} %get-tuple-element.85), channel_id=1, source_target_pairs={{0,2},{1,3},{2,0},{3,1},{4,6},{5,7},{6,4},{7,5},{8,10},{9,11},{10,... | collective-permute-start | bytes 2359304 | tf_op jit(solution)/shard_map/ppermute | solution.py:23
  280.5 68.0 %collective-permute-start.28 = (f32[8,48,512]{2,1,0:T(8,128)S(1)}, f32[8,48,512]{2,1,0:T(8,128)S(1)}, u32[]{:S(2)}, u32[]{:S(2)}) collective-permute-start(f32[8,48,512]{2,1,0:T(8,128)S(1)} %get-tuple-element.87), channel_id=1, source_target_pairs={{0,1},{1,0},{2,3},{3,2},{4,5},{5,4},{6,7},{7,6},{8,9},{9,8},{10,11... | collective-permute-start | bytes 2359304 | tf_op jit(solution)/shard_map/ppermute | solution.py:23
  281.0 47.4 %collective-permute-start.34 = (f32[8,24,512]{2,1,0:T(8,128)S(1)}, f32[8,24,512]{2,1,0:T(8,128)S(1)}, u32[]{:S(2)}, u32[]{:S(2)}) collective-permute-start(f32[8,24,512]{2,1,0:T(8,128)S(1)} %get-tuple-element.93), channel_id=1, source_target_pairs={{0,6},{1,7},{2,4},{3,5},{4,2},{5,3},{6,0},{7,1},{8,14},{9,15},{10,... | collective-permute-start | bytes 1179656 | tf_op jit(solution)/shard_map/ppermute | solution.py:23
  294.6 42.3 %collective-permute-start.35 = (f32[8,24,512]{2,1,0:T(8,128)S(1)}, f32[8,24,512]{2,1,0:T(8,128)S(1)}, u32[]{:S(2)}, u32[]{:S(2)}) collective-permute-start(f32[8,24,512]{2,1,0:T(8,128)S(1)} %get-tuple-element.94), channel_id=1, source_target_pairs={{0,5},{1,4},{2,7},{3,6},{4,1},{5,0},{6,3},{7,2},{8,13},{9,12},{10,... | collective-permute-start | bytes 1179656 | tf_op jit(solution)/shard_map/ppermute | solution.py:23
  328.4 30.6 %collective-permute-start.30 = (f32[8,16,512]{2,1,0:T(8,128)S(1)}, f32[8,16,512]{2,1,0:T(8,128)S(1)}, u32[]{:S(2)}, u32[]{:S(2)}) collective-permute-start(f32[8,16,512]{2,1,0:T(8,128)S(1)} %copy-done.40), channel_id=1, source_target_pairs={{0,7},{1,6},{2,5},{3,4},{4,3},{5,2},{6,1},{7,0},{8,15},{9,14},{10,... | collective-permute-start | bytes 786440 | tf_op jit(solution)/shard_map/ppermute | solution.py:23
  336.9 24.2 %collective-permute-start.31 = (f32[8,16,512]{2,1,0:T(8,128)S(1)}, f32[8,16,512]{2,1,0:T(8,128)S(1)}, u32[]{:S(2)}, u32[]{:S(2)}) collective-permute-start(f32[8,16,512]{2,1,0:T(8,128)S(1)} %copy-done.38), channel_id=1, source_target_pairs={{0,6},{1,7},{2,4},{3,5},{4,2},{5,3},{6,0},{7,1},{8,14},{9,15},{10,... | collective-permute-start | bytes 786440 | tf_op jit(solution)/shard_map/ppermute | solution.py:23
  336.9 34.9 %collective-permute-start.32 = (f32[8,16,512]{2,1,0:T(8,128)S(1)}, f32[8,16,512]{2,1,0:T(8,128)S(1)}, u32[]{:S(2)}, u32[]{:S(2)}) collective-permute-start(f32[8,16,512]{2,1,0:T(8,128)S(1)} %copy-done.36), channel_id=1, source_target_pairs={{0,5},{1,4},{2,7},{3,6},{4,1},{5,0},{6,3},{7,2},{8,13},{9,12},{10,... | collective-permute-start | bytes 786440 | tf_op jit(solution)/shard_map/ppermute | solution.py:23
  348.5 30.1 %collective-permute-start.23 = (f32[8,8,512]{2,1,0:T(8,128)S(1)}, f32[8,8,512]{2,1,0:T(8,128)S(1)}, u32[]{:S(2)}, u32[]{:S(2)}) collective-permute-start(f32[8,8,512]{2,1,0:T(8,128)S(1)} %get-tuple-element.82), channel_id=1, source_target_pairs={{0,4},{1,5},{2,6},{3,7},{4,0},{5,1},{6,2},{7,3},{8,12},{9,13},{10,... | collective-permute-start | bytes 393224 | tf_op jit(solution)/shard_map/ppermute | solution.py:23
  348.5 30.1 %collective-permute-start.25 = (f32[8,8,512]{2,1,0:T(8,128)S(1)}, f32[8,8,512]{2,1,0:T(8,128)S(1)}, u32[]{:S(2)}, u32[]{:S(2)}) collective-permute-start(f32[8,8,512]{2,1,0:T(8,128)S(1)} %get-tuple-element.84), channel_id=1, source_target_pairs={{0,7},{1,6},{2,5},{3,4},{4,3},{5,2},{6,1},{7,0},{8,15},{9,14},{10,... | collective-permute-start | bytes 393224 | tf_op jit(solution)/shard_map/ppermute | solution.py:23
  359.0 19.6 %collective-permute-start.27 = (f32[8,8,512]{2,1,0:T(8,128)S(1)}, f32[8,8,512]{2,1,0:T(8,128)S(1)}, u32[]{:S(2)}, u32[]{:S(2)}) collective-permute-start(f32[8,8,512]{2,1,0:T(8,128)S(1)} %get-tuple-element.86), channel_id=1, source_target_pairs={{0,6},{1,7},{2,4},{3,5},{4,2},{5,3},{6,0},{7,1},{8,14},{9,15},{10,... | collective-permute-start | bytes 393224 | tf_op jit(solution)/shard_map/ppermute | solution.py:23
  361.1 24.5 %collective-permute-start.29 = (f32[8,8,512]{2,1,0:T(8,128)S(1)}, f32[8,8,512]{2,1,0:T(8,128)S(1)}, u32[]{:S(2)}, u32[]{:S(2)}) collective-permute-start(f32[8,8,512]{2,1,0:T(8,128)S(1)} %get-tuple-element.88), channel_id=1, source_target_pairs={{0,5},{1,4},{2,7},{3,6},{4,1},{5,0},{6,3},{7,2},{8,13},{9,12},{10,... | collective-permute-start | bytes 393224 | tf_op jit(solution)/shard_map/ppermute | solution.py:23
  390.7 24.0 %all-to-all-start = ((f32[32,8,512]{2,1,0:T(8,128)}), f32[32,8,512]{2,1,0:T(8,128)S(1)}, u32[]{:S(2)}, u32[]{:S(2)}) async-start(f32[32,8,512]{2,1,0:T(8,128)} %bitcast.11), calls=%async_computation | async-start | bytes 1048576 | tf_op jit(solution)/shard_map/all_to_all | solution.py:438
  (50 other events, 1099.1 us)

commit v10 on v9

--- a/solution.py
+++ b/solution.py
@@ -386,13 +386,14 @@
     distances = partner_order(owners)
     partners = [0] + distances
     received, offsets, done = [], [], []
-    batches = [i for i in (0, 1, 3) if i < len(sizes)]
+    batches = list(range(max(1, len(sizes) - 1)))
     near_by = {}
 
     def send(i):
         after = [received[i - 1][distances[0]]] if i else []
         if i > 2:
-            after = after + done[i - 3 : i - 2]
+            behind = min(i - 2, len(sizes) - 4)
+            after = after + done[behind : behind + 1]
         batch = max(b for b in batches if b <= i)
         end = starts[min([b for b in batches if b > i] + [len(starts)])] if batch != batches[-1] else own // GROUP
         parts = []
@@ -410,7 +411,7 @@
     send(0)
     send(1)
     near = near_models(
-        place, cell_index, models, [received[0][k] for k in distances], received[1][distances[2]], sizes[0] * GROUP, lanes
+        place, cell_index, models, [received[0][k] for k in distances], received[0][distances[0]], sizes[0] * GROUP, lanes
     )
     blocks = [near] + [swap(near, "tile", k) for k in range(1, tiles)]
     borrowed = jnp.stack([b[block_cells, 0] for b in blocks]).astype(jnp.int32)

time: 427 us -> 424 us (level)
  waiting for transfers between devices: 223 us -> 173 us
  starting transfers between devices: 98.2 us -> 147 us
    ppermute x36 -> x42, starting transfers between devices: 90.5 us -> 143 us  [swap(): lax.ppermute(x, axis, [(i, i ^ k) for i in range(lax.axis_size(axis))])]
    ppermute x36 -> x42, waiting for transfers between devices: 214 us -> 164 us  [swap(): lax.ppermute(x, axis, [(i, i ^ k) for i in range(lax.axis_size(axis))])]
    unnamed x91 -> x47, local copies, waits for them, and re-layouts: 11.5 us -> 9.24 us
  transfers between devices with their start and end apart: 37 -> 43, of which waited for: 15 -> 15; matrix products, arithmetic and copies ran while one was open for 3% -> 3% of each run, Pallas kernels for 15% -> 15%
where the time goes in v10:
time: 424 us; the launch traced here: 423 us
  waiting for transfers between devices  173 us (41%)
  starting transfers between devices  147 us (35%)
  Pallas kernels  71.8 us (17%)
  local copies, waits for them, and re-layouts  15.3 us (4%)
  blocking collectives  9.82 us (2%)
  other arithmetic  4.85 us (1%)
    ppermute x42, waiting for transfers between devices, swap(): lax.ppermute(x, axis, [(i, i ^ k) for i in range(lax.axis_size(axis))])  164 us
    ppermute x42, starting transfers between devices, swap(): lax.ppermute(x, axis, [(i, i ^ k) for i in range(lax.axis_size(axis))])  143 us
    pallas_call x6, Pallas kernels, chunk_step(): pl.pallas_call(functools.partial(chunk_kernel, pieces, block_cells, last)...  50.9 us
    pallas_call x6, Pallas kernels, pack(): pl.pallas_call(functools.partial(pack_kernel, parts, own, lanes), in_spec...  16.1 us
    all_to_all x1, blocking collectives, body(): back = lax.all_to_all(step, both, split_axis=0, concat_axis=0, tiled=True)  9.82 us
    unnamed x47, local copies, waits for them, and re-layouts  9.24 us
    all_to_all x1, waiting for transfers between devices, body(): got = lax.all_to_all(sent, both, split_axis=0, concat_axis=0, tiled=True)  8.88 us
  transfers between devices with their start and end apart: 43, of which 15 were waited for; matrix products, arithmetic and copies ran while one was open for 3% of the time, Pallas kernels for 15%

profile of v10, /device:TPU:0, one launch (start us, length us, event | category | flops | bytes accessed | tf_op | source)
XLA Modules:
  0.0 423.1 jit_solution(17078637265458713993)
XLA Ops:
  3.6 4.1 collective-permute-start
  14.1 8.7 %collective-permute-done.refs_0_.refs_7_.refs_1_ = f32[9,16,512]{2,1,0:T(8,128)S(1)} collective-permute-done((f32[9,16,512]{2,1,0:T(8,128)S(1)}, f32[9,16,512]{2,1,0:T(8,128)S(1)}, u32[]{:S(2)}, u32[]{:S(2)}) %collective-permute-start) | collective-permute-done | bytes 294944 | tf_op jit(solution)/shard_map/ppermute | solution.py:23
  22.8 6.3 %collective-permute-start.5 = (f32[9,16,512]{2,1,0:T(8,128)S(1)}, f32[9,16,512]{2,1,0:T(8,128)S(1)}, u32[]{:S(2)}, u32[]{:S(2)}) collective-permute-start(f32[9,16,512]{2,1,0:T(8,128)S(1)} %get-tuple-element.64), channel_id=1, source_target_pairs={{0,1},{1,0},{2,3},{3,2},{4,5},{5,4},{6,7},{7,6},{8,9},{9,8},{10,11... | collective-permute-start | bytes 884744 | tf_op jit(solution)/shard_map/ppermute | solution.py:23
  29.6 3.6 pack.7
  33.3 5.3 %collective-permute-start.10 = (f32[8,32,512]{2,1,0:T(8,128)}, f32[8,32,512]{2,1,0:T(8,128)S(1)}, u32[]{:S(2)}, u32[]{:S(2)}) collective-permute-start(f32[8,32,512]{2,1,0:T(8,128)} %get-tuple-element.66), channel_id=1, source_target_pairs={{0,4},{1,5},{2,6},{3,7},{4,0},{5,1},{6,2},{7,3},{8,12},{9,13},{10,... | collective-permute-start | bytes 1572872 | tf_op jit(solution)/shard_map/ppermute | solution.py:23
  38.6 3.7 collective-permute-done.4.refs_4_.refs_5_
  42.4 30.0 %collective-permute-done.6.refs_6_.refs_7_ = f32[9,16,512]{2,1,0:T(8,128)S(1)} collective-permute-done((f32[9,16,512]{2,1,0:T(8,128)S(1)}, f32[9,16,512]{2,1,0:T(8,128)S(1)}, u32[]{:S(2)}, u32[]{:S(2)}) %collective-permute-start.6) | collective-permute-done | bytes 294944 | tf_op jit(solution)/shard_map/ppermute | solution.py:23
  97.0 8.2 %collective-permute-done.12.refs_2_ = f32[8,32,512]{2,1,0:T(8,128)} collective-permute-done((f32[8,32,512]{2,1,0:T(8,128)}, f32[8,32,512]{2,1,0:T(8,128)}, u32[]{:S(2)}, u32[]{:S(2)}) %collective-permute-start.12) | collective-permute-done | bytes 524320 | tf_op jit(solution)/shard_map/ppermute | solution.py:23
  106.7 5.1 %collective-permute-start.11 = (f32[8,32,512]{2,1,0:T(8,128)}, f32[8,32,512]{2,1,0:T(8,128)S(1)}, u32[]{:S(2)}, u32[]{:S(2)}) collective-permute-start(f32[8,32,512]{2,1,0:T(8,128)} %get-tuple-element.67), channel_id=1, source_target_pairs={{0,4},{1,5},{2,6},{3,7},{4,0},{5,1},{6,2},{7,3},{8,12},{9,13},{10,... | collective-permute-start | bytes 1572872 | tf_op jit(solution)/shard_map/ppermute | solution.py:23
  115.3 11.7 %collective-permute-start.19 = (f32[8,32,512]{2,1,0:T(8,128)}, f32[8,32,512]{2,1,0:T(8,128)}, u32[]{:S(2)}, u32[]{:S(2)}) collective-permute-start(f32[8,32,512]{2,1,0:T(8,128)} %get-tuple-element.82), channel_id=1, source_target_pairs={{0,3},{1,2},{2,1},{3,0},{4,7},{5,6},{6,5},{7,4},{8,11},{9,10},{10,... | collective-permute-start | bytes 1572872 | tf_op jit(solution)/shard_map/ppermute | solution.py:23
  133.7 7.0 %chunk_step.6 = (f32[256,512]{1,0:T(8,128)}, f32[256,128]{1,0:T(8,128)S(1)}) custom-call(s32[2]{0:T(128)S(1)} %pad_add_fusion.place_ref, f32[8,1024,512]{2,1,0:T(8,128)} %bitcast.19, f32[9,16,512]{2,1,0:T(8,128)S(1)} %collective-permute-done.refs_0_.refs_7_.refs_1_, ...), custom_call_target="tpu_custom_call", output_to_operand_aliasing={{0}: (15, {}), {1}: (16, {})} | custom-call | flops 3221225472 | bytes 2097152 | tf_op jit(solution)/shard_map/chunk_step/pallas_call | solution.py:248
  140.6 4.1 collective-permute-start.20
  144.7 12.6 %collective-permute-start.21 = (f32[8,32,512]{2,1,0:T(8,128)S(1)}, f32[8,32,512]{2,1,0:T(8,128)S(1)}, u32[]{:S(2)}, u32[]{:S(2)}) collective-permute-start(f32[8,32,512]{2,1,0:T(8,128)S(1)} %copy-done.12), channel_id=1, source_target_pairs={{0,2},{1,3},{2,0},{3,1},{4,6},{5,7},{6,4},{7,5},{8,10},{9,11},{10,... | collective-permute-start | bytes 1572872 | tf_op jit(solution)/shard_map/ppermute | solution.py:23
  157.3 21.1 %collective-permute-done.17.refs_7_ = f32[8,32,512]{2,1,0:T(8,128)} collective-permute-done((f32[8,32,512]{2,1,0:T(8,128)}, f32[8,32,512]{2,1,0:T(8,128)}, u32[]{:S(2)}, u32[]{:S(2)}) %collective-permute-start.17) | collective-permute-done | bytes 524320 | tf_op jit(solution)/shard_map/ppermute | solution.py:23
  180.2 20.2 %collective-permute-done.11.refs_0_.refs_1_ = f32[8,32,512]{2,1,0:T(8,128)S(1)} collective-permute-done((f32[8,32,512]{2,1,0:T(8,128)}, f32[8,32,512]{2,1,0:T(8,128)S(1)}, u32[]{:S(2)}, u32[]{:S(2)}) %collective-permute-start.11) | collective-permute-done | bytes 524320 | tf_op jit(solution)/shard_map/ppermute | solution.py:23
  201.5 11.5 %chunk_step.7 = (f32[256,512]{1,0:T(8,128)}, f32[256,128]{1,0:T(8,128)S(1)}) custom-call(s32[2]{0:T(128)S(1)} %pad_add_fusion.place_ref, f32[8,1024,512]{2,1,0:T(8,128)} %bitcast.20, f32[8,32,512]{2,1,0:T(8,128)S(1)} %collective-permute-done.10.refs_0_.refs_1_, ...), custom_call_target="tpu_custom_call", output_to_operand_aliasing={{0}: (15, {}), {1}: (16, {})} | custom-call | flops 6442450944 | bytes 4194304 | tf_op jit(solution)/shard_map/chunk_step/pallas_call | solution.py:248
  216.0 8.1 %collective-permute-start.18 = (f32[8,24,512]{2,1,0:T(8,128)S(1)}, f32[8,24,512]{2,1,0:T(8,128)S(1)}, u32[]{:S(2)}, u32[]{:S(2)}) collective-permute-start(f32[8,24,512]{2,1,0:T(8,128)S(1)} %get-tuple-element.81), channel_id=1, source_target_pairs={{0,4},{1,5},{2,6},{3,7},{4,0},{5,1},{6,2},{7,3},{8,12},{9,13},{10,... | collective-permute-start | bytes 1179656 | tf_op jit(solution)/shard_map/ppermute | solution.py:23
  226.8 35.7 %collective-permute-done.24.refs_7_ = f32[8,32,512]{2,1,0:T(8,128)S(1)} collective-permute-done((f32[8,32,512]{2,1,0:T(8,128)S(1)}, f32[8,32,512]{2,1,0:T(8,128)S(1)}, u32[]{:S(2)}, u32[]{:S(2)}) %collective-permute-start.24) | collective-permute-done | bytes 524320 | tf_op jit(solution)/shard_map/ppermute | solution.py:23
  262.5 11.3 %chunk_step.8 = (f32[256,512]{1,0:T(8,128)}, f32[256,128]{1,0:T(8,128)S(1)}) custom-call(s32[2]{0:T(128)S(1)} %pad_add_fusion.place_ref, f32[8,1024,512]{2,1,0:T(8,128)} %bitcast.22, f32[8,32,512]{2,1,0:T(8,128)S(1)} %collective-permute-done.11.refs_0_.refs_1_, ...), custom_call_target="tpu_custom_call", output_to_operand_aliasing={{0}: (15, {}), {1}: (16, {})} | custom-call | flops 6442450944 | bytes 4194304 | tf_op jit(solution)/shard_map/chunk_step/pallas_call | solution.py:248
  281.8 4.9 %collective-permute-start.41 = (f32[8,24,512]{2,1,0:T(8,128)S(1)}, f32[8,24,512]{2,1,0:T(8,128)S(1)}, u32[]{:S(2)}, u32[]{:S(2)}) collective-permute-start(f32[8,24,512]{2,1,0:T(8,128)S(1)} %get-tuple-element.106), channel_id=1, source_target_pairs={{0,5},{1,4},{2,7},{3,6},{4,1},{5,0},{6,3},{7,2},{8,13},{9,12},{10,... | collective-permute-start | bytes 1179656 | tf_op jit(solution)/shard_map/ppermute | solution.py:23
  295.1 8.0 %collective-permute-start.34 = (f32[8,16,512]{2,1,0:T(8,128)S(1)}, f32[8,16,512]{2,1,0:T(8,128)S(1)}, u32[]{:S(2)}, u32[]{:S(2)}) collective-permute-start(f32[8,16,512]{2,1,0:T(8,128)S(1)} %get-tuple-element.99), channel_id=1, source_target_pairs={{0,6},{1,7},{2,4},{3,5},{4,2},{5,3},{6,0},{7,1},{8,14},{9,15},{10,... | collective-permute-start | bytes 786440 | tf_op jit(solution)/shard_map/ppermute | solution.py:23
  303.1 25.0 %collective-permute-start.35 = (f32[8,16,512]{2,1,0:T(8,128)S(1)}, f32[8,16,512]{2,1,0:T(8,128)S(1)}, u32[]{:S(2)}, u32[]{:S(2)}) collective-permute-start(f32[8,16,512]{2,1,0:T(8,128)S(1)} %get-tuple-element.100), channel_id=1, source_target_pairs={{0,5},{1,4},{2,7},{3,6},{4,1},{5,0},{6,3},{7,2},{8,13},{9,12},{10,... | collective-permute-start | bytes 786440 | tf_op jit(solution)/shard_map/ppermute | solution.py:23
  328.2 13.5 %collective-permute-done.41.refs_7_ = f32[8,24,512]{2,1,0:T(8,128)S(1)} collective-permute-done((f32[8,24,512]{2,1,0:T(8,128)S(1)}, f32[8,24,512]{2,1,0:T(8,128)S(1)}, u32[]{:S(2)}, u32[]{:S(2)}) %collective-permute-start.41) | collective-permute-done | bytes 393248 | tf_op jit(solution)/shard_map/ppermute | solution.py:23
  342.3 9.2 %chunk_step.9 = (f32[256,512]{1,0:T(8,128)}, f32[256,128]{1,0:T(8,128)S(1)}) custom-call(s32[2]{0:T(128)S(1)} %pad_add_fusion.place_ref, f32[8,1024,512]{2,1,0:T(8,128)} %bitcast.25, f32[8,24,512]{2,1,0:T(8,128)S(1)} %collective-permute-done.18.refs_0_.refs_1_, ...), custom_call_target="tpu_custom_call", output_to_operand_aliasing={{0}: (15, {}), {1}: (16, {})} | custom-call | flops 4831838208 | bytes 3145728 | tf_op jit(solution)/shard_map/chunk_step/pallas_call | solution.py:248
  351.6 10.5 %collective-permute-start.26 = (f32[8,8,512]{2,1,0:T(8,128)S(1)}, f32[8,8,512]{2,1,0:T(8,128)S(1)}, u32[]{:S(2)}, u32[]{:S(2)}) collective-permute-start(f32[8,8,512]{2,1,0:T(8,128)S(1)} %get-tuple-element.91), channel_id=1, source_target_pairs={{0,4},{1,5},{2,6},{3,7},{4,0},{5,1},{6,2},{7,3},{8,12},{9,13},{10,... | collective-permute-start | bytes 393224 | tf_op jit(solution)/shard_map/ppermute | solution.py:23
  366.7 6.8 %chunk_step.10 = (f32[256,512]{1,0:T(8,128)}, f32[256,128]{1,0:T(8,128)S(1)}) custom-call(s32[2]{0:T(128)S(1)} %pad_add_fusion.place_ref, f32[8,1024,512]{2,1,0:T(8,128)} %bitcast.26, f32[8,16,512]{2,1,0:T(8,128)S(1)} %collective-permute-done.25.refs_0_.refs_1_, ...), custom_call_target="tpu_custom_call", output_to_operand_aliasing={{0}: (15, {}), {1}: (16, {})} | custom-call | flops 3221225472 | bytes 2097152 | tf_op jit(solution)/shard_map/chunk_step/pallas_call | solution.py:248
  373.5 4.0 collective-permute-done.26.refs_1_
  377.5 8.1 %collective-permute-done.32.refs_7_ = f32[8,8,512]{2,1,0:T(8,128)S(1)} collective-permute-done((f32[8,8,512]{2,1,0:T(8,128)S(1)}, f32[8,8,512]{2,1,0:T(8,128)S(1)}, u32[]{:S(2)}, u32[]{:S(2)}) %collective-permute-start.32) | collective-permute-done | bytes 131104 | tf_op jit(solution)/shard_map/ppermute | solution.py:23
  385.6 5.1 %chunk_step.11 = (f32[256,512]{1,0:T(8,128)}, f32[256,128]{1,0:T(8,128)S(1)}) custom-call(s32[2]{0:T(128)S(1)} %pad_add_fusion.place_ref, f32[8,1024,512]{2,1,0:T(8,128)} %bitcast.27, f32[8,8,512]{2,1,0:T(8,128)S(1)} %collective-permute-done.26.refs_1_, ...), custom_call_target="tpu_custom_call", output_to_operand_aliasing={{0}: (15, {}), {1}: (16, {})} | custom-call | flops 1610612736 | bytes 1048576 | tf_op jit(solution)/shard_map/chunk_step/pallas_call | solution.py:248
  390.8 4.4 %all-to-all-start = ((f32[32,8,512]{2,1,0:T(8,128)}), f32[32,8,512]{2,1,0:T(8,128)S(1)}, u32[]{:S(2)}, u32[]{:S(2)}) async-start(f32[32,8,512]{2,1,0:T(8,128)} %bitcast.11), calls=%async_computation | async-start | bytes 1048576 | tf_op jit(solution)/shard_map/all_to_all | solution.py:439
  402.7 8.9 %all-to-all-done.got_ref = f32[32,8,512]{2,1,0:T(8,128)S(1)} async-done(((f32[32,8,512]{2,1,0:T(8,128)}), f32[32,8,512]{2,1,0:T(8,128)S(1)}, u32[]{:S(2)}, u32[]{:S(2)}) %all-to-all-start) | async-done | bytes 524320 | tf_op jit(solution)/shard_map/all_to_all | solution.py:439
  412.3 9.8 %all_to_all.10.back_ref = f32[32,8,128]{2,1,0:T(8,128)S(1)} all-to-all(f32[32,8,128]{2,1,0:T(8,128)S(1)} %gradient_step.1), channel_id=1, replica_groups=mesh['tile'=4,'freq'=8] {'tile','freq'}, dimensions={0} | all-to-all | bytes 262144 | tf_op jit(solution)/shard_map/all_to_all | solution.py:442
  (139 shorter events, 85.8 us)
Async XLA Ops:
  7.7 21.9 %collective-permute-start.1 = (f32[9,16,512]{2,1,0:T(8,128)S(1)}, f32[9,16,512]{2,1,0:T(8,128)S(1)}, u32[]{:S(2)}, u32[]{:S(2)}) collective-permute-start(f32[9,16,512]{2,1,0:T(8,128)S(1)} %get-tuple-element.60), channel_id=1, source_target_pairs={{0,3},{1,2},{2,1},{3,0},{4,7},{5,6},{6,5},{7,4},{8,11},{9,10},{10,... | collective-permute-start | bytes 884744 | tf_op jit(solution)/shard_map/ppermute | solution.py:23
  10.2 23.0 %collective-permute-start.2 = (f32[9,16,512]{2,1,0:T(8,128)S(1)}, f32[9,16,512]{2,1,0:T(8,128)S(1)}, u32[]{:S(2)}, u32[]{:S(2)}) collective-permute-start(f32[9,16,512]{2,1,0:T(8,128)S(1)} %get-tuple-element.61), channel_id=1, source_target_pairs={{0,7},{1,6},{2,5},{3,4},{4,3},{5,2},{6,1},{7,0},{8,15},{9,14},{10,... | collective-permute-start | bytes 884744 | tf_op jit(solution)/shard_map/ppermute | solution.py:23
  10.3 28.4 %collective-permute-start.3 = (f32[9,16,512]{2,1,0:T(8,128)S(1)}, f32[9,16,512]{2,1,0:T(8,128)S(1)}, u32[]{:S(2)}, u32[]{:S(2)}) collective-permute-start(f32[9,16,512]{2,1,0:T(8,128)S(1)} %get-tuple-element.62), channel_id=1, source_target_pairs={{0,2},{1,3},{2,0},{3,1},{4,6},{5,7},{6,4},{7,5},{8,10},{9,11},{10,... | collective-permute-start | bytes 884744 | tf_op jit(solution)/shard_map/ppermute | solution.py:23
  11.1 31.3 %collective-permute-start.4 = (f32[9,16,512]{2,1,0:T(8,128)S(1)}, f32[9,16,512]{2,1,0:T(8,128)S(1)}, u32[]{:S(2)}, u32[]{:S(2)}) collective-permute-start(f32[9,16,512]{2,1,0:T(8,128)S(1)} %get-tuple-element.63), channel_id=1, source_target_pairs={{0,6},{1,7},{2,4},{3,5},{4,2},{5,3},{6,0},{7,1},{8,14},{9,15},{10,... | collective-permute-start | bytes 884744 | tf_op jit(solution)/shard_map/ppermute | solution.py:23
  29.6 42.8 %collective-permute-start.6 = (f32[9,16,512]{2,1,0:T(8,128)S(1)}, f32[9,16,512]{2,1,0:T(8,128)S(1)}, u32[]{:S(2)}, u32[]{:S(2)}) collective-permute-start(f32[9,16,512]{2,1,0:T(8,128)S(1)} %get-tuple-element.65), channel_id=1, source_target_pairs={{0,5},{1,4},{2,7},{3,6},{4,1},{5,0},{6,3},{7,2},{8,13},{9,12},{10,... | collective-permute-start | bytes 884744 | tf_op jit(solution)/shard_map/ppermute | solution.py:23
  33.3 49.3 %collective-permute-start.10 = (f32[8,32,512]{2,1,0:T(8,128)}, f32[8,32,512]{2,1,0:T(8,128)S(1)}, u32[]{:S(2)}, u32[]{:S(2)}) collective-permute-start(f32[8,32,512]{2,1,0:T(8,128)} %get-tuple-element.66), channel_id=1, source_target_pairs={{0,4},{1,5},{2,6},{3,7},{4,0},{5,1},{6,2},{7,3},{8,12},{9,13},{10,... | collective-permute-start | bytes 1572872 | tf_op jit(solution)/shard_map/ppermute | solution.py:23
  73.1 32.1 %collective-permute-start.12 = (f32[8,32,512]{2,1,0:T(8,128)}, f32[8,32,512]{2,1,0:T(8,128)}, u32[]{:S(2)}, u32[]{:S(2)}) collective-permute-start(f32[8,32,512]{2,1,0:T(8,128)} %get-tuple-element.68), channel_id=1, source_target_pairs={{0,3},{1,2},{2,1},{3,0},{4,7},{5,6},{6,5},{7,4},{8,11},{9,10},{10,... | collective-permute-start | bytes 1572872 | tf_op jit(solution)/shard_map/ppermute | solution.py:23
  73.7 33.0 %collective-permute-start.13 = (f32[8,32,512]{2,1,0:T(8,128)}, f32[8,32,512]{2,1,0:T(8,128)}, u32[]{:S(2)}, u32[]{:S(2)}) collective-permute-start(f32[8,32,512]{2,1,0:T(8,128)} %get-tuple-element.69), channel_id=1, source_target_pairs={{0,7},{1,6},{2,5},{3,4},{4,3},{5,2},{6,1},{7,0},{8,15},{9,14},{10,... | collective-permute-start | bytes 1572872 | tf_op jit(solution)/shard_map/ppermute | solution.py:23
  76.5 38.8 %collective-permute-start.14 = (f32[8,32,512]{2,1,0:T(8,128)}, f32[8,32,512]{2,1,0:T(8,128)}, u32[]{:S(2)}, u32[]{:S(2)}) collective-permute-start(f32[8,32,512]{2,1,0:T(8,128)} %get-tuple-element.70), channel_id=1, source_target_pairs={{0,2},{1,3},{2,0},{3,1},{4,6},{5,7},{6,4},{7,5},{8,10},{9,11},{10,... | collective-permute-start | bytes 1572872 | tf_op jit(solution)/shard_map/ppermute | solution.py:23
  92.1 48.5 %collective-permute-start.15 = (f32[8,32,512]{2,1,0:T(8,128)}, f32[8,32,512]{2,1,0:T(8,128)}, u32[]{:S(2)}, u32[]{:S(2)}) collective-permute-start(f32[8,32,512]{2,1,0:T(8,128)} %get-tuple-element.71), channel_id=1, source_target_pairs={{0,6},{1,7},{2,4},{3,5},{4,2},{5,3},{6,0},{7,1},{8,14},{9,15},{10,... | collective-permute-start | bytes 1572872 | tf_op jit(solution)/shard_map/ppermute | solution.py:23
  96.1 48.6 %collective-permute-start.16 = (f32[8,32,512]{2,1,0:T(8,128)}, f32[8,32,512]{2,1,0:T(8,128)}, u32[]{:S(2)}, u32[]{:S(2)}) collective-permute-start(f32[8,32,512]{2,1,0:T(8,128)} %get-tuple-element.72), channel_id=1, source_target_pairs={{0,1},{1,0},{2,3},{3,2},{4,5},{5,4},{6,7},{7,6},{8,9},{9,8},{10,11... | collective-permute-start | bytes 1572872 | tf_op jit(solution)/shard_map/ppermute | solution.py:23
  105.2 73.2 %collective-permute-start.17 = (f32[8,32,512]{2,1,0:T(8,128)}, f32[8,32,512]{2,1,0:T(8,128)}, u32[]{:S(2)}, u32[]{:S(2)}) collective-permute-start(f32[8,32,512]{2,1,0:T(8,128)} %get-tuple-element.73), channel_id=1, source_target_pairs={{0,5},{1,4},{2,7},{3,6},{4,1},{5,0},{6,3},{7,2},{8,13},{9,12},{10,... | collective-permute-start | bytes 1572872 | tf_op jit(solution)/shard_map/ppermute | solution.py:23
  106.7 93.7 %collective-permute-start.11 = (f32[8,32,512]{2,1,0:T(8,128)}, f32[8,32,512]{2,1,0:T(8,128)S(1)}, u32[]{:S(2)}, u32[]{:S(2)}) collective-permute-start(f32[8,32,512]{2,1,0:T(8,128)} %get-tuple-element.67), channel_id=1, source_target_pairs={{0,4},{1,5},{2,6},{3,7},{4,0},{5,1},{6,2},{7,3},{8,12},{9,13},{10,... | collective-permute-start | bytes 1572872 | tf_op jit(solution)/shard_map/ppermute | solution.py:23
  115.3 85.9 %collective-permute-start.19 = (f32[8,32,512]{2,1,0:T(8,128)}, f32[8,32,512]{2,1,0:T(8,128)}, u32[]{:S(2)}, u32[]{:S(2)}) collective-permute-start(f32[8,32,512]{2,1,0:T(8,128)} %get-tuple-element.82), channel_id=1, source_target_pairs={{0,3},{1,2},{2,1},{3,0},{4,7},{5,6},{6,5},{7,4},{8,11},{9,10},{10,... | collective-permute-start | bytes 1572872 | tf_op jit(solution)/shard_map/ppermute | solution.py:23
  140.6 75.4 %collective-permute-start.20 = (f32[8,32,512]{2,1,0:T(8,128)S(1)}, f32[8,32,512]{2,1,0:T(8,128)S(1)}, u32[]{:S(2)}, u32[]{:S(2)}) collective-permute-start(f32[8,32,512]{2,1,0:T(8,128)S(1)} %copy-done.14), channel_id=1, source_target_pairs={{0,7},{1,6},{2,5},{3,4},{4,3},{5,2},{6,1},{7,0},{8,15},{9,14},{10,... | collective-permute-start | bytes 1572872 | tf_op jit(solution)/shard_map/ppermute | solution.py:23
  144.7 79.4 %collective-permute-start.21 = (f32[8,32,512]{2,1,0:T(8,128)S(1)}, f32[8,32,512]{2,1,0:T(8,128)S(1)}, u32[]{:S(2)}, u32[]{:S(2)}) collective-permute-start(f32[8,32,512]{2,1,0:T(8,128)S(1)} %copy-done.12), channel_id=1, source_target_pairs={{0,2},{1,3},{2,0},{3,1},{4,6},{5,7},{6,4},{7,5},{8,10},{9,11},{10,... | collective-permute-start | bytes 1572872 | tf_op jit(solution)/shard_map/ppermute | solution.py:23
  178.3 46.1 %collective-permute-start.22 = (f32[8,32,512]{2,1,0:T(8,128)S(1)}, f32[8,32,512]{2,1,0:T(8,128)S(1)}, u32[]{:S(2)}, u32[]{:S(2)}) collective-permute-start(f32[8,32,512]{2,1,0:T(8,128)S(1)} %copy-done.10), channel_id=1, source_target_pairs={{0,6},{1,7},{2,4},{3,5},{4,2},{5,3},{6,0},{7,1},{8,14},{9,15},{10,... | collective-permute-start | bytes 1572872 | tf_op jit(solution)/shard_map/ppermute | solution.py:23
  200.4 26.4 %collective-permute-start.23 = (f32[8,32,512]{2,1,0:T(8,128)S(1)}, f32[8,32,512]{2,1,0:T(8,128)S(1)}, u32[]{:S(2)}, u32[]{:S(2)}) collective-permute-start(f32[8,32,512]{2,1,0:T(8,128)S(1)} %copy-done.8), channel_id=1, source_target_pairs={{0,1},{1,0},{2,3},{3,2},{4,5},{5,4},{6,7},{7,6},{8,9},{9,8},{10,11... | collective-permute-start | bytes 1572872 | tf_op jit(solution)/shard_map/ppermute | solution.py:23
  201.2 61.3 %collective-permute-start.24 = (f32[8,32,512]{2,1,0:T(8,128)S(1)}, f32[8,32,512]{2,1,0:T(8,128)S(1)}, u32[]{:S(2)}, u32[]{:S(2)}) collective-permute-start(f32[8,32,512]{2,1,0:T(8,128)S(1)} %copy-done.6), channel_id=1, source_target_pairs={{0,5},{1,4},{2,7},{3,6},{4,1},{5,0},{6,3},{7,2},{8,13},{9,12},{10,... | collective-permute-start | bytes 1572872 | tf_op jit(solution)/shard_map/ppermute | solution.py:23
  216.0 57.8 %collective-permute-start.18 = (f32[8,24,512]{2,1,0:T(8,128)S(1)}, f32[8,24,512]{2,1,0:T(8,128)S(1)}, u32[]{:S(2)}, u32[]{:S(2)}) collective-permute-start(f32[8,24,512]{2,1,0:T(8,128)S(1)} %get-tuple-element.81), channel_id=1, source_target_pairs={{0,4},{1,5},{2,6},{3,7},{4,0},{5,1},{6,2},{7,3},{8,12},{9,13},{10,... | collective-permute-start | bytes 1179656 | tf_op jit(solution)/shard_map/ppermute | solution.py:23
  224.1 56.5 %collective-permute-start.36 = (f32[8,24,512]{2,1,0:T(8,128)S(1)}, f32[8,24,512]{2,1,0:T(8,128)S(1)}, u32[]{:S(2)}, u32[]{:S(2)}) collective-permute-start(f32[8,24,512]{2,1,0:T(8,128)S(1)} %get-tuple-element.101), channel_id=1, source_target_pairs={{0,3},{1,2},{2,1},{3,0},{4,7},{5,6},{6,5},{7,4},{8,11},{9,10},{10,... | collective-permute-start | bytes 1179656 | tf_op jit(solution)/shard_map/ppermute | solution.py:23
  224.4 57.4 %collective-permute-start.37 = (f32[8,24,512]{2,1,0:T(8,128)S(1)}, f32[8,24,512]{2,1,0:T(8,128)S(1)}, u32[]{:S(2)}, u32[]{:S(2)}) collective-permute-start(f32[8,24,512]{2,1,0:T(8,128)S(1)} %get-tuple-element.102), channel_id=1, source_target_pairs={{0,7},{1,6},{2,5},{3,4},{4,3},{5,2},{6,1},{7,0},{8,15},{9,14},{10,... | collective-permute-start | bytes 1179656 | tf_op jit(solution)/shard_map/ppermute | solution.py:23
  278.6 24.5 %collective-permute-start.39 = (f32[8,24,512]{2,1,0:T(8,128)S(1)}, f32[8,24,512]{2,1,0:T(8,128)S(1)}, u32[]{:S(2)}, u32[]{:S(2)}) collective-permute-start(f32[8,24,512]{2,1,0:T(8,128)S(1)} %get-tuple-element.104), channel_id=1, source_target_pairs={{0,6},{1,7},{2,4},{3,5},{4,2},{5,3},{6,0},{7,1},{8,14},{9,15},{10,... | collective-permute-start | bytes 1179656 | tf_op jit(solution)/shard_map/ppermute | solution.py:23
  280.6 47.5 %collective-permute-start.40 = (f32[8,24,512]{2,1,0:T(8,128)S(1)}, f32[8,24,512]{2,1,0:T(8,128)S(1)}, u32[]{:S(2)}, u32[]{:S(2)}) collective-permute-start(f32[8,24,512]{2,1,0:T(8,128)S(1)} %get-tuple-element.105), channel_id=1, source_target_pairs={{0,1},{1,0},{2,3},{3,2},{4,5},{5,4},{6,7},{7,6},{8,9},{9,8},{10,11... | collective-permute-start | bytes 1179656 | tf_op jit(solution)/shard_map/ppermute | solution.py:23
  281.8 59.9 %collective-permute-start.41 = (f32[8,24,512]{2,1,0:T(8,128)S(1)}, f32[8,24,512]{2,1,0:T(8,128)S(1)}, u32[]{:S(2)}, u32[]{:S(2)}) collective-permute-start(f32[8,24,512]{2,1,0:T(8,128)S(1)} %get-tuple-element.106), channel_id=1, source_target_pairs={{0,5},{1,4},{2,7},{3,6},{4,1},{5,0},{6,3},{7,2},{8,13},{9,12},{10,... | collective-permute-start | bytes 1179656 | tf_op jit(solution)/shard_map/ppermute | solution.py:23
  290.3 51.5 %collective-permute-start.33 = (f32[8,16,512]{2,1,0:T(8,128)S(1)}, f32[8,16,512]{2,1,0:T(8,128)S(1)}, u32[]{:S(2)}, u32[]{:S(2)}) collective-permute-start(f32[8,16,512]{2,1,0:T(8,128)S(1)} %get-tuple-element.98), channel_id=1, source_target_pairs={{0,7},{1,6},{2,5},{3,4},{4,3},{5,2},{6,1},{7,0},{8,15},{9,14},{10,... | collective-permute-start | bytes 786440 | tf_op jit(solution)/shard_map/ppermute | solution.py:23
  295.1 56.5 %collective-permute-start.34 = (f32[8,16,512]{2,1,0:T(8,128)S(1)}, f32[8,16,512]{2,1,0:T(8,128)S(1)}, u32[]{:S(2)}, u32[]{:S(2)}) collective-permute-start(f32[8,16,512]{2,1,0:T(8,128)S(1)} %get-tuple-element.99), channel_id=1, source_target_pairs={{0,6},{1,7},{2,4},{3,5},{4,2},{5,3},{6,0},{7,1},{8,14},{9,15},{10,... | collective-permute-start | bytes 786440 | tf_op jit(solution)/shard_map/ppermute | solution.py:23
  303.1 58.9 %collective-permute-start.35 = (f32[8,16,512]{2,1,0:T(8,128)S(1)}, f32[8,16,512]{2,1,0:T(8,128)S(1)}, u32[]{:S(2)}, u32[]{:S(2)}) collective-permute-start(f32[8,16,512]{2,1,0:T(8,128)S(1)} %get-tuple-element.100), channel_id=1, source_target_pairs={{0,5},{1,4},{2,7},{3,6},{4,1},{5,0},{6,3},{7,2},{8,13},{9,12},{10,... | collective-permute-start | bytes 786440 | tf_op jit(solution)/shard_map/ppermute | solution.py:23
  328.1 36.8 %collective-permute-start.27 = (f32[8,24,512]{2,1,0:T(8,128)S(1)}, f32[8,24,512]{2,1,0:T(8,128)S(1)}, u32[]{:S(2)}, u32[]{:S(2)}) collective-permute-start(f32[8,24,512]{2,1,0:T(8,128)S(1)} %get-tuple-element.92), channel_id=1, source_target_pairs={{0,3},{1,2},{2,1},{3,0},{4,7},{5,6},{6,5},{7,4},{8,11},{9,10},{10,... | collective-permute-start | bytes 1179656 | tf_op jit(solution)/shard_map/ppermute | solution.py:23
  341.8 24.9 %collective-permute-start.29 = (f32[8,24,512]{2,1,0:T(8,128)S(1)}, f32[8,24,512]{2,1,0:T(8,128)S(1)}, u32[]{:S(2)}, u32[]{:S(2)}) collective-permute-start(f32[8,24,512]{2,1,0:T(8,128)S(1)} %get-tuple-element.94), channel_id=1, source_target_pairs={{0,2},{1,3},{2,0},{3,1},{4,6},{5,7},{6,4},{7,5},{8,10},{9,11},{10,... | collective-permute-start | bytes 1179656 | tf_op jit(solution)/shard_map/ppermute | solution.py:23
  341.8 24.9 %collective-permute-start.31 = (f32[8,24,512]{2,1,0:T(8,128)S(1)}, f32[8,24,512]{2,1,0:T(8,128)S(1)}, u32[]{:S(2)}, u32[]{:S(2)}) collective-permute-start(f32[8,24,512]{2,1,0:T(8,128)S(1)} %get-tuple-element.96), channel_id=1, source_target_pairs={{0,1},{1,0},{2,3},{3,2},{4,5},{5,4},{6,7},{7,6},{8,9},{9,8},{10,11... | collective-permute-start | bytes 1179656 | tf_op jit(solution)/shard_map/ppermute | solution.py:23
  351.6 26.0 %collective-permute-start.26 = (f32[8,8,512]{2,1,0:T(8,128)S(1)}, f32[8,8,512]{2,1,0:T(8,128)S(1)}, u32[]{:S(2)}, u32[]{:S(2)}) collective-permute-start(f32[8,8,512]{2,1,0:T(8,128)S(1)} %get-tuple-element.91), channel_id=1, source_target_pairs={{0,4},{1,5},{2,6},{3,7},{4,0},{5,1},{6,2},{7,3},{8,12},{9,13},{10,... | collective-permute-start | bytes 393224 | tf_op jit(solution)/shard_map/ppermute | solution.py:23
  (34 other events, 618.1 us)

commit v11 on v7

--- a/solution.py
+++ b/solution.py
@@ -25,7 +25,9 @@
 
 def partner_order(size):
     assert size & (size - 1) == 0
-    return list(range(1, size))[::-1]
+    half = size // 2
+    pairs = zip(range(size - 1, half, -1), range(half - 1, 0, -1))
+    return [half] + [k for pair in pairs for k in pair]
 
 
 def gate_table(owner_order, own_freqs, freqs, waveform, gate_index):

time: 423 us -> 421 us (level)
  waiting for transfers between devices: 144 us -> 119 us
  starting transfers between devices: 172 us -> 196 us
    ppermute x45, waiting for transfers between devices: 135 us -> 110 us  [swap(): lax.ppermute(x, axis, [(i, i ^ k) for i in range(lax.axis_size(axis))])]
    ppermute x45, starting transfers between devices: 169 us -> 193 us  [swap(): lax.ppermute(x, axis, [(i, i ^ k) for i in range(lax.axis_size(axis))])]
  transfers between devices with their start and end apart: 46 -> 46, of which waited for: 17 -> 12; matrix products, arithmetic and copies ran while one was open for 3% -> 3% of each run, Pallas kernels for 15% -> 15%
where the time goes in v11:
time: 421 us
  starting transfers between devices  196 us (47%)
  waiting for transfers between devices  119 us (28%)
  Pallas kernels  72.3 us (17%)
  local copies, waits for them, and re-layouts  17.7 us (4%)
  blocking collectives  9.82 us (2%)
  other arithmetic  4.77 us (1%)
    ppermute x45, starting transfers between devices, swap(): lax.ppermute(x, axis, [(i, i ^ k) for i in range(lax.axis_size(axis))])  193 us
    ppermute x45, waiting for transfers between devices, swap(): lax.ppermute(x, axis, [(i, i ^ k) for i in range(lax.axis_size(axis))])  110 us
    pallas_call x6, Pallas kernels, chunk_step(): pl.pallas_call(functools.partial(chunk_kernel, pieces, block_cells, last)...  51 us
    pallas_call x6, Pallas kernels, pack(): pl.pallas_call(functools.partial(pack_kernel, distances, own, first, rows...  16.5 us
    unnamed x65, local copies, waits for them, and re-layouts  11.7 us
    all_to_all x1, blocking collectives, body(): back = lax.all_to_all(step, both, split_axis=0, concat_axis=0, tiled=True)  9.82 us
    all_to_all x1, waiting for transfers between devices, body(): got = lax.all_to_all(sent, both, split_axis=0, concat_axis=0, tiled=True)  9.01 us
  transfers between devices with their start and end apart: 46, of which 12 were waited for; matrix products, arithmetic and copies ran while one was open for 3% of the time, Pallas kernels for 15%

profile of v11, /device:TPU:0, one launch (start us, length us, event | category | flops | bytes accessed | tf_op | source)
XLA Modules:
  0.0 420.7 jit_solution(7012772988897492837)
XLA Ops:
  3.6 4.1 collective-permute-start
  13.6 15.5 %collective-permute-done.refs_0_.refs_1_ = f32[9,16,512]{2,1,0:T(8,128)S(1)} collective-permute-done((f32[9,16,512]{2,1,0:T(8,128)S(1)}, f32[9,16,512]{2,1,0:T(8,128)S(1)}, u32[]{:S(2)}, u32[]{:S(2)}) %collective-permute-start) | collective-permute-done | bytes 294944 | tf_op jit(solution)/shard_map/ppermute | solution.py:23
  31.3 3.6 pack.7
  34.9 3.8 collective-permute-done.2.refs_2_.refs_3_
  38.7 10.4 %collective-permute-start.10 = (f32[8,32,512]{2,1,0:T(8,128)}, f32[8,32,512]{2,1,0:T(8,128)S(1)}, u32[]{:S(2)}, u32[]{:S(2)}) collective-permute-start(f32[8,32,512]{2,1,0:T(8,128)} %get-tuple-element.69), channel_id=1, source_target_pairs={{0,4},{1,5},{2,6},{3,7},{4,0},{5,1},{6,2},{7,3},{8,12},{9,13},{10,... | collective-permute-start | bytes 1572872 | tf_op jit(solution)/shard_map/ppermute | solution.py:23
  49.2 23.2 %collective-permute-done.5.refs_5_.refs_6_ = f32[9,16,512]{2,1,0:T(8,128)S(1)} collective-permute-done((f32[9,16,512]{2,1,0:T(8,128)S(1)}, f32[9,16,512]{2,1,0:T(8,128)S(1)}, u32[]{:S(2)}, u32[]{:S(2)}) %collective-permute-start.5) | collective-permute-done | bytes 294944 | tf_op jit(solution)/shard_map/ppermute | solution.py:23
  73.2 3.4 collective-permute-start.13
  76.9 4.9 %collective-permute-done.9.refs_3_ = f32[264,256]{1,0:T(8,128)} collective-permute-done((f32[264,256]{1,0:T(8,128)S(1)}, f32[264,256]{1,0:T(8,128)}, u32[]{:S(2)}, u32[]{:S(2)}) %collective-permute-start.9) | collective-permute-done | bytes 270368 | tf_op jit(solution)/shard_map/ppermute | solution.py:23
  82.5 11.1 %collective-permute-done.10.refs_0_.refs_1_ = f32[8,32,512]{2,1,0:T(8,128)S(1)} collective-permute-done((f32[8,32,512]{2,1,0:T(8,128)}, f32[8,32,512]{2,1,0:T(8,128)S(1)}, u32[]{:S(2)}, u32[]{:S(2)}) %collective-permute-start.10) | collective-permute-done | bytes 524320 | tf_op jit(solution)/shard_map/ppermute | solution.py:23
  102.1 4.2 %collective-permute-start.17 = (f32[8,32,512]{2,1,0:T(8,128)}, f32[8,32,512]{2,1,0:T(8,128)}, u32[]{:S(2)}, u32[]{:S(2)}) collective-permute-start(f32[8,32,512]{2,1,0:T(8,128)} %get-tuple-element.81), channel_id=1, source_target_pairs={{0,5},{1,4},{2,7},{3,6},{4,1},{5,0},{6,3},{7,2},{8,13},{9,12},{10,... | collective-permute-start | bytes 1572872 | tf_op jit(solution)/shard_map/ppermute | solution.py:23
  108.6 18.6 %collective-permute-start.11 = (f32[8,32,512]{2,1,0:T(8,128)}, f32[8,32,512]{2,1,0:T(8,128)S(1)}, u32[]{:S(2)}, u32[]{:S(2)}) collective-permute-start(f32[8,32,512]{2,1,0:T(8,128)} %get-tuple-element.70), channel_id=1, source_target_pairs={{0,4},{1,5},{2,6},{3,7},{4,0},{5,1},{6,2},{7,3},{8,12},{9,13},{10,... | collective-permute-start | bytes 1572872 | tf_op jit(solution)/shard_map/ppermute | solution.py:23
  137.7 39.6 %collective-permute-start.21 = (f32[8,32,512]{2,1,0:T(8,128)S(1)}, f32[8,32,512]{2,1,0:T(8,128)S(1)}, u32[]{:S(2)}, u32[]{:S(2)}) collective-permute-start(f32[8,32,512]{2,1,0:T(8,128)S(1)} %copy-done.20), channel_id=1, source_target_pairs={{0,3},{1,2},{2,1},{3,0},{4,7},{5,6},{6,5},{7,4},{8,11},{9,10},{10,... | collective-permute-start | bytes 1572872 | tf_op jit(solution)/shard_map/ppermute | solution.py:23
  182.6 6.0 %collective-permute-done.11.refs_0_.refs_1_ = f32[8,32,512]{2,1,0:T(8,128)S(1)} collective-permute-done((f32[8,32,512]{2,1,0:T(8,128)}, f32[8,32,512]{2,1,0:T(8,128)S(1)}, u32[]{:S(2)}, u32[]{:S(2)}) %collective-permute-start.11) | collective-permute-done | bytes 524320 | tf_op jit(solution)/shard_map/ppermute | solution.py:23
  191.8 6.9 %chunk_step.6 = (f32[256,512]{1,0:T(8,128)}, f32[256,128]{1,0:T(8,128)S(1)}) custom-call(s32[2]{0:T(128)S(1)} %pad_add_fusion.place_ref, f32[8,1024,512]{2,1,0:T(8,128)} %bitcast.19, f32[9,16,512]{2,1,0:T(8,128)S(1)} %collective-permute-done.refs_0_.refs_1_, ...), custom_call_target="tpu_custom_call", output_to_operand_aliasing={{0}: (15, {}), {1}: (16, {})} | custom-call | flops 3221225472 | bytes 2097152 | tf_op jit(solution)/shard_map/chunk_step/pallas_call | solution.py:252
  201.8 14.3 %collective-permute-start.12 = (f32[8,24,512]{2,1,0:T(8,128)S(1)}, f32[8,24,512]{2,1,0:T(8,128)S(1)}, u32[]{:S(2)}, u32[]{:S(2)}) collective-permute-start(f32[8,24,512]{2,1,0:T(8,128)S(1)} %get-tuple-element.76), channel_id=1, source_target_pairs={{0,4},{1,5},{2,6},{3,7},{4,0},{5,1},{6,2},{7,3},{8,12},{9,13},{10,... | collective-permute-start | bytes 1179656 | tf_op jit(solution)/shard_map/ppermute | solution.py:23
  221.5 33.3 %collective-permute-start.40 = (f32[8,24,512]{2,1,0:T(8,128)S(1)}, f32[8,24,512]{2,1,0:T(8,128)S(1)}, u32[]{:S(2)}, u32[]{:S(2)}) collective-permute-start(f32[8,24,512]{2,1,0:T(8,128)S(1)} %get-tuple-element.108), channel_id=1, source_target_pairs={{0,3},{1,2},{2,1},{3,0},{4,7},{5,6},{6,5},{7,4},{8,11},{9,10},{10,... | collective-permute-start | bytes 1179656 | tf_op jit(solution)/shard_map/ppermute | solution.py:23
  254.7 8.8 %collective-permute-done.24.refs_6_ = f32[8,32,512]{2,1,0:T(8,128)S(1)} collective-permute-done((f32[8,32,512]{2,1,0:T(8,128)S(1)}, f32[8,32,512]{2,1,0:T(8,128)S(1)}, u32[]{:S(2)}, u32[]{:S(2)}) %collective-permute-start.24) | collective-permute-done | bytes 524320 | tf_op jit(solution)/shard_map/ppermute | solution.py:23
  266.8 11.9 %collective-permute-done.12.refs_0_.refs_1_ = f32[8,24,512]{2,1,0:T(8,128)S(1)} collective-permute-done((f32[8,24,512]{2,1,0:T(8,128)S(1)}, f32[8,24,512]{2,1,0:T(8,128)S(1)}, u32[]{:S(2)}, u32[]{:S(2)}) %collective-permute-start.12) | collective-permute-done | bytes 393248 | tf_op jit(solution)/shard_map/ppermute | solution.py:23
  279.5 11.5 %chunk_step.7 = (f32[256,512]{1,0:T(8,128)}, f32[256,128]{1,0:T(8,128)S(1)}) custom-call(s32[2]{0:T(128)S(1)} %pad_add_fusion.place_ref, f32[8,1024,512]{2,1,0:T(8,128)} %bitcast.21, f32[8,32,512]{2,1,0:T(8,128)S(1)} %collective-permute-done.10.refs_0_.refs_1_, f32[8,32,512]{2,1,0:T(8,128)S(1)} %copy-done.6, ...), custom_call_target="tpu_custom_call", output_to_operand_aliasing={{0}: (15, {}), {1}: (16, {})} | custom-call | flops 6442450944 | bytes 4194304 | tf_op jit(solution)/shard_map/chunk_step/pallas_call | solution.py:252
  293.1 3.4 collective-permute-start.19
  298.5 3.2 collective-permute-start.33
  302.4 19.8 %collective-permute-done.19.refs_0_.refs_1_ = f32[8,16,512]{2,1,0:T(8,128)S(1)} collective-permute-done((f32[8,16,512]{2,1,0:T(8,128)S(1)}, f32[8,16,512]{2,1,0:T(8,128)S(1)}, u32[]{:S(2)}, u32[]{:S(2)}) %collective-permute-start.19) | collective-permute-done | bytes 262176 | tf_op jit(solution)/shard_map/ppermute | solution.py:23
  322.2 3.6 collective-permute-start.35
  325.8 11.4 %chunk_step.8 = (f32[256,512]{1,0:T(8,128)}, f32[256,128]{1,0:T(8,128)S(1)}) custom-call(s32[2]{0:T(128)S(1)} %pad_add_fusion.place_ref, f32[8,1024,512]{2,1,0:T(8,128)} %bitcast.23, f32[8,32,512]{2,1,0:T(8,128)S(1)} %collective-permute-done.11.refs_0_.refs_1_, ...), custom_call_target="tpu_custom_call", output_to_operand_aliasing={{0}: (15, {}), {1}: (16, {})} | custom-call | flops 6442450944 | bytes 4194304 | tf_op jit(solution)/shard_map/chunk_step/pallas_call | solution.py:252
  343.1 3.2 collective-permute-start.26
  347.5 9.3 %chunk_step.9 = (f32[256,512]{1,0:T(8,128)}, f32[256,128]{1,0:T(8,128)S(1)}) custom-call(s32[2]{0:T(128)S(1)} %pad_add_fusion.place_ref, f32[8,1024,512]{2,1,0:T(8,128)} %bitcast.25, f32[8,24,512]{2,1,0:T(8,128)S(1)} %collective-permute-done.12.refs_0_.refs_1_, ...), custom_call_target="tpu_custom_call", output_to_operand_aliasing={{0}: (15, {}), {1}: (16, {})} | custom-call | flops 4831838208 | bytes 3145728 | tf_op jit(solution)/shard_map/chunk_step/pallas_call | solution.py:252
  356.7 15.4 %collective-permute-start.28 = (f32[8,8,512]{2,1,0:T(8,128)S(1)}, f32[8,8,512]{2,1,0:T(8,128)S(1)}, u32[]{:S(2)}, u32[]{:S(2)}) collective-permute-start(f32[8,8,512]{2,1,0:T(8,128)S(1)} %get-tuple-element.96), channel_id=1, source_target_pairs={{0,3},{1,2},{2,1},{3,0},{4,7},{5,6},{6,5},{7,4},{8,11},{9,10},{10,... | collective-permute-start | bytes 393224 | tf_op jit(solution)/shard_map/ppermute | solution.py:23
  373.4 4.4 %collective-permute-start.31 = (f32[8,8,512]{2,1,0:T(8,128)S(1)}, f32[8,8,512]{2,1,0:T(8,128)S(1)}, u32[]{:S(2)}, u32[]{:S(2)}) collective-permute-start(f32[8,8,512]{2,1,0:T(8,128)S(1)} %get-tuple-element.99), channel_id=1, source_target_pairs={{0,5},{1,4},{2,7},{3,6},{4,1},{5,0},{6,3},{7,2},{8,13},{9,12},{10,... | collective-permute-start | bytes 393224 | tf_op jit(solution)/shard_map/ppermute | solution.py:23
  378.0 6.9 %chunk_step.10 = (f32[256,512]{1,0:T(8,128)}, f32[256,128]{1,0:T(8,128)S(1)}) custom-call(s32[2]{0:T(128)S(1)} %pad_add_fusion.place_ref, f32[8,1024,512]{2,1,0:T(8,128)} %bitcast.26, f32[8,16,512]{2,1,0:T(8,128)S(1)} %collective-permute-done.19.refs_0_.refs_1_, ...), custom_call_target="tpu_custom_call", output_to_operand_aliasing={{0}: (15, {}), {1}: (16, {})} | custom-call | flops 3221225472 | bytes 2097152 | tf_op jit(solution)/shard_map/chunk_step/pallas_call | solution.py:252
  384.9 5.1 %chunk_step.11 = (f32[256,512]{1,0:T(8,128)}, f32[256,128]{1,0:T(8,128)S(1)}) custom-call(s32[2]{0:T(128)S(1)} %pad_add_fusion.place_ref, f32[8,1024,512]{2,1,0:T(8,128)} %bitcast.27, f32[8,8,512]{2,1,0:T(8,128)S(1)} %collective-permute-done.26.refs_1_, ...), custom_call_target="tpu_custom_call", output_to_operand_aliasing={{0}: (15, {}), {1}: (16, {})} | custom-call | flops 1610612736 | bytes 1048576 | tf_op jit(solution)/shard_map/chunk_step/pallas_call | solution.py:252
  400.1 9.0 %all-to-all-done.got_ref = f32[32,8,512]{2,1,0:T(8,128)S(1)} async-done(((f32[32,8,512]{2,1,0:T(8,128)}), f32[32,8,512]{2,1,0:T(8,128)S(1)}, u32[]{:S(2)}, u32[]{:S(2)}) %all-to-all-start) | async-done | bytes 524320 | tf_op jit(solution)/shard_map/all_to_all | solution.py:425
  409.9 9.8 %all_to_all.10.back_ref = f32[32,8,128]{2,1,0:T(8,128)S(1)} all-to-all(f32[32,8,128]{2,1,0:T(8,128)S(1)} %gradient_step.1), channel_id=1, replica_groups=mesh['tile'=4,'freq'=8] {'tile','freq'}, dimensions={0} | all-to-all | bytes 262144 | tf_op jit(solution)/shard_map/all_to_all | solution.py:428
  (163 shorter events, 80.0 us)
Async XLA Ops:
  10.0 28.7 %collective-permute-start.2 = (f32[9,16,512]{2,1,0:T(8,128)S(1)}, f32[9,16,512]{2,1,0:T(8,128)S(1)}, u32[]{:S(2)}, u32[]{:S(2)}) collective-permute-start(f32[9,16,512]{2,1,0:T(8,128)S(1)} %get-tuple-element.64), channel_id=1, source_target_pairs={{0,3},{1,2},{2,1},{3,0},{4,7},{5,6},{6,5},{7,4},{8,11},{9,10},{10,... | collective-permute-start | bytes 884744 | tf_op jit(solution)/shard_map/ppermute | solution.py:23
  10.2 39.0 %collective-permute-start.3 = (f32[9,16,512]{2,1,0:T(8,128)S(1)}, f32[9,16,512]{2,1,0:T(8,128)S(1)}, u32[]{:S(2)}, u32[]{:S(2)}) collective-permute-start(f32[9,16,512]{2,1,0:T(8,128)S(1)} %get-tuple-element.65), channel_id=1, source_target_pairs={{0,6},{1,7},{2,4},{3,5},{4,2},{5,3},{6,0},{7,1},{8,14},{9,15},{10,... | collective-permute-start | bytes 884744 | tf_op jit(solution)/shard_map/ppermute | solution.py:23
  13.1 36.1 %collective-permute-start.4 = (f32[9,16,512]{2,1,0:T(8,128)S(1)}, f32[9,16,512]{2,1,0:T(8,128)S(1)}, u32[]{:S(2)}, u32[]{:S(2)}) collective-permute-start(f32[9,16,512]{2,1,0:T(8,128)S(1)} %get-tuple-element.66), channel_id=1, source_target_pairs={{0,2},{1,3},{2,0},{3,1},{4,6},{5,7},{6,4},{7,5},{8,10},{9,11},{10,... | collective-permute-start | bytes 884744 | tf_op jit(solution)/shard_map/ppermute | solution.py:23
  29.1 43.3 %collective-permute-start.5 = (f32[9,16,512]{2,1,0:T(8,128)S(1)}, f32[9,16,512]{2,1,0:T(8,128)S(1)}, u32[]{:S(2)}, u32[]{:S(2)}) collective-permute-start(f32[9,16,512]{2,1,0:T(8,128)S(1)} %get-tuple-element.67), channel_id=1, source_target_pairs={{0,5},{1,4},{2,7},{3,6},{4,1},{5,0},{6,3},{7,2},{8,13},{9,12},{10,... | collective-permute-start | bytes 884744 | tf_op jit(solution)/shard_map/ppermute | solution.py:23
  29.8 42.6 %collective-permute-start.6 = (f32[9,16,512]{2,1,0:T(8,128)S(1)}, f32[9,16,512]{2,1,0:T(8,128)S(1)}, u32[]{:S(2)}, u32[]{:S(2)}) collective-permute-start(f32[9,16,512]{2,1,0:T(8,128)S(1)} %get-tuple-element.68), channel_id=1, source_target_pairs={{0,1},{1,0},{2,3},{3,2},{4,5},{5,4},{6,7},{7,6},{8,9},{9,8},{10,11... | collective-permute-start | bytes 884744 | tf_op jit(solution)/shard_map/ppermute | solution.py:23
  38.7 54.9 %collective-permute-start.10 = (f32[8,32,512]{2,1,0:T(8,128)}, f32[8,32,512]{2,1,0:T(8,128)S(1)}, u32[]{:S(2)}, u32[]{:S(2)}) collective-permute-start(f32[8,32,512]{2,1,0:T(8,128)} %get-tuple-element.69), channel_id=1, source_target_pairs={{0,4},{1,5},{2,6},{3,7},{4,0},{5,1},{6,2},{7,3},{8,12},{9,13},{10,... | collective-permute-start | bytes 1572872 | tf_op jit(solution)/shard_map/ppermute | solution.py:23
  73.2 33.2 %collective-permute-start.13 = (f32[8,32,512]{2,1,0:T(8,128)}, f32[8,32,512]{2,1,0:T(8,128)S(1)}, u32[]{:S(2)}, u32[]{:S(2)}) collective-permute-start(f32[8,32,512]{2,1,0:T(8,128)} %copy-done.23), channel_id=1, source_target_pairs={{0,7},{1,6},{2,5},{3,4},{4,3},{5,2},{6,1},{7,0},{8,15},{9,14},{10,... | collective-permute-start | bytes 1572872 | tf_op jit(solution)/shard_map/ppermute | solution.py:23
  76.6 31.1 %collective-permute-start.14 = (f32[8,32,512]{2,1,0:T(8,128)}, f32[8,32,512]{2,1,0:T(8,128)S(1)}, u32[]{:S(2)}, u32[]{:S(2)}) collective-permute-start(f32[8,32,512]{2,1,0:T(8,128)} %copy-done.22), channel_id=1, source_target_pairs={{0,3},{1,2},{2,1},{3,0},{4,7},{5,6},{6,5},{7,4},{8,11},{9,10},{10,... | collective-permute-start | bytes 1572872 | tf_op jit(solution)/shard_map/ppermute | solution.py:23
  76.6 52.4 %collective-permute-start.15 = (f32[8,32,512]{2,1,0:T(8,128)}, f32[8,32,512]{2,1,0:T(8,128)S(1)}, u32[]{:S(2)}, u32[]{:S(2)}) collective-permute-start(f32[8,32,512]{2,1,0:T(8,128)} %copy-done.21), channel_id=1, source_target_pairs={{0,6},{1,7},{2,4},{3,5},{4,2},{5,3},{6,0},{7,1},{8,14},{9,15},{10,... | collective-permute-start | bytes 1572872 | tf_op jit(solution)/shard_map/ppermute | solution.py:23
  101.4 36.3 %collective-permute-start.16 = (f32[8,32,512]{2,1,0:T(8,128)}, f32[8,32,512]{2,1,0:T(8,128)}, u32[]{:S(2)}, u32[]{:S(2)}) collective-permute-start(f32[8,32,512]{2,1,0:T(8,128)} %get-tuple-element.80), channel_id=1, source_target_pairs={{0,2},{1,3},{2,0},{3,1},{4,6},{5,7},{6,4},{7,5},{8,10},{9,11},{10,... | collective-permute-start | bytes 1572872 | tf_op jit(solution)/shard_map/ppermute | solution.py:23
  102.1 77.2 %collective-permute-start.17 = (f32[8,32,512]{2,1,0:T(8,128)}, f32[8,32,512]{2,1,0:T(8,128)}, u32[]{:S(2)}, u32[]{:S(2)}) collective-permute-start(f32[8,32,512]{2,1,0:T(8,128)} %get-tuple-element.81), channel_id=1, source_target_pairs={{0,5},{1,4},{2,7},{3,6},{4,1},{5,0},{6,3},{7,2},{8,13},{9,12},{10,... | collective-permute-start | bytes 1572872 | tf_op jit(solution)/shard_map/ppermute | solution.py:23
  107.2 75.4 %collective-permute-start.18 = (f32[8,32,512]{2,1,0:T(8,128)}, f32[8,32,512]{2,1,0:T(8,128)}, u32[]{:S(2)}, u32[]{:S(2)}) collective-permute-start(f32[8,32,512]{2,1,0:T(8,128)} %get-tuple-element.82), channel_id=1, source_target_pairs={{0,1},{1,0},{2,3},{3,2},{4,5},{5,4},{6,7},{7,6},{8,9},{9,8},{10,11... | collective-permute-start | bytes 1572872 | tf_op jit(solution)/shard_map/ppermute | solution.py:23
  108.6 80.0 %collective-permute-start.11 = (f32[8,32,512]{2,1,0:T(8,128)}, f32[8,32,512]{2,1,0:T(8,128)S(1)}, u32[]{:S(2)}, u32[]{:S(2)}) collective-permute-start(f32[8,32,512]{2,1,0:T(8,128)} %get-tuple-element.70), channel_id=1, source_target_pairs={{0,4},{1,5},{2,6},{3,7},{4,0},{5,1},{6,2},{7,3},{8,12},{9,13},{10,... | collective-permute-start | bytes 1572872 | tf_op jit(solution)/shard_map/ppermute | solution.py:23
  129.9 71.9 %collective-permute-start.20 = (f32[8,32,512]{2,1,0:T(8,128)}, f32[8,32,512]{2,1,0:T(8,128)}, u32[]{:S(2)}, u32[]{:S(2)}) collective-permute-start(f32[8,32,512]{2,1,0:T(8,128)} %get-tuple-element.86), channel_id=1, source_target_pairs={{0,7},{1,6},{2,5},{3,4},{4,3},{5,2},{6,1},{7,0},{8,15},{9,14},{10,... | collective-permute-start | bytes 1572872 | tf_op jit(solution)/shard_map/ppermute | solution.py:23
  137.7 78.3 %collective-permute-start.21 = (f32[8,32,512]{2,1,0:T(8,128)S(1)}, f32[8,32,512]{2,1,0:T(8,128)S(1)}, u32[]{:S(2)}, u32[]{:S(2)}) collective-permute-start(f32[8,32,512]{2,1,0:T(8,128)S(1)} %copy-done.20), channel_id=1, source_target_pairs={{0,3},{1,2},{2,1},{3,0},{4,7},{5,6},{6,5},{7,4},{8,11},{9,10},{10,... | collective-permute-start | bytes 1572872 | tf_op jit(solution)/shard_map/ppermute | solution.py:23
  179.4 36.9 %collective-permute-start.22 = (f32[8,32,512]{2,1,0:T(8,128)S(1)}, f32[8,32,512]{2,1,0:T(8,128)S(1)}, u32[]{:S(2)}, u32[]{:S(2)}) collective-permute-start(f32[8,32,512]{2,1,0:T(8,128)S(1)} %copy-done.18), channel_id=1, source_target_pairs={{0,6},{1,7},{2,4},{3,5},{4,2},{5,3},{6,0},{7,1},{8,14},{9,15},{10,... | collective-permute-start | bytes 1572872 | tf_op jit(solution)/shard_map/ppermute | solution.py:23
  182.6 38.9 %collective-permute-start.23 = (f32[8,32,512]{2,1,0:T(8,128)S(1)}, f32[8,32,512]{2,1,0:T(8,128)S(1)}, u32[]{:S(2)}, u32[]{:S(2)}) collective-permute-start(f32[8,32,512]{2,1,0:T(8,128)S(1)} %copy-done.16), channel_id=1, source_target_pairs={{0,2},{1,3},{2,0},{3,1},{4,6},{5,7},{6,4},{7,5},{8,10},{9,11},{10,... | collective-permute-start | bytes 1572872 | tf_op jit(solution)/shard_map/ppermute | solution.py:23
  188.6 74.9 %collective-permute-start.24 = (f32[8,32,512]{2,1,0:T(8,128)S(1)}, f32[8,32,512]{2,1,0:T(8,128)S(1)}, u32[]{:S(2)}, u32[]{:S(2)}) collective-permute-start(f32[8,32,512]{2,1,0:T(8,128)S(1)} %copy-done.14), channel_id=1, source_target_pairs={{0,5},{1,4},{2,7},{3,6},{4,1},{5,0},{6,3},{7,2},{8,13},{9,12},{10,... | collective-permute-start | bytes 1572872 | tf_op jit(solution)/shard_map/ppermute | solution.py:23
  201.8 76.9 %collective-permute-start.12 = (f32[8,24,512]{2,1,0:T(8,128)S(1)}, f32[8,24,512]{2,1,0:T(8,128)S(1)}, u32[]{:S(2)}, u32[]{:S(2)}) collective-permute-start(f32[8,24,512]{2,1,0:T(8,128)S(1)} %get-tuple-element.76), channel_id=1, source_target_pairs={{0,4},{1,5},{2,6},{3,7},{4,0},{5,1},{6,2},{7,3},{8,12},{9,13},{10,... | collective-permute-start | bytes 1179656 | tf_op jit(solution)/shard_map/ppermute | solution.py:23
  216.0 77.1 %collective-permute-start.25 = (f32[8,32,512]{2,1,0:T(8,128)S(1)}, f32[8,32,512]{2,1,0:T(8,128)S(1)}, u32[]{:S(2)}, u32[]{:S(2)}) collective-permute-start(f32[8,32,512]{2,1,0:T(8,128)S(1)} %copy-done.12), channel_id=1, source_target_pairs={{0,1},{1,0},{2,3},{3,2},{4,5},{5,4},{6,7},{7,6},{8,9},{9,8},{10,11... | collective-permute-start | bytes 1572872 | tf_op jit(solution)/shard_map/ppermute | solution.py:23
  216.2 80.3 %collective-permute-start.39 = (f32[8,24,512]{2,1,0:T(8,128)S(1)}, f32[8,24,512]{2,1,0:T(8,128)S(1)}, u32[]{:S(2)}, u32[]{:S(2)}) collective-permute-start(f32[8,24,512]{2,1,0:T(8,128)S(1)} %get-tuple-element.107), channel_id=1, source_target_pairs={{0,7},{1,6},{2,5},{3,4},{4,3},{5,2},{6,1},{7,0},{8,15},{9,14},{10,... | collective-permute-start | bytes 1179656 | tf_op jit(solution)/shard_map/ppermute | solution.py:23
  221.5 76.4 %collective-permute-start.40 = (f32[8,24,512]{2,1,0:T(8,128)S(1)}, f32[8,24,512]{2,1,0:T(8,128)S(1)}, u32[]{:S(2)}, u32[]{:S(2)}) collective-permute-start(f32[8,24,512]{2,1,0:T(8,128)S(1)} %get-tuple-element.108), channel_id=1, source_target_pairs={{0,3},{1,2},{2,1},{3,0},{4,7},{5,6},{6,5},{7,4},{8,11},{9,10},{10,... | collective-permute-start | bytes 1179656 | tf_op jit(solution)/shard_map/ppermute | solution.py:23
  263.6 34.9 %collective-permute-start.41 = (f32[8,24,512]{2,1,0:T(8,128)S(1)}, f32[8,24,512]{2,1,0:T(8,128)S(1)}, u32[]{:S(2)}, u32[]{:S(2)}) collective-permute-start(f32[8,24,512]{2,1,0:T(8,128)S(1)} %get-tuple-element.109), channel_id=1, source_target_pairs={{0,6},{1,7},{2,4},{3,5},{4,2},{5,3},{6,0},{7,1},{8,14},{9,15},{10,... | collective-permute-start | bytes 1179656 | tf_op jit(solution)/shard_map/ppermute | solution.py:23
  293.1 29.1 %collective-permute-start.19 = (f32[8,16,512]{2,1,0:T(8,128)S(1)}, f32[8,16,512]{2,1,0:T(8,128)S(1)}, u32[]{:S(2)}, u32[]{:S(2)}) collective-permute-start(f32[8,16,512]{2,1,0:T(8,128)S(1)} %get-tuple-element.85), channel_id=1, source_target_pairs={{0,4},{1,5},{2,6},{3,7},{4,0},{5,1},{6,2},{7,3},{8,12},{9,13},{10,... | collective-permute-start | bytes 786440 | tf_op jit(solution)/shard_map/ppermute | solution.py:23
  296.6 43.4 %collective-permute-start.43 = (f32[8,24,512]{2,1,0:T(8,128)S(1)}, f32[8,24,512]{2,1,0:T(8,128)S(1)}, u32[]{:S(2)}, u32[]{:S(2)}) collective-permute-start(f32[8,24,512]{2,1,0:T(8,128)S(1)} %get-tuple-element.111), channel_id=1, source_target_pairs={{0,5},{1,4},{2,7},{3,6},{4,1},{5,0},{6,3},{7,2},{8,13},{9,12},{10,... | collective-permute-start | bytes 1179656 | tf_op jit(solution)/shard_map/ppermute | solution.py:23
  297.9 42.1 %collective-permute-start.44 = (f32[8,24,512]{2,1,0:T(8,128)S(1)}, f32[8,24,512]{2,1,0:T(8,128)S(1)}, u32[]{:S(2)}, u32[]{:S(2)}) collective-permute-start(f32[8,24,512]{2,1,0:T(8,128)S(1)} %get-tuple-element.112), channel_id=1, source_target_pairs={{0,1},{1,0},{2,3},{3,2},{4,5},{5,4},{6,7},{7,6},{8,9},{9,8},{10,11... | collective-permute-start | bytes 1179656 | tf_op jit(solution)/shard_map/ppermute | solution.py:23
  298.5 43.6 %collective-permute-start.33 = (f32[8,16,512]{2,1,0:T(8,128)S(1)}, f32[8,16,512]{2,1,0:T(8,128)S(1)}, u32[]{:S(2)}, u32[]{:S(2)}) collective-permute-start(f32[8,16,512]{2,1,0:T(8,128)S(1)} %get-tuple-element.101), channel_id=1, source_target_pairs={{0,7},{1,6},{2,5},{3,4},{4,3},{5,2},{6,1},{7,0},{8,15},{9,14},{10,... | collective-permute-start | bytes 786440 | tf_op jit(solution)/shard_map/ppermute | solution.py:23
  301.7 41.4 %collective-permute-start.34 = (f32[8,16,512]{2,1,0:T(8,128)S(1)}, f32[8,16,512]{2,1,0:T(8,128)S(1)}, u32[]{:S(2)}, u32[]{:S(2)}) collective-permute-start(f32[8,16,512]{2,1,0:T(8,128)S(1)} %get-tuple-element.102), channel_id=1, source_target_pairs={{0,3},{1,2},{2,1},{3,0},{4,7},{5,6},{6,5},{7,4},{8,11},{9,10},{10,... | collective-permute-start | bytes 786440 | tf_op jit(solution)/shard_map/ppermute | solution.py:23
  340.0 32.1 %collective-permute-start.37 = (f32[8,16,512]{2,1,0:T(8,128)S(1)}, f32[8,16,512]{2,1,0:T(8,128)S(1)}, u32[]{:S(2)}, u32[]{:S(2)}) collective-permute-start(f32[8,16,512]{2,1,0:T(8,128)S(1)} %get-tuple-element.105), channel_id=1, source_target_pairs={{0,5},{1,4},{2,7},{3,6},{4,1},{5,0},{6,3},{7,2},{8,13},{9,12},{10,... | collective-permute-start | bytes 786440 | tf_op jit(solution)/shard_map/ppermute | solution.py:23
  342.0 31.3 %collective-permute-start.38 = (f32[8,16,512]{2,1,0:T(8,128)S(1)}, f32[8,16,512]{2,1,0:T(8,128)S(1)}, u32[]{:S(2)}, u32[]{:S(2)}) collective-permute-start(f32[8,16,512]{2,1,0:T(8,128)S(1)} %get-tuple-element.106), channel_id=1, source_target_pairs={{0,1},{1,0},{2,3},{3,2},{4,5},{5,4},{6,7},{7,6},{8,9},{9,8},{10,11... | collective-permute-start | bytes 786440 | tf_op jit(solution)/shard_map/ppermute | solution.py:23
  343.1 30.3 %collective-permute-start.26 = (f32[8,8,512]{2,1,0:T(8,128)S(1)}, f32[8,8,512]{2,1,0:T(8,128)S(1)}, u32[]{:S(2)}, u32[]{:S(2)}) collective-permute-start(f32[8,8,512]{2,1,0:T(8,128)S(1)} %get-tuple-element.94), channel_id=1, source_target_pairs={{0,4},{1,5},{2,6},{3,7},{4,0},{5,1},{6,2},{7,3},{8,12},{9,13},{10,... | collective-permute-start | bytes 393224 | tf_op jit(solution)/shard_map/ppermute | solution.py:23
  346.3 31.4 %collective-permute-start.27 = (f32[8,8,512]{2,1,0:T(8,128)S(1)}, f32[8,8,512]{2,1,0:T(8,128)S(1)}, u32[]{:S(2)}, u32[]{:S(2)}) collective-permute-start(f32[8,8,512]{2,1,0:T(8,128)S(1)} %get-tuple-element.95), channel_id=1, source_target_pairs={{0,7},{1,6},{2,5},{3,4},{4,3},{5,2},{6,1},{7,0},{8,15},{9,14},{10,... | collective-permute-start | bytes 393224 | tf_op jit(solution)/shard_map/ppermute | solution.py:23
  (46 other events, 1062.4 us)

commit v12 on v11

--- a/solution.py
+++ b/solution.py
@@ -361,7 +361,7 @@
 def chunk_groups(groups):
     if groups < 16:
         return [1] * groups
-    ends = [groups // 8, groups * 3 // 16, groups // 8, groups // 16]
+    ends = [groups // 8, groups * 3 // 16, groups // 16]
     rest = groups - sum(ends)
     return [ends[0], rest - rest // 2, rest // 2] + ends[1:]
 

time: 421 us -> 425 us (level)
  waiting for transfers between devices: 119 us -> 170 us
  starting transfers between devices: 196 us -> 156 us
    ppermute x45 -> x38, waiting for transfers between devices: 110 us -> 160 us  [swap(): lax.ppermute(x, axis, [(i, i ^ k) for i in range(lax.axis_size(axis))])]
    ppermute x45 -> x38, starting transfers between devices: 193 us -> 152 us  [swap(): lax.ppermute(x, axis, [(i, i ^ k) for i in range(lax.axis_size(axis))])]
    unnamed x65 -> x47, local copies, waits for them, and re-layouts: 11.7 us -> 7.56 us
    pallas_call x6 -> x5, Pallas kernels: 51 us -> 48 us  [chunk_step(): pl.pallas_call(functools.partial(chunk_kernel, pieces, block_cells, last)...]
    pallas_call x6 -> x5, Pallas kernels: 16.5 us -> 15.8 us  [pack(): pl.pallas_call(functools.partial(pack_kernel, distances, own, first, rows...]
  transfers between devices with their start and end apart: 46 -> 39, of which waited for: 12 -> 11; matrix products, arithmetic and copies ran while one was open for 3% -> 3% of each run, Pallas kernels for 15% -> 14%
where the time goes in v12:
time: 425 us; the launch traced here: 424 us
  waiting for transfers between devices  170 us (40%)
  starting transfers between devices  156 us (37%)
  Pallas kernels  68.6 us (16%)
  local copies, waits for them, and re-layouts  14.5 us (3%)
  blocking collectives  9.82 us (2%)
  other arithmetic  4.85 us (1%)
    ppermute x38, waiting for transfers between devices, swap(): lax.ppermute(x, axis, [(i, i ^ k) for i in range(lax.axis_size(axis))])  160 us
    ppermute x38, starting transfers between devices, swap(): lax.ppermute(x, axis, [(i, i ^ k) for i in range(lax.axis_size(axis))])  152 us
    pallas_call x5, Pallas kernels, chunk_step(): pl.pallas_call(functools.partial(chunk_kernel, pieces, block_cells, last)...  48 us
    pallas_call x5, Pallas kernels, pack(): pl.pallas_call(functools.partial(pack_kernel, distances, own, first, rows...  15.8 us
    all_to_all x1, blocking collectives, body(): back = lax.all_to_all(step, both, split_axis=0, concat_axis=0, tiled=True)  9.82 us
    all_to_all x1, waiting for transfers between devices, body(): got = lax.all_to_all(sent, both, split_axis=0, concat_axis=0, tiled=True)  9.59 us
  transfers between devices with their start and end apart: 39, of which 11 were waited for; matrix products, arithmetic and copies ran while one was open for 3% of the time, Pallas kernels for 14%

profile of v12, /device:TPU:0, one launch (start us, length us, event | category | flops | bytes accessed | tf_op | source)
XLA Modules:
  0.0 424.4 jit_solution(9899435171963642589)
XLA Ops:
  3.6 4.1 collective-permute-start
  13.1 15.9 %collective-permute-done.refs_0_.refs_1_ = f32[9,16,512]{2,1,0:T(8,128)S(1)} collective-permute-done((f32[9,16,512]{2,1,0:T(8,128)S(1)}, f32[9,16,512]{2,1,0:T(8,128)S(1)}, u32[]{:S(2)}, u32[]{:S(2)}) %collective-permute-start) | collective-permute-done | bytes 294944 | tf_op jit(solution)/shard_map/ppermute | solution.py:23
  29.1 4.5 %pack.6 = (f32[8,40,512]{2,1,0:T(8,128)}, f32[8,40,512]{2,1,0:T(8,128)}, f32[8,40,512]{2,1,0:T(8,128)S(1)}, f32[8,40,512]{2,1,0:T(8,128)}, f32[8,40,512]{2,1,0:T...) custom-call(s32[2]{0:T(128)S(1)} %pad_add_fusion.place_ref, f32[8,1024,512]{2,1,0:T(8,128)} %bitcast.17, ...), custom_call_target="tpu_custom_call" | custom-call | bytes 9175040 | tf_op jit(solution)/shard_map/pack/pallas_call | solution.py:100
  33.6 3.7 collective-permute-start.4
  37.3 20.4 %collective-permute-start.5 = (f32[9,16,512]{2,1,0:T(8,128)S(1)}, f32[9,16,512]{2,1,0:T(8,128)S(1)}, u32[]{:S(2)}, u32[]{:S(2)}) collective-permute-start(f32[9,16,512]{2,1,0:T(8,128)S(1)} %get-tuple-element.58), channel_id=1, source_target_pairs={{0,5},{1,4},{2,7},{3,6},{4,1},{5,0},{6,3},{7,2},{8,13},{9,12},{10,... | collective-permute-start | bytes 884744 | tf_op jit(solution)/shard_map/ppermute | solution.py:23
  60.3 42.9 %collective-permute-done.5.refs_5_.refs_6_ = f32[9,16,512]{2,1,0:T(8,128)S(1)} collective-permute-done((f32[9,16,512]{2,1,0:T(8,128)S(1)}, f32[9,16,512]{2,1,0:T(8,128)S(1)}, u32[]{:S(2)}, u32[]{:S(2)}) %collective-permute-start.5) | collective-permute-done | bytes 294944 | tf_op jit(solution)/shard_map/ppermute | solution.py:23
  106.1 3.4 pack.7
  118.6 3.0 collective-permute-start.17
  121.6 5.8 %collective-permute-start.11 = (f32[8,40,512]{2,1,0:T(8,128)}, f32[8,40,512]{2,1,0:T(8,128)}, u32[]{:S(2)}, u32[]{:S(2)}) collective-permute-start(f32[8,40,512]{2,1,0:T(8,128)} %get-tuple-element.61), channel_id=1, source_target_pairs={{0,4},{1,5},{2,6},{3,7},{4,0},{5,1},{6,2},{7,3},{8,12},{9,13},{10,... | collective-permute-start | bytes 1966088 | tf_op jit(solution)/shard_map/ppermute | solution.py:23
  135.6 10.2 %collective-permute-done.15.refs_4_ = f32[8,40,512]{2,1,0:T(8,128)} collective-permute-done((f32[8,40,512]{2,1,0:T(8,128)}, f32[8,40,512]{2,1,0:T(8,128)}, u32[]{:S(2)}, u32[]{:S(2)}) %collective-permute-start.15) | collective-permute-done | bytes 655392 | tf_op jit(solution)/shard_map/ppermute | solution.py:23
  147.0 15.8 %collective-permute-done.16.refs_5_ = f32[8,40,512]{2,1,0:T(8,128)} collective-permute-done((f32[8,40,512]{2,1,0:T(8,128)}, f32[8,40,512]{2,1,0:T(8,128)}, u32[]{:S(2)}, u32[]{:S(2)}) %collective-permute-start.16) | collective-permute-done | bytes 655392 | tf_op jit(solution)/shard_map/ppermute | solution.py:23
  162.7 44.4 %collective-permute-done.17.refs_6_ = f32[8,40,512]{2,1,0:T(8,128)} collective-permute-done((f32[8,40,512]{2,1,0:T(8,128)}, f32[8,40,512]{2,1,0:T(8,128)}, u32[]{:S(2)}, u32[]{:S(2)}) %collective-permute-start.17) | collective-permute-done | bytes 655392 | tf_op jit(solution)/shard_map/ppermute | solution.py:23
  207.1 4.5 %collective-permute-start.34 = (f32[8,40,512]{2,1,0:T(8,128)S(1)}, f32[8,40,512]{2,1,0:T(8,128)S(1)}, u32[]{:S(2)}, u32[]{:S(2)}) collective-permute-start(f32[8,40,512]{2,1,0:T(8,128)S(1)} %copy-done.12), channel_id=1, source_target_pairs={{0,6},{1,7},{2,4},{3,5},{4,2},{5,3},{6,0},{7,1},{8,14},{9,15},{10,... | collective-permute-start | bytes 1966088 | tf_op jit(solution)/shard_map/ppermute | solution.py:23
  211.6 21.6 %collective-permute-done.11.refs_0_.refs_1_ = f32[8,40,512]{2,1,0:T(8,128)} collective-permute-done((f32[8,40,512]{2,1,0:T(8,128)}, f32[8,40,512]{2,1,0:T(8,128)}, u32[]{:S(2)}, u32[]{:S(2)}) %collective-permute-start.11) | collective-permute-done | bytes 655392 | tf_op jit(solution)/shard_map/ppermute | solution.py:23
  235.9 6.8 %chunk_step.5 = (f32[256,512]{1,0:T(8,128)}, f32[256,128]{1,0:T(8,128)S(1)}) custom-call(s32[2]{0:T(128)S(1)} %pad_add_fusion.place_ref, f32[8,1024,512]{2,1,0:T(8,128)} %bitcast.19, f32[9,16,512]{2,1,0:T(8,128)S(1)} %collective-permute-done.refs_0_.refs_1_, ...), custom_call_target="tpu_custom_call", output_to_operand_aliasing={{0}: (15, {}), {1}: (16, {})} | custom-call | flops 3221225472 | bytes 2097152 | tf_op jit(solution)/shard_map/chunk_step/pallas_call | solution.py:252
  242.7 3.0 pack.8
  245.7 3.4 collective-permute-start.12
  254.8 42.4 %collective-permute-start.27 = (f32[8,24,512]{2,1,0:T(8,128)S(1)}, f32[8,24,512]{2,1,0:T(8,128)S(1)}, u32[]{:S(2)}, u32[]{:S(2)}) collective-permute-start(f32[8,24,512]{2,1,0:T(8,128)S(1)} %get-tuple-element.84), channel_id=1, source_target_pairs={{0,3},{1,2},{2,1},{3,0},{4,7},{5,6},{6,5},{7,4},{8,11},{9,10},{10,... | collective-permute-start | bytes 1179656 | tf_op jit(solution)/shard_map/ppermute | solution.py:23
  297.3 3.3 collective-permute-done.12.refs_0_.refs_1_
  300.6 4.6 %collective-permute-start.28 = (f32[8,24,512]{2,1,0:T(8,128)S(1)}, f32[8,24,512]{2,1,0:T(8,128)S(1)}, u32[]{:S(2)}, u32[]{:S(2)}) collective-permute-start(f32[8,24,512]{2,1,0:T(8,128)S(1)} %get-tuple-element.85), channel_id=1, source_target_pairs={{0,6},{1,7},{2,4},{3,5},{4,2},{5,3},{6,0},{7,1},{8,14},{9,15},{10,... | collective-permute-start | bytes 1179656 | tf_op jit(solution)/shard_map/ppermute | solution.py:23
  305.2 13.5 %chunk_step.6 = (f32[256,512]{1,0:T(8,128)}, f32[256,128]{1,0:T(8,128)S(1)}) custom-call(s32[2]{0:T(128)S(1)} %pad_add_fusion.place_ref, f32[8,1024,512]{2,1,0:T(8,128)} %bitcast.21, f32[8,40,512]{2,1,0:T(8,128)S(1)} %collective-permute-done.10.refs_0_.refs_1_, ...), custom_call_target="tpu_custom_call", output_to_operand_aliasing={{0}: (15, {}), {1}: (16, {})} | custom-call | flops 8053063680 | bytes 5242880 | tf_op jit(solution)/shard_map/chunk_step/pallas_call | solution.py:252
  321.5 3.5 collective-permute-done.36.refs_6_
  325.0 4.1 collective-permute-start.30
  332.3 4.7 %collective-permute-start.19 = (f32[8,8,512]{2,1,0:T(8,128)S(1)}, f32[8,8,512]{2,1,0:T(8,128)S(1)}, u32[]{:S(2)}, u32[]{:S(2)}) collective-permute-start(f32[8,8,512]{2,1,0:T(8,128)S(1)} %get-tuple-element.76), channel_id=1, source_target_pairs={{0,4},{1,5},{2,6},{3,7},{4,0},{5,1},{6,2},{7,3},{8,12},{9,13},{10,... | collective-permute-start | bytes 393224 | tf_op jit(solution)/shard_map/ppermute | solution.py:23
  337.8 13.4 %chunk_step.7 = (f32[256,512]{1,0:T(8,128)}, f32[256,128]{1,0:T(8,128)S(1)}) custom-call(s32[2]{0:T(128)S(1)} %pad_add_fusion.place_ref, f32[8,1024,512]{2,1,0:T(8,128)} %bitcast.23, f32[8,40,512]{2,1,0:T(8,128)} %collective-permute-done.11.refs_0_.refs_1_, ...), custom_call_target="tpu_custom_call", output_to_operand_aliasing={{0}: (15, {}), {1}: (16, {})} | custom-call | flops 8053063680 | bytes 5242880 | tf_op jit(solution)/shard_map/chunk_step/pallas_call | solution.py:252
  351.2 21.3 %collective-permute-start.21 = (f32[8,8,512]{2,1,0:T(8,128)S(1)}, f32[8,8,512]{2,1,0:T(8,128)S(1)}, u32[]{:S(2)}, u32[]{:S(2)}) collective-permute-start(f32[8,8,512]{2,1,0:T(8,128)S(1)} %get-tuple-element.78), channel_id=1, source_target_pairs={{0,3},{1,2},{2,1},{3,0},{4,7},{5,6},{6,5},{7,4},{8,11},{9,10},{10,... | collective-permute-start | bytes 393224 | tf_op jit(solution)/shard_map/ppermute | solution.py:23
  374.3 4.4 %collective-permute-start.24 = (f32[8,8,512]{2,1,0:T(8,128)S(1)}, f32[8,8,512]{2,1,0:T(8,128)S(1)}, u32[]{:S(2)}, u32[]{:S(2)}) collective-permute-start(f32[8,8,512]{2,1,0:T(8,128)S(1)} %get-tuple-element.81), channel_id=1, source_target_pairs={{0,5},{1,4},{2,7},{3,6},{4,1},{5,0},{6,3},{7,2},{8,13},{9,12},{10,... | collective-permute-start | bytes 393224 | tf_op jit(solution)/shard_map/ppermute | solution.py:23
  378.7 9.2 %chunk_step.8 = (f32[256,512]{1,0:T(8,128)}, f32[256,128]{1,0:T(8,128)S(1)}) custom-call(s32[2]{0:T(128)S(1)} %pad_add_fusion.place_ref, f32[8,1024,512]{2,1,0:T(8,128)} %bitcast.24, f32[8,24,512]{2,1,0:T(8,128)S(1)} %collective-permute-done.12.refs_0_.refs_1_, ...), custom_call_target="tpu_custom_call", output_to_operand_aliasing={{0}: (15, {}), {1}: (16, {})} | custom-call | flops 4831838208 | bytes 3145728 | tf_op jit(solution)/shard_map/chunk_step/pallas_call | solution.py:252
  388.0 5.1 %chunk_step.9 = (f32[256,512]{1,0:T(8,128)}, f32[256,128]{1,0:T(8,128)S(1)}) custom-call(s32[2]{0:T(128)S(1)} %pad_add_fusion.place_ref, f32[8,1024,512]{2,1,0:T(8,128)} %bitcast.25, f32[8,8,512]{2,1,0:T(8,128)S(1)} %collective-permute-done.19.refs_1_, ...), custom_call_target="tpu_custom_call", output_to_operand_aliasing={{0}: (15, {}), {1}: (16, {})} | custom-call | flops 1610612736 | bytes 1048576 | tf_op jit(solution)/shard_map/chunk_step/pallas_call | solution.py:252
  393.0 3.4 all-to-all-start
  403.2 9.6 %all-to-all-done.got_ref = f32[32,8,512]{2,1,0:T(8,128)S(1)} async-done(((f32[32,8,512]{2,1,0:T(8,128)}), f32[32,8,512]{2,1,0:T(8,128)S(1)}, u32[]{:S(2)}, u32[]{:S(2)}) %all-to-all-start) | async-done | bytes 524320 | tf_op jit(solution)/shard_map/all_to_all | solution.py:425
  413.6 9.8 %all_to_all.10.back_ref = f32[32,8,128]{2,1,0:T(8,128)S(1)} all-to-all(f32[32,8,128]{2,1,0:T(8,128)S(1)} %gradient_step.1), channel_id=1, replica_groups=mesh['tile'=4,'freq'=8] {'tile','freq'}, dimensions={0} | all-to-all | bytes 262144 | tf_op jit(solution)/shard_map/all_to_all | solution.py:428
  (129 shorter events, 57.7 us)
Async XLA Ops:
  3.6 25.4 %collective-permute-start = (f32[9,16,512]{2,1,0:T(8,128)S(1)}, f32[9,16,512]{2,1,0:T(8,128)S(1)}, u32[]{:S(2)}, u32[]{:S(2)}) collective-permute-start(f32[9,16,512]{2,1,0:T(8,128)S(1)} %get-tuple-element.53), channel_id=1, source_target_pairs={{0,4},{1,5},{2,6},{3,7},{4,0},{5,1},{6,2},{7,3},{8,12},{9,13},{10,... | collective-permute-start | bytes 884744 | tf_op jit(solution)/shard_map/ppermute | solution.py:23
  7.7 29.6 %collective-permute-start.1 = (f32[9,16,512]{2,1,0:T(8,128)S(1)}, f32[9,16,512]{2,1,0:T(8,128)S(1)}, u32[]{:S(2)}, u32[]{:S(2)}) collective-permute-start(f32[9,16,512]{2,1,0:T(8,128)S(1)} %get-tuple-element.54), channel_id=1, source_target_pairs={{0,7},{1,6},{2,5},{3,4},{4,3},{5,2},{6,1},{7,0},{8,15},{9,14},{10,... | collective-permute-start | bytes 884744 | tf_op jit(solution)/shard_map/ppermute | solution.py:23
  10.0 47.7 %collective-permute-start.2 = (f32[9,16,512]{2,1,0:T(8,128)S(1)}, f32[9,16,512]{2,1,0:T(8,128)S(1)}, u32[]{:S(2)}, u32[]{:S(2)}) collective-permute-start(f32[9,16,512]{2,1,0:T(8,128)S(1)} %get-tuple-element.55), channel_id=1, source_target_pairs={{0,3},{1,2},{2,1},{3,0},{4,7},{5,6},{6,5},{7,4},{8,11},{9,10},{10,... | collective-permute-start | bytes 884744 | tf_op jit(solution)/shard_map/ppermute | solution.py:23
  10.3 49.0 %collective-permute-start.3 = (f32[9,16,512]{2,1,0:T(8,128)S(1)}, f32[9,16,512]{2,1,0:T(8,128)S(1)}, u32[]{:S(2)}, u32[]{:S(2)}) collective-permute-start(f32[9,16,512]{2,1,0:T(8,128)S(1)} %get-tuple-element.56), channel_id=1, source_target_pairs={{0,6},{1,7},{2,4},{3,5},{4,2},{5,3},{6,0},{7,1},{8,14},{9,15},{10,... | collective-permute-start | bytes 884744 | tf_op jit(solution)/shard_map/ppermute | solution.py:23
  33.6 72.3 %collective-permute-start.10 = (f32[8,40,512]{2,1,0:T(8,128)}, f32[8,40,512]{2,1,0:T(8,128)S(1)}, u32[]{:S(2)}, u32[]{:S(2)}) collective-permute-start(f32[8,40,512]{2,1,0:T(8,128)} %get-tuple-element.60), channel_id=1, source_target_pairs={{0,4},{1,5},{2,6},{3,7},{4,0},{5,1},{6,2},{7,3},{8,12},{9,13},{10,... | collective-permute-start | bytes 1966088 | tf_op jit(solution)/shard_map/ppermute | solution.py:23
  33.6 26.7 %collective-permute-start.4 = (f32[9,16,512]{2,1,0:T(8,128)S(1)}, f32[9,16,512]{2,1,0:T(8,128)S(1)}, u32[]{:S(2)}, u32[]{:S(2)}) collective-permute-start(f32[9,16,512]{2,1,0:T(8,128)S(1)} %get-tuple-element.57), channel_id=1, source_target_pairs={{0,2},{1,3},{2,0},{3,1},{4,6},{5,7},{6,4},{7,5},{8,10},{9,11},{10,... | collective-permute-start | bytes 884744 | tf_op jit(solution)/shard_map/ppermute | solution.py:23
  37.3 65.9 %collective-permute-start.5 = (f32[9,16,512]{2,1,0:T(8,128)S(1)}, f32[9,16,512]{2,1,0:T(8,128)S(1)}, u32[]{:S(2)}, u32[]{:S(2)}) collective-permute-start(f32[9,16,512]{2,1,0:T(8,128)S(1)} %get-tuple-element.58), channel_id=1, source_target_pairs={{0,5},{1,4},{2,7},{3,6},{4,1},{5,0},{6,3},{7,2},{8,13},{9,12},{10,... | collective-permute-start | bytes 884744 | tf_op jit(solution)/shard_map/ppermute | solution.py:23
  57.8 45.5 %collective-permute-start.6 = (f32[9,16,512]{2,1,0:T(8,128)S(1)}, f32[9,16,512]{2,1,0:T(8,128)S(1)}, u32[]{:S(2)}, u32[]{:S(2)}) collective-permute-start(f32[9,16,512]{2,1,0:T(8,128)S(1)} %get-tuple-element.59), channel_id=1, source_target_pairs={{0,1},{1,0},{2,3},{3,2},{4,5},{5,4},{6,7},{7,6},{8,9},{9,8},{10,11... | collective-permute-start | bytes 884744 | tf_op jit(solution)/shard_map/ppermute | solution.py:23
  59.2 62.4 %collective-permute-start.13 = (f32[8,40,512]{2,1,0:T(8,128)}, f32[8,40,512]{2,1,0:T(8,128)}, u32[]{:S(2)}, u32[]{:S(2)}) collective-permute-start(f32[8,40,512]{2,1,0:T(8,128)} %get-tuple-element.68), channel_id=1, source_target_pairs={{0,7},{1,6},{2,5},{3,4},{4,3},{5,2},{6,1},{7,0},{8,15},{9,14},{10,... | collective-permute-start | bytes 1966088 | tf_op jit(solution)/shard_map/ppermute | solution.py:23
  105.9 23.5 %collective-permute-start.14 = (f32[8,40,512]{2,1,0:T(8,128)}, f32[8,40,512]{2,1,0:T(8,128)S(1)}, u32[]{:S(2)}, u32[]{:S(2)}) collective-permute-start(f32[8,40,512]{2,1,0:T(8,128)} %copy-done.17), channel_id=1, source_target_pairs={{0,3},{1,2},{2,1},{3,0},{4,7},{5,6},{6,5},{7,4},{8,11},{9,10},{10,... | collective-permute-start | bytes 1966088 | tf_op jit(solution)/shard_map/ppermute | solution.py:23
  114.6 31.2 %collective-permute-start.15 = (f32[8,40,512]{2,1,0:T(8,128)}, f32[8,40,512]{2,1,0:T(8,128)}, u32[]{:S(2)}, u32[]{:S(2)}) collective-permute-start(f32[8,40,512]{2,1,0:T(8,128)} %get-tuple-element.70), channel_id=1, source_target_pairs={{0,6},{1,7},{2,4},{3,5},{4,2},{5,3},{6,0},{7,1},{8,14},{9,15},{10,... | collective-permute-start | bytes 1966088 | tf_op jit(solution)/shard_map/ppermute | solution.py:23
  118.6 44.1 %collective-permute-start.16 = (f32[8,40,512]{2,1,0:T(8,128)}, f32[8,40,512]{2,1,0:T(8,128)}, u32[]{:S(2)}, u32[]{:S(2)}) collective-permute-start(f32[8,40,512]{2,1,0:T(8,128)} %get-tuple-element.71), channel_id=1, source_target_pairs={{0,2},{1,3},{2,0},{3,1},{4,6},{5,7},{6,4},{7,5},{8,10},{9,11},{10,... | collective-permute-start | bytes 1966088 | tf_op jit(solution)/shard_map/ppermute | solution.py:23
  118.6 88.5 %collective-permute-start.17 = (f32[8,40,512]{2,1,0:T(8,128)}, f32[8,40,512]{2,1,0:T(8,128)}, u32[]{:S(2)}, u32[]{:S(2)}) collective-permute-start(f32[8,40,512]{2,1,0:T(8,128)} %get-tuple-element.72), channel_id=1, source_target_pairs={{0,5},{1,4},{2,7},{3,6},{4,1},{5,0},{6,3},{7,2},{8,13},{9,12},{10,... | collective-permute-start | bytes 1966088 | tf_op jit(solution)/shard_map/ppermute | solution.py:23
  121.6 111.6 %collective-permute-start.11 = (f32[8,40,512]{2,1,0:T(8,128)}, f32[8,40,512]{2,1,0:T(8,128)}, u32[]{:S(2)}, u32[]{:S(2)}) collective-permute-start(f32[8,40,512]{2,1,0:T(8,128)} %get-tuple-element.61), channel_id=1, source_target_pairs={{0,4},{1,5},{2,6},{3,7},{4,0},{5,1},{6,2},{7,3},{8,12},{9,13},{10,... | collective-permute-start | bytes 1966088 | tf_op jit(solution)/shard_map/ppermute | solution.py:23
  130.2 115.5 %collective-permute-start.18 = (f32[8,40,512]{2,1,0:T(8,128)}, f32[8,40,512]{2,1,0:T(8,128)}, u32[]{:S(2)}, u32[]{:S(2)}) collective-permute-start(f32[8,40,512]{2,1,0:T(8,128)} %get-tuple-element.73), channel_id=1, source_target_pairs={{0,1},{1,0},{2,3},{3,2},{4,5},{5,4},{6,7},{7,6},{8,9},{9,8},{10,11... | collective-permute-start | bytes 1966088 | tf_op jit(solution)/shard_map/ppermute | solution.py:23
  145.8 103.3 %collective-permute-start.32 = (f32[8,40,512]{2,1,0:T(8,128)S(1)}, f32[8,40,512]{2,1,0:T(8,128)S(1)}, u32[]{:S(2)}, u32[]{:S(2)}) collective-permute-start(f32[8,40,512]{2,1,0:T(8,128)S(1)} %copy-done.16), channel_id=1, source_target_pairs={{0,7},{1,6},{2,5},{3,4},{4,3},{5,2},{6,1},{7,0},{8,15},{9,14},{10,... | collective-permute-start | bytes 1966088 | tf_op jit(solution)/shard_map/ppermute | solution.py:23
  162.7 89.0 %collective-permute-start.33 = (f32[8,40,512]{2,1,0:T(8,128)S(1)}, f32[8,40,512]{2,1,0:T(8,128)S(1)}, u32[]{:S(2)}, u32[]{:S(2)}) collective-permute-start(f32[8,40,512]{2,1,0:T(8,128)S(1)} %copy-done.14), channel_id=1, source_target_pairs={{0,3},{1,2},{2,1},{3,0},{4,7},{5,6},{6,5},{7,4},{8,11},{9,10},{10,... | collective-permute-start | bytes 1966088 | tf_op jit(solution)/shard_map/ppermute | solution.py:23
  207.1 47.1 %collective-permute-start.34 = (f32[8,40,512]{2,1,0:T(8,128)S(1)}, f32[8,40,512]{2,1,0:T(8,128)S(1)}, u32[]{:S(2)}, u32[]{:S(2)}) collective-permute-start(f32[8,40,512]{2,1,0:T(8,128)S(1)} %copy-done.12), channel_id=1, source_target_pairs={{0,6},{1,7},{2,4},{3,5},{4,2},{5,3},{6,0},{7,1},{8,14},{9,15},{10,... | collective-permute-start | bytes 1966088 | tf_op jit(solution)/shard_map/ppermute | solution.py:23
  233.2 21.6 %collective-permute-start.35 = (f32[8,40,512]{2,1,0:T(8,128)S(1)}, f32[8,40,512]{2,1,0:T(8,128)S(1)}, u32[]{:S(2)}, u32[]{:S(2)}) collective-permute-start(f32[8,40,512]{2,1,0:T(8,128)S(1)} %copy-done.10), channel_id=1, source_target_pairs={{0,2},{1,3},{2,0},{3,1},{4,6},{5,7},{6,4},{7,5},{8,10},{9,11},{10,... | collective-permute-start | bytes 1966088 | tf_op jit(solution)/shard_map/ppermute | solution.py:23
  245.7 54.9 %collective-permute-start.12 = (f32[8,24,512]{2,1,0:T(8,128)S(1)}, f32[8,24,512]{2,1,0:T(8,128)S(1)}, u32[]{:S(2)}, u32[]{:S(2)}) collective-permute-start(f32[8,24,512]{2,1,0:T(8,128)S(1)} %get-tuple-element.67), channel_id=1, source_target_pairs={{0,4},{1,5},{2,6},{3,7},{4,0},{5,1},{6,2},{7,3},{8,12},{9,13},{10,... | collective-permute-start | bytes 1179656 | tf_op jit(solution)/shard_map/ppermute | solution.py:23
  249.2 75.8 %collective-permute-start.36 = (f32[8,40,512]{2,1,0:T(8,128)S(1)}, f32[8,40,512]{2,1,0:T(8,128)S(1)}, u32[]{:S(2)}, u32[]{:S(2)}) collective-permute-start(f32[8,40,512]{2,1,0:T(8,128)S(1)} %copy-done.6), channel_id=1, source_target_pairs={{0,5},{1,4},{2,7},{3,6},{4,1},{5,0},{6,3},{7,2},{8,13},{9,12},{10,... | collective-permute-start | bytes 1966088 | tf_op jit(solution)/shard_map/ppermute | solution.py:23
  251.8 73.2 %collective-permute-start.37 = (f32[8,40,512]{2,1,0:T(8,128)S(1)}, f32[8,40,512]{2,1,0:T(8,128)S(1)}, u32[]{:S(2)}, u32[]{:S(2)}) collective-permute-start(f32[8,40,512]{2,1,0:T(8,128)S(1)} %copy-done.4), channel_id=1, source_target_pairs={{0,1},{1,0},{2,3},{3,2},{4,5},{5,4},{6,7},{7,6},{8,9},{9,8},{10,11... | collective-permute-start | bytes 1966088 | tf_op jit(solution)/shard_map/ppermute | solution.py:23
  254.2 74.9 %collective-permute-start.26 = (f32[8,24,512]{2,1,0:T(8,128)S(1)}, f32[8,24,512]{2,1,0:T(8,128)S(1)}, u32[]{:S(2)}, u32[]{:S(2)}) collective-permute-start(f32[8,24,512]{2,1,0:T(8,128)S(1)} %get-tuple-element.83), channel_id=1, source_target_pairs={{0,7},{1,6},{2,5},{3,4},{4,3},{5,2},{6,1},{7,0},{8,15},{9,14},{10,... | collective-permute-start | bytes 1179656 | tf_op jit(solution)/shard_map/ppermute | solution.py:23
  254.8 77.5 %collective-permute-start.27 = (f32[8,24,512]{2,1,0:T(8,128)S(1)}, f32[8,24,512]{2,1,0:T(8,128)S(1)}, u32[]{:S(2)}, u32[]{:S(2)}) collective-permute-start(f32[8,24,512]{2,1,0:T(8,128)S(1)} %get-tuple-element.84), channel_id=1, source_target_pairs={{0,3},{1,2},{2,1},{3,0},{4,7},{5,6},{6,5},{7,4},{8,11},{9,10},{10,... | collective-permute-start | bytes 1179656 | tf_op jit(solution)/shard_map/ppermute | solution.py:23
  300.6 36.4 %collective-permute-start.28 = (f32[8,24,512]{2,1,0:T(8,128)S(1)}, f32[8,24,512]{2,1,0:T(8,128)S(1)}, u32[]{:S(2)}, u32[]{:S(2)}) collective-permute-start(f32[8,24,512]{2,1,0:T(8,128)S(1)} %get-tuple-element.85), channel_id=1, source_target_pairs={{0,6},{1,7},{2,4},{3,5},{4,2},{5,3},{6,0},{7,1},{8,14},{9,15},{10,... | collective-permute-start | bytes 1179656 | tf_op jit(solution)/shard_map/ppermute | solution.py:23
  325.0 26.2 %collective-permute-start.29 = (f32[8,24,512]{2,1,0:T(8,128)S(1)}, f32[8,24,512]{2,1,0:T(8,128)S(1)}, u32[]{:S(2)}, u32[]{:S(2)}) collective-permute-start(f32[8,24,512]{2,1,0:T(8,128)S(1)} %get-tuple-element.86), channel_id=1, source_target_pairs={{0,2},{1,3},{2,0},{3,1},{4,6},{5,7},{6,4},{7,5},{8,10},{9,11},{10,... | collective-permute-start | bytes 1179656 | tf_op jit(solution)/shard_map/ppermute | solution.py:23
  325.0 47.5 %collective-permute-start.30 = (f32[8,24,512]{2,1,0:T(8,128)S(1)}, f32[8,24,512]{2,1,0:T(8,128)S(1)}, u32[]{:S(2)}, u32[]{:S(2)}) collective-permute-start(f32[8,24,512]{2,1,0:T(8,128)S(1)} %get-tuple-element.87), channel_id=1, source_target_pairs={{0,5},{1,4},{2,7},{3,6},{4,1},{5,0},{6,3},{7,2},{8,13},{9,12},{10,... | collective-permute-start | bytes 1179656 | tf_op jit(solution)/shard_map/ppermute | solution.py:23
  329.1 45.2 %collective-permute-start.31 = (f32[8,24,512]{2,1,0:T(8,128)S(1)}, f32[8,24,512]{2,1,0:T(8,128)S(1)}, u32[]{:S(2)}, u32[]{:S(2)}) collective-permute-start(f32[8,24,512]{2,1,0:T(8,128)S(1)} %get-tuple-element.88), channel_id=1, source_target_pairs={{0,1},{1,0},{2,3},{3,2},{4,5},{5,4},{6,7},{7,6},{8,9},{9,8},{10,11... | collective-permute-start | bytes 1179656 | tf_op jit(solution)/shard_map/ppermute | solution.py:23
  332.3 42.0 %collective-permute-start.19 = (f32[8,8,512]{2,1,0:T(8,128)S(1)}, f32[8,8,512]{2,1,0:T(8,128)S(1)}, u32[]{:S(2)}, u32[]{:S(2)}) collective-permute-start(f32[8,8,512]{2,1,0:T(8,128)S(1)} %get-tuple-element.76), channel_id=1, source_target_pairs={{0,4},{1,5},{2,6},{3,7},{4,0},{5,1},{6,2},{7,3},{8,12},{9,13},{10,... | collective-permute-start | bytes 393224 | tf_op jit(solution)/shard_map/ppermute | solution.py:23
  337.0 41.7 %collective-permute-start.20 = (f32[8,8,512]{2,1,0:T(8,128)S(1)}, f32[8,8,512]{2,1,0:T(8,128)S(1)}, u32[]{:S(2)}, u32[]{:S(2)}) collective-permute-start(f32[8,8,512]{2,1,0:T(8,128)S(1)} %get-tuple-element.77), channel_id=1, source_target_pairs={{0,7},{1,6},{2,5},{3,4},{4,3},{5,2},{6,1},{7,0},{8,15},{9,14},{10,... | collective-permute-start | bytes 393224 | tf_op jit(solution)/shard_map/ppermute | solution.py:23
  351.2 36.7 %collective-permute-start.21 = (f32[8,8,512]{2,1,0:T(8,128)S(1)}, f32[8,8,512]{2,1,0:T(8,128)S(1)}, u32[]{:S(2)}, u32[]{:S(2)}) collective-permute-start(f32[8,8,512]{2,1,0:T(8,128)S(1)} %get-tuple-element.78), channel_id=1, source_target_pairs={{0,3},{1,2},{2,1},{3,0},{4,7},{5,6},{6,5},{7,4},{8,11},{9,10},{10,... | collective-permute-start | bytes 393224 | tf_op jit(solution)/shard_map/ppermute | solution.py:23
  393.0 19.7 %all-to-all-start = ((f32[32,8,512]{2,1,0:T(8,128)}), f32[32,8,512]{2,1,0:T(8,128)S(1)}, u32[]{:S(2)}, u32[]{:S(2)}) async-start(f32[32,8,512]{2,1,0:T(8,128)} %bitcast.11), calls=%async_computation | async-start | bytes 1048576 | tf_op jit(solution)/shard_map/all_to_all | solution.py:425
  (30 other events, 771.9 us)

commit v13 on v11

--- a/solution.py
+++ b/solution.py
@@ -243,9 +243,9 @@
             terms_ref[...] = dot(high, pick) + (dot(middle, pick) + dot(low, pick))
 
 
-def chunk_step(place, block, sens, first, models_t, gates, obs, cell_index, terms, square, block_cells, last):
+def chunk_step(place, block, sens, first, skip, count, models_t, gates, obs, cell_index, terms, square, block_cells, last):
     spectra, soundings, cells = block.shape
-    rows = sens[0].shape[1]
+    rows = count * GROUP
     pieces = len(sens) + 1
     members = terms.shape[0]
     own_groups = soundings // (pieces * GROUP)
@@ -253,13 +253,13 @@
         functools.partial(chunk_kernel, pieces, block_cells, last),
         grid_spec=pltpu.PrefetchScalarGridSpec(
             num_scalar_prefetch=1,
-            grid=(rows // GROUP,),
+            grid=(count,),
             in_specs=[
-                pl.BlockSpec((spectra, GROUP, cells), lambda i, place: (0, place[1] * own_groups + first + i, 0))
+                pl.BlockSpec((spectra, GROUP, cells), lambda i, place: (0, place[1] * own_groups + first + skip + i, 0))
             ]
-            + [pl.BlockSpec((spectra, GROUP, cells), lambda i, place: (0, i, 0))] * len(sens)
+            + [pl.BlockSpec((spectra, GROUP, cells), lambda i, place: (0, skip + i, 0))] * len(sens)
             + [whole(a) for a in (*models_t, *gates)]
-            + [pl.BlockSpec((1, 1, obs.shape[2]), lambda i, place: (first + i, 0, 0)), whole(cell_index)]
+            + [pl.BlockSpec((1, 1, obs.shape[2]), lambda i, place: (first + skip + i, 0, 0)), whole(cell_index)]
             + [whole(terms), whole(square)],
             out_specs=[whole(terms), whole(square)],
         ),
@@ -415,9 +415,12 @@
         if i > 1:
             send(i)
         last = i == len(starts) - 1
-        terms, square = chunk_step(
-            place, block, received[i], start, models_t, wide, obs, cell_index, terms, square, block_cells, last
-        )
+        cuts = [0, sizes[i]] if sizes[i] < 3 else [0, sizes[i] // 2, sizes[i]]
+        for skip, end in zip(cuts, cuts[1:]):
+            terms, square = chunk_step(
+                place, block, received[i], start, skip, end - skip, models_t, wide, obs, cell_index, terms, square,
+                block_cells, last and end == sizes[i],
+            )
         done.append(square)
 
     slab = members // devices

time: 421 us -> 422 us (level)
  starting transfers between devices: 196 us -> 152 us
  waiting for transfers between devices: 119 us -> 157 us
  Pallas kernels: 72.3 us -> 79.8 us
    ppermute x45, starting transfers between devices: 193 us -> 146 us  [swap(): lax.ppermute(x, axis, [(i, i ^ k) for i in range(lax.axis_size(axis))])]
    ppermute x45, waiting for transfers between devices: 110 us -> 148 us  [swap(): lax.ppermute(x, axis, [(i, i ^ k) for i in range(lax.axis_size(axis))])]
    pallas_call x6 -> x9, Pallas kernels: 51 us -> 57.7 us  [chunk_step(): pl.pallas_call(functools.partial(chunk_kernel, pieces, block_cells, last)...]
    unnamed x65 -> x69, local copies, waits for them, and re-layouts: 11.7 us -> 8.98 us
  transfers between devices with their start and end apart: 46 -> 46, of which waited for: 12 -> 17; matrix products, arithmetic and copies ran while one was open for 3% -> 3% of each run, Pallas kernels for 15% -> 17%
where the time goes in v13:
time: 422 us; the launch traced here: 421 us
  waiting for transfers between devices  157 us (37%)
  starting transfers between devices  152 us (36%)
  Pallas kernels  79.8 us (19%)
  local copies, waits for them, and re-layouts  16.5 us (4%)
  blocking collectives  9.82 us (2%)
  other arithmetic  4.77 us (1%)
    ppermute x45, waiting for transfers between devices, swap(): lax.ppermute(x, axis, [(i, i ^ k) for i in range(lax.axis_size(axis))])  148 us
    ppermute x45, starting transfers between devices, swap(): lax.ppermute(x, axis, [(i, i ^ k) for i in range(lax.axis_size(axis))])  146 us
    pallas_call x9, Pallas kernels, chunk_step(): pl.pallas_call(functools.partial(chunk_kernel, pieces, block_cells, last)...  57.7 us
    pallas_call x6, Pallas kernels, pack(): pl.pallas_call(functools.partial(pack_kernel, distances, own, first, rows...  16.3 us
    all_to_all x1, blocking collectives, body(): back = lax.all_to_all(step, both, split_axis=0, concat_axis=0, tiled=True)  9.82 us
    all_to_all x1, waiting for transfers between devices, body(): got = lax.all_to_all(sent, both, split_axis=0, concat_axis=0, tiled=True)  9.03 us
    unnamed x69, local copies, waits for them, and re-layouts  8.98 us
  transfers between devices with their start and end apart: 46, of which 17 were waited for; matrix products, arithmetic and copies ran while one was open for 3% of the time, Pallas kernels for 17%

profile of v13, /device:TPU:0, one launch (start us, length us, event | category | flops | bytes accessed | tf_op | source)
XLA Modules:
  0.0 420.9 jit_solution(11703856027626337788)
XLA Ops:
  3.6 4.1 collective-permute-start
  13.6 15.5 %collective-permute-done.refs_0_.refs_1_ = f32[9,16,512]{2,1,0:T(8,128)S(1)} collective-permute-done((f32[9,16,512]{2,1,0:T(8,128)S(1)}, f32[9,16,512]{2,1,0:T(8,128)S(1)}, u32[]{:S(2)}, u32[]{:S(2)}) %collective-permute-start) | collective-permute-done | bytes 294944 | tf_op jit(solution)/shard_map/ppermute | solution.py:23
  38.7 12.8 %collective-permute-start.10 = (f32[8,32,512]{2,1,0:T(8,128)}, f32[8,32,512]{2,1,0:T(8,128)S(1)}, u32[]{:S(2)}, u32[]{:S(2)}) collective-permute-start(f32[8,32,512]{2,1,0:T(8,128)} %get-tuple-element.75), channel_id=1, source_target_pairs={{0,4},{1,5},{2,6},{3,7},{4,0},{5,1},{6,2},{7,3},{8,12},{9,13},{10,... | collective-permute-start | bytes 1572872 | tf_op jit(solution)/shard_map/ppermute | solution.py:23
  53.8 29.8 %collective-permute-done.5.refs_5_.refs_6_ = f32[9,16,512]{2,1,0:T(8,128)S(1)} collective-permute-done((f32[9,16,512]{2,1,0:T(8,128)S(1)}, f32[9,16,512]{2,1,0:T(8,128)S(1)}, u32[]{:S(2)}, u32[]{:S(2)}) %collective-permute-start.5) | collective-permute-done | bytes 294944 | tf_op jit(solution)/shard_map/ppermute | solution.py:23
  87.0 7.0 %collective-permute-done.9.refs_3_ = f32[264,256]{1,0:T(8,128)} collective-permute-done((f32[264,256]{1,0:T(8,128)}, f32[264,256]{1,0:T(8,128)}, u32[]{:S(2)}, u32[]{:S(2)}) %collective-permute-start.9) | collective-permute-done | bytes 270368 | tf_op jit(solution)/shard_map/ppermute | solution.py:23
  94.0 5.9 %collective-permute-done.8.refs_2_ = f32[264,256]{1,0:T(8,128)} collective-permute-done((f32[264,256]{1,0:T(8,128)}, f32[264,256]{1,0:T(8,128)}, u32[]{:S(2)}, u32[]{:S(2)}) %collective-permute-start.8) | collective-permute-done | bytes 270368 | tf_op jit(solution)/shard_map/ppermute | solution.py:23
  113.8 8.2 %collective-permute-start.11 = (f32[8,32,512]{2,1,0:T(8,128)}, f32[8,32,512]{2,1,0:T(8,128)S(1)}, u32[]{:S(2)}, u32[]{:S(2)}) collective-permute-start(f32[8,32,512]{2,1,0:T(8,128)} %get-tuple-element.76), channel_id=1, source_target_pairs={{0,4},{1,5},{2,6},{3,7},{4,0},{5,1},{6,2},{7,3},{8,12},{9,13},{10,... | collective-permute-start | bytes 1572872 | tf_op jit(solution)/shard_map/ppermute | solution.py:23
  123.9 5.1 %collective-permute-done.15.refs_4_ = f32[8,32,512]{2,1,0:T(8,128)S(1)} collective-permute-done((f32[8,32,512]{2,1,0:T(8,128)}, f32[8,32,512]{2,1,0:T(8,128)S(1)}, u32[]{:S(2)}, u32[]{:S(2)}) %collective-permute-start.15) | collective-permute-done | bytes 524320 | tf_op jit(solution)/shard_map/ppermute | solution.py:23
  130.8 5.6 %collective-permute-done.16.refs_5_ = f32[8,32,512]{2,1,0:T(8,128)S(1)} collective-permute-done((f32[8,32,512]{2,1,0:T(8,128)}, f32[8,32,512]{2,1,0:T(8,128)S(1)}, u32[]{:S(2)}, u32[]{:S(2)}) %collective-permute-start.16) | collective-permute-done | bytes 524320 | tf_op jit(solution)/shard_map/ppermute | solution.py:23
  140.2 39.5 %collective-permute-done.17.refs_6_ = f32[8,32,512]{2,1,0:T(8,128)S(1)} collective-permute-done((f32[8,32,512]{2,1,0:T(8,128)}, f32[8,32,512]{2,1,0:T(8,128)S(1)}, u32[]{:S(2)}, u32[]{:S(2)}) %collective-permute-start.17) | collective-permute-done | bytes 524320 | tf_op jit(solution)/shard_map/ppermute | solution.py:23
  180.5 4.4 %collective-permute-start.22 = (f32[8,32,512]{2,1,0:T(8,128)}, f32[8,32,512]{2,1,0:T(8,128)}, u32[]{:S(2)}, u32[]{:S(2)}) collective-permute-start(f32[8,32,512]{2,1,0:T(8,128)} %get-tuple-element.96), channel_id=1, source_target_pairs={{0,6},{1,7},{2,4},{3,5},{4,2},{5,3},{6,0},{7,1},{8,14},{9,15},{10,... | collective-permute-start | bytes 1572872 | tf_op jit(solution)/shard_map/ppermute | solution.py:23
  190.5 9.7 %collective-permute-done.11.refs_0_.refs_1_ = f32[8,32,512]{2,1,0:T(8,128)S(1)} collective-permute-done((f32[8,32,512]{2,1,0:T(8,128)}, f32[8,32,512]{2,1,0:T(8,128)S(1)}, u32[]{:S(2)}, u32[]{:S(2)}) %collective-permute-start.11) | collective-permute-done | bytes 524320 | tf_op jit(solution)/shard_map/ppermute | solution.py:23
  202.8 6.8 %chunk_step.9 = (f32[256,512]{1,0:T(8,128)}, f32[256,128]{1,0:T(8,128)S(1)}) custom-call(s32[2]{0:T(128)S(1)} %pad_add_fusion.place_ref, f32[8,1024,512]{2,1,0:T(8,128)} %bitcast.19, f32[9,16,512]{2,1,0:T(8,128)S(1)} %collective-permute-done.refs_0_.refs_1_, ...), custom_call_target="tpu_custom_call", output_to_operand_aliasing={{0}: (15, {}), {1}: (16, {})} | custom-call | flops 3221225472 | bytes 2097152 | tf_op jit(solution)/shard_map/chunk_step/pallas_call | solution.py:252
  212.9 15.4 %collective-permute-start.12 = (f32[8,24,512]{2,1,0:T(8,128)S(1)}, f32[8,24,512]{2,1,0:T(8,128)S(1)}, u32[]{:S(2)}, u32[]{:S(2)}) collective-permute-start(f32[8,24,512]{2,1,0:T(8,128)S(1)} %get-tuple-element.82), channel_id=1, source_target_pairs={{0,4},{1,5},{2,6},{3,7},{4,0},{5,1},{6,2},{7,3},{8,12},{9,13},{10,... | collective-permute-start | bytes 1179656 | tf_op jit(solution)/shard_map/ppermute | solution.py:23
  229.1 27.0 %collective-permute-start.40 = (f32[8,24,512]{2,1,0:T(8,128)S(1)}, f32[8,24,512]{2,1,0:T(8,128)S(1)}, u32[]{:S(2)}, u32[]{:S(2)}) collective-permute-start(f32[8,24,512]{2,1,0:T(8,128)S(1)} %get-tuple-element.118), channel_id=1, source_target_pairs={{0,3},{1,2},{2,1},{3,0},{4,7},{5,6},{6,5},{7,4},{8,11},{9,10},{10,... | collective-permute-start | bytes 1179656 | tf_op jit(solution)/shard_map/ppermute | solution.py:23
  256.1 6.8 %chunk_step.10 = (f32[256,512]{1,0:T(8,128)}, f32[256,128]{1,0:T(8,128)S(1)}) custom-call(s32[2]{0:T(128)S(1)} %pad_add_fusion.place_ref, f32[8,1024,512]{2,1,0:T(8,128)} %bitcast.21, f32[8,32,512]{2,1,0:T(8,128)S(1)} %collective-permute-done.10.refs_0_.refs_1_, ...), custom_call_target="tpu_custom_call", output_to_operand_aliasing={{0}: (15, {}), {1}: (16, {})} | custom-call | flops 3221225472 | bytes 2097152 | tf_op jit(solution)/shard_map/chunk_step/pallas_call | solution.py:252
  264.1 4.4 %collective-permute-start.41 = (f32[8,24,512]{2,1,0:T(8,128)S(1)}, f32[8,24,512]{2,1,0:T(8,128)S(1)}, u32[]{:S(2)}, u32[]{:S(2)}) collective-permute-start(f32[8,24,512]{2,1,0:T(8,128)S(1)} %get-tuple-element.119), channel_id=1, source_target_pairs={{0,6},{1,7},{2,4},{3,5},{4,2},{5,3},{6,0},{7,1},{8,14},{9,15},{10,... | collective-permute-start | bytes 1179656 | tf_op jit(solution)/shard_map/ppermute | solution.py:23
  268.5 10.4 %collective-permute-done.12.refs_0_.refs_1_ = f32[8,24,512]{2,1,0:T(8,128)S(1)} collective-permute-done((f32[8,24,512]{2,1,0:T(8,128)S(1)}, f32[8,24,512]{2,1,0:T(8,128)S(1)}, u32[]{:S(2)}, u32[]{:S(2)}) %collective-permute-start.12) | collective-permute-done | bytes 393248 | tf_op jit(solution)/shard_map/ppermute | solution.py:23
  280.7 6.8 %chunk_step.11 = (f32[256,512]{1,0:T(8,128)}, f32[256,128]{1,0:T(8,128)S(1)}) custom-call(s32[2]{0:T(128)S(1)} %pad_add_fusion.place_ref, f32[8,1024,512]{2,1,0:T(8,128)} %bitcast.22, f32[8,32,512]{2,1,0:T(8,128)S(1)} %collective-permute-done.10.refs_0_.refs_1_, ...), custom_call_target="tpu_custom_call", output_to_operand_aliasing={{0}: (15, {}), {1}: (16, {})} | custom-call | flops 3221225472 | bytes 2097152 | tf_op jit(solution)/shard_map/chunk_step/pallas_call | solution.py:252
  289.7 5.2 %collective-permute-start.43 = (f32[8,24,512]{2,1,0:T(8,128)S(1)}, f32[8,24,512]{2,1,0:T(8,128)S(1)}, u32[]{:S(2)}, u32[]{:S(2)}) collective-permute-start(f32[8,24,512]{2,1,0:T(8,128)S(1)} %get-tuple-element.121), channel_id=1, source_target_pairs={{0,5},{1,4},{2,7},{3,6},{4,1},{5,0},{6,3},{7,2},{8,13},{9,12},{10,... | collective-permute-start | bytes 1179656 | tf_op jit(solution)/shard_map/ppermute | solution.py:23
  295.6 7.1 %chunk_step.12 = (f32[256,512]{1,0:T(8,128)}, f32[256,128]{1,0:T(8,128)S(1)}) custom-call(s32[2]{0:T(128)S(1)} %pad_add_fusion.place_ref, f32[8,1024,512]{2,1,0:T(8,128)} %bitcast.24, f32[8,32,512]{2,1,0:T(8,128)S(1)} %collective-permute-done.11.refs_0_.refs_1_, ...), custom_call_target="tpu_custom_call", output_to_operand_aliasing={{0}: (15, {}), {1}: (16, {})} | custom-call | flops 3221225472 | bytes 2097152 | tf_op jit(solution)/shard_map/chunk_step/pallas_call | solution.py:252
  305.9 14.7 %collective-permute-start.34 = (f32[8,16,512]{2,1,0:T(8,128)S(1)}, f32[8,16,512]{2,1,0:T(8,128)S(1)}, u32[]{:S(2)}, u32[]{:S(2)}) collective-permute-start(f32[8,16,512]{2,1,0:T(8,128)S(1)} %get-tuple-element.112), channel_id=1, source_target_pairs={{0,3},{1,2},{2,1},{3,0},{4,7},{5,6},{6,5},{7,4},{8,11},{9,10},{10,... | collective-permute-start | bytes 786440 | tf_op jit(solution)/shard_map/ppermute | solution.py:23
  320.6 8.4 %collective-permute-done.19.refs_0_.refs_1_ = f32[8,16,512]{2,1,0:T(8,128)S(1)} collective-permute-done((f32[8,16,512]{2,1,0:T(8,128)S(1)}, f32[8,16,512]{2,1,0:T(8,128)S(1)}, u32[]{:S(2)}, u32[]{:S(2)}) %collective-permute-start.19) | collective-permute-done | bytes 262176 | tf_op jit(solution)/shard_map/ppermute | solution.py:23
  329.1 5.1 %collective-permute-start.35 = (f32[8,16,512]{2,1,0:T(8,128)S(1)}, f32[8,16,512]{2,1,0:T(8,128)S(1)}, u32[]{:S(2)}, u32[]{:S(2)}) collective-permute-start(f32[8,16,512]{2,1,0:T(8,128)S(1)} %get-tuple-element.113), channel_id=1, source_target_pairs={{0,6},{1,7},{2,4},{3,5},{4,2},{5,3},{6,0},{7,1},{8,14},{9,15},{10,... | collective-permute-start | bytes 786440 | tf_op jit(solution)/shard_map/ppermute | solution.py:23
  334.2 7.0 %chunk_step.13 = (f32[256,512]{1,0:T(8,128)}, f32[256,128]{1,0:T(8,128)S(1)}) custom-call(s32[2]{0:T(128)S(1)} %pad_add_fusion.place_ref, f32[8,1024,512]{2,1,0:T(8,128)} %bitcast.25, f32[8,32,512]{2,1,0:T(8,128)S(1)} %collective-permute-done.11.refs_0_.refs_1_, ...), custom_call_target="tpu_custom_call", output_to_operand_aliasing={{0}: (15, {}), {1}: (16, {})} | custom-call | flops 3221225472 | bytes 2097152 | tf_op jit(solution)/shard_map/chunk_step/pallas_call | solution.py:252
  346.3 4.6 %chunk_step.14 = (f32[256,512]{1,0:T(8,128)}, f32[256,128]{1,0:T(8,128)S(1)}) custom-call(s32[2]{0:T(128)S(1)} %pad_add_fusion.place_ref, f32[8,1024,512]{2,1,0:T(8,128)} %bitcast.27, f32[8,24,512]{2,1,0:T(8,128)S(1)} %collective-permute-done.12.refs_0_.refs_1_, ...), custom_call_target="tpu_custom_call", output_to_operand_aliasing={{0}: (15, {}), {1}: (16, {})} | custom-call | flops 1610612736 | bytes 1048576 | tf_op jit(solution)/shard_map/chunk_step/pallas_call | solution.py:252
  356.2 6.8 %chunk_step.15 = (f32[256,512]{1,0:T(8,128)}, f32[256,128]{1,0:T(8,128)S(1)}) custom-call(s32[2]{0:T(128)S(1)} %pad_add_fusion.place_ref, f32[8,1024,512]{2,1,0:T(8,128)} %bitcast.28, f32[8,24,512]{2,1,0:T(8,128)S(1)} %collective-permute-done.12.refs_0_.refs_1_, ...), custom_call_target="tpu_custom_call", output_to_operand_aliasing={{0}: (15, {}), {1}: (16, {})} | custom-call | flops 3221225472 | bytes 2097152 | tf_op jit(solution)/shard_map/chunk_step/pallas_call | solution.py:252
  372.5 6.8 %chunk_step.16 = (f32[256,512]{1,0:T(8,128)}, f32[256,128]{1,0:T(8,128)S(1)}) custom-call(s32[2]{0:T(128)S(1)} %pad_add_fusion.place_ref, f32[8,1024,512]{2,1,0:T(8,128)} %bitcast.29, f32[8,16,512]{2,1,0:T(8,128)S(1)} %collective-permute-done.19.refs_0_.refs_1_, ...), custom_call_target="tpu_custom_call", output_to_operand_aliasing={{0}: (15, {}), {1}: (16, {})} | custom-call | flops 3221225472 | bytes 2097152 | tf_op jit(solution)/shard_map/chunk_step/pallas_call | solution.py:252
  381.8 5.1 %chunk_step.17 = (f32[256,512]{1,0:T(8,128)}, f32[256,128]{1,0:T(8,128)S(1)}) custom-call(s32[2]{0:T(128)S(1)} %pad_add_fusion.place_ref, f32[8,1024,512]{2,1,0:T(8,128)} %bitcast.30, f32[8,8,512]{2,1,0:T(8,128)S(1)} %collective-permute-done.26.refs_1_, ...), custom_call_target="tpu_custom_call", output_to_operand_aliasing={{0}: (15, {}), {1}: (16, {})} | custom-call | flops 1610612736 | bytes 1048576 | tf_op jit(solution)/shard_map/chunk_step/pallas_call | solution.py:252
  386.9 6.0 %all-to-all-start = ((f32[32,8,512]{2,1,0:T(8,128)}), f32[32,8,512]{2,1,0:T(8,128)S(1)}, u32[]{:S(2)}, u32[]{:S(2)}) async-start(f32[32,8,512]{2,1,0:T(8,128)} %bitcast.11), calls=%async_computation | async-start | bytes 1048576 | tf_op jit(solution)/shard_map/all_to_all | solution.py:428
  400.2 9.0 %all-to-all-done.got_ref = f32[32,8,512]{2,1,0:T(8,128)S(1)} async-done(((f32[32,8,512]{2,1,0:T(8,128)}), f32[32,8,512]{2,1,0:T(8,128)S(1)}, u32[]{:S(2)}, u32[]{:S(2)}) %all-to-all-start) | async-done | bytes 524320 | tf_op jit(solution)/shard_map/all_to_all | solution.py:428
  410.1 9.8 %all_to_all.10.back_ref = f32[32,8,128]{2,1,0:T(8,128)S(1)} all-to-all(f32[32,8,128]{2,1,0:T(8,128)S(1)} %gradient_step.1), channel_id=1, replica_groups=mesh['tile'=4,'freq'=8] {'tile','freq'}, dimensions={0} | all-to-all | bytes 262144 | tf_op jit(solution)/shard_map/all_to_all | solution.py:431
  (170 shorter events, 99.1 us)
Async XLA Ops:
  3.6 25.4 %collective-permute-start = (f32[9,16,512]{2,1,0:T(8,128)S(1)}, f32[9,16,512]{2,1,0:T(8,128)S(1)}, u32[]{:S(2)}, u32[]{:S(2)}) collective-permute-start(f32[9,16,512]{2,1,0:T(8,128)S(1)} %get-tuple-element.68), channel_id=1, source_target_pairs={{0,4},{1,5},{2,6},{3,7},{4,0},{5,1},{6,2},{7,3},{8,12},{9,13},{10,... | collective-permute-start | bytes 884744 | tf_op jit(solution)/shard_map/ppermute | solution.py:23
  10.0 28.7 %collective-permute-start.2 = (f32[9,16,512]{2,1,0:T(8,128)S(1)}, f32[9,16,512]{2,1,0:T(8,128)S(1)}, u32[]{:S(2)}, u32[]{:S(2)}) collective-permute-start(f32[9,16,512]{2,1,0:T(8,128)S(1)} %get-tuple-element.70), channel_id=1, source_target_pairs={{0,3},{1,2},{2,1},{3,0},{4,7},{5,6},{6,5},{7,4},{8,11},{9,10},{10,... | collective-permute-start | bytes 884744 | tf_op jit(solution)/shard_map/ppermute | solution.py:23
  10.2 41.3 %collective-permute-start.3 = (f32[9,16,512]{2,1,0:T(8,128)S(1)}, f32[9,16,512]{2,1,0:T(8,128)S(1)}, u32[]{:S(2)}, u32[]{:S(2)}) collective-permute-start(f32[9,16,512]{2,1,0:T(8,128)S(1)} %get-tuple-element.71), channel_id=1, source_target_pairs={{0,6},{1,7},{2,4},{3,5},{4,2},{5,3},{6,0},{7,1},{8,14},{9,15},{10,... | collective-permute-start | bytes 884744 | tf_op jit(solution)/shard_map/ppermute | solution.py:23
  13.1 40.7 %collective-permute-start.4 = (f32[9,16,512]{2,1,0:T(8,128)S(1)}, f32[9,16,512]{2,1,0:T(8,128)S(1)}, u32[]{:S(2)}, u32[]{:S(2)}) collective-permute-start(f32[9,16,512]{2,1,0:T(8,128)S(1)} %get-tuple-element.72), channel_id=1, source_target_pairs={{0,2},{1,3},{2,0},{3,1},{4,6},{5,7},{6,4},{7,5},{8,10},{9,11},{10,... | collective-permute-start | bytes 884744 | tf_op jit(solution)/shard_map/ppermute | solution.py:23
  29.1 54.5 %collective-permute-start.5 = (f32[9,16,512]{2,1,0:T(8,128)S(1)}, f32[9,16,512]{2,1,0:T(8,128)S(1)}, u32[]{:S(2)}, u32[]{:S(2)}) collective-permute-start(f32[9,16,512]{2,1,0:T(8,128)S(1)} %get-tuple-element.73), channel_id=1, source_target_pairs={{0,5},{1,4},{2,7},{3,6},{4,1},{5,0},{6,3},{7,2},{8,13},{9,12},{10,... | collective-permute-start | bytes 884744 | tf_op jit(solution)/shard_map/ppermute | solution.py:23
  29.8 53.8 %collective-permute-start.6 = (f32[9,16,512]{2,1,0:T(8,128)S(1)}, f32[9,16,512]{2,1,0:T(8,128)S(1)}, u32[]{:S(2)}, u32[]{:S(2)}) collective-permute-start(f32[9,16,512]{2,1,0:T(8,128)S(1)} %get-tuple-element.74), channel_id=1, source_target_pairs={{0,1},{1,0},{2,3},{3,2},{4,5},{5,4},{6,7},{7,6},{8,9},{9,8},{10,11... | collective-permute-start | bytes 884744 | tf_op jit(solution)/shard_map/ppermute | solution.py:23
  38.7 63.6 %collective-permute-start.10 = (f32[8,32,512]{2,1,0:T(8,128)}, f32[8,32,512]{2,1,0:T(8,128)S(1)}, u32[]{:S(2)}, u32[]{:S(2)}) collective-permute-start(f32[8,32,512]{2,1,0:T(8,128)} %get-tuple-element.75), channel_id=1, source_target_pairs={{0,4},{1,5},{2,6},{3,7},{4,0},{5,1},{6,2},{7,3},{8,12},{9,13},{10,... | collective-permute-start | bytes 1572872 | tf_op jit(solution)/shard_map/ppermute | solution.py:23
  51.5 52.4 %collective-permute-start.13 = (f32[8,32,512]{2,1,0:T(8,128)}, f32[8,32,512]{2,1,0:T(8,128)S(1)}, u32[]{:S(2)}, u32[]{:S(2)}) collective-permute-start(f32[8,32,512]{2,1,0:T(8,128)} %get-tuple-element.83), channel_id=1, source_target_pairs={{0,7},{1,6},{2,5},{3,4},{4,3},{5,2},{6,1},{7,0},{8,15},{9,14},{10,... | collective-permute-start | bytes 1572872 | tf_op jit(solution)/shard_map/ppermute | solution.py:23
  99.9 29.1 %collective-permute-start.15 = (f32[8,32,512]{2,1,0:T(8,128)}, f32[8,32,512]{2,1,0:T(8,128)S(1)}, u32[]{:S(2)}, u32[]{:S(2)}) collective-permute-start(f32[8,32,512]{2,1,0:T(8,128)} %copy-done.28), channel_id=1, source_target_pairs={{0,6},{1,7},{2,4},{3,5},{4,2},{5,3},{6,0},{7,1},{8,14},{9,15},{10,... | collective-permute-start | bytes 1572872 | tf_op jit(solution)/shard_map/ppermute | solution.py:23
  102.3 34.0 %collective-permute-start.16 = (f32[8,32,512]{2,1,0:T(8,128)}, f32[8,32,512]{2,1,0:T(8,128)S(1)}, u32[]{:S(2)}, u32[]{:S(2)}) collective-permute-start(f32[8,32,512]{2,1,0:T(8,128)} %copy-done.27), channel_id=1, source_target_pairs={{0,2},{1,3},{2,0},{3,1},{4,6},{5,7},{6,4},{7,5},{8,10},{9,11},{10,... | collective-permute-start | bytes 1572872 | tf_op jit(solution)/shard_map/ppermute | solution.py:23
  102.3 77.4 %collective-permute-start.17 = (f32[8,32,512]{2,1,0:T(8,128)}, f32[8,32,512]{2,1,0:T(8,128)S(1)}, u32[]{:S(2)}, u32[]{:S(2)}) collective-permute-start(f32[8,32,512]{2,1,0:T(8,128)} %copy-done.24), channel_id=1, source_target_pairs={{0,5},{1,4},{2,7},{3,6},{4,1},{5,0},{6,3},{7,2},{8,13},{9,12},{10,... | collective-permute-start | bytes 1572872 | tf_op jit(solution)/shard_map/ppermute | solution.py:23
  103.9 81.0 %collective-permute-start.18 = (f32[8,32,512]{2,1,0:T(8,128)}, f32[8,32,512]{2,1,0:T(8,128)S(1)}, u32[]{:S(2)}, u32[]{:S(2)}) collective-permute-start(f32[8,32,512]{2,1,0:T(8,128)} %copy-done.23), channel_id=1, source_target_pairs={{0,1},{1,0},{2,3},{3,2},{4,5},{5,4},{6,7},{7,6},{8,9},{9,8},{10,11... | collective-permute-start | bytes 1572872 | tf_op jit(solution)/shard_map/ppermute | solution.py:23
  113.8 86.4 %collective-permute-start.11 = (f32[8,32,512]{2,1,0:T(8,128)}, f32[8,32,512]{2,1,0:T(8,128)S(1)}, u32[]{:S(2)}, u32[]{:S(2)}) collective-permute-start(f32[8,32,512]{2,1,0:T(8,128)} %get-tuple-element.76), channel_id=1, source_target_pairs={{0,4},{1,5},{2,6},{3,7},{4,0},{5,1},{6,2},{7,3},{8,12},{9,13},{10,... | collective-permute-start | bytes 1572872 | tf_op jit(solution)/shard_map/ppermute | solution.py:23
  129.8 83.0 %collective-permute-start.20 = (f32[8,32,512]{2,1,0:T(8,128)}, f32[8,32,512]{2,1,0:T(8,128)S(1)}, u32[]{:S(2)}, u32[]{:S(2)}) collective-permute-start(f32[8,32,512]{2,1,0:T(8,128)} %get-tuple-element.94), channel_id=1, source_target_pairs={{0,7},{1,6},{2,5},{3,4},{4,3},{5,2},{6,1},{7,0},{8,15},{9,14},{10,... | collective-permute-start | bytes 1572872 | tf_op jit(solution)/shard_map/ppermute | solution.py:23
  137.2 91.1 %collective-permute-start.21 = (f32[8,32,512]{2,1,0:T(8,128)}, f32[8,32,512]{2,1,0:T(8,128)}, u32[]{:S(2)}, u32[]{:S(2)}) collective-permute-start(f32[8,32,512]{2,1,0:T(8,128)} %get-tuple-element.95), channel_id=1, source_target_pairs={{0,3},{1,2},{2,1},{3,0},{4,7},{5,6},{6,5},{7,4},{8,11},{9,10},{10,... | collective-permute-start | bytes 1572872 | tf_op jit(solution)/shard_map/ppermute | solution.py:23
  180.5 47.7 %collective-permute-start.22 = (f32[8,32,512]{2,1,0:T(8,128)}, f32[8,32,512]{2,1,0:T(8,128)}, u32[]{:S(2)}, u32[]{:S(2)}) collective-permute-start(f32[8,32,512]{2,1,0:T(8,128)} %get-tuple-element.96), channel_id=1, source_target_pairs={{0,6},{1,7},{2,4},{3,5},{4,2},{5,3},{6,0},{7,1},{8,14},{9,15},{10,... | collective-permute-start | bytes 1572872 | tf_op jit(solution)/shard_map/ppermute | solution.py:23
  185.7 43.4 %collective-permute-start.23 = (f32[8,32,512]{2,1,0:T(8,128)}, f32[8,32,512]{2,1,0:T(8,128)}, u32[]{:S(2)}, u32[]{:S(2)}) collective-permute-start(f32[8,32,512]{2,1,0:T(8,128)} %get-tuple-element.97), channel_id=1, source_target_pairs={{0,2},{1,3},{2,0},{3,1},{4,6},{5,7},{6,4},{7,5},{8,10},{9,11},{10,... | collective-permute-start | bytes 1572872 | tf_op jit(solution)/shard_map/ppermute | solution.py:23
  200.2 63.9 %collective-permute-start.24 = (f32[8,32,512]{2,1,0:T(8,128)S(1)}, f32[8,32,512]{2,1,0:T(8,128)S(1)}, u32[]{:S(2)}, u32[]{:S(2)}) collective-permute-start(f32[8,32,512]{2,1,0:T(8,128)S(1)} %copy-done.26), channel_id=1, source_target_pairs={{0,5},{1,4},{2,7},{3,6},{4,1},{5,0},{6,3},{7,2},{8,13},{9,12},{10,... | collective-permute-start | bytes 1572872 | tf_op jit(solution)/shard_map/ppermute | solution.py:23
  212.9 66.0 %collective-permute-start.12 = (f32[8,24,512]{2,1,0:T(8,128)S(1)}, f32[8,24,512]{2,1,0:T(8,128)S(1)}, u32[]{:S(2)}, u32[]{:S(2)}) collective-permute-start(f32[8,24,512]{2,1,0:T(8,128)S(1)} %get-tuple-element.82), channel_id=1, source_target_pairs={{0,4},{1,5},{2,6},{3,7},{4,0},{5,1},{6,2},{7,3},{8,12},{9,13},{10,... | collective-permute-start | bytes 1179656 | tf_op jit(solution)/shard_map/ppermute | solution.py:23
  228.2 61.4 %collective-permute-start.25 = (f32[8,32,512]{2,1,0:T(8,128)S(1)}, f32[8,32,512]{2,1,0:T(8,128)S(1)}, u32[]{:S(2)}, u32[]{:S(2)}) collective-permute-start(f32[8,32,512]{2,1,0:T(8,128)S(1)} %copy-done.22), channel_id=1, source_target_pairs={{0,1},{1,0},{2,3},{3,2},{4,5},{5,4},{6,7},{7,6},{8,9},{9,8},{10,11... | collective-permute-start | bytes 1572872 | tf_op jit(solution)/shard_map/ppermute | solution.py:23
  228.2 66.7 %collective-permute-start.39 = (f32[8,24,512]{2,1,0:T(8,128)S(1)}, f32[8,24,512]{2,1,0:T(8,128)S(1)}, u32[]{:S(2)}, u32[]{:S(2)}) collective-permute-start(f32[8,24,512]{2,1,0:T(8,128)S(1)} %get-tuple-element.117), channel_id=1, source_target_pairs={{0,7},{1,6},{2,5},{3,4},{4,3},{5,2},{6,1},{7,0},{8,15},{9,14},{10,... | collective-permute-start | bytes 1179656 | tf_op jit(solution)/shard_map/ppermute | solution.py:23
  229.1 65.8 %collective-permute-start.40 = (f32[8,24,512]{2,1,0:T(8,128)S(1)}, f32[8,24,512]{2,1,0:T(8,128)S(1)}, u32[]{:S(2)}, u32[]{:S(2)}) collective-permute-start(f32[8,24,512]{2,1,0:T(8,128)S(1)} %get-tuple-element.118), channel_id=1, source_target_pairs={{0,3},{1,2},{2,1},{3,0},{4,7},{5,6},{6,5},{7,4},{8,11},{9,10},{10,... | collective-permute-start | bytes 1179656 | tf_op jit(solution)/shard_map/ppermute | solution.py:23
  264.1 38.6 %collective-permute-start.41 = (f32[8,24,512]{2,1,0:T(8,128)S(1)}, f32[8,24,512]{2,1,0:T(8,128)S(1)}, u32[]{:S(2)}, u32[]{:S(2)}) collective-permute-start(f32[8,24,512]{2,1,0:T(8,128)S(1)} %get-tuple-element.119), channel_id=1, source_target_pairs={{0,6},{1,7},{2,4},{3,5},{4,2},{5,3},{6,0},{7,1},{8,14},{9,15},{10,... | collective-permute-start | bytes 1179656 | tf_op jit(solution)/shard_map/ppermute | solution.py:23
  278.9 27.0 %collective-permute-start.42 = (f32[8,24,512]{2,1,0:T(8,128)S(1)}, f32[8,24,512]{2,1,0:T(8,128)S(1)}, u32[]{:S(2)}, u32[]{:S(2)}) collective-permute-start(f32[8,24,512]{2,1,0:T(8,128)S(1)} %get-tuple-element.120), channel_id=1, source_target_pairs={{0,2},{1,3},{2,0},{3,1},{4,6},{5,7},{6,4},{7,5},{8,10},{9,11},{10,... | collective-permute-start | bytes 1179656 | tf_op jit(solution)/shard_map/ppermute | solution.py:23
  289.7 54.2 %collective-permute-start.43 = (f32[8,24,512]{2,1,0:T(8,128)S(1)}, f32[8,24,512]{2,1,0:T(8,128)S(1)}, u32[]{:S(2)}, u32[]{:S(2)}) collective-permute-start(f32[8,24,512]{2,1,0:T(8,128)S(1)} %get-tuple-element.121), channel_id=1, source_target_pairs={{0,5},{1,4},{2,7},{3,6},{4,1},{5,0},{6,3},{7,2},{8,13},{9,12},{10,... | collective-permute-start | bytes 1179656 | tf_op jit(solution)/shard_map/ppermute | solution.py:23
  294.9 49.0 %collective-permute-start.44 = (f32[8,24,512]{2,1,0:T(8,128)S(1)}, f32[8,24,512]{2,1,0:T(8,128)S(1)}, u32[]{:S(2)}, u32[]{:S(2)}) collective-permute-start(f32[8,24,512]{2,1,0:T(8,128)S(1)} %get-tuple-element.122), channel_id=1, source_target_pairs={{0,1},{1,0},{2,3},{3,2},{4,5},{5,4},{6,7},{7,6},{8,9},{9,8},{10,11... | collective-permute-start | bytes 1179656 | tf_op jit(solution)/shard_map/ppermute | solution.py:23
  294.9 34.1 %collective-permute-start.19 = (f32[8,16,512]{2,1,0:T(8,128)S(1)}, f32[8,16,512]{2,1,0:T(8,128)S(1)}, u32[]{:S(2)}, u32[]{:S(2)}) collective-permute-start(f32[8,16,512]{2,1,0:T(8,128)S(1)} %get-tuple-element.93), channel_id=1, source_target_pairs={{0,4},{1,5},{2,6},{3,7},{4,0},{5,1},{6,2},{7,3},{8,12},{9,13},{10,... | collective-permute-start | bytes 786440 | tf_op jit(solution)/shard_map/ppermute | solution.py:23
  302.7 48.2 %collective-permute-start.33 = (f32[8,16,512]{2,1,0:T(8,128)S(1)}, f32[8,16,512]{2,1,0:T(8,128)S(1)}, u32[]{:S(2)}, u32[]{:S(2)}) collective-permute-start(f32[8,16,512]{2,1,0:T(8,128)S(1)} %get-tuple-element.111), channel_id=1, source_target_pairs={{0,7},{1,6},{2,5},{3,4},{4,3},{5,2},{6,1},{7,0},{8,15},{9,14},{10,... | collective-permute-start | bytes 786440 | tf_op jit(solution)/shard_map/ppermute | solution.py:23
  305.9 45.1 %collective-permute-start.34 = (f32[8,16,512]{2,1,0:T(8,128)S(1)}, f32[8,16,512]{2,1,0:T(8,128)S(1)}, u32[]{:S(2)}, u32[]{:S(2)}) collective-permute-start(f32[8,16,512]{2,1,0:T(8,128)S(1)} %get-tuple-element.112), channel_id=1, source_target_pairs={{0,3},{1,2},{2,1},{3,0},{4,7},{5,6},{6,5},{7,4},{8,11},{9,10},{10,... | collective-permute-start | bytes 786440 | tf_op jit(solution)/shard_map/ppermute | solution.py:23
  329.1 24.3 %collective-permute-start.35 = (f32[8,16,512]{2,1,0:T(8,128)S(1)}, f32[8,16,512]{2,1,0:T(8,128)S(1)}, u32[]{:S(2)}, u32[]{:S(2)}) collective-permute-start(f32[8,16,512]{2,1,0:T(8,128)S(1)} %get-tuple-element.113), channel_id=1, source_target_pairs={{0,6},{1,7},{2,4},{3,5},{4,2},{5,3},{6,0},{7,1},{8,14},{9,15},{10,... | collective-permute-start | bytes 786440 | tf_op jit(solution)/shard_map/ppermute | solution.py:23
  344.0 22.4 %collective-permute-start.37 = (f32[8,16,512]{2,1,0:T(8,128)S(1)}, f32[8,16,512]{2,1,0:T(8,128)S(1)}, u32[]{:S(2)}, u32[]{:S(2)}) collective-permute-start(f32[8,16,512]{2,1,0:T(8,128)S(1)} %get-tuple-element.115), channel_id=1, source_target_pairs={{0,5},{1,4},{2,7},{3,6},{4,1},{5,0},{6,3},{7,2},{8,13},{9,12},{10,... | collective-permute-start | bytes 786440 | tf_op jit(solution)/shard_map/ppermute | solution.py:23
  386.9 22.4 %all-to-all-start = ((f32[32,8,512]{2,1,0:T(8,128)}), f32[32,8,512]{2,1,0:T(8,128)S(1)}, u32[]{:S(2)}, u32[]{:S(2)}) async-start(f32[32,8,512]{2,1,0:T(8,128)} %bitcast.11), calls=%async_computation | async-start | bytes 1048576 | tf_op jit(solution)/shard_map/all_to_all | solution.py:428
  (48 other events, 1062.8 us)
